TPU v7x, 32 devices: a whole 2x2x4 slice. The times are simulated.
32 devices in a mesh: grp: 2 (over y), seq: 16 (over z, x, core).
Axes of the slice: x: 2, y: 2, z: 4, core: 2. Of those that a mesh axis runs over, the one named last changes fastest.
Arguments:
- student_rows: bfloat16 [16384, 3584], P(('grp', 'seq')), parts along dimension 0, may hold values from -6 to 6
- teacher_rows: bfloat16 [16384, 4608], P(('grp', 'seq')), parts along dimension 0, may hold values from -6 to 6
- student_head: bfloat16 [2048, 3584], P('seq'), may hold values from -0.09375 to 0.09375
- teacher_head: bfloat16 [2048, 4608], P('seq'), may hold values from -0.09375 to 0.09375
- student_lse: bfloat16 [16384], P(('grp', 'seq')), parts along dimension 0, may hold values from 0.5 to 2.5
- teacher_lse: bfloat16 [16384], P(('grp', 'seq')), parts along dimension 0, may hold values from 0.5 to 2.5
- targets: int32 [16384], P(('grp', 'seq')), parts along dimension 0, may hold values from 0 to 2047
Outputs:
- head_grad: bfloat16 [4096, 3584], P(('grp', 'seq')), parts along dimension 0
- rows_grad: bfloat16 [16384, 3584], P(('grp', 'seq')), parts along dimension 0
- row_loss: float32 [16384], P(('grp', 'seq')), parts along dimension 0
There are 2 independent parts, one for each index of `grp`. A program takes and returns all parts, laid end to end along the dimension named above; an argument that names none is the same for every part. Nothing has to cross between parts.
All inputs are finite; a program needn't handle non-finite values.
Results may differ from a plain program's by a relative error of at most 0.006.
Values may be sent and summed in bfloat16 or wider, within the bound.
No kernel may reach another device: no remote copies, remote signals or barrier semaphores. Data moves between devices by JAX's collectives and lax.ppermute only.
A program may use at most 64 MiB of HBM per device.

v0:
```python
import jax
import jax.numpy as jnp
from jax import lax
from jax.sharding import PartitionSpec as P

STEPS = 4


hard_weight = 0.5


def passed_along(value, axis, steps):
    count = lax.axis_size(axis)
    pairs = [(source, (source + steps) % count) for source in range(count)]
    return lax.ppermute(value, axis, pairs)


def panel_terms(
    student_block,
    teacher_block,
    student_norm,
    teacher_norm,
    target_block,
    student_panel,
    teacher_panel,
    panel,
):
    width = student_panel.shape[0]
    zs = lax.dot_general(
        student_block, student_panel, (((1,), (1,)), ((), ())), preferred_element_type=jnp.float32
    )
    zt = lax.dot_general(
        teacher_block, teacher_panel, (((1,), (1,)), ((), ())), preferred_element_type=jnp.float32
    )
    ls = zs - student_norm.astype(jnp.float32)[:, None]
    lt = zt - teacher_norm.astype(jnp.float32)[:, None]
    ps = jnp.exp(ls)
    pt = jnp.exp(lt)
    vocab_ids = panel * width + jnp.arange(width, dtype=jnp.int32)
    onehot = (target_block[:, None] == vocab_ids[None, :]).astype(jnp.float32)
    scores = ((1.0 + hard_weight) * ps - pt - hard_weight * onehot).astype(jnp.bfloat16)
    losses = jnp.sum(pt * (lt - ls) - hard_weight * onehot * ls, axis=1)
    rows_part = jnp.dot(scores, student_panel, preferred_element_type=jnp.float32)
    head_part = lax.dot_general(
        scores, student_block, (((0,), (0,)), ((), ())), preferred_element_type=jnp.float32
    )
    return (rows_part, losses, head_part)


def body(student_rows, teacher_rows, student_head, teacher_head, student_lse, teacher_lse, targets):
    device = lax.axis_index("seq")
    count = lax.axis_size("seq")
    panels = (student_head, teacher_head)
    rows_total = jnp.zeros(student_rows.shape, jnp.float32)
    loss_total = jnp.zeros(targets.shape, jnp.float32)
    arrived = None
    head_acc = None
    for step in range(STEPS):
        current = panels
        if step < STEPS - 1:
            panels = passed_along((current[0], current[1]), "seq", 1)
        panel = (device - step) % count
        rows_part, losses, head_part = panel_terms(
            student_rows,
            teacher_rows,
            student_lse,
            teacher_lse,
            targets,
            current[0],
            current[1],
            panel,
        )
        rows_total = rows_total + rows_part
        loss_total = loss_total + losses
        if step == 0:
            head_acc = head_part.astype(jnp.bfloat16)
        else:
            head_acc = (arrived.astype(jnp.float32) + head_part).astype(jnp.bfloat16)
        if step < STEPS - 1:
            arrived = passed_along(head_acc, "seq", 1)
    head_grad = passed_along(head_acc, "seq", -(STEPS - 1))
    return (head_grad, rows_total.astype(jnp.bfloat16), loss_total)


def solution(mesh):
    placed = (
        P(("grp", "seq"), None),
        P(("grp", "seq"), None),
        P("seq", None),
        P("seq", None),
        P(("grp", "seq")),
        P(("grp", "seq")),
        P(("grp", "seq")),
    )
    return jax.shard_map(
        body,
        mesh=mesh,
        in_specs=placed,
        out_specs=(P(("grp", "seq"), None), P(("grp", "seq"), None), P(("grp", "seq"))),
        check_vma=False,
    )
```

profile of v0, /device:TPU:0, one launch (start us, length us, event | category | flops | bytes accessed | tf_op | source)
XLA Modules:
  0.0 142.9 jit_solution(2500193660938152858)
XLA Ops:
  1.1 2.6 %collective-permute-start.1 = (bf16[128,3584]{1,0:T(8,128)(2,1)}, bf16[128,3584]{1,0:T(8,128)(2,1)S(1)}, u32[]{:S(2)}, u32[]{:S(2)}) collective-permute-start(bf16[128,3584]{1,0:T(8,128)(2,1)} %param.9), channel_id=1, source_target_pairs={{0,1},{1,2},{2,3},{3,4},{4,5},{5,6},{6,7},{7,8},{8,9},{9,10},{10,1... | collective-permute-start | bytes 2752520 | tf_op jit(solution)/shard_map/ppermute | solution.py:15
  3.7 0.8 convert_element_type.52
  4.6 0.9 convert_element_type.53
  5.4 14.8 %collective-permute-done.2 = bf16[128,4608]{1,0:T(8,128)(2,1)S(1)} collective-permute-done((bf16[128,4608]{1,0:T(8,128)(2,1)}, bf16[128,4608]{1,0:T(8,128)(2,1)S(1)}, u32[]{:S(2)}, u32[]{:S(2)}) %collective-permute-start.2) | collective-permute-done | bytes 1179680 | tf_op jit(solution)/shard_map/ppermute | solution.py:15
  20.2 3.6 %convolution_subtract_fusion.7 = f32[512,128]{0,1:T(8,128)S(1)} fusion(bf16[512,3584]{1,0:T(8,128)(2,1)} %param.7, bf16[128,3584]{1,0:T(8,128)(2,1)} %param.9, f32[512]{0:T(512)S(1)} %convert_element_type.52), kind=kOutput, calls=%fused_computation.12 | convolution fusion | flops 469827584 | bytes 4851712 | tf_op jit(solution)/shard_map/dot_general | solution.py:29
  23.8 3.6 %convolution_subtract_fusion.6 = f32[512,128]{0,1:T(8,128)} fusion(bf16[512,4608]{1,0:T(8,128)(2,1)S(1)} %copy-done.1, bf16[128,4608]{1,0:T(8,128)(2,1)} %param.10, f32[512]{0:T(512)S(1)} %convert_element_type.53), kind=kOutput, calls=%fused_computation.11 | convolution fusion | flops 604045312 | bytes 6162432 | tf_op jit(solution)/shard_map/dot_general | solution.py:32
  27.4 2.6 %collective-permute-done.1 = bf16[128,3584]{1,0:T(8,128)(2,1)S(1)} collective-permute-done((bf16[128,3584]{1,0:T(8,128)(2,1)}, bf16[128,3584]{1,0:T(8,128)(2,1)S(1)}, u32[]{:S(2)}, u32[]{:S(2)}) %collective-permute-start.1) | collective-permute-done | bytes 917536 | tf_op jit(solution)/shard_map/ppermute | solution.py:15
  30.1 3.6 %convolution_subtract_fusion.5 = f32[512,128]{0,1:T(8,128)S(1)} fusion(bf16[512,3584]{1,0:T(8,128)(2,1)} %param.7, bf16[128,3584]{1,0:T(8,128)(2,1)S(1)} %collective-permute-done.1, f32[512]{0:T(512)S(1)} %convert_element_type.52), kind=kOutput, calls=%fused_computation.10 | convolution fusion | flops 469827584 | bytes 4851712 | tf_op jit(solution)/shard_map/dot_general | solution.py:29
  33.7 9.0 %collective-permute-done.5 = bf16[128,4608]{1,0:T(8,128)(2,1)} collective-permute-done((bf16[128,4608]{1,0:T(8,128)(2,1)S(1)}, bf16[128,4608]{1,0:T(8,128)(2,1)}, u32[]{:S(2)}, u32[]{:S(2)}) %collective-permute-start.5) | collective-permute-done | bytes 1179680 | tf_op jit(solution)/shard_map/ppermute | solution.py:15
  42.8 3.9 %convolution_subtract_fusion.4 = f32[512,128]{0,1:T(8,128)S(1)} fusion(bf16[512,4608]{1,0:T(8,128)(2,1)} %param.8, bf16[128,4608]{1,0:T(8,128)(2,1)S(1)} %collective-permute-done.2, f32[512]{0:T(512)S(1)} %convert_element_type.53), kind=kOutput, calls=%fused_computation.9 | convolution fusion | flops 604045312 | bytes 6162432 | tf_op jit(solution)/shard_map/dot_general | solution.py:32
  46.8 5.7 %collective-permute-done.4 = bf16[128,3584]{1,0:T(8,128)(2,1)S(1)} collective-permute-done((bf16[128,3584]{1,0:T(8,128)(2,1)S(1)}, bf16[128,3584]{1,0:T(8,128)(2,1)S(1)}, u32[]{:S(2)}, u32[]{:S(2)}) %collective-permute-start.4) | collective-permute-done | bytes 917536 | tf_op jit(solution)/shard_map/ppermute | solution.py:15
  52.5 1.3 convolution_subtract_fusion.3
  53.8 2.9 %convolution_subtract_fusion.2 = f32[512,128]{0,1:T(8,128)S(1)} fusion(bf16[512,4608]{1,0:T(8,128)(2,1)S(1)} %copy-done.2, bf16[128,4608]{1,0:T(8,128)(2,1)} %collective-permute-done.5, f32[512]{0:T(512)S(1)} %convert_element_type.53), kind=kOutput, calls=%fused_computation.7 | convolution fusion | flops 604045312 | bytes 6162432 | tf_op jit(solution)/shard_map/dot_general | solution.py:32
  56.7 8.4 %collective-permute-done.8 = bf16[128,4608]{1,0:T(8,128)(2,1)S(1)} collective-permute-done((bf16[128,4608]{1,0:T(8,128)(2,1)}, bf16[128,4608]{1,0:T(8,128)(2,1)S(1)}, u32[]{:S(2)}, u32[]{:S(2)}) %collective-permute-start.8) | collective-permute-done | bytes 1179680 | tf_op jit(solution)/shard_map/ppermute | solution.py:15
  65.1 1.6 %convolution_subtract_fusion = f32[512,128]{0,1:T(8,128)S(1)} fusion(bf16[512,4608]{1,0:T(8,128)(2,1)S(1)} %copy-done.2, bf16[128,4608]{1,0:T(8,128)(2,1)S(1)} %collective-permute-done.8, f32[512]{0:T(512)S(1)} %convert_element_type.53), kind=kOutput, calls=%fused_computation.5 | convolution fusion | flops 604045312 | bytes 6162432 | tf_op jit(solution)/shard_map/dot_general | solution.py:32
  66.8 8.2 %collective-permute-done.7 = bf16[128,3584]{1,0:T(8,128)(2,1)S(1)} collective-permute-done((bf16[128,3584]{1,0:T(8,128)(2,1)S(1)}, bf16[128,3584]{1,0:T(8,128)(2,1)S(1)}, u32[]{:S(2)}, u32[]{:S(2)}) %collective-permute-start.7) | collective-permute-done | bytes 917536 | tf_op jit(solution)/shard_map/ppermute | solution.py:15
  75.0 1.7 %fusion.5 = (f32[512]{0:T(512)S(1)}, f32[512]{0:T(512)S(1)}, f32[512]{0:T(512)S(1)}, f32[512]{0:T(512)S(1)}, bf16[512,128]{0,1:T(8,128)(2,1)S(1)}, /*index=5*/bf...) fusion(f32[512,128]{0,1:T(8,128)S(1)} %convolution_subtract_fusion.5, ...), kind=kOutput, calls=%fused_computation.26 | convolution fusion | flops 472709120 | bytes 6961152 | tf_op jit(solution)/shard_map/dot_general | solution.py:29
  76.6 0.7 convolution_convert_fusion
  77.4 15.5 %collective-permute-done = bf16[128,3584]{1,0:T(8,128)(2,1)S(1)} collective-permute-done((bf16[128,3584]{1,0:T(8,128)(2,1)S(1)}, bf16[128,3584]{1,0:T(8,128)(2,1)S(1)}, u32[]{:S(2)}, u32[]{:S(2)}) %collective-permute-start) | collective-permute-done | bytes 917536 | tf_op jit(solution)/shard_map/ppermute | solution.py:15
  92.9 0.7 add_convert_fusion.3
  93.6 0.6 fusion.12
  94.3 0.6 fusion.13
  95.5 1.1 fusion.14
  96.6 12.5 %collective-permute-done.3 = bf16[128,3584]{1,0:T(8,128)(2,1)S(1)} collective-permute-done((bf16[128,3584]{1,0:T(8,128)(2,1)S(1)}, bf16[128,3584]{1,0:T(8,128)(2,1)S(1)}, u32[]{:S(2)}, u32[]{:S(2)}) %collective-permute-start.3) | collective-permute-done | bytes 917536 | tf_op jit(solution)/shard_map/ppermute | solution.py:15
  109.5 0.6 add_add_fusion
  110.1 1.1 fusion.16
  111.3 1.1 fusion.15
  112.4 13.6 %collective-permute-done.6 = bf16[128,3584]{1,0:T(8,128)(2,1)S(1)} collective-permute-done((bf16[128,3584]{1,0:T(8,128)(2,1)S(1)}, bf16[128,3584]{1,0:T(8,128)(2,1)S(1)}, u32[]{:S(2)}, u32[]{:S(2)}) %collective-permute-start.6) | collective-permute-done | bytes 917536 | tf_op jit(solution)/shard_map/ppermute | solution.py:15
  126.0 1.1 add_convert_fusion.1
  127.1 4.3 %add_convert_fusion = bf16[512,3584]{1,0:T(8,128)(2,1)} fusion(f32[512,3584]{1,0:T(8,128)S(1)} %fusion.16, f32[512,3584]{1,0:T(8,128)S(1)} %fusion.14, f32[512,3584]{1,0:T(8,128)S(1)} %fusion.15, bf16[512,128]{0,1:T(8,128)(2,1)S(1)} %get-tuple-element.8, bf16[128,3584]{1,0:T(8,128)(2,1)} %copy-done.6), kind=kOutput, calls=%fused_computation | convolution fusion | flops 477102080 | bytes 26738688 | tf_op jit(solution)/shard_map/dot_general | solution.py:43
  131.3 9.4 %collective-permute-done.9 = bf16[128,3584]{1,0:T(8,128)(2,1)} collective-permute-done((bf16[128,3584]{1,0:T(8,128)(2,1)}, bf16[128,3584]{1,0:T(8,128)(2,1)}, u32[]{:S(2)}, u32[]{:S(2)}) %collective-permute-start.9) | collective-permute-done | bytes 917536 | tf_op jit(solution)/shard_map/ppermute | solution.py:15
  140.8 2.2 %copy.11 = bf16[128,3584]{1,0:T(8,128)(2,1)} copy(bf16[128,3584]{1,0:T(8,128)(2,1)} %collective-permute-done.9) | data formatting | bytes 1835008
  (30 shorter events, 1.6 us)
Async XLA Ops:
  0.6 19.6 %collective-permute-start.2 = (bf16[128,4608]{1,0:T(8,128)(2,1)}, bf16[128,4608]{1,0:T(8,128)(2,1)S(1)}, u32[]{:S(2)}, u32[]{:S(2)}) collective-permute-start(bf16[128,4608]{1,0:T(8,128)(2,1)} %param.10), channel_id=1, source_target_pairs={{0,1},{1,2},{2,3},{3,4},{4,5},{5,6},{6,7},{7,8},{8,9},{9,10},{10,1... | collective-permute-start | bytes 3538952 | tf_op jit(solution)/shard_map/ppermute | solution.py:15
  1.1 28.9 %collective-permute-start.1 = (bf16[128,3584]{1,0:T(8,128)(2,1)}, bf16[128,3584]{1,0:T(8,128)(2,1)S(1)}, u32[]{:S(2)}, u32[]{:S(2)}) collective-permute-start(bf16[128,3584]{1,0:T(8,128)(2,1)} %param.9), channel_id=1, source_target_pairs={{0,1},{1,2},{2,3},{3,4},{4,5},{5,6},{6,7},{7,8},{8,9},{9,10},{10,1... | collective-permute-start | bytes 2752520 | tf_op jit(solution)/shard_map/ppermute | solution.py:15
  3.7 20.0 %copy-start.1 = (bf16[512,4608]{1,0:T(8,128)(2,1)S(1)}, bf16[512,4608]{1,0:T(8,128)(2,1)}, u32[]{:S(2)}) copy-start(bf16[512,4608]{1,0:T(8,128)(2,1)} %param.8) | copy-start | bytes 14155780
  20.2 22.6 %collective-permute-start.5 = (bf16[128,4608]{1,0:T(8,128)(2,1)S(1)}, bf16[128,4608]{1,0:T(8,128)(2,1)}, u32[]{:S(2)}, u32[]{:S(2)}) collective-permute-start(bf16[128,4608]{1,0:T(8,128)(2,1)S(1)} %collective-permute-done.2), channel_id=1, source_target_pairs={{0,1},{1,2},{2,3},{3,4},{4,5},{5,6},{6,7},{7,8},{8,9},{9,10},{10,1... | collective-permute-start | bytes 3538952 | tf_op jit(solution)/shard_map/ppermute | solution.py:15
  30.0 16.7 %copy-start.4 = (bf16[128,3584]{1,0:T(8,128)(2,1)}, bf16[128,3584]{1,0:T(8,128)(2,1)S(1)}, u32[]{:S(2)}) copy-start(bf16[128,3584]{1,0:T(8,128)(2,1)S(1)} %collective-permute-done.1) | copy-start | bytes 2752516
  30.0 22.5 %collective-permute-start.4 = (bf16[128,3584]{1,0:T(8,128)(2,1)S(1)}, bf16[128,3584]{1,0:T(8,128)(2,1)S(1)}, u32[]{:S(2)}, u32[]{:S(2)}) collective-permute-start(bf16[128,3584]{1,0:T(8,128)(2,1)S(1)} %collective-permute-done.1), channel_id=1, source_target_pairs={{0,1},{1,2},{2,3},{3,4},{4,5},{5,6},{6,7},{7,8},{8,9},{9,10},{10,1... | collective-permute-start | bytes 2752520 | tf_op jit(solution)/shard_map/ppermute | solution.py:15
  33.7 18.8 %copy-start = (bf16[512,3584]{1,0:T(8,128)(2,1)S(1)}, bf16[512,3584]{1,0:T(8,128)(2,1)}, u32[]{:S(2)}) copy-start(bf16[512,3584]{1,0:T(8,128)(2,1)} %param.7) | copy-start | bytes 11010052
  42.8 22.4 %collective-permute-start.8 = (bf16[128,4608]{1,0:T(8,128)(2,1)}, bf16[128,4608]{1,0:T(8,128)(2,1)S(1)}, u32[]{:S(2)}, u32[]{:S(2)}) collective-permute-start(bf16[128,4608]{1,0:T(8,128)(2,1)} %collective-permute-done.5), channel_id=1, source_target_pairs={{0,1},{1,2},{2,3},{3,4},{4,5},{5,6},{6,7},{7,8},{8,9},{9,10},{10,1... | collective-permute-start | bytes 3538952 | tf_op jit(solution)/shard_map/ppermute | solution.py:15
  46.7 7.1 %copy-start.2 = (bf16[512,4608]{1,0:T(8,128)(2,1)S(1)}, bf16[512,4608]{1,0:T(8,128)(2,1)}, u32[]{:S(2)}) copy-start(bf16[512,4608]{1,0:T(8,128)(2,1)} %param.8) | copy-start | bytes 14155780
  52.5 22.5 %collective-permute-start.7 = (bf16[128,3584]{1,0:T(8,128)(2,1)S(1)}, bf16[128,3584]{1,0:T(8,128)(2,1)S(1)}, u32[]{:S(2)}, u32[]{:S(2)}) collective-permute-start(bf16[128,3584]{1,0:T(8,128)(2,1)S(1)} %collective-permute-done.4), channel_id=1, source_target_pairs={{0,1},{1,2},{2,3},{3,4},{4,5},{5,6},{6,7},{7,8},{8,9},{9,10},{10,1... | collective-permute-start | bytes 2752520 | tf_op jit(solution)/shard_map/ppermute | solution.py:15
  56.7 18.3 %copy-start.7 = (f32[512,128]{0,1:T(8,128)S(1)}, f32[512,128]{0,1:T(8,128)}, u32[]{:S(2)}) copy-start(f32[512,128]{0,1:T(8,128)} %convolution_subtract_fusion.6) | copy-start | bytes 786436
  56.7 18.3 %copy-start.8 = (s32[512]{0:T(512)S(1)}, s32[512]{0:T(512)}, u32[]{:S(2)}) copy-start(s32[512]{0:T(512)} %param.13) | copy-start | bytes 6148
  75.0 19.3 %copy-start.6 = (bf16[128,3584]{1,0:T(8,128)(2,1)}, bf16[128,3584]{1,0:T(8,128)(2,1)S(1)}, u32[]{:S(2)}) copy-start(bf16[128,3584]{1,0:T(8,128)(2,1)S(1)} %collective-permute-done.7) | copy-start | bytes 2752516
  77.3 15.6 %collective-permute-start = (bf16[128,3584]{1,0:T(8,128)(2,1)S(1)}, bf16[128,3584]{1,0:T(8,128)(2,1)S(1)}, u32[]{:S(2)}, u32[]{:S(2)}) collective-permute-start(bf16[128,3584]{1,0:T(8,128)(2,1)S(1)} %convolution_convert_fusion), channel_id=1, source_target_pairs={{0,1},{1,2},{2,3},{3,4},{4,5},{5,6},{6,7},{7,8},{8,9},{9,10},{10,1... | collective-permute-start | bytes 2752520 | tf_op jit(solution)/shard_map/ppermute | solution.py:15
  93.5 15.6 %collective-permute-start.3 = (bf16[128,3584]{1,0:T(8,128)(2,1)S(1)}, bf16[128,3584]{1,0:T(8,128)(2,1)S(1)}, u32[]{:S(2)}, u32[]{:S(2)}) collective-permute-start(bf16[128,3584]{1,0:T(8,128)(2,1)S(1)} %add_convert_fusion.3), channel_id=1, source_target_pairs={{0,1},{1,2},{2,3},{3,4},{4,5},{5,6},{6,7},{7,8},{8,9},{9,10},{10,1... | collective-permute-start | bytes 2752520 | tf_op jit(solution)/shard_map/ppermute | solution.py:15
  94.3 1.2 copy-start.3
  109.3 16.7 %collective-permute-start.6 = (bf16[128,3584]{1,0:T(8,128)(2,1)S(1)}, bf16[128,3584]{1,0:T(8,128)(2,1)S(1)}, u32[]{:S(2)}, u32[]{:S(2)}) collective-permute-start(bf16[128,3584]{1,0:T(8,128)(2,1)S(1)} %add_convert_fusion.2), channel_id=1, source_target_pairs={{0,1},{1,2},{2,3},{3,4},{4,5},{5,6},{6,7},{7,8},{8,9},{9,10},{10,1... | collective-permute-start | bytes 2752520 | tf_op jit(solution)/shard_map/ppermute | solution.py:15
  110.1 1.2 copy-start.5
  127.1 13.7 %collective-permute-start.9 = (bf16[128,3584]{1,0:T(8,128)(2,1)}, bf16[128,3584]{1,0:T(8,128)(2,1)}, u32[]{:S(2)}, u32[]{:S(2)}) collective-permute-start(bf16[128,3584]{1,0:T(8,128)(2,1)} %add_convert_fusion.1), channel_id=1, source_target_pairs={{0,13},{1,14},{2,15},{3,0},{4,1},{5,2},{6,3},{7,4},{8,5},{9,6},{10... | collective-permute-start | bytes 2752520 | tf_op jit(solution)/shard_map/ppermute | solution.py:15
where the time goes:
time: 143 us
  waiting for transfers between devices  99.9 us (70%)
  matrix products  32.5 us (23%)
  other arithmetic  3.51 us (2%)
  starting transfers between devices  3.47 us (2%)
  local copies, waits for them, and re-layouts  2.76 us (2%)
    ppermute x10, waiting for transfers between devices, passed_along(): return lax.ppermute(value, axis, pairs)  99.9 us
    dot_general x4, matrix products, panel_terms(): lax.dot_general(teacher_block, teacher_panel, (((1,), (1,)), ((), ())), p...  12 us
    dot_general x4, matrix products, panel_terms(): lax.dot_general(student_block, student_panel, (((1,), (1,)), ((), ())), p...  10.2 us
    dot_general x4, matrix products, panel_terms(): jnp.dot(scores, student_panel, preferred_element_type=jnp.float32)  7.67 us
    ppermute x10, starting transfers between devices, passed_along(): return lax.ppermute(value, axis, pairs)  3.47 us
  transfers between devices with their start and end apart: 10, of which 10 were waited for; matrix products, arithmetic and copies ran while one was open for 22% of the time, Pallas kernels for 0%

commit v1 on v0

v1 whole, which is shorter than its diff:
```python
import jax
import jax.numpy as jnp
from jax import lax
from jax.sharding import PartitionSpec as P

hard_weight = 0.5
CHUNKS = 4
STAGES = 2
BOTH = ("grp", "seq")


def permuted(value, move):
    groups, count = lax.axis_size("grp"), lax.axis_size("seq")
    pairs = []
    for group in range(groups):
        for place in range(count):
            to_group, to_place = move(group, place)
            pairs.append((group * count + place, to_group * count + to_place % count))
    return lax.ppermute(value, BOTH, pairs)


def next_chip(group, place):
    return group, place + 2


def previous_chip(group, place):
    return group, place - 2


def other_plane(group, place):
    return 1 - group, place


def other_core(group, place):
    return group, place + 1 - 2 * (place % 2)


def extra_out(group, place):
    return group, place + 1 + 2 * (place % 2)


def extra_back(group, place):
    return group, place - 3 + 2 * (place % 2)


def body(student_rows, teacher_rows, student_head, teacher_head, student_lse, teacher_lse, targets):
    count = lax.axis_size("seq")
    place = lax.axis_index("seq")
    plane = lax.axis_index("grp")
    core = place % 2
    width, depth = student_head.shape
    half = width // 2
    piece = half // CHUNKS
    student_norm = student_lse.astype(jnp.float32)[:, None]
    teacher_norm = teacher_lse.astype(jnp.float32)[:, None]

    def meeting(student_panel, teacher_panel, ids):
        zs = lax.dot_general(
            student_rows, student_panel, (((1,), (1,)), ((), ())), preferred_element_type=jnp.float32
        )
        zt = lax.dot_general(
            teacher_rows, teacher_panel, (((1,), (1,)), ((), ())), preferred_element_type=jnp.float32
        )
        ls = zs - student_norm
        lt = zt - teacher_norm
        ps = jnp.exp(ls)
        pt = jnp.exp(lt)
        onehot = (targets[:, None] == ids[None, :]).astype(jnp.float32)
        scores = ((1.0 + hard_weight) * ps - pt - hard_weight * onehot).astype(jnp.bfloat16)
        losses = jnp.sum(pt * (lt - ls) - hard_weight * onehot * ls, axis=1)
        part = lax.dot_general(
            scores, student_rows, (((0,), (0,)), ((), ())), preferred_element_type=jnp.float32
        )
        return scores, losses, part

    mine_rows = lax.dynamic_slice_in_dim(student_head, plane * half, half, 0)
    mine_rows_t = lax.dynamic_slice_in_dim(teacher_head, plane * half, half, 0)
    crossed = []
    for k in range(CHUNKS):
        lo, hi = k * piece, (k + 1) * piece
        chunk = jnp.concatenate([mine_rows[lo:hi], mine_rows_t[lo:hi]], axis=1)
        crossed.append(permuted(chunk, next_chip))
    swapped = [permuted(chunk, other_plane) for chunk in crossed]

    whole, _ = lax.optimization_barrier((jnp.concatenate([student_head, teacher_head], axis=1), crossed[-1]))
    extra = permuted(whole, extra_out)

    ids_in = jnp.arange(width, dtype=jnp.int32)
    own_scores, losses, own_part = meeting(student_head, teacher_head, place * width + ids_in)
    loss_total = losses
    score_list, panel_list = [own_scores], [student_head]

    per_stage = CHUNKS // STAGES
    near = (place - 2) % count
    far = (place - 1 - 2 * core) % count
    mine_parts, other_parts = [], []
    for stage in range(STAGES):
        picks = range(stage * per_stage, (stage + 1) * per_stage)
        mine = jnp.concatenate([crossed[k] for k in picks] + [swapped[k] for k in picks], axis=0)
        theirs = permuted(mine, other_core)
        both = jnp.concatenate([mine, theirs], axis=0)
        rows = jnp.arange(per_stage * piece, dtype=jnp.int32) + stage * per_stage * piece
        inside = jnp.concatenate([plane * half + rows, (1 - plane) * half + rows])
        ids = jnp.concatenate([near * width + inside, far * width + inside])
        scores, losses, part = meeting(both[:, :depth], both[:, depth:], ids)
        loss_total = loss_total + losses
        score_list.append(scores)
        panel_list.append(both[:, :depth])
        keep, give = part[: mine.shape[0]], part[mine.shape[0] :]
        got = permuted(give.astype(jnp.bfloat16), other_core)
        total = (keep + got.astype(jnp.float32)).astype(jnp.bfloat16)
        back = permuted(total, previous_chip)
        mine_parts.append(back[: per_stage * piece])
        other_parts.append(back[per_stage * piece :])

    extra_id = jnp.where(core == 1, place - 1, place - 3) % count
    scores, losses, part = meeting(extra[:, :depth], extra[:, depth:], extra_id * width + ids_in)
    loss_total = loss_total + losses
    score_list.append(scores)
    panel_list.append(extra[:, :depth])
    extra_part = permuted(part.astype(jnp.bfloat16), extra_back)

    rows_grad = jnp.dot(
        jnp.concatenate(score_list, axis=1),
        jnp.concatenate(panel_list, axis=0),
        preferred_element_type=jnp.float32,
    ).astype(jnp.bfloat16)

    mine_parts = jnp.concatenate(mine_parts, axis=0)
    other_parts = jnp.concatenate(other_parts, axis=0)
    first = jnp.where(plane == 0, mine_parts, other_parts)
    second = jnp.where(plane == 0, other_parts, mine_parts)
    from_next = jnp.concatenate([first, second], axis=0)
    head_grad = (
        own_part + from_next.astype(jnp.float32) + extra_part.astype(jnp.float32)
    ).astype(jnp.bfloat16)
    return (head_grad, rows_grad, loss_total)


def solution(mesh):
    placed = (
        P(("grp", "seq"), None),
        P(("grp", "seq"), None),
        P("seq", None),
        P("seq", None),
        P(("grp", "seq")),
        P(("grp", "seq")),
        P(("grp", "seq")),
    )
    return jax.shard_map(
        body,
        mesh=mesh,
        in_specs=placed,
        out_specs=(P(("grp", "seq"), None), P(("grp", "seq"), None), P(("grp", "seq"))),
        check_vma=False,
    )
```

time: 143 us -> 97.1 us (0.68)
  waiting for transfers between devices: 99.9 us -> 47.5 us
  starting transfers between devices: 3.47 us -> 18.1 us
  matrix products: 32.5 us -> 21.8 us
  other arithmetic: 3.51 us -> 5.06 us
    ppermute x10 -> x16, waiting for transfers between devices: 99.9 us -> 47.5 us  [permuted(): return lax.ppermute(value, BOTH, pairs)]
    ppermute x10 -> x16, starting transfers between devices: 3.47 us -> 18.1 us  [permuted(): return lax.ppermute(value, BOTH, pairs)]
    dot_general x16 -> x13, matrix products: 32.5 us -> 21.8 us  [the longest x4 9.06 us: meeting(): lax.dot_general(teacher_rows, teacher_panel, (((1,), (1,)), ((), ())), pr...]
    concatenate x0 -> x9, other arithmetic: none -> 4 us  [the longest x4 2.17 us: body(): chunk = jnp.concatenate([mine_rows[lo:hi], mine_rows_t[lo:hi]], axis=1)]
    slice x0 -> x9, local copies, waits for them, and re-layouts: none -> 2.77 us  [the longest x2 2.43 us: body(): chunk = jnp.concatenate([mine_rows[lo:hi], mine_rows_t[lo:hi]], axis=1)]
    convert_element_type x4, other arithmetic: 2.92 us -> 0.16 us  [the longest x2 0.15 us: body(): total = (keep + got.astype(jnp.float32)).astype(jnp.bfloat16)]
    unnamed x19 -> x26, local copies, waits for them, and re-layouts: 2.76 us -> 0.47 us
  transfers between devices with their start and end apart: 10 -> 16, of which waited for: 10 -> 9; matrix products, arithmetic and copies ran while one was open for 22% -> 20% of each run, Pallas kernels for 0% -> 0%
where the time goes in v1:
time: 97.1 us; the launch traced here: 96.9 us
  waiting for transfers between devices  47.5 us (49%)
  matrix products  21.8 us (22%)
  starting transfers between devices  18.1 us (19%)
  other arithmetic  5.06 us (5%)
  local copies, waits for them, and re-layouts  3.38 us (3%)
  between operations  1.08 us (1%)
    ppermute x16, waiting for transfers between devices, permuted(): return lax.ppermute(value, BOTH, pairs)  47.5 us
    ppermute x16, starting transfers between devices, permuted(): return lax.ppermute(value, BOTH, pairs)  18.1 us
    dot_general x4, matrix products, meeting(): lax.dot_general(teacher_rows, teacher_panel, (((1,), (1,)), ((), ())), pr...  9.06 us
    dot_general x4, matrix products, meeting(): lax.dot_general(student_rows, student_panel, (((1,), (1,)), ((), ())), pr...  5.62 us
    dot_general x1, matrix products, body(): jnp.dot(jnp.concatenate(score_list, axis=1), jnp.concatenate(panel_list,...  3.57 us
    dot_general x4, matrix products, meeting(): lax.dot_general(scores, student_rows, (((0,), (0,)), ((), ())), preferred...  3.57 us
    slice x2, local copies, waits for them, and re-layouts, body(): chunk = jnp.concatenate([mine_rows[lo:hi], mine_rows_t[lo:hi]], axis=1)  2.43 us
    concatenate x4, other arithmetic, body(): chunk = jnp.concatenate([mine_rows[lo:hi], mine_rows_t[lo:hi]], axis=1)  2.17 us
  transfers between devices with their start and end apart: 16, of which 9 were waited for; matrix products, arithmetic and copies ran while one was open for 20% of the time, Pallas kernels for 0%

profile of v1, /device:TPU:0, one launch (start us, length us, event | category | flops | bytes accessed | tf_op | source)
XLA Modules:
  0.0 96.9 jit_solution(17476670815542184271)
XLA Ops:
  0.7 1.3 %constant_dynamic-slice_fusion.2 = (bf16[16,4608]{1,0:T(8,128)(2,1)S(1)}, bf16[16,4608]{1,0:T(8,128)(2,1)S(1)}, bf16[16,4608]{1,0:T(8,128)(2,1)S(1)}, bf16[16,4608]{1,0:T(8,128)(2,1)S(1)}) fusion(bf16[128,4608]{1,0:T(8,128)(2,1)} %param.10, s32[]{:T(128)S(6)} %add.143, s32[]{:T(128)S(6)} %add.145, s32[]{:T(128)S(6)} %select_n.39, s32[]{:T(128)S(6)} %add.147), kind=kLoop, calls=%fused_computation.88 | loop fusion | bytes 1179664 | tf_op jit(solution)/shard_map/slice | solution.py:81
  2.0 1.1 %constant_dynamic-slice_fusion.3 = (bf16[16,3584]{1,0:T(8,128)(2,1)S(1)}, bf16[16,3584]{1,0:T(8,128)(2,1)S(1)}, bf16[16,3584]{1,0:T(8,128)(2,1)S(1)}, bf16[16,3584]{1,0:T(8,128)(2,1)S(1)}) fusion(bf16[128,3584]{1,0:T(8,128)(2,1)} %param.9, s32[]{:T(128)S(6)} %add.143, s32[]{:T(128)S(6)} %add.145, s32[]{:T(128)S(6)} %select_n.39, s32[]{:T(128)S(6)} %add.147), kind=kLoop, calls=%fused_computation.89 | loop fusion | bytes 917520 | tf_op jit(solution)/shard_map/slice | solution.py:81
  3.8 2.9 %collective-permute-start.8 = (bf16[16,8192]{1,0:T(8,128)(2,1)}, bf16[16,8192]{1,0:T(8,128)(2,1)S(1)}, u32[]{:S(2)}, u32[]{:S(2)}) collective-permute-start(bf16[16,8192]{1,0:T(8,128)(2,1)} %pad_maximum_fusion.8), channel_id=1, source_target_pairs={{0,2},{1,3},{2,4},{3,5},{4,6},{5,7},{6,8},{7,9},{8,10},{9,11},{10,... | collective-permute-start | bytes 786440 | tf_op jit(solution)/shard_map/ppermute | solution.py:19
  6.7 0.7 pad_maximum_fusion.7
  7.5 1.5 %collective-permute-start.7 = (bf16[16,8192]{1,0:T(8,128)(2,1)}, bf16[16,8192]{1,0:T(8,128)(2,1)S(1)}, u32[]{:S(2)}, u32[]{:S(2)}) collective-permute-start(bf16[16,8192]{1,0:T(8,128)(2,1)} %pad_maximum_fusion.7), channel_id=1, source_target_pairs={{0,2},{1,3},{2,4},{3,5},{4,6},{5,7},{6,8},{7,9},{8,10},{9,11},{10,... | collective-permute-start | bytes 786440 | tf_op jit(solution)/shard_map/ppermute | solution.py:19
  9.7 1.5 %collective-permute-start = (bf16[16,8192]{1,0:T(8,128)(2,1)}, bf16[16,8192]{1,0:T(8,128)(2,1)S(1)}, u32[]{:S(2)}, u32[]{:S(2)}) collective-permute-start(bf16[16,8192]{1,0:T(8,128)(2,1)} %pad_maximum_fusion.5), channel_id=1, source_target_pairs={{0,2},{1,3},{2,4},{3,5},{4,6},{5,7},{6,8},{7,9},{8,10},{9,11},{10,... | collective-permute-start | bytes 786440 | tf_op jit(solution)/shard_map/ppermute | solution.py:19
  11.2 1.6 %collective-permute-start.1 = (bf16[16,8192]{1,0:T(8,128)(2,1)S(1)}, bf16[16,8192]{1,0:T(8,128)(2,1)S(1)}, u32[]{:S(2)}, u32[]{:S(2)}) collective-permute-start(bf16[16,8192]{1,0:T(8,128)(2,1)S(1)} %pad_maximum_fusion.6), channel_id=1, source_target_pairs={{0,2},{1,3},{2,4},{3,5},{4,6},{5,7},{6,8},{7,9},{8,10},{9,11},{10,... | collective-permute-start | bytes 786440 | tf_op jit(solution)/shard_map/ppermute | solution.py:19
  12.9 1.5 %pad_maximum_fusion = bf16[128,8192]{1,0:T(8,128)(2,1)} fusion(bf16[128,4608]{1,0:T(8,128)(2,1)S(1)} %copy-done.1, bf16[128,3584]{1,0:T(8,128)(2,1)S(1)} %copy-done.2), kind=kLoop, calls=%fused_computation.10 | loop fusion | flops 4194304 | bytes 4194304 | tf_op jit(solution)/shard_map/concatenate | solution.py:85
  14.8 4.1 %convolution_subtract_fusion.3 = f32[512,128]{0,1:T(8,128)S(1)} fusion(bf16[512,4608]{1,0:T(8,128)(2,1)} %param.8, bf16[128,4608]{1,0:T(8,128)(2,1)S(1)} %copy-done.1, f32[512]{0:T(512)S(1)} %convert_element_type.52), kind=kOutput, calls=%fused_computation.27 | convolution fusion | flops 604045312 | bytes 6162432 | tf_op jit(solution)/shard_map/dot_general | solution.py:61
  18.9 1.3 %convolution_subtract_fusion.4 = f32[512,128]{0,1:T(8,128)S(1)} fusion(bf16[512,3584]{1,0:T(8,128)(2,1)S(1)} %copy-done, bf16[128,3584]{1,0:T(8,128)(2,1)S(1)} %copy-done.2, f32[512]{0:T(512)S(1)} %convert_element_type.51), kind=kOutput, calls=%fused_computation.28 | convolution fusion | flops 469827584 | bytes 4851712 | tf_op jit(solution)/shard_map/dot_general | solution.py:58
  20.5 2.2 %collective-permute-done.7 = bf16[16,8192]{1,0:T(8,128)(2,1)S(1)} collective-permute-done((bf16[16,8192]{1,0:T(8,128)(2,1)}, bf16[16,8192]{1,0:T(8,128)(2,1)S(1)}, u32[]{:S(2)}, u32[]{:S(2)}) %collective-permute-start.7) | collective-permute-done | bytes 262176 | tf_op jit(solution)/shard_map/ppermute | solution.py:19
  22.8 1.8 %collective-permute-start.9 = (bf16[16,8192]{1,0:T(8,128)(2,1)S(1)}, bf16[16,8192]{1,0:T(8,128)(2,1)S(1)}, u32[]{:S(2)}, u32[]{:S(2)}) collective-permute-start(bf16[16,8192]{1,0:T(8,128)(2,1)S(1)} %collective-permute-done.7), channel_id=1, source_target_pairs={{0,16},{1,17},{2,18},{3,19},{4,20},{5,21},{6,22},{7,23},{8,24},{9,... | collective-permute-start | bytes 786440 | tf_op jit(solution)/shard_map/ppermute | solution.py:19
  24.9 3.5 %collective-permute-done = bf16[16,8192]{1,0:T(8,128)(2,1)S(1)} collective-permute-done((bf16[16,8192]{1,0:T(8,128)(2,1)}, bf16[16,8192]{1,0:T(8,128)(2,1)S(1)}, u32[]{:S(2)}, u32[]{:S(2)}) %collective-permute-start) | collective-permute-done | bytes 262176 | tf_op jit(solution)/shard_map/ppermute | solution.py:19
  28.4 1.8 %collective-permute-start.2 = (bf16[16,8192]{1,0:T(8,128)(2,1)S(1)}, bf16[16,8192]{1,0:T(8,128)(2,1)S(1)}, u32[]{:S(2)}, u32[]{:S(2)}) collective-permute-start(bf16[16,8192]{1,0:T(8,128)(2,1)S(1)} %collective-permute-done), channel_id=1, source_target_pairs={{0,16},{1,17},{2,18},{3,19},{4,20},{5,21},{6,22},{7,23},{8,24},{9,... | collective-permute-start | bytes 786440 | tf_op jit(solution)/shard_map/ppermute | solution.py:19
  30.2 3.8 %collective-permute-done.1 = bf16[16,8192]{1,0:T(8,128)(2,1)S(1)} collective-permute-done((bf16[16,8192]{1,0:T(8,128)(2,1)S(1)}, bf16[16,8192]{1,0:T(8,128)(2,1)S(1)}, u32[]{:S(2)}, u32[]{:S(2)}) %collective-permute-start.1) | collective-permute-done | bytes 262176 | tf_op jit(solution)/shard_map/ppermute | solution.py:19
  34.0 1.7 %collective-permute-start.3 = (bf16[16,8192]{1,0:T(8,128)(2,1)S(1)}, bf16[16,8192]{1,0:T(8,128)(2,1)S(1)}, u32[]{:S(2)}, u32[]{:S(2)}) collective-permute-start(bf16[16,8192]{1,0:T(8,128)(2,1)S(1)} %collective-permute-done.1), channel_id=1, source_target_pairs={{0,16},{1,17},{2,18},{3,19},{4,20},{5,21},{6,22},{7,23},{8,24},{9,... | collective-permute-start | bytes 786440 | tf_op jit(solution)/shard_map/ppermute | solution.py:19
  35.7 1.9 %collective-permute-done.10 = bf16[16,8192]{1,0:T(8,128)(2,1)S(1)} collective-permute-done((bf16[16,8192]{1,0:T(8,128)(2,1)S(1)}, bf16[16,8192]{1,0:T(8,128)(2,1)S(1)}, u32[]{:S(2)}, u32[]{:S(2)}) %collective-permute-start.10) | collective-permute-done | bytes 262176 | tf_op jit(solution)/shard_map/ppermute | solution.py:19
  37.8 5.5 %collective-permute-done.2 = bf16[16,8192]{1,0:T(8,128)(2,1)S(1)} collective-permute-done((bf16[16,8192]{1,0:T(8,128)(2,1)S(1)}, bf16[16,8192]{1,0:T(8,128)(2,1)S(1)}, u32[]{:S(2)}, u32[]{:S(2)}) %collective-permute-start.2) | collective-permute-done | bytes 262176 | tf_op jit(solution)/shard_map/ppermute | solution.py:19
  43.3 4.1 %collective-permute-done.3 = bf16[16,8192]{1,0:T(8,128)(2,1)S(1)} collective-permute-done((bf16[16,8192]{1,0:T(8,128)(2,1)S(1)}, bf16[16,8192]{1,0:T(8,128)(2,1)S(1)}, u32[]{:S(2)}, u32[]{:S(2)}) %collective-permute-start.3) | collective-permute-done | bytes 262176 | tf_op jit(solution)/shard_map/ppermute | solution.py:19
  47.8 2.4 %collective-permute-done.4 = bf16[64,8192]{1,0:T(8,128)(2,1)S(1)} collective-permute-done((bf16[64,8192]{1,0:T(8,128)(2,1)S(1)}, bf16[64,8192]{1,0:T(8,128)(2,1)S(1)}, u32[]{:S(2)}, u32[]{:S(2)}) %collective-permute-start.4) | collective-permute-done | bytes 1048608 | tf_op jit(solution)/shard_map/ppermute | solution.py:19
  50.3 1.3 %fusion.23 = f32[512,128]{0,1:T(8,128)S(1)} fusion(bf16[512,3584]{1,0:T(8,128)(2,1)S(1)} %copy-done, f32[512]{0:T(512)S(1)} %convert_element_type.51, bf16[128,8192]{1,0:T(8,128)(2,1)S(1)} %constant_dynamic-update-slice_fusion.5), kind=kOutput, calls=%fused_computation.24 | convolution fusion | flops 469827584 | bytes 4851712 | tf_op jit(solution)/shard_map/dot_general | solution.py:58
  51.7 1.7 %fusion.28 = f32[512,128]{0,1:T(8,128)S(1)} fusion(bf16[512,4608]{1,0:T(8,128)(2,1)S(1)} %bitcast.31, bf16[128,8192]{1,0:T(8,128)(2,1)S(1)} %constant_dynamic-update-slice_fusion.5, f32[512]{0:T(512)S(1)} %convert_element_type.52), kind=kOutput, calls=%fused_computation.30 | convolution fusion | flops 604045312 | bytes 6162432 | tf_op jit(solution)/shard_map/dot_general | solution.py:61
  53.3 1.7 %fusion.31 = f32[512,128]{0,1:T(8,128)S(1)} fusion(bf16[512,4608]{1,0:T(8,128)(2,1)S(1)} %bitcast.31, bf16[128,8192]{1,0:T(8,128)(2,1)S(1)} %constant_dynamic-update-slice_fusion, f32[512]{0:T(512)S(1)} %convert_element_type.52), kind=kOutput, calls=%fused_computation.31 | convolution fusion | flops 604045312 | bytes 6162432 | tf_op jit(solution)/shard_map/dot_general | solution.py:61
  55.0 1.3 %fusion.22 = f32[512,128]{0,1:T(8,128)S(1)} fusion(bf16[512,3584]{1,0:T(8,128)(2,1)S(1)} %copy-done, f32[512]{0:T(512)S(1)} %convert_element_type.51, bf16[128,8192]{1,0:T(8,128)(2,1)S(1)} %collective-permute-done.14), kind=kOutput, calls=%fused_computation.22 | convolution fusion | flops 469827584 | bytes 4851712 | tf_op jit(solution)/shard_map/dot_general | solution.py:58
  56.3 1.7 %fusion.25 = f32[512,128]{0,1:T(8,128)S(1)} fusion(bf16[512,4608]{1,0:T(8,128)(2,1)S(1)} %bitcast.31, bf16[128,8192]{1,0:T(8,128)(2,1)S(1)} %collective-permute-done.14, f32[512]{0:T(512)S(1)} %convert_element_type.52), kind=kOutput, calls=%fused_computation.29 | convolution fusion | flops 604045312 | bytes 6162432 | tf_op jit(solution)/shard_map/dot_general | solution.py:61
  58.0 1.7 %fusion.48 = (f32[512]{0:T(512)S(1)}, f32[512]{0:T(512)S(1)}, f32[512]{0:T(512)S(1)}, f32[512]{0:T(512)S(1)}, bf16[512,128]{0,1:T(8,128)(2,1)S(1)}, /*index=5*/b...) fusion(f32[512,128]{0,1:T(8,128)S(1)} %fusion.31, s32[512]{0:T(512)S(1)} %copy-done.6, ...), kind=kOutput, calls=%fused_computation.64 | convolution fusion | flops 472709120 | bytes 6961152 | tf_op jit(solution)/shard_map/dot_general | solution.py:58
  62.4 2.0 %collective-permute-start.15 = (bf16[128,3584]{1,0:T(8,128)(2,1)S(1)}, bf16[128,3584]{1,0:T(8,128)(2,1)S(1)}, u32[]{:S(2)}, u32[]{:S(2)}) collective-permute-start(bf16[128,3584]{1,0:T(8,128)(2,1)S(1)} %convolution_convert_fusion.1), channel_id=1, source_target_pairs={{0,13},{1,0},{2,15},{3,2},{4,1},{5,4},{6,3},{7,6},{8,5},{9,8},{10,... | collective-permute-start | bytes 2752520 | tf_op jit(solution)/shard_map/ppermute | solution.py:19
  65.1 3.6 %convolution_convert_fusion = bf16[512,3584]{1,0:T(8,128)(2,1)} fusion(bf16[128,3584]{1,0:T(8,128)(2,1)S(1)} %slice.105, bf16[128,3584]{1,0:T(8,128)(2,1)S(1)} %slice.98, bf16[128,3584]{1,0:T(8,128)(2,1)S(1)} %slice.93, bf16[128,3584]{1,0:T(8,128)(2,1)S(1)} %copy-done.2, bf16[512,128]{0,1:T(8,128)(2,1)S(1)} %get-tuple-element.20, ...), kind=kOutput, calls=%fused_computation | convolution fusion | flops 1897660416 | bytes 7864320 | tf_op jit(solution)/shard_map/dot_general | solution.py:123
  68.8 1.4 %collective-permute-start.6 = (bf16[64,3584]{1,0:T(8,128)(2,1)S(1)}, bf16[64,3584]{1,0:T(8,128)(2,1)S(1)}, u32[]{:S(2)}, u32[]{:S(2)}) collective-permute-start(bf16[64,3584]{1,0:T(8,128)(2,1)S(1)} %fusion.35), channel_id=1, source_target_pairs={{0,14},{1,15},{2,0},{3,1},{4,2},{5,3},{6,4},{7,5},{8,6},{9,7},{10,... | collective-permute-start | bytes 1376264 | tf_op jit(solution)/shard_map/ppermute | solution.py:19
  70.9 19.0 %collective-permute-done.6 = bf16[64,3584]{1,0:T(8,128)(2,1)S(1)} collective-permute-done((bf16[64,3584]{1,0:T(8,128)(2,1)S(1)}, bf16[64,3584]{1,0:T(8,128)(2,1)S(1)}, u32[]{:S(2)}, u32[]{:S(2)}) %collective-permute-start.6) | collective-permute-done | bytes 458784 | tf_op jit(solution)/shard_map/ppermute | solution.py:19
  89.9 5.1 %collective-permute-done.13 = bf16[64,3584]{1,0:T(8,128)(2,1)S(1)} collective-permute-done((bf16[64,3584]{1,0:T(8,128)(2,1)S(1)}, bf16[64,3584]{1,0:T(8,128)(2,1)S(1)}, u32[]{:S(2)}, u32[]{:S(2)}) %collective-permute-start.13) | collective-permute-done | bytes 458784 | tf_op jit(solution)/shard_map/ppermute | solution.py:19
  95.2 1.6 %add_convert_fusion = bf16[128,3584]{1,0:T(8,128)(2,1)} fusion(bf16[128,3584]{1,0:T(8,128)(2,1)S(1)} %collective-permute-done.15, bf16[512,128]{0,1:T(8,128)(2,1)S(1)} %get-tuple-element.21, bf16[512,3584]{1,0:T(8,128)(2,1)S(1)} %copy-done, bf16[64,3584]{1,0:T(8,128)(2,1)S(1)} %get-tuple-element.14, bf16[64,3584]{1,0:T(8,128)(2,1)S(1)} %get-tuple-element.13), kind=kOutput, calls=%fused_computation.11 | convolution fusion | flops 473432064 | bytes 6553600 | tf_op jit(solution)/shard_map/dot_general | solution.py:71
  (71 shorter events, 7.4 us)
Async XLA Ops:
  0.6 12.2 %copy-start.1 = (bf16[128,4608]{1,0:T(8,128)(2,1)S(1)}, bf16[128,4608]{1,0:T(8,128)(2,1)}, u32[]{:S(2)}) copy-start(bf16[128,4608]{1,0:T(8,128)(2,1)} %param.10) | copy-start | bytes 3538948
  0.6 12.2 %copy-start.2 = (bf16[128,3584]{1,0:T(8,128)(2,1)S(1)}, bf16[128,3584]{1,0:T(8,128)(2,1)}, u32[]{:S(2)}) copy-start(bf16[128,3584]{1,0:T(8,128)(2,1)} %param.9) | copy-start | bytes 2752516
  3.8 16.4 %collective-permute-start.8 = (bf16[16,8192]{1,0:T(8,128)(2,1)}, bf16[16,8192]{1,0:T(8,128)(2,1)S(1)}, u32[]{:S(2)}, u32[]{:S(2)}) collective-permute-start(bf16[16,8192]{1,0:T(8,128)(2,1)} %pad_maximum_fusion.8), channel_id=1, source_target_pairs={{0,2},{1,3},{2,4},{3,5},{4,6},{5,7},{6,8},{7,9},{8,10},{9,11},{10,... | collective-permute-start | bytes 786440 | tf_op jit(solution)/shard_map/ppermute | solution.py:19
  7.5 15.3 %collective-permute-start.7 = (bf16[16,8192]{1,0:T(8,128)(2,1)}, bf16[16,8192]{1,0:T(8,128)(2,1)S(1)}, u32[]{:S(2)}, u32[]{:S(2)}) collective-permute-start(bf16[16,8192]{1,0:T(8,128)(2,1)} %pad_maximum_fusion.7), channel_id=1, source_target_pairs={{0,2},{1,3},{2,4},{3,5},{4,6},{5,7},{6,8},{7,9},{8,10},{9,11},{10,... | collective-permute-start | bytes 786440 | tf_op jit(solution)/shard_map/ppermute | solution.py:19
  9.7 18.6 %collective-permute-start = (bf16[16,8192]{1,0:T(8,128)(2,1)}, bf16[16,8192]{1,0:T(8,128)(2,1)S(1)}, u32[]{:S(2)}, u32[]{:S(2)}) collective-permute-start(bf16[16,8192]{1,0:T(8,128)(2,1)} %pad_maximum_fusion.5), channel_id=1, source_target_pairs={{0,2},{1,3},{2,4},{3,5},{4,6},{5,7},{6,8},{7,9},{8,10},{9,11},{10,... | collective-permute-start | bytes 786440 | tf_op jit(solution)/shard_map/ppermute | solution.py:19
  11.2 22.7 %collective-permute-start.1 = (bf16[16,8192]{1,0:T(8,128)(2,1)S(1)}, bf16[16,8192]{1,0:T(8,128)(2,1)S(1)}, u32[]{:S(2)}, u32[]{:S(2)}) collective-permute-start(bf16[16,8192]{1,0:T(8,128)(2,1)S(1)} %pad_maximum_fusion.6), channel_id=1, source_target_pairs={{0,2},{1,3},{2,4},{3,5},{4,6},{5,7},{6,8},{7,9},{8,10},{9,11},{10,... | collective-permute-start | bytes 786440 | tf_op jit(solution)/shard_map/ppermute | solution.py:19
  12.9 1.6 %copy-start.4 = (bf16[512]{0:T(512)(128)(2,1)S(1)}, bf16[512]{0:T(512)(128)(2,1)}, u32[]{:S(2)}) copy-start(bf16[512]{0:T(512)(128)(2,1)} %param.11) | copy-start | bytes 3076
  12.9 1.6 %copy-start.5 = (bf16[512]{0:T(512)(128)(2,1)S(1)}, bf16[512]{0:T(512)(128)(2,1)}, u32[]{:S(2)}) copy-start(bf16[512]{0:T(512)(128)(2,1)} %param.12) | copy-start | bytes 3076
  14.8 4.1 %copy-start = (bf16[512,3584]{1,0:T(8,128)(2,1)S(1)}, bf16[512,3584]{1,0:T(8,128)(2,1)}, u32[]{:S(2)}) copy-start(bf16[512,3584]{1,0:T(8,128)(2,1)} %param.7) | copy-start | bytes 11010052
  18.9 1.6 %copy-start.3 = (bf16[128,8192]{1,0:T(8,128)(2,1)S(1)}, bf16[128,8192]{1,0:T(8,128)(2,1)}, u32[]{:S(2)}) copy-start(bf16[128,8192]{1,0:T(8,128)(2,1)} %pad_maximum_fusion) | copy-start | bytes 6291460
  20.5 34.5 %collective-permute-start.14 = (bf16[128,8192]{1,0:T(8,128)(2,1)S(1)}, bf16[128,8192]{1,0:T(8,128)(2,1)S(1)}, u32[]{:S(2)}, u32[]{:S(2)}) collective-permute-start(bf16[128,8192]{1,0:T(8,128)(2,1)S(1)} %copy-done.3), channel_id=1, source_target_pairs={{0,1},{1,4},{2,3},{3,6},{4,5},{5,8},{6,7},{7,10},{8,9},{9,12},{10,... | collective-permute-start | bytes 6291464 | tf_op jit(solution)/shard_map/ppermute | solution.py:19
  22.8 13.0 %collective-permute-start.9 = (bf16[16,8192]{1,0:T(8,128)(2,1)S(1)}, bf16[16,8192]{1,0:T(8,128)(2,1)S(1)}, u32[]{:S(2)}, u32[]{:S(2)}) collective-permute-start(bf16[16,8192]{1,0:T(8,128)(2,1)S(1)} %collective-permute-done.7), channel_id=1, source_target_pairs={{0,16},{1,17},{2,18},{3,19},{4,20},{5,21},{6,22},{7,23},{8,24},{9,... | collective-permute-start | bytes 786440 | tf_op jit(solution)/shard_map/ppermute | solution.py:19
  24.6 13.1 %collective-permute-start.10 = (bf16[16,8192]{1,0:T(8,128)(2,1)S(1)}, bf16[16,8192]{1,0:T(8,128)(2,1)S(1)}, u32[]{:S(2)}, u32[]{:S(2)}) collective-permute-start(bf16[16,8192]{1,0:T(8,128)(2,1)S(1)} %collective-permute-done.8), channel_id=1, source_target_pairs={{0,16},{1,17},{2,18},{3,19},{4,20},{5,21},{6,22},{7,23},{8,24},{9,... | collective-permute-start | bytes 786440 | tf_op jit(solution)/shard_map/ppermute | solution.py:19
  28.4 14.9 %collective-permute-start.2 = (bf16[16,8192]{1,0:T(8,128)(2,1)S(1)}, bf16[16,8192]{1,0:T(8,128)(2,1)S(1)}, u32[]{:S(2)}, u32[]{:S(2)}) collective-permute-start(bf16[16,8192]{1,0:T(8,128)(2,1)S(1)} %collective-permute-done), channel_id=1, source_target_pairs={{0,16},{1,17},{2,18},{3,19},{4,20},{5,21},{6,22},{7,23},{8,24},{9,... | collective-permute-start | bytes 786440 | tf_op jit(solution)/shard_map/ppermute | solution.py:19
  34.0 13.4 %collective-permute-start.3 = (bf16[16,8192]{1,0:T(8,128)(2,1)S(1)}, bf16[16,8192]{1,0:T(8,128)(2,1)S(1)}, u32[]{:S(2)}, u32[]{:S(2)}) collective-permute-start(bf16[16,8192]{1,0:T(8,128)(2,1)S(1)} %collective-permute-done.1), channel_id=1, source_target_pairs={{0,16},{1,17},{2,18},{3,19},{4,20},{5,21},{6,22},{7,23},{8,24},{9,... | collective-permute-start | bytes 786440 | tf_op jit(solution)/shard_map/ppermute | solution.py:19
  37.8 9.9 %collective-permute-start.11 = (bf16[64,8192]{1,0:T(8,128)(2,1)S(1)}, bf16[64,8192]{1,0:T(8,128)(2,1)S(1)}, u32[]{:S(2)}, u32[]{:S(2)}) collective-permute-start(bf16[64,8192]{1,0:T(8,128)(2,1)S(1)} %pad_maximum_fusion.2), channel_id=1, source_target_pairs={{0,1},{1,0},{2,3},{3,2},{4,5},{5,4},{6,7},{7,6},{8,9},{9,8},{10,11... | collective-permute-start | bytes 3145736 | tf_op jit(solution)/shard_map/ppermute | solution.py:19
  47.4 2.7 %collective-permute-start.4 = (bf16[64,8192]{1,0:T(8,128)(2,1)S(1)}, bf16[64,8192]{1,0:T(8,128)(2,1)S(1)}, u32[]{:S(2)}, u32[]{:S(2)}) collective-permute-start(bf16[64,8192]{1,0:T(8,128)(2,1)S(1)} %pad_maximum_fusion.1), channel_id=1, source_target_pairs={{0,1},{1,0},{2,3},{3,2},{4,5},{5,4},{6,7},{7,6},{8,9},{9,8},{10,11... | collective-permute-start | bytes 3145736 | tf_op jit(solution)/shard_map/ppermute | solution.py:19
  47.6 4.1 %slice-start = ((s8[4718592]{0:T(1024)(128)(4,1)}), s8[4194304]{0:T(1024)(128)(4,1)S(1)}, s32[]{:S(2)}) async-start(s8[4718592]{0:T(1024)(128)(4,1)} %bitcast.30), calls=%async_computation | async-start | bytes 8388608
  47.8 3.8 %slice-start.1 = ((s8[4718592]{0:T(1024)(128)(4,1)}), s8[524288]{0:T(1024)(128)(4,1)S(1)}, s32[]{:S(2)}) async-start(s8[4718592]{0:T(1024)(128)(4,1)} %bitcast.30), calls=%async_computation.1 | async-start | bytes 1048576
  56.3 1.7 %copy-start.6 = (s32[512]{0:T(512)S(1)}, s32[512]{0:T(512)}, u32[]{:S(2)}) copy-start(s32[512]{0:T(512)} %param.13) | copy-start | bytes 6148
  60.4 8.3 %collective-permute-start.5 = (bf16[64,3584]{1,0:T(8,128)(2,1)S(1)}, bf16[64,3584]{1,0:T(8,128)(2,1)S(1)}, u32[]{:S(2)}, u32[]{:S(2)}) collective-permute-start(bf16[64,3584]{1,0:T(8,128)(2,1)S(1)} %slice.140), channel_id=1, source_target_pairs={{0,1},{1,0},{2,3},{3,2},{4,5},{5,4},{6,7},{7,6},{8,9},{9,8},{10,11... | collective-permute-start | bytes 1376264 | tf_op jit(solution)/shard_map/ppermute | solution.py:19
  61.3 8.9 %collective-permute-start.12 = (bf16[64,3584]{1,0:T(8,128)(2,1)S(1)}, bf16[64,3584]{1,0:T(8,128)(2,1)S(1)}, u32[]{:S(2)}, u32[]{:S(2)}) collective-permute-start(bf16[64,3584]{1,0:T(8,128)(2,1)S(1)} %slice.139), channel_id=1, source_target_pairs={{0,1},{1,0},{2,3},{3,2},{4,5},{5,4},{6,7},{7,6},{8,9},{9,8},{10,11... | collective-permute-start | bytes 1376264 | tf_op jit(solution)/shard_map/ppermute | solution.py:19
  62.4 32.8 %collective-permute-start.15 = (bf16[128,3584]{1,0:T(8,128)(2,1)S(1)}, bf16[128,3584]{1,0:T(8,128)(2,1)S(1)}, u32[]{:S(2)}, u32[]{:S(2)}) collective-permute-start(bf16[128,3584]{1,0:T(8,128)(2,1)S(1)} %convolution_convert_fusion.1), channel_id=1, source_target_pairs={{0,13},{1,0},{2,15},{3,2},{4,1},{5,4},{6,3},{7,6},{8,5},{9,8},{10,... | collective-permute-start | bytes 2752520 | tf_op jit(solution)/shard_map/ppermute | solution.py:19
  68.8 21.1 %collective-permute-start.6 = (bf16[64,3584]{1,0:T(8,128)(2,1)S(1)}, bf16[64,3584]{1,0:T(8,128)(2,1)S(1)}, u32[]{:S(2)}, u32[]{:S(2)}) collective-permute-start(bf16[64,3584]{1,0:T(8,128)(2,1)S(1)} %fusion.35), channel_id=1, source_target_pairs={{0,14},{1,15},{2,0},{3,1},{4,2},{5,3},{6,4},{7,5},{8,6},{9,7},{10,... | collective-permute-start | bytes 1376264 | tf_op jit(solution)/shard_map/ppermute | solution.py:19
  70.3 24.8 %collective-permute-start.13 = (bf16[64,3584]{1,0:T(8,128)(2,1)S(1)}, bf16[64,3584]{1,0:T(8,128)(2,1)S(1)}, u32[]{:S(2)}, u32[]{:S(2)}) collective-permute-start(bf16[64,3584]{1,0:T(8,128)(2,1)S(1)} %fusion.34), channel_id=1, source_target_pairs={{0,14},{1,15},{2,0},{3,1},{4,2},{5,3},{6,4},{7,5},{8,6},{9,7},{10,... | collective-permute-start | bytes 1376264 | tf_op jit(solution)/shard_map/ppermute | solution.py:19

commit v2 on v1

v2 whole, which is shorter than its diff:
```python
import jax
import jax.numpy as jnp
from jax import lax
from jax.experimental import pallas as pl
from jax.sharding import PartitionSpec as P

hard_weight = 0.5
CHUNKS = 4
BOTH = ("grp", "seq")


def permuted(value, move):
    groups, count = lax.axis_size("grp"), lax.axis_size("seq")
    pairs = []
    for group in range(groups):
        for place in range(count):
            to_group, to_place = move(group, place)
            pairs.append((group * count + place, to_group * count + to_place % count))
    return lax.ppermute(value, BOTH, pairs)


def next_chip(group, place):
    return group, place + 2


def previous_chip(group, place):
    return group, place - 2


def other_plane(group, place):
    return 1 - group, place


def other_core(group, place):
    return group, place + 1 - 2 * (place % 2)


def extra_out(group, place):
    return group, place + 1 + 2 * (place % 2)


def extra_back(group, place):
    return group, place - 3 + 2 * (place % 2)


def gate(values, ready):
    operands = list(values) + list(ready)
    anywhere = pl.BlockSpec(memory_space=pl.ANY)
    return pl.pallas_call(
        lambda *refs: None,
        out_shape=[jax.ShapeDtypeStruct(value.shape, value.dtype) for value in values],
        in_specs=[anywhere] * len(operands),
        out_specs=[anywhere] * len(values),
        input_output_aliases={index: index for index in range(len(values))},
    )(*operands)


def body(student_rows, teacher_rows, student_head, teacher_head, student_lse, teacher_lse, targets):
    count = lax.axis_size("seq")
    place = lax.axis_index("seq")
    plane = lax.axis_index("grp")
    core = place % 2
    width, depth = student_head.shape
    half = width // 2
    piece = half // CHUNKS
    student_norm = student_lse.astype(jnp.float32)
    teacher_norm = teacher_lse.astype(jnp.float32)

    def logits(rows, panel, norm):
        return lax.dot_general(
            rows, panel, (((1,), (1,)), ((), ())), preferred_element_type=jnp.float32
        ) - norm[:, None]

    def terms(ls, lt, ids):
        ps = jnp.exp(ls)
        pt = jnp.exp(lt)
        onehot = (targets[:, None] == ids[None, :]).astype(jnp.float32)
        scores = ((1.0 + hard_weight) * ps - pt - hard_weight * onehot).astype(jnp.bfloat16)
        losses = jnp.sum(pt * (lt - ls) - hard_weight * onehot * ls, axis=1)
        return scores, losses

    def head_part(scores):
        return lax.dot_general(
            scores, student_rows, (((0,), (0,)), ((), ())), preferred_element_type=jnp.float32
        )

    def chunk(k):
        at = plane * half + k * piece
        return jnp.concatenate(
            [
                lax.dynamic_slice_in_dim(student_head, at, piece, 0),
                lax.dynamic_slice_in_dim(teacher_head, at, piece, 0),
            ],
            axis=1,
        )

    def own_half(k):
        lo, hi = k * half, (k + 1) * half
        return jnp.concatenate([student_head[lo:hi], teacher_head[lo:hi]], axis=1)

    ids_in = jnp.arange(width, dtype=jnp.int32)
    chunks = [chunk(k) for k in range(CHUNKS)]
    sends = [own_half(0), own_half(1)]

    crossed = [permuted(chunks[0], next_chip), permuted(chunks[1], next_chip), None, None]
    crossed[0], chunks[2], norm = gate([crossed[0], chunks[2], student_norm], [])
    swapped = [permuted(crossed[0], other_plane), None, None, None]
    crossed[2] = permuted(chunks[2], next_chip)
    ls = logits(student_rows, student_head, norm)
    crossed[1], chunks[3], norm = gate([crossed[1], chunks[3], teacher_norm], [ls])
    swapped[1] = permuted(crossed[1], other_plane)
    crossed[3] = permuted(chunks[3], next_chip)
    lt = logits(teacher_rows, teacher_head, norm)
    own_scores, losses = terms(ls, lt, place * width + ids_in)
    loss_total = losses
    score_list, panel_list = [], []
    crossed[2], sends[0], own_scores = gate([crossed[2], sends[0], own_scores], [])
    swapped[2] = permuted(crossed[2], other_plane)
    extra = [permuted(sends[0], extra_out), None]

    near = (place - 2) % count
    far = (place - 1 - 2 * core) % count

    def stage_ids(stage):
        rows = jnp.arange(half // 2, dtype=jnp.int32) + stage * (half // 2)
        inside = jnp.concatenate([plane * half + rows, (1 - plane) * half + rows])
        return jnp.concatenate([near * width + inside, far * width + inside])

    def stage_terms(stage, mine, theirs, norm, norm_t):
        both = jnp.concatenate([mine, theirs], axis=0)
        panel = both[:, :depth]
        scores, losses = terms(
            logits(student_rows, panel, norm), logits(teacher_rows, both[:, depth:], norm_t), stage_ids(stage)
        )
        part = head_part(scores)
        return panel, scores, losses, part[:half], part[half:].astype(jnp.bfloat16)

    mine0 = jnp.concatenate([crossed[0], crossed[1], swapped[0], swapped[1]], axis=0)
    mine0, own_scores = gate([mine0, own_scores], [])
    theirs0 = permuted(mine0, other_core)
    own_part = head_part(own_scores)
    score_list.append(own_scores)
    panel_list.append(student_head)
    crossed[3], = gate([crossed[3]], [own_part])
    swapped[3] = permuted(crossed[3], other_plane)
    theirs0, norm, norm_t = gate([theirs0, student_norm, teacher_norm], [])
    panel, scores, losses, keep, give = stage_terms(0, mine0, theirs0, norm, norm_t)
    loss_total = loss_total + losses
    score_list.append(scores)
    panel_list.append(panel)
    got = permuted(give, other_core)
    total = (keep + got.astype(jnp.float32)).astype(jnp.bfloat16)
    back0 = permuted(total, previous_chip)

    swapped[2], swapped[3], sends[1] = gate([swapped[2], swapped[3], sends[1]], [total])
    mine1 = jnp.concatenate([crossed[2], crossed[3], swapped[2], swapped[3]], axis=0)
    theirs1 = permuted(mine1, other_core)
    extra[1] = permuted(sends[1], extra_out)
    theirs1, norm, norm_t = gate([theirs1, student_norm, teacher_norm], [])
    panel, scores, losses, keep, give = stage_terms(1, mine1, theirs1, norm, norm_t)
    loss_total = loss_total + losses
    score_list.append(scores)
    panel_list.append(panel)
    got = permuted(give, other_core)

    extra_id = jnp.where(core == 1, place - 1, place - 3) % count
    extra_parts = []

    def extra_terms(k, value, norm, norm_t):
        ids = extra_id * width + k * half + jnp.arange(half, dtype=jnp.int32)
        scores, losses = terms(
            logits(student_rows, value[:, :depth], norm), logits(teacher_rows, value[:, depth:], norm_t), ids
        )
        return scores, losses, head_part(scores).astype(jnp.bfloat16)

    value, norm, norm_t = gate([extra[0], student_norm, teacher_norm], [give])
    scores, losses, part = extra_terms(0, value, norm, norm_t)
    loss_total = loss_total + losses
    score_list.append(scores)
    panel_list.append(value[:, :depth])
    total = (keep + got.astype(jnp.float32)).astype(jnp.bfloat16)
    total, part = gate([total, part], [])
    back1 = permuted(total, previous_chip)
    extra_parts.append(permuted(part, extra_back))

    value, norm, norm_t = gate([extra[1], student_norm, teacher_norm], [total])
    scores, losses, part = extra_terms(1, value, norm, norm_t)
    loss_total = loss_total + losses
    score_list.append(scores)
    panel_list.append(value[:, :depth])
    part, scores = gate([part, scores], [])
    extra_parts.append(permuted(part, extra_back))
    score_list[-1] = scores

    rows_grad = jnp.dot(
        jnp.concatenate(score_list, axis=1),
        jnp.concatenate(panel_list, axis=0),
        preferred_element_type=jnp.float32,
    ).astype(jnp.bfloat16)

    quarter = half // 2
    mine_parts = jnp.concatenate([back0[:quarter], back1[:quarter]], axis=0)
    other_parts = jnp.concatenate([back0[quarter:], back1[quarter:]], axis=0)
    first = jnp.where(plane == 0, mine_parts, other_parts)
    second = jnp.where(plane == 0, other_parts, mine_parts)
    from_next = jnp.concatenate([first, second], axis=0)
    extra_part = jnp.concatenate(extra_parts, axis=0)
    head_grad = (
        own_part + from_next.astype(jnp.float32) + extra_part.astype(jnp.float32)
    ).astype(jnp.bfloat16)
    return (head_grad, rows_grad, loss_total)


def solution(mesh):
    placed = (
        P(("grp", "seq"), None),
        P(("grp", "seq"), None),
        P("seq", None),
        P("seq", None),
        P(("grp", "seq")),
        P(("grp", "seq")),
        P(("grp", "seq")),
    )
    return jax.shard_map(
        body,
        mesh=mesh,
        in_specs=placed,
        out_specs=(P(("grp", "seq"), None), P(("grp", "seq"), None), P(("grp", "seq"))),
        check_vma=False,
    )
```

time: 97.1 us -> 130 us (1.34); the launches traced: 96.9 us -> 128 us
  waiting for transfers between devices: 47.5 us -> 10.1 us
  local copies, waits for them, and re-layouts: 3.38 us -> 31.2 us
  matrix products: 21.8 us -> 47.9 us
  other arithmetic: 5.06 us -> 15.1 us
  starting transfers between devices: 18.1 us -> 22.3 us
    ppermute x16 -> x18, waiting for transfers between devices: 47.5 us -> 10.1 us  [permuted(): return lax.ppermute(value, BOTH, pairs)]
    dot_general x12 -> x15, matrix products: 18.2 us -> 41.9 us  [the longest x10 33.3 us: logits(): lax.dot_general(rows, panel, (((1,), (1,)), ((), ())), preferred_element_...]
    unnamed x26 -> x137, local copies, waits for them, and re-layouts: 0.47 us -> 19.9 us
    concatenate x9, other arithmetic: 4 us -> 9.37 us  [the longest x2 3.16 us: own_half(): return jnp.concatenate([student_head[lo:hi], teacher_head[lo:hi]], axis=1)]
    concatenate x2 -> x4, local copies, waits for them, and re-layouts: 0.14 us -> 5.47 us  [the longest x2 3.56 us: stage_terms(): both = jnp.concatenate([mine, theirs], axis=0)]
    ppermute x16 -> x18, starting transfers between devices: 18.1 us -> 22.3 us  [permuted(): return lax.ppermute(value, BOTH, pairs)]
    dynamic_slice x0 -> x2, local copies, waits for them, and re-layouts: none -> 3.87 us  [the longest x1 2.01 us: chunk(): lax.dynamic_slice_in_dim(teacher_head, at, piece, 0)]
    dot_general x1, matrix products: 3.57 us -> 6 us  [body(): jnp.dot(jnp.concatenate(score_list, axis=1), jnp.concatenate(panel_list,...]
  transfers between devices with their start and end apart: 16 -> 18, of which waited for: 9 -> 3; matrix products, arithmetic and copies ran while one was open for 20% -> 66% of each run, Pallas kernels for 0% -> 0%
where the time goes in v2:
time: 130 us; the launch traced here: 128 us
  matrix products  47.9 us (37%)
  local copies, waits for them, and re-layouts  31.2 us (24%)
  starting transfers between devices  22.3 us (17%)
  other arithmetic  15.1 us (12%)
  waiting for transfers between devices  10.1 us (8%)
  between operations  1.31 us (1%)
    dot_general x10, matrix products, logits(): lax.dot_general(rows, panel, (((1,), (1,)), ((), ())), preferred_element_...  33.3 us
    ppermute x18, starting transfers between devices, permuted(): return lax.ppermute(value, BOTH, pairs)  22.3 us
    unnamed x137, local copies, waits for them, and re-layouts  19.9 us
    ppermute x18, waiting for transfers between devices, permuted(): return lax.ppermute(value, BOTH, pairs)  10.1 us
    dot_general x5, matrix products, head_part(): lax.dot_general(scores, student_rows, (((0,), (0,)), ((), ())), preferred...  8.56 us
    dot_general x1, matrix products, body(): jnp.dot(jnp.concatenate(score_list, axis=1), jnp.concatenate(panel_list,...  6 us
    concatenate x2, local copies, waits for them, and re-layouts, stage_terms(): both = jnp.concatenate([mine, theirs], axis=0)  3.56 us
    concatenate x2, other arithmetic, own_half(): return jnp.concatenate([student_head[lo:hi], teacher_head[lo:hi]], axis=1)  3.16 us
  transfers between devices with their start and end apart: 18, of which 3 were waited for; matrix products, arithmetic and copies ran while one was open for 66% of the time, Pallas kernels for 0%

profile of v2, /device:TPU:0, one launch (start us, length us, event | category | flops | bytes accessed | tf_op | source)
XLA Modules:
  0.0 128.0 jit_solution(9852349113544868726)
XLA Ops:
  0.6 1.9 %constant_dynamic-slice_fusion.5 = (bf16[16,3584]{1,0:T(8,128)(2,1)}, bf16[16,3584]{1,0:T(8,128)(2,1)}, bf16[16,3584]{1,0:T(8,128)(2,1)S(1)}, bf16[16,3584]{1,0:T(8,128)(2,1)S(1)}) fusion(bf16[128,3584]{1,0:T(8,128)(2,1)} %param.9, s32[]{:T(128)S(6)} %select_n.51, s32[]{:T(128)S(6)} %select_n.53, s32[]{:T(128)S(6)} %select_n.52, s32[]{:T(128)S(6)} %select_n.50), kind=kLoop, calls=%fused_computation.92 | loop fusion | bytes 917520 | tf_op jit(solution)/shard_map/dynamic_slice | solution.py:91
  2.5 2.0 %constant_dynamic-slice_fusion.4 = (bf16[16,4608]{1,0:T(8,128)(2,1)}, bf16[16,4608]{1,0:T(8,128)(2,1)}, bf16[16,4608]{1,0:T(8,128)(2,1)S(1)}, bf16[16,4608]{1,0:T(8,128)(2,1)S(1)}) fusion(bf16[128,4608]{1,0:T(8,128)(2,1)} %param.10, s32[]{:T(128)S(6)} %select_n.51, s32[]{:T(128)S(6)} %select_n.53, s32[]{:T(128)S(6)} %select_n.52, s32[]{:T(128)S(6)} %select_n.50), kind=kLoop, calls=%fused_computation.91 | loop fusion | bytes 1179664 | tf_op jit(solution)/shard_map/dynamic_slice | solution.py:92
  5.3 2.9 %collective-permute-start = (bf16[16,8192]{1,0:T(8,128)(2,1)}, bf16[16,8192]{1,0:T(8,128)(2,1)S(1)}, u32[]{:S(2)}, u32[]{:S(2)}) collective-permute-start(bf16[16,8192]{1,0:T(8,128)(2,1)} %pad_maximum_fusion.6), channel_id=1, source_target_pairs={{0,2},{1,3},{2,4},{3,5},{4,6},{5,7},{6,8},{7,9},{8,10},{9,11},{10,... | collective-permute-start | bytes 786440 | tf_op jit(solution)/shard_map/ppermute | solution.py:19
  9.0 1.5 %collective-permute-start.1 = (bf16[16,8192]{1,0:T(8,128)(2,1)}, bf16[16,8192]{1,0:T(8,128)(2,1)}, u32[]{:S(2)}, u32[]{:S(2)}) collective-permute-start(bf16[16,8192]{1,0:T(8,128)(2,1)} %pad_maximum_fusion.8), channel_id=1, source_target_pairs={{0,2},{1,3},{2,4},{3,5},{4,6},{5,7},{6,8},{7,9},{8,10},{9,11},{10,... | collective-permute-start | bytes 786440 | tf_op jit(solution)/shard_map/ppermute | solution.py:19
  14.2 2.1 %pad_maximum_fusion.2.refs_2_ = bf16[64,8192]{1,0:T(8,128)(2,1)} fusion(bf16[64,4608]{1,0:T(8,128)(2,1)S(1)} %get-tuple-element.68, bf16[64,3584]{1,0:T(8,128)(2,1)} %get-tuple-element.76), kind=kLoop, calls=%fused_computation.26 | loop fusion | flops 2097152 | bytes 2097152 | tf_op jit(solution)/shard_map/concatenate | solution.py:99
  25.9 1.5 %collective-permute-start.2 = (bf16[16,8192]{1,0:T(8,128)(2,1)}, bf16[16,8192]{1,0:T(8,128)(2,1)S(1)}, u32[]{:S(2)}, u32[]{:S(2)}) collective-permute-start(bf16[16,8192]{1,0:T(8,128)(2,1)} %get-tuple-element.33), channel_id=1, source_target_pairs={{0,16},{1,17},{2,18},{3,19},{4,20},{5,21},{6,22},{7,23},{8,24},{9,... | collective-permute-start | bytes 786440 | tf_op jit(solution)/shard_map/ppermute | solution.py:19
  27.4 3.9 %broadcast_subtract_fusion.refs_3_ = f32[512,128]{1,0:T(8,128)} fusion(f32[512]{0:T(512)} %get-tuple-element.34, bf16[512,3584]{1,0:T(8,128)(2,1)} %param.7, bf16[128,3584]{1,0:T(8,128)(2,1)S(1)} %copy-done.5), kind=kOutput, calls=%fused_computation.77 | convolution fusion | flops 469827584 | bytes 4851712 | tf_op jit(solution)/shard_map/dot_general | solution.py:70
  31.3 1.6 %collective-permute-start.8 = (bf16[16,8192]{1,0:T(8,128)(2,1)}, bf16[16,8192]{1,0:T(8,128)(2,1)}, u32[]{:S(2)}, u32[]{:S(2)}) collective-permute-start(bf16[16,8192]{1,0:T(8,128)(2,1)} %get-tuple-element.45), channel_id=1, source_target_pairs={{0,2},{1,3},{2,4},{3,5},{4,6},{5,7},{6,8},{7,9},{8,10},{9,11},{10,... | collective-permute-start | bytes 786440 | tf_op jit(solution)/shard_map/ppermute | solution.py:19
  33.4 4.6 %fusion.30 = (bf16[512,128]{1,0:T(8,128)(2,1)}, f32[512,128]{1,0:T(8,128)}) fusion(f32[512,128]{1,0:T(8,128)} %broadcast_subtract_fusion.refs_3_, s32[128]{0:T(128)S(1)} %copy-done.57, f32[512]{0:T(512)} %get-tuple-element.37, s32[512]{0:T(512)S(1)} %copy-done.46, bf16[512,4608]{1,0:T(8,128)(2,1)} %param.8, bf16[128,4608]{1,0:T(8,128)(2,1)S(1)} %copy-done.9), kind=kOutput, calls=%fused_computation.58 | convolution fusion | flops 604438528 | bytes 6558208 | tf_op jit(solution)/shard_map/dot_general | solution.py:70
  40.2 1.7 %constant_dynamic-update-slice_fusion.6 = bf16[128,8192]{1,0:T(8,128)(2,1)} fusion(bf16[16,8192]{1,0:T(8,128)(2,1)} %get-tuple-element.44), kind=kLoop, calls=%fused_computation.84 | loop fusion | bytes 524288
  41.9 2.0 %pad_maximum_fusion.refs_0_ = bf16[64,8192]{1,0:T(8,128)(2,1)} fusion(bf16[16,8192]{1,0:T(8,128)(2,1)S(1)} %collective-permute-done.3, bf16[16,8192]{1,0:T(8,128)(2,1)S(1)} %collective-permute-done.2, bf16[16,8192]{1,0:T(8,128)(2,1)} %get-tuple-element.35, bf16[16,8192]{1,0:T(8,128)(2,1)S(1)} %copy-done.28), kind=kLoop, calls=%fused_computation.24 | loop fusion | flops 4194304 | bytes 2097152 | tf_op jit(solution)/shard_map/concatenate | solution.py:138
  44.4 4.1 %fusion.51.refs_1_ = f32[128,3584]{1,0:T(8,128)} fusion(bf16[512,128]{1,0:T(8,128)(2,1)} %get-tuple-element.39, bf16[512,3584]{1,0:T(8,128)(2,1)} %param.7), kind=kOutput, calls=%fused_computation.115 | convolution fusion | flops 469762048 | bytes 5636096 | tf_op jit(solution)/shard_map/dot_general | solution.py:83
  49.0 1.7 %constant_dynamic-update-slice_fusion.5 = bf16[128,8192]{1,0:T(8,128)(2,1)} fusion(bf16[128,8192]{1,0:T(8,128)(2,1)} %constant_dynamic-update-slice_fusion.6, bf16[16,8192]{1,0:T(8,128)(2,1)} %shard_map.99), kind=kLoop, calls=%fused_computation.83 | loop fusion | bytes 524288
  52.1 3.9 %fusion.15 = f32[512,128]{1,0:T(8,128)S(1)} fusion(bf16[512,4608]{1,0:T(8,128)(2,1)} %param.8, bf16[128,8192]{1,0:T(8,128)(2,1)S(1)} %constant_dynamic-update-slice_fusion, f32[512]{0:T(512)S(1)} %copy-done.44), kind=kOutput, calls=%fused_computation.15 | convolution fusion | flops 604045312 | bytes 6162432 | tf_op jit(solution)/shard_map/dot_general | solution.py:70
  56.1 1.8 %fusion.33 = (bf16[512,128]{1,0:T(8,128)(2,1)S(1)}, f32[512,128]{1,0:T(8,128)}) fusion(f32[512,128]{1,0:T(8,128)S(1)} %fusion.15, s32[128]{0:T(128)S(1)} %pad_add_fusion.1, s32[512]{0:T(512)S(1)} %copy-done.46, f32[512]{0:T(512)S(1)} %copy-done.45, bf16[512,3584]{1,0:T(8,128)(2,1)S(1)} %copy-done, bf16[128,8192]{1,0:T(8,128)(2,1)S(1)} %constant_dynamic-update-slice_fusion), kind=kOutput, calls=%fused_computation.61 | convolution fusion | flops 470220800 | bytes 5247488 | tf_op jit(solution)/shard_map/dot_general | solution.py:70
  61.2 3.2 %collective-permute-start.7 = (bf16[64,3584]{1,0:T(8,128)(2,1)S(1)}, bf16[64,3584]{1,0:T(8,128)(2,1)S(1)}, u32[]{:S(2)}, u32[]{:S(2)}) collective-permute-start(bf16[64,3584]{1,0:T(8,128)(2,1)S(1)} %fusion.23.refs_3_), channel_id=1, source_target_pairs={{0,14},{1,15},{2,0},{3,1},{4,2},{5,3},{6,4},{7,5},{8,6},{9,7},{10,... | collective-permute-start | bytes 1376264 | tf_op jit(solution)/shard_map/ppermute | solution.py:19
  67.7 1.7 %constant_dynamic-update-slice_fusion.3 = bf16[128,8192]{1,0:T(8,128)(2,1)} fusion(bf16[128,8192]{1,0:T(8,128)(2,1)} %constant_dynamic-update-slice_fusion.4, bf16[16,8192]{1,0:T(8,128)(2,1)} %get-tuple-element.47), kind=kLoop, calls=%fused_computation.81 | loop fusion | bytes 524288
  69.3 6.0 %collective-permute-done.7 = bf16[64,3584]{1,0:T(8,128)(2,1)S(1)} collective-permute-done((bf16[64,3584]{1,0:T(8,128)(2,1)S(1)}, bf16[64,3584]{1,0:T(8,128)(2,1)S(1)}, u32[]{:S(2)}, u32[]{:S(2)}) %collective-permute-start.7) | collective-permute-done | bytes 458784 | tf_op jit(solution)/shard_map/ppermute | solution.py:19
  76.1 2.3 %constant_dynamic-update-slice_fusion.2 = bf16[128,8192]{1,0:T(8,128)(2,1)} fusion(bf16[128,8192]{1,0:T(8,128)(2,1)} %constant_dynamic-update-slice_fusion.3, bf16[64,8192]{1,0:T(8,128)(2,1)} %get-tuple-element.48), kind=kLoop, calls=%fused_computation.80 | loop fusion | bytes 2097152 | tf_op jit(solution)/shard_map/concatenate | solution.py:130
  78.5 4.2 %fusion.12 = f32[512,128]{1,0:T(8,128)S(1)} fusion(bf16[512,4608]{1,0:T(8,128)(2,1)} %param.8, bf16[128,8192]{1,0:T(8,128)(2,1)} %constant_dynamic-update-slice_fusion.2, f32[512]{0:T(512)S(1)} %copy-done.43), kind=kOutput, calls=%fused_computation.14 | convolution fusion | flops 604045312 | bytes 6162432 | tf_op jit(solution)/shard_map/dot_general | solution.py:70
  82.8 3.0 %fusion.35 = (f32[512]{0:T(512)S(1)}, f32[512]{0:T(512)S(1)}, f32[512]{0:T(512)}, bf16[512,128]{1,0:T(8,128)(2,1)S(1)}) fusion(f32[512,128]{1,0:T(8,128)S(1)} %copy-done.37, f32[512,128]{1,0:T(8,128)S(1)} %copy-done.24, s32[128]{0:T(128)S(1)} %copy-done.54, s32[512]{0:T(512)S(1)} %copy-done.46, s32[128]{0:T(128)S(1)} %copy-done.55, ...), kind=kOutput, calls=%fused_computation.63 | convolution fusion | flops 471529984 | bytes 6043136 | tf_op jit(solution)/shard_map/dot_general | solution.py:70
  86.6 2.3 %slice_dynamic-update-slice_fusion = bf16[512,3584]{1,0:T(8,128)(2,1)} fusion(bf16[512,3584]{1,0:T(8,128)(2,1)} %slice_dynamic-update-slice_fusion.1, bf16[128,8192]{1,0:T(8,128)(2,1)} %constant_dynamic-update-slice_fusion.2), kind=kLoop, calls=%fused_computation.34 | loop fusion | bytes 1835008
  88.9 4.0 %fusion.20 = f32[512,64]{1,0:T(8,128)S(1)} fusion(bf16[512,4608]{1,0:T(8,128)(2,1)} %param.8, bf16[64,8192]{1,0:T(8,128)(2,1)} %get-tuple-element.52, f32[512]{0:T(512)} %get-tuple-element.54), kind=kOutput, calls=%fused_computation.21 | convolution fusion | flops 302022656 | bytes 5441536 | tf_op jit(solution)/shard_map/dot_general | solution.py:70
  92.9 1.9 %slice_dynamic-update-slice_fusion.3 = bf16[512,3584]{1,0:T(8,128)(2,1)} fusion(bf16[512,3584]{1,0:T(8,128)(2,1)} %slice_dynamic-update-slice_fusion, bf16[64,8192]{1,0:T(8,128)(2,1)} %get-tuple-element.52), kind=kLoop, calls=%fused_computation.46 | loop fusion | bytes 917504
  94.9 2.8 %fusion.39 = (bf16[512,64]{1,0:T(8,128)(2,1)S(1)}, f32[512,64]{1,0:T(8,128)}) fusion(f32[512,64]{1,0:T(8,128)S(1)} %fusion.20, s32[64]{0:T(128)S(1)} %copy-done.52, s32[512]{0:T(512)S(1)} %copy-done.46, f32[512]{0:T(512)S(1)} %copy-done.42, bf16[512,3584]{1,0:T(8,128)(2,1)S(1)} %copy-done.2, bf16[64,8192]{1,0:T(8,128)(2,1)} %get-tuple-element.52), kind=kOutput, calls=%fused_computation.67 | convolution fusion | flops 235110400 | bytes 4460800 | tf_op jit(solution)/shard_map/dot_general | solution.py:70
  97.7 1.6 %convolution_convert_fusion.2.refs_1_ = bf16[64,3584]{1,0:T(8,128)(2,1)} fusion(bf16[512,64]{1,0:T(8,128)(2,1)S(1)} %get-tuple-element.96, bf16[512,3584]{1,0:T(8,128)(2,1)S(1)} %copy-done.2), kind=kOutput, calls=%fused_computation.2 | convolution fusion | flops 235110400 | bytes 4194304 | tf_op jit(solution)/shard_map/dot_general | solution.py:83
  99.3 1.9 %fusion.22.refs_0_ = bf16[64,3584]{1,0:T(8,128)(2,1)} fusion(f32[128,3584]{1,0:T(8,128)S(1)} %fusion.53, bf16[64,3584]{1,0:T(8,128)(2,1)} %collective-permute-done.12), kind=kLoop, calls=%fused_computation.30 | loop fusion | flops 688128 | bytes 1835008 | tf_op jit(solution)/shard_map/convert_element_type | solution.py:181
  101.2 5.2 %collective-permute-start.14 = (bf16[64,3584]{1,0:T(8,128)(2,1)}, bf16[64,3584]{1,0:T(8,128)(2,1)S(1)}, u32[]{:S(2)}, u32[]{:S(2)}) collective-permute-start(bf16[64,3584]{1,0:T(8,128)(2,1)} %get-tuple-element.55.refs_3_), channel_id=1, source_target_pairs={{0,14},{1,15},{2,0},{3,1},{4,2},{5,3},{6,4},{7,5},{8,6},{9,7},{10,... | collective-permute-start | bytes 1376264 | tf_op jit(solution)/shard_map/ppermute | solution.py:19
  107.3 4.0 %fusion.18 = f32[512,64]{1,0:T(8,128)S(1)} fusion(bf16[512,4608]{1,0:T(8,128)(2,1)} %param.8, bf16[64,8192]{1,0:T(8,128)(2,1)} %get-tuple-element.58, f32[512]{0:T(512)} %get-tuple-element.60), kind=kOutput, calls=%fused_computation.17 | convolution fusion | flops 302022656 | bytes 5441536 | tf_op jit(solution)/shard_map/dot_general | solution.py:70
  112.7 1.6 %convolution_convert_fusion.1.refs_0_ = bf16[64,3584]{1,0:T(8,128)(2,1)} fusion(bf16[512,64]{1,0:T(8,128)(2,1)S(1)} %get-tuple-element.83.refs_1_, bf16[512,3584]{1,0:T(8,128)(2,1)S(1)} %copy-done.3), kind=kOutput, calls=%fused_computation.1 | convolution fusion | flops 235110400 | bytes 4194304 | tf_op jit(solution)/shard_map/dot_general | solution.py:83
  116.9 6.0 %convolution_convert_fusion = bf16[512,3584]{1,0:T(8,128)(2,1)} fusion(bf16[512,512]{1,0:T(8,128)(2,1)S(1)} %concatenate.79, bf16[512,3584]{1,0:T(8,128)(2,1)} %slice_dynamic-update-slice_fusion.2), kind=kOutput, calls=%fused_computation | convolution fusion | flops 1880883200 | bytes 7864320 | tf_op jit(solution)/shard_map/dot_general | solution.py:195
  123.1 3.6 %collective-permute-done.15 = bf16[64,3584]{1,0:T(8,128)(2,1)S(1)} collective-permute-done((bf16[64,3584]{1,0:T(8,128)(2,1)S(1)}, bf16[64,3584]{1,0:T(8,128)(2,1)S(1)}, u32[]{:S(2)}, u32[]{:S(2)}) %collective-permute-start.15) | collective-permute-done | bytes 458784 | tf_op jit(solution)/shard_map/ppermute | solution.py:19
  (204 shorter events, 34.3 us)
Async XLA Ops:
  0.6 10.5 %copy-start.5 = (bf16[128,3584]{1,0:T(8,128)(2,1)S(1)}, bf16[128,3584]{1,0:T(8,128)(2,1)}, u32[]{:S(2)}) copy-start(bf16[128,3584]{1,0:T(8,128)(2,1)} %param.9) | copy-start | bytes 2752516
  2.5 9.6 %copy-start.9 = (bf16[128,4608]{1,0:T(8,128)(2,1)S(1)}, bf16[128,4608]{1,0:T(8,128)(2,1)}, u32[]{:S(2)}) copy-start(bf16[128,4608]{1,0:T(8,128)(2,1)} %param.10) | copy-start | bytes 3538948
  5.3 18.4 %collective-permute-start = (bf16[16,8192]{1,0:T(8,128)(2,1)}, bf16[16,8192]{1,0:T(8,128)(2,1)S(1)}, u32[]{:S(2)}, u32[]{:S(2)}) collective-permute-start(bf16[16,8192]{1,0:T(8,128)(2,1)} %pad_maximum_fusion.6), channel_id=1, source_target_pairs={{0,2},{1,3},{2,4},{3,5},{4,6},{5,7},{6,8},{7,9},{8,10},{9,11},{10,... | collective-permute-start | bytes 786440 | tf_op jit(solution)/shard_map/ppermute | solution.py:19
  9.0 22.3 %collective-permute-start.1 = (bf16[16,8192]{1,0:T(8,128)(2,1)}, bf16[16,8192]{1,0:T(8,128)(2,1)}, u32[]{:S(2)}, u32[]{:S(2)}) collective-permute-start(bf16[16,8192]{1,0:T(8,128)(2,1)} %pad_maximum_fusion.8), channel_id=1, source_target_pairs={{0,2},{1,3},{2,4},{3,5},{4,6},{5,7},{6,8},{7,9},{8,10},{9,11},{10,... | collective-permute-start | bytes 786440 | tf_op jit(solution)/shard_map/ppermute | solution.py:19
  16.4 4.4 %copy-start.51 = (bf16[512]{0:T(512)(128)(2,1)S(1)}, bf16[512]{0:T(512)(128)(2,1)}, u32[]{:S(2)}) copy-start(bf16[512]{0:T(512)(128)(2,1)} %param.11) | copy-start | bytes 3076
  18.4 37.6 %copy-start.53 = (s32[128]{0:T(128)}, s32[128]{0:T(128)S(1)}, u32[]{:S(2)}) copy-start(s32[128]{0:T(128)S(1)} %pad_add_fusion.1) | copy-start | bytes 1540
  18.4 12.8 %copy-start.40 = (f32[512]{0:T(512)}, f32[512]{0:T(512)S(1)}, u32[]{:S(2)}) copy-start(f32[512]{0:T(512)S(1)} %convert_element_type.59.refs_2_) | copy-start | bytes 6148
  24.4 13.6 %collective-permute-start.4 = (bf16[16,8192]{1,0:T(8,128)(2,1)}, bf16[16,8192]{1,0:T(8,128)(2,1)S(1)}, u32[]{:S(2)}, u32[]{:S(2)}) collective-permute-start(bf16[16,8192]{1,0:T(8,128)(2,1)} %get-tuple-element.36), channel_id=1, source_target_pairs={{0,2},{1,3},{2,4},{3,5},{4,6},{5,7},{6,8},{7,9},{8,10},{9,11},{10,... | collective-permute-start | bytes 786440 | tf_op jit(solution)/shard_map/ppermute | solution.py:19
  25.9 16.0 %collective-permute-start.2 = (bf16[16,8192]{1,0:T(8,128)(2,1)}, bf16[16,8192]{1,0:T(8,128)(2,1)S(1)}, u32[]{:S(2)}, u32[]{:S(2)}) collective-permute-start(bf16[16,8192]{1,0:T(8,128)(2,1)} %get-tuple-element.33), channel_id=1, source_target_pairs={{0,16},{1,17},{2,18},{3,19},{4,20},{5,21},{6,22},{7,23},{8,24},{9,... | collective-permute-start | bytes 786440 | tf_op jit(solution)/shard_map/ppermute | solution.py:19
  27.4 6.0 %copy-start.46 = (s32[512]{0:T(512)S(1)}, s32[512]{0:T(512)}, u32[]{:S(2)}) copy-start(s32[512]{0:T(512)} %param.13) | copy-start | bytes 6148
  27.4 6.0 %copy-start.57 = (s32[128]{0:T(128)S(1)}, s32[128]{0:T(128)}, u32[]{:S(2)}) copy-start(s32[128]{0:T(128)} %iota_add_fusion.5) | copy-start | bytes 1540
  31.3 17.2 %collective-permute-start.8 = (bf16[16,8192]{1,0:T(8,128)(2,1)}, bf16[16,8192]{1,0:T(8,128)(2,1)}, u32[]{:S(2)}, u32[]{:S(2)}) collective-permute-start(bf16[16,8192]{1,0:T(8,128)(2,1)} %get-tuple-element.45), channel_id=1, source_target_pairs={{0,2},{1,3},{2,4},{3,5},{4,6},{5,7},{6,8},{7,9},{8,10},{9,11},{10,... | collective-permute-start | bytes 786440 | tf_op jit(solution)/shard_map/ppermute | solution.py:19
  32.9 9.0 %collective-permute-start.3 = (bf16[16,8192]{1,0:T(8,128)(2,1)}, bf16[16,8192]{1,0:T(8,128)(2,1)S(1)}, u32[]{:S(2)}, u32[]{:S(2)}) collective-permute-start(bf16[16,8192]{1,0:T(8,128)(2,1)} %get-tuple-element.35), channel_id=1, source_target_pairs={{0,16},{1,17},{2,18},{3,19},{4,20},{5,21},{6,22},{7,23},{8,24},{9,... | collective-permute-start | bytes 786440 | tf_op jit(solution)/shard_map/ppermute | solution.py:19
  38.7 25.8 %collective-permute-start.9 = (bf16[16,8192]{1,0:T(8,128)(2,1)}, bf16[16,8192]{1,0:T(8,128)(2,1)S(1)}, u32[]{:S(2)}, u32[]{:S(2)}) collective-permute-start(bf16[16,8192]{1,0:T(8,128)(2,1)} %get-tuple-element.44), channel_id=1, source_target_pairs={{0,16},{1,17},{2,18},{3,19},{4,20},{5,21},{6,22},{7,23},{8,24},{9,... | collective-permute-start | bytes 786440 | tf_op jit(solution)/shard_map/ppermute | solution.py:19
  43.9 6.9 %collective-permute-start.5 = (bf16[64,8192]{1,0:T(8,128)(2,1)}, bf16[64,8192]{1,0:T(8,128)(2,1)}, u32[]{:S(2)}, u32[]{:S(2)}) collective-permute-start(bf16[64,8192]{1,0:T(8,128)(2,1)} %get-tuple-element.40), channel_id=1, source_target_pairs={{0,1},{1,0},{2,3},{3,2},{4,5},{5,4},{6,7},{7,6},{8,9},{9,8},{10,11... | collective-permute-start | bytes 3145736 | tf_op jit(solution)/shard_map/ppermute | solution.py:19
  43.9 45.0 %collective-permute-start.13 = (bf16[64,8192]{1,0:T(8,128)(2,1)}, bf16[64,8192]{1,0:T(8,128)(2,1)}, u32[]{:S(2)}, u32[]{:S(2)}) collective-permute-start(bf16[64,8192]{1,0:T(8,128)(2,1)} %get-tuple-element.51), channel_id=1, source_target_pairs={{0,1},{1,4},{2,3},{3,6},{4,5},{5,8},{6,7},{7,10},{8,9},{9,12},{10,... | collective-permute-start | bytes 3145736 | tf_op jit(solution)/shard_map/ppermute | solution.py:19
  48.5 15.9 %collective-permute-start.10 = (bf16[16,8192]{1,0:T(8,128)(2,1)}, bf16[16,8192]{1,0:T(8,128)(2,1)}, u32[]{:S(2)}, u32[]{:S(2)}) collective-permute-start(bf16[16,8192]{1,0:T(8,128)(2,1)} %shard_map.99), channel_id=1, source_target_pairs={{0,16},{1,17},{2,18},{3,19},{4,20},{5,21},{6,22},{7,23},{8,24},{9,... | collective-permute-start | bytes 786440 | tf_op jit(solution)/shard_map/ppermute | solution.py:19
  58.6 2.5 %collective-permute-start.6 = (bf16[64,3584]{1,0:T(8,128)(2,1)S(1)}, bf16[64,3584]{1,0:T(8,128)(2,1)S(1)}, u32[]{:S(2)}, u32[]{:S(2)}) collective-permute-start(bf16[64,3584]{1,0:T(8,128)(2,1)S(1)} %slice.133), channel_id=1, source_target_pairs={{0,1},{1,0},{2,3},{3,2},{4,5},{5,4},{6,7},{7,6},{8,9},{9,8},{10,11... | collective-permute-start | bytes 1376264 | tf_op jit(solution)/shard_map/ppermute | solution.py:19
  60.6 4.5 %copy-start.11 = (bf16[16,8192]{1,0:T(8,128)(2,1)S(1)}, bf16[16,8192]{1,0:T(8,128)(2,1)}, u32[]{:S(2)}) copy-start(bf16[16,8192]{1,0:T(8,128)(2,1)} %get-tuple-element.44) | copy-start | bytes 786436
  61.2 14.1 %collective-permute-start.7 = (bf16[64,3584]{1,0:T(8,128)(2,1)S(1)}, bf16[64,3584]{1,0:T(8,128)(2,1)S(1)}, u32[]{:S(2)}, u32[]{:S(2)}) collective-permute-start(bf16[64,3584]{1,0:T(8,128)(2,1)S(1)} %fusion.23.refs_3_), channel_id=1, source_target_pairs={{0,14},{1,15},{2,0},{3,1},{4,2},{5,3},{6,4},{7,5},{8,6},{9,7},{10,... | collective-permute-start | bytes 1376264 | tf_op jit(solution)/shard_map/ppermute | solution.py:19
  66.4 9.8 %collective-permute-start.11 = (bf16[64,8192]{1,0:T(8,128)(2,1)S(1)}, bf16[64,8192]{1,0:T(8,128)(2,1)}, u32[]{:S(2)}, u32[]{:S(2)}) collective-permute-start(bf16[64,8192]{1,0:T(8,128)(2,1)S(1)} %pad_maximum_fusion.3), channel_id=1, source_target_pairs={{0,1},{1,0},{2,3},{3,2},{4,5},{5,4},{6,7},{7,6},{8,9},{9,8},{10,11... | collective-permute-start | bytes 3145736 | tf_op jit(solution)/shard_map/ppermute | solution.py:19
  66.5 39.8 %collective-permute-start.16 = (bf16[64,8192]{1,0:T(8,128)(2,1)}, bf16[64,8192]{1,0:T(8,128)(2,1)S(1)}, u32[]{:S(2)}, u32[]{:S(2)}) collective-permute-start(bf16[64,8192]{1,0:T(8,128)(2,1)} %get-tuple-element.57), channel_id=1, source_target_pairs={{0,1},{1,4},{2,3},{3,6},{4,5},{5,8},{6,7},{7,10},{8,9},{9,12},{10,... | collective-permute-start | bytes 3145736 | tf_op jit(solution)/shard_map/ppermute | solution.py:19
  86.5 12.7 %collective-permute-start.12 = (bf16[64,3584]{1,0:T(8,128)(2,1)S(1)}, bf16[64,3584]{1,0:T(8,128)(2,1)}, u32[]{:S(2)}, u32[]{:S(2)}) collective-permute-start(bf16[64,3584]{1,0:T(8,128)(2,1)S(1)} %slice.132.refs_3_), channel_id=1, source_target_pairs={{0,1},{1,0},{2,3},{3,2},{4,5},{5,4},{6,7},{7,6},{8,9},{9,8},{10,11... | collective-permute-start | bytes 1376264 | tf_op jit(solution)/shard_map/ppermute | solution.py:19
  88.9 6.0 %copy-start.2 = (bf16[512,3584]{1,0:T(8,128)(2,1)S(1)}, bf16[512,3584]{1,0:T(8,128)(2,1)}, u32[]{:S(2)}) copy-start(bf16[512,3584]{1,0:T(8,128)(2,1)} %param.7) | copy-start | bytes 11010052
  88.9 5.9 %copy-start.42 = (f32[512]{0:T(512)S(1)}, f32[512]{0:T(512)}, u32[]{:S(2)}) copy-start(f32[512]{0:T(512)} %get-tuple-element.53) | copy-start | bytes 6148
  88.9 5.9 %copy-start.52 = (s32[64]{0:T(128)S(1)}, s32[64]{0:T(128)}, u32[]{:S(2)}) copy-start(s32[64]{0:T(128)} %iota_add_fusion.1) | copy-start | bytes 772
  92.9 4.8 %copy-start.25 = (f32[512,64]{1,0:T(8,128)}, f32[512,64]{1,0:T(8,128)S(1)}, u32[]{:S(2)}) copy-start(f32[512,64]{1,0:T(8,128)S(1)} %fusion.20) | copy-start | bytes 393220
  101.2 21.7 %collective-permute-start.14 = (bf16[64,3584]{1,0:T(8,128)(2,1)}, bf16[64,3584]{1,0:T(8,128)(2,1)S(1)}, u32[]{:S(2)}, u32[]{:S(2)}) collective-permute-start(bf16[64,3584]{1,0:T(8,128)(2,1)} %get-tuple-element.55.refs_3_), channel_id=1, source_target_pairs={{0,14},{1,15},{2,0},{3,1},{4,2},{5,3},{6,4},{7,5},{8,6},{9,7},{10,... | collective-permute-start | bytes 1376264 | tf_op jit(solution)/shard_map/ppermute | solution.py:19
  115.3 7.8 %collective-permute-start.17 = (bf16[64,3584]{1,0:T(8,128)(2,1)}, bf16[64,3584]{1,0:T(8,128)(2,1)S(1)}, u32[]{:S(2)}, u32[]{:S(2)}) collective-permute-start(bf16[64,3584]{1,0:T(8,128)(2,1)} %get-tuple-element.61), channel_id=1, source_target_pairs={{0,13},{1,0},{2,15},{3,2},{4,1},{5,4},{6,3},{7,6},{8,5},{9,8},{10,... | collective-permute-start | bytes 1376264 | tf_op jit(solution)/shard_map/ppermute | solution.py:19
  115.4 11.3 %collective-permute-start.15 = (bf16[64,3584]{1,0:T(8,128)(2,1)S(1)}, bf16[64,3584]{1,0:T(8,128)(2,1)S(1)}, u32[]{:S(2)}, u32[]{:S(2)}) collective-permute-start(bf16[64,3584]{1,0:T(8,128)(2,1)S(1)} %copy-done.15), channel_id=1, source_target_pairs={{0,13},{1,0},{2,15},{3,2},{4,1},{5,4},{6,3},{7,6},{8,5},{9,8},{10,... | collective-permute-start | bytes 1376264 | tf_op jit(solution)/shard_map/ppermute | solution.py:19
  116.9 6.0 %copy-start.29 = (bf16[32,3584]{1,0:T(8,128)(2,1)S(1)}, bf16[32,3584]{1,0:T(8,128)(2,1)}, u32[]{:S(2)}) copy-start(bf16[32,3584]{1,0:T(8,128)(2,1)} %get-tuple-element.84) | copy-start | bytes 688132
  116.9 6.1 %copy-start.30 = (bf16[32,3584]{1,0:T(8,128)(2,1)S(1)}, bf16[32,3584]{1,0:T(8,128)(2,1)}, u32[]{:S(2)}) copy-start(bf16[32,3584]{1,0:T(8,128)(2,1)} %get-tuple-element.85) | copy-start | bytes 688132
  (46 other events, 136.1 us)

commit v3 on v2

--- a/solution.py
+++ b/solution.py
@@ -2,10 +2,12 @@
 import jax.numpy as jnp
 from jax import lax
 from jax.experimental import pallas as pl
+from jax.experimental.pallas import tpu as pltpu
 from jax.sharding import PartitionSpec as P
 
 hard_weight = 0.5
 CHUNKS = 4
+GATE_VMEM = 128 * 1024
 BOTH = ("grp", "seq")
 
 
@@ -52,6 +54,8 @@
         in_specs=[anywhere] * len(operands),
         out_specs=[anywhere] * len(values),
         input_output_aliases={index: index for index in range(len(values))},
+        compiler_params=pltpu.CompilerParams(vmem_limit_bytes=GATE_VMEM),
+        cost_estimate=pl.CostEstimate(flops=0, bytes_accessed=0, transcendentals=0),
     )(*operands)
 
 
@@ -107,10 +111,10 @@
     swapped = [permuted(crossed[0], other_plane), None, None, None]
     crossed[2] = permuted(chunks[2], next_chip)
     ls = logits(student_rows, student_head, norm)
-    crossed[1], chunks[3], norm = gate([crossed[1], chunks[3], teacher_norm], [ls])
+    crossed[1], chunks[3], norm_t = gate([crossed[1], chunks[3], teacher_norm], [ls])
     swapped[1] = permuted(crossed[1], other_plane)
     crossed[3] = permuted(chunks[3], next_chip)
-    lt = logits(teacher_rows, teacher_head, norm)
+    lt = logits(teacher_rows, teacher_head, norm_t)
     own_scores, losses = terms(ls, lt, place * width + ids_in)
     loss_total = losses
     score_list, panel_list = [], []
@@ -143,7 +147,7 @@
     panel_list.append(student_head)
     crossed[3], = gate([crossed[3]], [own_part])
     swapped[3] = permuted(crossed[3], other_plane)
-    theirs0, norm, norm_t = gate([theirs0, student_norm, teacher_norm], [])
+    theirs0, norm, norm_t = gate([theirs0, norm, norm_t], [])
     panel, scores, losses, keep, give = stage_terms(0, mine0, theirs0, norm, norm_t)
     loss_total = loss_total + losses
     score_list.append(scores)
@@ -156,7 +160,7 @@
     mine1 = jnp.concatenate([crossed[2], crossed[3], swapped[2], swapped[3]], axis=0)
     theirs1 = permuted(mine1, other_core)
     extra[1] = permuted(sends[1], extra_out)
-    theirs1, norm, norm_t = gate([theirs1, student_norm, teacher_norm], [])
+    theirs1, norm, norm_t = gate([theirs1, norm, norm_t], [])
     panel, scores, losses, keep, give = stage_terms(1, mine1, theirs1, norm, norm_t)
     loss_total = loss_total + losses
     score_list.append(scores)
@@ -173,7 +177,7 @@
         )
         return scores, losses, head_part(scores).astype(jnp.bfloat16)
 
-    value, norm, norm_t = gate([extra[0], student_norm, teacher_norm], [give])
+    value, norm, norm_t = gate([extra[0], norm, norm_t], [give])
     scores, losses, part = extra_terms(0, value, norm, norm_t)
     loss_total = loss_total + losses
     score_list.append(scores)
@@ -183,7 +187,7 @@
     back1 = permuted(total, previous_chip)
     extra_parts.append(permuted(part, extra_back))
 
-    value, norm, norm_t = gate([extra[1], student_norm, teacher_norm], [total])
+    value, norm, norm_t = gate([extra[1], norm, norm_t], [total])
     scores, losses, part = extra_terms(1, value, norm, norm_t)
     loss_total = loss_total + losses
     score_list.append(scores)
@@ -199,6 +203,7 @@
     ).astype(jnp.bfloat16)
 
     quarter = half // 2
+    back0, back1 = gate([back0, back1], [part])
     mine_parts = jnp.concatenate([back0[:quarter], back1[:quarter]], axis=0)
     other_parts = jnp.concatenate([back0[quarter:], back1[quarter:]], axis=0)
     first = jnp.where(plane == 0, mine_parts, other_parts)

time: 130 us -> 101 us (0.78); the launches traced: 128 us -> 100 us
  matrix products: 47.9 us -> 26.8 us
  local copies, waits for them, and re-layouts: 31.2 us -> 17.1 us
  waiting for transfers between devices: 10.1 us -> 20.2 us
  other arithmetic: 15.1 us -> 8.02 us
  starting transfers between devices: 22.3 us -> 27.2 us
    dot_general x10, matrix products: 33.3 us -> 17.1 us  [logits(): lax.dot_general(rows, panel, (((1,), (1,)), ((), ())), preferred_element_...]
    unnamed x137 -> x50, local copies, waits for them, and re-layouts: 19.9 us -> 6.2 us
    ppermute x18, waiting for transfers between devices: 10.1 us -> 20.2 us  [permuted(): return lax.ppermute(value, BOTH, pairs)]
    dot_general x5, matrix products: 8.56 us -> 3.55 us  [head_part(): lax.dot_general(scores, student_rows, (((0,), (0,)), ((), ())), preferred...]
    ppermute x18, starting transfers between devices: 22.3 us -> 27.2 us  [permuted(): return lax.ppermute(value, BOTH, pairs)]
    concatenate x2, local copies, waits for them, and re-layouts: 3.56 us -> 0.14 us  [stage_terms(): both = jnp.concatenate([mine, theirs], axis=0)]
    concatenate x1, other arithmetic: 1.98 us -> 0.08 us  [body(): jnp.concatenate([crossed[0], crossed[1], swapped[0], swapped[1]], axis=0)]
    slice x2, local copies, waits for them, and re-layouts: 0.82 us -> 2.16 us  [body(): mine_parts = jnp.concatenate([back0[:quarter], back1[:quarter]], axis=0)]
  transfers between devices with their start and end apart: 18 -> 18, of which waited for: 3 -> 8; matrix products, arithmetic and copies ran while one was open for 66% -> 44% of each run, Pallas kernels for 0% -> 0%
where the time goes in v3:
time: 101 us; the launch traced here: 100 us
  starting transfers between devices  27.2 us (27%)
  matrix products  26.8 us (27%)
  waiting for transfers between devices  20.2 us (20%)
  local copies, waits for them, and re-layouts  17.1 us (17%)
  other arithmetic  8.02 us (8%)
  between operations  1.1 us (1%)
    ppermute x18, starting transfers between devices, permuted(): return lax.ppermute(value, BOTH, pairs)  27.2 us
    ppermute x18, waiting for transfers between devices, permuted(): return lax.ppermute(value, BOTH, pairs)  20.2 us
    dot_general x10, matrix products, logits(): lax.dot_general(rows, panel, (((1,), (1,)), ((), ())), preferred_element_...  17.1 us
    unnamed x50, local copies, waits for them, and re-layouts  6.2 us
    dot_general x1, matrix products, body(): jnp.dot(jnp.concatenate(score_list, axis=1), jnp.concatenate(panel_list,...  6.12 us
    dot_general x5, matrix products, head_part(): lax.dot_general(scores, student_rows, (((0,), (0,)), ((), ())), preferred...  3.55 us
    concatenate x2, other arithmetic, own_half(): return jnp.concatenate([student_head[lo:hi], teacher_head[lo:hi]], axis=1)  2.39 us
    slice x2, local copies, waits for them, and re-layouts, body(): mine_parts = jnp.concatenate([back0[:quarter], back1[:quarter]], axis=0)  2.16 us
  transfers between devices with their start and end apart: 18, of which 8 were waited for; matrix products, arithmetic and copies ran while one was open for 44% of the time, Pallas kernels for 0%

profile of v3, /device:TPU:0, one launch (start us, length us, event | category | flops | bytes accessed | tf_op | source)
XLA Modules:
  0.0 100.3 jit_solution(1786077101408486239)
XLA Ops:
  0.6 1.9 %constant_dynamic-slice_fusion.5 = (bf16[16,3584]{1,0:T(8,128)(2,1)}, bf16[16,3584]{1,0:T(8,128)(2,1)}, bf16[16,3584]{1,0:T(8,128)(2,1)S(1)}, bf16[16,3584]{1,0:T(8,128)(2,1)S(1)}) fusion(bf16[128,3584]{1,0:T(8,128)(2,1)} %param.9, s32[]{:T(128)S(6)} %select_n.51, s32[]{:T(128)S(6)} %select_n.53, s32[]{:T(128)S(6)} %select_n.52, s32[]{:T(128)S(6)} %select_n.50), kind=kLoop, calls=%fused_computation.92 | loop fusion | bytes 917520 | tf_op jit(solution)/shard_map/dynamic_slice | solution.py:95
  2.5 2.0 %constant_dynamic-slice_fusion.4 = (bf16[16,4608]{1,0:T(8,128)(2,1)}, bf16[16,4608]{1,0:T(8,128)(2,1)}, bf16[16,4608]{1,0:T(8,128)(2,1)S(1)}, bf16[16,4608]{1,0:T(8,128)(2,1)S(1)}) fusion(bf16[128,4608]{1,0:T(8,128)(2,1)} %param.10, s32[]{:T(128)S(6)} %select_n.51, s32[]{:T(128)S(6)} %select_n.53, s32[]{:T(128)S(6)} %select_n.52, s32[]{:T(128)S(6)} %select_n.50), kind=kLoop, calls=%fused_computation.91 | loop fusion | bytes 1179664 | tf_op jit(solution)/shard_map/dynamic_slice | solution.py:96
  5.2 2.9 %collective-permute-start = (bf16[16,8192]{1,0:T(8,128)(2,1)}, bf16[16,8192]{1,0:T(8,128)(2,1)S(1)}, u32[]{:S(2)}, u32[]{:S(2)}) collective-permute-start(bf16[16,8192]{1,0:T(8,128)(2,1)} %pad_maximum_fusion.6), channel_id=1, source_target_pairs={{0,2},{1,3},{2,4},{3,5},{4,6},{5,7},{6,8},{7,9},{8,10},{9,11},{10,... | collective-permute-start | bytes 786440 | tf_op jit(solution)/shard_map/ppermute | solution.py:21
  8.9 1.5 %collective-permute-start.1 = (bf16[16,8192]{1,0:T(8,128)(2,1)}, bf16[16,8192]{1,0:T(8,128)(2,1)S(1)}, u32[]{:S(2)}, u32[]{:S(2)}) collective-permute-start(bf16[16,8192]{1,0:T(8,128)(2,1)} %pad_maximum_fusion.8), channel_id=1, source_target_pairs={{0,2},{1,3},{2,4},{3,5},{4,6},{5,7},{6,8},{7,9},{8,10},{9,11},{10,... | collective-permute-start | bytes 786440 | tf_op jit(solution)/shard_map/ppermute | solution.py:21
  11.3 1.1 %fusion.47 = (bf16[64,4608]{1,0:T(8,128)(2,1)}, bf16[64,4608]{1,0:T(8,128)(2,1)}) fusion(bf16[128,4608]{1,0:T(8,128)(2,1)S(1)} %copy-done.5), kind=kLoop, calls=%fused_computation.111 | loop fusion | bytes 2359296 | tf_op jit(solution)/shard_map/slice | solution.py:103
  13.5 1.3 %pad_maximum_fusion.2.refs_2_ = bf16[64,8192]{1,0:T(8,128)(2,1)S(1)} fusion(bf16[64,4608]{1,0:T(8,128)(2,1)} %get-tuple-element.72, bf16[64,3584]{1,0:T(8,128)(2,1)} %get-tuple-element.80), kind=kLoop, calls=%fused_computation.26 | loop fusion | flops 2097152 | bytes 2097152 | tf_op jit(solution)/shard_map/concatenate | solution.py:103
  14.9 1.0 %pad_maximum_fusion.1.refs_1_ = bf16[64,8192]{1,0:T(8,128)(2,1)} fusion(bf16[64,4608]{1,0:T(8,128)(2,1)S(1)} %copy-done.7, bf16[64,3584]{1,0:T(8,128)(2,1)S(1)} %get-tuple-element.81), kind=kLoop, calls=%fused_computation.25 | loop fusion | flops 2097152 | bytes 2097152 | tf_op jit(solution)/shard_map/concatenate | solution.py:103
  16.3 2.3 %collective-permute-done.refs_0_ = bf16[16,8192]{1,0:T(8,128)(2,1)S(1)} collective-permute-done((bf16[16,8192]{1,0:T(8,128)(2,1)}, bf16[16,8192]{1,0:T(8,128)(2,1)S(1)}, u32[]{:S(2)}, u32[]{:S(2)}) %collective-permute-start) | collective-permute-done | bytes 262176 | tf_op jit(solution)/shard_map/ppermute | solution.py:21
  18.6 1.7 %collective-permute-start.2 = (bf16[16,8192]{1,0:T(8,128)(2,1)S(1)}, bf16[16,8192]{1,0:T(8,128)(2,1)S(1)}, u32[]{:S(2)}, u32[]{:S(2)}) collective-permute-start(bf16[16,8192]{1,0:T(8,128)(2,1)S(1)} %get-tuple-element.35), channel_id=1, source_target_pairs={{0,16},{1,17},{2,18},{3,19},{4,20},{5,21},{6,22},{7,23},{8,24},{9,... | collective-permute-start | bytes 786440 | tf_op jit(solution)/shard_map/ppermute | solution.py:21
  20.3 3.2 %broadcast_subtract_fusion.refs_3_ = f32[512,128]{1,0:T(8,128)S(1)} fusion(f32[512]{0:T(512)S(1)} %get-tuple-element.36.refs_1_, bf16[512,3584]{1,0:T(8,128)(2,1)} %param.7, bf16[128,3584]{1,0:T(8,128)(2,1)S(1)} %copy-done.4), kind=kOutput, calls=%fused_computation.77 | convolution fusion | flops 469827584 | bytes 4851712 | tf_op jit(solution)/shard_map/dot_general | solution.py:74
  25.9 3.7 %fusion.30 = (bf16[512,128]{1,0:T(8,128)(2,1)S(1)}, f32[512,128]{1,0:T(8,128)S(1)}) fusion(f32[512,128]{1,0:T(8,128)S(1)} %broadcast_subtract_fusion.refs_3_, s32[128]{0:T(128)S(1)} %iota_add_fusion.5, f32[512]{0:T(512)S(1)} %get-tuple-element.39, s32[512]{0:T(512)S(1)} %copy-done.15, bf16[512,4608]{1,0:T(8,128)(2,1)} %param.8, ...), kind=kOutput, calls=%fused_computation.58 | convolution fusion | flops 604438528 | bytes 6558208 | tf_op jit(solution)/shard_map/dot_general | solution.py:74
  29.9 1.7 %collective-permute-start.9 = (bf16[16,8192]{1,0:T(8,128)(2,1)S(1)}, bf16[16,8192]{1,0:T(8,128)(2,1)S(1)}, u32[]{:S(2)}, u32[]{:S(2)}) collective-permute-start(bf16[16,8192]{1,0:T(8,128)(2,1)S(1)} %get-tuple-element.46), channel_id=1, source_target_pairs={{0,16},{1,17},{2,18},{3,19},{4,20},{5,21},{6,22},{7,23},{8,24},{9,... | collective-permute-start | bytes 786440 | tf_op jit(solution)/shard_map/ppermute | solution.py:21
  34.6 1.5 %collective-permute-start.10 = (bf16[16,8192]{1,0:T(8,128)(2,1)S(1)}, bf16[16,8192]{1,0:T(8,128)(2,1)S(1)}, u32[]{:S(2)}, u32[]{:S(2)}) collective-permute-start(bf16[16,8192]{1,0:T(8,128)(2,1)S(1)} %shard_map.99), channel_id=1, source_target_pairs={{0,16},{1,17},{2,18},{3,19},{4,20},{5,21},{6,22},{7,23},{8,24},{9,... | collective-permute-start | bytes 786440 | tf_op jit(solution)/shard_map/ppermute | solution.py:21
  36.3 1.4 %fusion.15 = f32[512,128]{1,0:T(8,128)S(1)} fusion(bf16[512,4608]{1,0:T(8,128)(2,1)S(1)} %bitcast.41, bf16[128,8192]{1,0:T(8,128)(2,1)S(1)} %constant_dynamic-update-slice_fusion, f32[512]{0:T(512)S(1)} %get-tuple-element.45.refs_2_), kind=kOutput, calls=%fused_computation.15 | convolution fusion | flops 604045312 | bytes 6162432 | tf_op jit(solution)/shard_map/dot_general | solution.py:74
  37.7 1.1 %fusion.33 = (bf16[512,128]{1,0:T(8,128)(2,1)S(1)}, f32[512,128]{1,0:T(8,128)S(1)}) fusion(f32[512,128]{1,0:T(8,128)S(1)} %fusion.15, s32[128]{0:T(128)S(1)} %pad_add_fusion.1, s32[512]{0:T(512)S(1)} %copy-done.15, f32[512]{0:T(512)S(1)} %get-tuple-element.44.refs_1_, bf16[512,3584]{1,0:T(8,128)(2,1)S(1)} %copy-done.3, ...), kind=kOutput, calls=%fused_computation.61 | convolution fusion | flops 470220800 | bytes 5247488 | tf_op jit(solution)/shard_map/dot_general | solution.py:74
  39.6 1.3 %collective-permute-start.6 = (bf16[64,3584]{1,0:T(8,128)(2,1)S(1)}, bf16[64,3584]{1,0:T(8,128)(2,1)S(1)}, u32[]{:S(2)}, u32[]{:S(2)}) collective-permute-start(bf16[64,3584]{1,0:T(8,128)(2,1)S(1)} %slice.129), channel_id=1, source_target_pairs={{0,1},{1,0},{2,3},{3,2},{4,5},{5,4},{6,7},{7,6},{8,9},{9,8},{10,11... | collective-permute-start | bytes 1376264 | tf_op jit(solution)/shard_map/ppermute | solution.py:21
  43.3 3.2 %collective-permute-start.7 = (bf16[64,3584]{1,0:T(8,128)(2,1)}, bf16[64,3584]{1,0:T(8,128)(2,1)}, u32[]{:S(2)}, u32[]{:S(2)}) collective-permute-start(bf16[64,3584]{1,0:T(8,128)(2,1)} %fusion.23.refs_3_), channel_id=1, source_target_pairs={{0,14},{1,15},{2,0},{3,1},{4,2},{5,3},{6,4},{7,5},{8,6},{9,7},{10,... | collective-permute-start | bytes 1376264 | tf_op jit(solution)/shard_map/ppermute | solution.py:21
  47.5 1.8 %collective-permute-done.11.refs_0_ = bf16[64,8192]{1,0:T(8,128)(2,1)S(1)} collective-permute-done((bf16[64,8192]{1,0:T(8,128)(2,1)S(1)}, bf16[64,8192]{1,0:T(8,128)(2,1)S(1)}, u32[]{:S(2)}, u32[]{:S(2)}) %collective-permute-start.11) | collective-permute-done | bytes 1048608 | tf_op jit(solution)/shard_map/ppermute | solution.py:21
  49.3 1.4 %fusion.12 = f32[512,128]{1,0:T(8,128)S(1)} fusion(bf16[512,4608]{1,0:T(8,128)(2,1)S(1)} %bitcast.41, bf16[128,8192]{1,0:T(8,128)(2,1)S(1)} %constant_dynamic-update-slice_fusion.2, f32[512]{0:T(512)S(1)} %get-tuple-element.52.refs_2_), kind=kOutput, calls=%fused_computation.14 | convolution fusion | flops 604045312 | bytes 6162432 | tf_op jit(solution)/shard_map/dot_general | solution.py:74
  50.7 1.3 %fusion.35 = (f32[512]{0:T(512)S(1)}, f32[512]{0:T(512)S(1)}, f32[512]{0:T(512)S(1)}, bf16[512,128]{1,0:T(8,128)(2,1)S(1)}) fusion(f32[512,128]{1,0:T(8,128)S(1)} %get-tuple-element.99, f32[512,128]{1,0:T(8,128)S(1)} %fusion.15, s32[128]{0:T(128)S(1)} %pad_add_fusion.1, s32[512]{0:T(512)S(1)} %copy-done.15, s32[128]{0:T(128)S(1)} %pad_add_fusion.3, ...), kind=kOutput, calls=%fused_computation.63 | convolution fusion | flops 471529984 | bytes 6043136 | tf_op jit(solution)/shard_map/dot_general | solution.py:74
  54.6 1.4 %fusion.20 = f32[512,64]{1,0:T(8,128)S(1)} fusion(bf16[512,4608]{1,0:T(8,128)(2,1)S(1)} %bitcast.41, bf16[64,8192]{1,0:T(8,128)(2,1)S(1)} %get-tuple-element.54, f32[512]{0:T(512)S(1)} %get-tuple-element.56.refs_2_), kind=kOutput, calls=%fused_computation.21 | convolution fusion | flops 302022656 | bytes 5441536 | tf_op jit(solution)/shard_map/dot_general | solution.py:74
  56.8 1.1 %fusion.39 = (bf16[512,64]{1,0:T(8,128)(2,1)S(1)}, f32[512,64]{1,0:T(8,128)S(1)}) fusion(f32[512,64]{1,0:T(8,128)S(1)} %fusion.20, s32[64]{0:T(128)S(1)} %iota_add_fusion.1, s32[512]{0:T(512)S(1)} %copy-done.15, f32[512]{0:T(512)S(1)} %get-tuple-element.55.refs_1_, bf16[512,3584]{1,0:T(8,128)(2,1)S(1)} %copy-done.3, bf16[64,8192]{1,0:T(8,128)(2,1)S(1)} %get-tuple-element.54), kind=kOutput, calls=%fused_computation.67 | convolution fusion | flops 235110400 | bytes 4592128 | tf_op jit(solution)/shard_map/dot_general | solution.py:74
  59.6 1.9 %collective-permute-start.14 = (bf16[64,3584]{1,0:T(8,128)(2,1)}, bf16[64,3584]{1,0:T(8,128)(2,1)}, u32[]{:S(2)}, u32[]{:S(2)}) collective-permute-start(bf16[64,3584]{1,0:T(8,128)(2,1)} %get-tuple-element.57.refs_3_), channel_id=1, source_target_pairs={{0,14},{1,15},{2,0},{3,1},{4,2},{5,3},{6,4},{7,5},{8,6},{9,7},{10,... | collective-permute-start | bytes 1376264 | tf_op jit(solution)/shard_map/ppermute | solution.py:21
  61.4 13.2 %collective-permute-done.15.refs_0_ = bf16[64,8192]{1,0:T(8,128)(2,1)S(1)} collective-permute-done((bf16[64,8192]{1,0:T(8,128)(2,1)}, bf16[64,8192]{1,0:T(8,128)(2,1)S(1)}, u32[]{:S(2)}, u32[]{:S(2)}) %collective-permute-start.15) | collective-permute-done | bytes 1048608 | tf_op jit(solution)/shard_map/ppermute | solution.py:21
  74.7 1.4 %fusion.18 = f32[512,64]{1,0:T(8,128)S(1)} fusion(bf16[512,4608]{1,0:T(8,128)(2,1)S(1)} %bitcast.41, bf16[64,8192]{1,0:T(8,128)(2,1)S(1)} %get-tuple-element.59, f32[512]{0:T(512)S(1)} %get-tuple-element.61), kind=kOutput, calls=%fused_computation.17 | convolution fusion | flops 302022656 | bytes 5441536 | tf_op jit(solution)/shard_map/dot_general | solution.py:74
  76.0 1.2 %fusion.41 = (f32[512]{0:T(512)S(1)}, f32[512]{0:T(512)S(1)}, bf16[512,64]{1,0:T(8,128)(2,1)S(1)}) fusion(f32[512,64]{1,0:T(8,128)S(1)} %get-tuple-element.101, f32[512,64]{1,0:T(8,128)S(1)} %fusion.20, s32[64]{0:T(128)S(1)} %iota_add_fusion.1, s32[512]{0:T(512)S(1)} %copy-done.15, s32[64]{0:T(128)S(1)} %iota_add_fusion, f32[512,64]{1,0:T(8,128)S(1)} %fusion.18, ...), kind=kOutput, calls=%fused_computation.69 | convolution fusion | flops 235502592 | bytes 4989952 | tf_op jit(solution)/shard_map/dot_general | solution.py:74
  78.7 1.9 %concatenate.79 = bf16[512,512]{1,0:T(8,128)(2,1)} concatenate(bf16[512,128]{1,0:T(8,128)(2,1)S(1)} %get-tuple-element.41, bf16[512,128]{1,0:T(8,128)(2,1)} %copy-done.8, bf16[512,128]{1,0:T(8,128)(2,1)} %copy-done.12, bf16[512,64]{1,0:T(8,128)(2,1)} %copy-done.9, bf16[512,64]{1,0:T(8,128)(2,1)} %copy-done.2), dimensions={1} | concatenate | bytes 1048576 | tf_op jit(solution)/shard_map/concatenate | solution.py:200
  80.6 8.7 %collective-permute-start.16 = (bf16[64,3584]{1,0:T(8,128)(2,1)}, bf16[64,3584]{1,0:T(8,128)(2,1)S(1)}, u32[]{:S(2)}, u32[]{:S(2)}) collective-permute-start(bf16[64,3584]{1,0:T(8,128)(2,1)} %copy-done.1), channel_id=1, source_target_pairs={{0,13},{1,0},{2,15},{3,2},{4,1},{5,4},{6,3},{7,6},{8,5},{9,8},{10,... | collective-permute-start | bytes 1376264 | tf_op jit(solution)/shard_map/ppermute | solution.py:21
  90.7 6.1 %convolution_convert_fusion = bf16[512,3584]{1,0:T(8,128)(2,1)} fusion(bf16[512,512]{1,0:T(8,128)(2,1)} %concatenate.79, bf16[512,3584]{1,0:T(8,128)(2,1)} %slice_dynamic-update-slice_fusion.2), kind=kOutput, calls=%fused_computation | convolution fusion | flops 1880883200 | bytes 7864320 | tf_op jit(solution)/shard_map/dot_general | solution.py:199
  96.8 1.1 %fusion.49 = (bf16[32,3584]{1,0:T(8,128)(2,1)S(1)}, bf16[32,3584]{1,0:T(8,128)(2,1)S(1)}) fusion(bf16[64,3584]{1,0:T(8,128)(2,1)} %get-tuple-element.63), kind=kLoop, calls=%fused_computation.113 | loop fusion | bytes 917504 | tf_op jit(solution)/shard_map/slice | solution.py:207
  97.9 1.1 %fusion.50 = (bf16[32,3584]{1,0:T(8,128)(2,1)S(1)}, bf16[32,3584]{1,0:T(8,128)(2,1)S(1)}) fusion(bf16[64,3584]{1,0:T(8,128)(2,1)} %get-tuple-element.64), kind=kLoop, calls=%fused_computation.114 | loop fusion | bytes 917504 | tf_op jit(solution)/shard_map/slice | solution.py:207
  99.1 1.2 %add_convert_fusion = bf16[128,3584]{1,0:T(8,128)(2,1)} fusion(f32[128,3584]{1,0:T(8,128)S(1)} %fusion.51.refs_1_, bf16[64,3584]{1,0:T(8,128)(2,1)S(1)} %get-tuple-element.79, bf16[64,3584]{1,0:T(8,128)(2,1)S(1)} %get-tuple-element.78, bf16[64,3584]{1,0:T(8,128)(2,1)S(1)} %collective-permute-done.17, bf16[64,3584]{1,0:T(8,128)(2,1)S(1)} %collective-permute-done.16), kind=kLoop, calls=%fused_computation.3 | loop fusion | flops 5046272 | bytes 4587520 | tf_op jit(solution)/shard_map/convert_element_type | solution.py:215
  (119 shorter events, 21.6 us)
Async XLA Ops:
  0.6 9.8 %copy-start.4 = (bf16[128,3584]{1,0:T(8,128)(2,1)S(1)}, bf16[128,3584]{1,0:T(8,128)(2,1)}, u32[]{:S(2)}) copy-start(bf16[128,3584]{1,0:T(8,128)(2,1)} %param.9) | copy-start | bytes 2752516
  2.5 8.8 %copy-start.5 = (bf16[128,4608]{1,0:T(8,128)(2,1)S(1)}, bf16[128,4608]{1,0:T(8,128)(2,1)}, u32[]{:S(2)}) copy-start(bf16[128,4608]{1,0:T(8,128)(2,1)} %param.10) | copy-start | bytes 3538948
  5.2 13.3 %collective-permute-start = (bf16[16,8192]{1,0:T(8,128)(2,1)}, bf16[16,8192]{1,0:T(8,128)(2,1)S(1)}, u32[]{:S(2)}, u32[]{:S(2)}) collective-permute-start(bf16[16,8192]{1,0:T(8,128)(2,1)} %pad_maximum_fusion.6), channel_id=1, source_target_pairs={{0,2},{1,3},{2,4},{3,5},{4,6},{5,7},{6,8},{7,9},{8,10},{9,11},{10,... | collective-permute-start | bytes 786440 | tf_op jit(solution)/shard_map/ppermute | solution.py:21
  8.9 15.3 %collective-permute-start.1 = (bf16[16,8192]{1,0:T(8,128)(2,1)}, bf16[16,8192]{1,0:T(8,128)(2,1)S(1)}, u32[]{:S(2)}, u32[]{:S(2)}) collective-permute-start(bf16[16,8192]{1,0:T(8,128)(2,1)} %pad_maximum_fusion.8), channel_id=1, source_target_pairs={{0,2},{1,3},{2,4},{3,5},{4,6},{5,7},{6,8},{7,9},{8,10},{9,11},{10,... | collective-permute-start | bytes 786440 | tf_op jit(solution)/shard_map/ppermute | solution.py:21
  13.4 1.4 %copy-start.7 = (bf16[64,4608]{1,0:T(8,128)(2,1)S(1)}, bf16[64,4608]{1,0:T(8,128)(2,1)}, u32[]{:S(2)}) copy-start(bf16[64,4608]{1,0:T(8,128)(2,1)} %get-tuple-element.73) | copy-start | bytes 1769476
  13.4 2.5 %copy-start.10 = (bf16[16,4608]{1,0:T(8,128)(2,1)S(1)}, bf16[16,4608]{1,0:T(8,128)(2,1)}, u32[]{:S(2)}) copy-start(bf16[16,4608]{1,0:T(8,128)(2,1)} %get-tuple-element.74) | copy-start | bytes 442372
  13.5 2.5 %copy-start.11 = (bf16[16,4608]{1,0:T(8,128)(2,1)S(1)}, bf16[16,4608]{1,0:T(8,128)(2,1)}, u32[]{:S(2)}) copy-start(bf16[16,4608]{1,0:T(8,128)(2,1)} %get-tuple-element.75) | copy-start | bytes 442372
  13.5 2.5 %copy-start.13 = (bf16[16,3584]{1,0:T(8,128)(2,1)S(1)}, bf16[16,3584]{1,0:T(8,128)(2,1)}, u32[]{:S(2)}) copy-start(bf16[16,3584]{1,0:T(8,128)(2,1)} %get-tuple-element.82) | copy-start | bytes 344068
  13.5 2.5 %copy-start.14 = (bf16[16,3584]{1,0:T(8,128)(2,1)S(1)}, bf16[16,3584]{1,0:T(8,128)(2,1)}, u32[]{:S(2)}) copy-start(bf16[16,3584]{1,0:T(8,128)(2,1)} %get-tuple-element.83) | copy-start | bytes 344068
  14.8 1.3 %copy-start.16 = (bf16[512]{0:T(512)(128)(2,1)S(1)}, bf16[512]{0:T(512)(128)(2,1)}, u32[]{:S(2)}) copy-start(bf16[512]{0:T(512)(128)(2,1)} %param.11) | copy-start | bytes 3076
  18.6 11.4 %collective-permute-start.4 = (bf16[16,8192]{1,0:T(8,128)(2,1)S(1)}, bf16[16,8192]{1,0:T(8,128)(2,1)S(1)}, u32[]{:S(2)}, u32[]{:S(2)}) collective-permute-start(bf16[16,8192]{1,0:T(8,128)(2,1)S(1)} %get-tuple-element.38), channel_id=1, source_target_pairs={{0,2},{1,3},{2,4},{3,5},{4,6},{5,7},{6,8},{7,9},{8,10},{9,11},{10,... | collective-permute-start | bytes 786440 | tf_op jit(solution)/shard_map/ppermute | solution.py:21
  18.6 13.1 %collective-permute-start.2 = (bf16[16,8192]{1,0:T(8,128)(2,1)S(1)}, bf16[16,8192]{1,0:T(8,128)(2,1)S(1)}, u32[]{:S(2)}, u32[]{:S(2)}) collective-permute-start(bf16[16,8192]{1,0:T(8,128)(2,1)S(1)} %get-tuple-element.35), channel_id=1, source_target_pairs={{0,16},{1,17},{2,18},{3,19},{4,20},{5,21},{6,22},{7,23},{8,24},{9,... | collective-permute-start | bytes 786440 | tf_op jit(solution)/shard_map/ppermute | solution.py:21
  20.3 5.6 %copy-start.6 = (bf16[128,4608]{1,0:T(8,128)(2,1)S(1)}, bf16[128,4608]{1,0:T(8,128)(2,1)}, u32[]{:S(2)}) copy-start(bf16[128,4608]{1,0:T(8,128)(2,1)} %param.10) | copy-start | bytes 3538948
  20.3 5.6 %copy-start.15 = (s32[512]{0:T(512)S(1)}, s32[512]{0:T(512)}, u32[]{:S(2)}) copy-start(s32[512]{0:T(512)} %param.13) | copy-start | bytes 6148
  24.2 10.4 %collective-permute-start.8 = (bf16[16,8192]{1,0:T(8,128)(2,1)S(1)}, bf16[16,8192]{1,0:T(8,128)(2,1)S(1)}, u32[]{:S(2)}, u32[]{:S(2)}) collective-permute-start(bf16[16,8192]{1,0:T(8,128)(2,1)S(1)} %get-tuple-element.47), channel_id=1, source_target_pairs={{0,2},{1,3},{2,4},{3,5},{4,6},{5,7},{6,8},{7,9},{8,10},{9,11},{10,... | collective-permute-start | bytes 786440 | tf_op jit(solution)/shard_map/ppermute | solution.py:21
  24.9 7.4 %collective-permute-start.3 = (bf16[16,8192]{1,0:T(8,128)(2,1)S(1)}, bf16[16,8192]{1,0:T(8,128)(2,1)S(1)}, u32[]{:S(2)}, u32[]{:S(2)}) collective-permute-start(bf16[16,8192]{1,0:T(8,128)(2,1)S(1)} %get-tuple-element.37), channel_id=1, source_target_pairs={{0,16},{1,17},{2,18},{3,19},{4,20},{5,21},{6,22},{7,23},{8,24},{9,... | collective-permute-start | bytes 786440 | tf_op jit(solution)/shard_map/ppermute | solution.py:21
  29.9 3.0 %copy-start.3 = (bf16[512,3584]{1,0:T(8,128)(2,1)S(1)}, bf16[512,3584]{1,0:T(8,128)(2,1)}, u32[]{:S(2)}) copy-start(bf16[512,3584]{1,0:T(8,128)(2,1)} %param.7) | copy-start | bytes 11010052
  29.9 16.5 %collective-permute-start.9 = (bf16[16,8192]{1,0:T(8,128)(2,1)S(1)}, bf16[16,8192]{1,0:T(8,128)(2,1)S(1)}, u32[]{:S(2)}, u32[]{:S(2)}) collective-permute-start(bf16[16,8192]{1,0:T(8,128)(2,1)S(1)} %get-tuple-element.46), channel_id=1, source_target_pairs={{0,16},{1,17},{2,18},{3,19},{4,20},{5,21},{6,22},{7,23},{8,24},{9,... | collective-permute-start | bytes 786440 | tf_op jit(solution)/shard_map/ppermute | solution.py:21
  32.4 3.8 %collective-permute-start.5 = (bf16[64,8192]{1,0:T(8,128)(2,1)S(1)}, bf16[64,8192]{1,0:T(8,128)(2,1)S(1)}, u32[]{:S(2)}, u32[]{:S(2)}) collective-permute-start(bf16[64,8192]{1,0:T(8,128)(2,1)S(1)} %get-tuple-element.42), channel_id=1, source_target_pairs={{0,1},{1,0},{2,3},{3,2},{4,5},{5,4},{6,7},{7,6},{8,9},{9,8},{10,11... | collective-permute-start | bytes 3145736 | tf_op jit(solution)/shard_map/ppermute | solution.py:21
  32.5 22.1 %collective-permute-start.13 = (bf16[64,8192]{1,0:T(8,128)(2,1)}, bf16[64,8192]{1,0:T(8,128)(2,1)S(1)}, u32[]{:S(2)}, u32[]{:S(2)}) collective-permute-start(bf16[64,8192]{1,0:T(8,128)(2,1)} %get-tuple-element.53), channel_id=1, source_target_pairs={{0,1},{1,4},{2,3},{3,6},{4,5},{5,8},{6,7},{7,10},{8,9},{9,12},{10,... | collective-permute-start | bytes 3145736 | tf_op jit(solution)/shard_map/ppermute | solution.py:21
  33.0 3.3 %slice-start = ((s8[4718592]{0:T(1024)(128)(4,1)}), s8[4194304]{0:T(1024)(128)(4,1)S(1)}, s32[]{:S(2)}) async-start(s8[4718592]{0:T(1024)(128)(4,1)} %bitcast.40), calls=%async_computation | async-start | bytes 8388608
  33.7 2.7 %slice-start.1 = ((s8[4718592]{0:T(1024)(128)(4,1)}), s8[524288]{0:T(1024)(128)(4,1)S(1)}, s32[]{:S(2)}) async-start(s8[4718592]{0:T(1024)(128)(4,1)} %bitcast.40), calls=%async_computation.1 | async-start | bytes 1048576
  34.6 11.9 %collective-permute-start.10 = (bf16[16,8192]{1,0:T(8,128)(2,1)S(1)}, bf16[16,8192]{1,0:T(8,128)(2,1)S(1)}, u32[]{:S(2)}, u32[]{:S(2)}) collective-permute-start(bf16[16,8192]{1,0:T(8,128)(2,1)S(1)} %shard_map.99), channel_id=1, source_target_pairs={{0,16},{1,17},{2,18},{3,19},{4,20},{5,21},{6,22},{7,23},{8,24},{9,... | collective-permute-start | bytes 786440 | tf_op jit(solution)/shard_map/ppermute | solution.py:21
  39.6 2.8 %collective-permute-start.6 = (bf16[64,3584]{1,0:T(8,128)(2,1)S(1)}, bf16[64,3584]{1,0:T(8,128)(2,1)S(1)}, u32[]{:S(2)}, u32[]{:S(2)}) collective-permute-start(bf16[64,3584]{1,0:T(8,128)(2,1)S(1)} %slice.129), channel_id=1, source_target_pairs={{0,1},{1,0},{2,3},{3,2},{4,5},{5,4},{6,7},{7,6},{8,9},{9,8},{10,11... | collective-permute-start | bytes 1376264 | tf_op jit(solution)/shard_map/ppermute | solution.py:21
  43.3 53.5 %collective-permute-start.7 = (bf16[64,3584]{1,0:T(8,128)(2,1)}, bf16[64,3584]{1,0:T(8,128)(2,1)}, u32[]{:S(2)}, u32[]{:S(2)}) collective-permute-start(bf16[64,3584]{1,0:T(8,128)(2,1)} %fusion.23.refs_3_), channel_id=1, source_target_pairs={{0,14},{1,15},{2,0},{3,1},{4,2},{5,3},{6,4},{7,5},{8,6},{9,7},{10,... | collective-permute-start | bytes 1376264 | tf_op jit(solution)/shard_map/ppermute | solution.py:21
  46.5 2.7 %collective-permute-start.11 = (bf16[64,8192]{1,0:T(8,128)(2,1)S(1)}, bf16[64,8192]{1,0:T(8,128)(2,1)S(1)}, u32[]{:S(2)}, u32[]{:S(2)}) collective-permute-start(bf16[64,8192]{1,0:T(8,128)(2,1)S(1)} %pad_maximum_fusion.3), channel_id=1, source_target_pairs={{0,1},{1,0},{2,3},{3,2},{4,5},{5,4},{6,7},{7,6},{8,9},{9,8},{10,11... | collective-permute-start | bytes 3145736 | tf_op jit(solution)/shard_map/ppermute | solution.py:21
  47.4 27.2 %collective-permute-start.15 = (bf16[64,8192]{1,0:T(8,128)(2,1)}, bf16[64,8192]{1,0:T(8,128)(2,1)S(1)}, u32[]{:S(2)}, u32[]{:S(2)}) collective-permute-start(bf16[64,8192]{1,0:T(8,128)(2,1)} %copy-done), channel_id=1, source_target_pairs={{0,1},{1,4},{2,3},{3,6},{4,5},{5,8},{6,7},{7,10},{8,9},{9,12},{10,... | collective-permute-start | bytes 3145736 | tf_op jit(solution)/shard_map/ppermute | solution.py:21
  53.4 5.3 %collective-permute-start.12 = (bf16[64,3584]{1,0:T(8,128)(2,1)S(1)}, bf16[64,3584]{1,0:T(8,128)(2,1)S(1)}, u32[]{:S(2)}, u32[]{:S(2)}) collective-permute-start(bf16[64,3584]{1,0:T(8,128)(2,1)S(1)} %slice.128.refs_3_), channel_id=1, source_target_pairs={{0,1},{1,0},{2,3},{3,2},{4,5},{5,4},{6,7},{7,6},{8,9},{9,8},{10,11... | collective-permute-start | bytes 1376264 | tf_op jit(solution)/shard_map/ppermute | solution.py:21
  59.6 15.1 %copy-start.1 = (bf16[64,3584]{1,0:T(8,128)(2,1)}, bf16[64,3584]{1,0:T(8,128)(2,1)S(1)}, u32[]{:S(2)}) copy-start(bf16[64,3584]{1,0:T(8,128)(2,1)S(1)} %get-tuple-element.65) | copy-start | bytes 1376260
  59.6 37.2 %collective-permute-start.14 = (bf16[64,3584]{1,0:T(8,128)(2,1)}, bf16[64,3584]{1,0:T(8,128)(2,1)}, u32[]{:S(2)}, u32[]{:S(2)}) collective-permute-start(bf16[64,3584]{1,0:T(8,128)(2,1)} %get-tuple-element.57.refs_3_), channel_id=1, source_target_pairs={{0,14},{1,15},{2,0},{3,1},{4,2},{5,3},{6,4},{7,5},{8,6},{9,7},{10,... | collective-permute-start | bytes 1376264 | tf_op jit(solution)/shard_map/ppermute | solution.py:21
  80.6 18.6 %collective-permute-start.17 = (bf16[64,3584]{1,0:T(8,128)(2,1)S(1)}, bf16[64,3584]{1,0:T(8,128)(2,1)S(1)}, u32[]{:S(2)}, u32[]{:S(2)}) collective-permute-start(bf16[64,3584]{1,0:T(8,128)(2,1)S(1)} %get-tuple-element.62.refs_2_), channel_id=1, source_target_pairs={{0,13},{1,0},{2,15},{3,2},{4,1},{5,4},{6,3},{7,6},{8,5},{9,8},{10,... | collective-permute-start | bytes 1376264 | tf_op jit(solution)/shard_map/ppermute | solution.py:21
  80.6 18.6 %collective-permute-start.16 = (bf16[64,3584]{1,0:T(8,128)(2,1)}, bf16[64,3584]{1,0:T(8,128)(2,1)S(1)}, u32[]{:S(2)}, u32[]{:S(2)}) collective-permute-start(bf16[64,3584]{1,0:T(8,128)(2,1)} %copy-done.1), channel_id=1, source_target_pairs={{0,13},{1,0},{2,15},{3,2},{4,1},{5,4},{6,3},{7,6},{8,5},{9,8},{10,... | collective-permute-start | bytes 1376264 | tf_op jit(solution)/shard_map/ppermute | solution.py:21
  (6 other events, 5.1 us)

commit v4 on v1

v4 whole, which is shorter than its diff:
```python
import jax
import jax.numpy as jnp
from jax import lax
from jax.experimental import pallas as pl
from jax.experimental.pallas import tpu as pltpu
from jax.sharding import PartitionSpec as P

hard_weight = 0.5
CHUNKS = 4
GATE_VMEM = 128 * 1024
BOTH = ("grp", "seq")


def permuted(value, move):
    groups, count = lax.axis_size("grp"), lax.axis_size("seq")
    pairs = []
    for group in range(groups):
        for place in range(count):
            target = move(group, place)
            if target is not None:
                pairs.append((group * count + place, target[0] * count + target[1] % count))
    return lax.ppermute(value, BOTH, pairs)


def next_chip(group, place):
    return group, place + 2


def previous_chip(group, place):
    return group, place - 2


def other_plane(group, place):
    return 1 - group, place


def other_core(group, place):
    return group, place + 1 - 2 * (place % 2)


def extra_early(group, place):
    if place % 2 == 0:
        return group, place + 1
    return (group, place + 3) if place // 2 % 2 == 0 else None


def extra_late(group, place):
    return (group, place + 3) if place % 2 == 1 and place // 2 % 2 == 1 else None


def extra_back(group, place):
    return group, place - 3 + 2 * (place % 2)


def gate(values, ready, flops=0):
    operands = list(values) + list(ready)
    anywhere = pl.BlockSpec(memory_space=pl.ANY)
    return pl.pallas_call(
        lambda *refs: None,
        out_shape=[jax.ShapeDtypeStruct(value.shape, value.dtype) for value in values],
        in_specs=[anywhere] * len(operands),
        out_specs=[anywhere] * len(values),
        input_output_aliases={index: index for index in range(len(values))},
        compiler_params=pltpu.CompilerParams(vmem_limit_bytes=GATE_VMEM),
        cost_estimate=pl.CostEstimate(flops=flops, bytes_accessed=0, transcendentals=0),
    )(*operands)


def packed(at, student_head, teacher_head, places, ready=()):
    depth, depth_t = student_head.shape[1], teacher_head.shape[1]

    def kernel(at_ref, student_ref, teacher_ref, *refs):
        outs, sems = refs[len(ready) : -1], refs[-1]
        copies = []
        for index, (moves, start, rows) in enumerate(places):
            first = pl.multiple_of(at_ref[0] + start, 16) if moves else start
            for half, (source, lo, wide) in enumerate(
                [(student_ref, 0, depth), (teacher_ref, depth, depth_t)]
            ):
                copies.append(
                    pltpu.make_async_copy(
                        source.at[pl.ds(first, rows), :],
                        outs[index].at[:, pl.ds(lo, wide)],
                        sems.at[2 * index + half],
                    )
                )
        for copy in copies:
            copy.start()
        for copy in copies:
            copy.wait()

    anywhere = pl.BlockSpec(memory_space=pl.ANY)
    return pl.pallas_call(
        kernel,
        out_shape=[
            jax.ShapeDtypeStruct((rows, depth + depth_t), student_head.dtype) for _, _, rows in places
        ],
        in_specs=[pl.BlockSpec(memory_space=pltpu.SMEM)]
        + [pl.BlockSpec(memory_space=pltpu.HBM)] * 2
        + [anywhere] * len(ready),
        out_specs=[anywhere] * len(places),
        scratch_shapes=[pltpu.SemaphoreType.DMA((2 * len(places),))],
        compiler_params=pltpu.CompilerParams(vmem_limit_bytes=GATE_VMEM),
    )(at, student_head, teacher_head, *ready)


def head_total(at, own_part, backs, extras):
    width, depth = own_part.shape
    half = width // 2
    quarter = half // 2
    block = depth // 4

    def kernel(at_ref, own_ref, back0, back1, extra0, extra1, out_ref):
        for side in range(2):
            base = at_ref[0] if side == 0 else half - at_ref[0]
            low = base == 0
            for stage, back in enumerate((back0, back1)):
                rows = pl.ds(pl.multiple_of(base + stage * quarter, quarter), quarter)
                picked = pl.ds(stage * quarter, quarter)
                upper = extra0[pl.ds(half, quarter), :] if stage == 0 else extra1[...]
                extra = jnp.where(low, extra0[picked, :], upper)
                out_ref[rows, :] = (
                    own_ref[rows, :]
                    + back[pl.ds(side * quarter, quarter), :].astype(jnp.float32)
                    + extra.astype(jnp.float32)
                ).astype(out_ref.dtype)

    def columns(rows):
        return pl.BlockSpec((rows, block), lambda index: (0, index))

    return pl.pallas_call(
        kernel,
        grid=(4,),
        out_shape=jax.ShapeDtypeStruct((width, depth), jnp.bfloat16),
        in_specs=[pl.BlockSpec(memory_space=pltpu.SMEM), columns(width)]
        + [columns(half)] * 2
        + [columns(extra.shape[0]) for extra in extras],
        out_specs=columns(width),
        compiler_params=pltpu.CompilerParams(vmem_limit_bytes=8 * 1024 * 1024),
    )(at, own_part, *backs, *extras)


def pause(order, ready):
    return gate([order], ready, 30_000_000_000)[0]


def free():
    return pl.CostEstimate(flops=0, bytes_accessed=0, transcendentals=0)


def meeting(rows_s, rows_t, panels, panels_t, norm, norm_t, targets, ids, loss, kinds, ready=()):
    count, depth = rows_s.shape
    depth_t = rows_t.shape[1]
    pieces = len(panels)
    width = sum(panel.shape[0] for panel in panels)
    block = count // 2
    part_rows = width // len(kinds)
    whole = pl.BlockSpec(memory_space=pltpu.VMEM)
    contract = (((1,), (1,)), ((), ()))

    def kernel(*refs):
        s_ref, t_ref, norm_ref, norm_t_ref, target_ref, ids_ref, loss_in = refs[:7]
        panel_refs = refs[7 : 7 + pieces]
        panel_t_refs = refs[7 + pieces : 7 + 2 * pieces]
        score_ref, loss_ref = refs[7 + 2 * pieces + len(ready) :][:2]
        part_refs = refs[9 + 2 * pieces + len(ready) :]
        panel = jnp.concatenate([ref[:, :depth] for ref in panel_refs], axis=0)
        panel_t = jnp.concatenate([ref[:, ref.shape[1] - depth_t :] for ref in panel_t_refs], axis=0)

        @pl.loop(0, 2)
        def _(step):
            rows = pl.ds(pl.multiple_of(step * block, block), block)
            zs = lax.dot_general(s_ref[rows, :], panel, contract, preferred_element_type=jnp.float32)
            zt = lax.dot_general(t_ref[rows, :], panel_t, contract, preferred_element_type=jnp.float32)
            ls = zs - norm_ref[rows, :]
            lt = zt - norm_t_ref[rows, :]
            ps = jnp.exp(ls)
            pt = jnp.exp(lt)
            onehot = (target_ref[rows, :] == ids_ref[...]).astype(jnp.float32)
            scores = ((1.0 + hard_weight) * ps - pt - hard_weight * onehot).astype(jnp.bfloat16)
            score_ref[rows, :] = scores
            loss_ref[rows, :] = loss_in[rows, :] + jnp.sum(
                pt * (lt - ls) - hard_weight * onehot * ls, axis=1, keepdims=True
            )

        part = lax.dot_general(
            score_ref[...], s_ref[...], (((0,), (0,)), ((), ())), preferred_element_type=jnp.float32
        )
        for index, part_ref in enumerate(part_refs):
            part_ref[...] = part[index * part_rows : (index + 1) * part_rows].astype(part_ref.dtype)

    return pl.pallas_call(
        kernel,
        out_shape=[
            jax.ShapeDtypeStruct((count, width), jnp.bfloat16),
            jax.ShapeDtypeStruct((count, 1), jnp.float32),
        ]
        + [jax.ShapeDtypeStruct((part_rows, depth), kind) for kind in kinds],
        in_specs=[whole] * (7 + 2 * pieces) + [pl.BlockSpec(memory_space=pl.ANY)] * len(ready),
        out_specs=[whole] * (2 + len(kinds)),
        compiler_params=pltpu.CompilerParams(vmem_limit_bytes=16 * 1024 * 1024),
        cost_estimate=free(),
    )(rows_s, rows_t, norm, norm_t, targets, ids, loss, *panels, *panels_t, *ready)


def rows_product(scores, panels, depth, ready):
    count = scores[0].shape[0]
    block = depth // 7
    inner = sum(panel.shape[0] for panel in panels)
    whole = pl.BlockSpec(memory_space=pltpu.VMEM)

    def kernel(*refs):
        score_refs = refs[: len(scores)]
        panel_refs = refs[len(scores) : len(scores) + len(panels)]
        out_ref, left_ref = refs[-2:]

        @pl.when(pl.program_id(0) == 0)
        def _():
            left_ref[...] = jnp.concatenate([ref[...] for ref in score_refs], axis=1)

        right = jnp.concatenate([ref[...] for ref in panel_refs], axis=0)
        out_ref[...] = jnp.dot(
            left_ref[...], right, preferred_element_type=jnp.float32
        ).astype(out_ref.dtype)

    return pl.pallas_call(
        kernel,
        grid=(7,),
        out_shape=jax.ShapeDtypeStruct((count, depth), jnp.bfloat16),
        in_specs=[whole] * len(scores)
        + [pl.BlockSpec((panel.shape[0], block), lambda index: (0, index)) for panel in panels]
        + [pl.BlockSpec(memory_space=pl.ANY)] * len(ready),
        out_specs=pl.BlockSpec((count, block), lambda index: (0, index)),
        scratch_shapes=[pltpu.VMEM((count, inner), jnp.bfloat16)],
        compiler_params=pltpu.CompilerParams(vmem_limit_bytes=16 * 1024 * 1024),
        cost_estimate=free(),
    )(*scores, *panels, *ready)


def body(student_rows, teacher_rows, student_head, teacher_head, student_lse, teacher_lse, targets):
    count = lax.axis_size("seq")
    place = lax.axis_index("seq")
    plane = lax.axis_index("grp")
    core = place % 2
    width, depth = student_head.shape
    half = width // 2
    quarter = half // 2
    piece = half // CHUNKS
    norm = student_lse.astype(jnp.float32)[:, None]
    norm_t = teacher_lse.astype(jnp.float32)[:, None]
    wanted = targets[:, None]
    order = jnp.zeros((8, 128), jnp.float32)
    ids_in = jnp.arange(width, dtype=jnp.int32)
    near = (place - 2) % count
    far = (place - 1 - 2 * core) % count
    extra_id = jnp.where(core == 1, place - 1, place - 3) % count
    from_late = jnp.logical_and(core == 0, place // 2 % 2 == 1)

    def stage_ids(stage):
        rows = jnp.arange(half // 2, dtype=jnp.int32) + stage * (half // 2)
        inside = jnp.concatenate([plane * half + rows, (1 - plane) * half + rows])
        return jnp.concatenate([near * width + inside, far * width + inside])

    def meet(panels, panels_t, ids, loss, kinds, ready):
        return meeting(
            student_rows, teacher_rows, panels, panels_t, norm, norm_t, wanted, ids[None, :], loss, kinds, ready
        )

    at = jnp.reshape(plane * half, (1,)).astype(jnp.int32)
    chunks = packed(at, student_head, teacher_head, [(True, k * piece, piece) for k in range(2)])
    chunks = list(chunks)
    chunks += packed(
        at,
        student_head,
        teacher_head,
        [(True, k * piece, piece) for k in range(2, 4)] + [(False, 0, width)],
    )
    send = chunks.pop()

    crossed = [permuted(chunks[0], next_chip), permuted(chunks[1], next_chip), None, None]
    early = permuted(send, extra_early)
    swapped = [None] * 4
    order = pause(order, [chunks[0]])
    crossed[0], chunks[2], order = gate([crossed[0], chunks[2], order], [])
    swapped[0] = permuted(crossed[0], other_plane)
    crossed[2] = permuted(chunks[2], next_chip)
    own_scores, loss, own_part = meet(
        [student_head],
        [teacher_head],
        place * width + ids_in,
        jnp.zeros_like(norm),
        [jnp.float32],
        [order],
    )
    crossed[1], chunks[3], order = gate([crossed[1], chunks[3], order], [own_scores])
    swapped[1] = permuted(crossed[1], other_plane)
    crossed[3] = permuted(chunks[3], next_chip)
    order = pause(order, [])
    crossed[2], order = gate([crossed[2], order], [])
    swapped[2] = permuted(crossed[2], other_plane)
    send, = packed(at, student_head, teacher_head, [(False, 0, width - quarter)], [order])
    late = [permuted(send, extra_late), None]
    order = pause(order, [])
    swapped[0], swapped[1], order = gate([swapped[0], swapped[1], order], [])
    mine0 = jnp.concatenate([crossed[0], crossed[1], swapped[0], swapped[1]], axis=0)
    theirs0 = permuted(mine0, other_core)
    order = pause(order, [mine0])
    crossed[3], order = gate([crossed[3], order], [])
    swapped[3] = permuted(crossed[3], other_plane)

    order = pause(order, [])
    theirs0, early, order = gate([theirs0, early, order], [])
    pair = [mine0, theirs0]
    scores0, loss, keep, give = meet(pair, pair, stage_ids(0), loss, [jnp.float32, jnp.bfloat16], [order])
    got = permuted(give, other_core)
    order = pause(order, [give])
    got, order = gate([got, order], [])
    total = (keep + got.astype(jnp.float32)).astype(jnp.bfloat16)
    back0 = permuted(total, previous_chip)

    swapped[2], swapped[3], order = gate([swapped[2], swapped[3], order], [total])
    mine1 = jnp.concatenate([crossed[2], crossed[3], swapped[2], swapped[3]], axis=0)
    theirs1 = permuted(mine1, other_core)
    send, = packed(at, student_head, teacher_head, [(False, width - quarter, quarter)], [order])
    late[1] = permuted(send, extra_late)
    order = pause(order, [mine1])
    theirs1, order = gate([theirs1, order], [])
    pair = [mine1, theirs1]
    scores1, loss, keep, give = meet(pair, pair, stage_ids(1), loss, [jnp.float32, jnp.bfloat16], [order])
    got = permuted(give, other_core)
    order = pause(order, [give])
    got, order = gate([got, order], [])
    total = (keep + got.astype(jnp.float32)).astype(jnp.bfloat16)
    back1 = permuted(total, previous_chip)

    extra_parts, extra_scores, extras = [], [], []
    last = total
    for k in range(2):
        order = pause(order, [last])
        late[k], order = gate([late[k], order], [])
        lo, hi = (0, width - quarter) if k == 0 else (width - quarter, width)
        value = jnp.where(from_late, late[k], early[lo:hi])
        ids = extra_id * width + ids_in[lo:hi]
        scores, loss, last = meet([value], [value], ids, loss, [jnp.bfloat16], [order])
        extra_parts.append(permuted(last, extra_back))
        extra_scores.append(scores)
        extras.append(value)

    rows_grad = rows_product(
        [own_scores, scores0, scores1] + extra_scores,
        [student_head, mine0, theirs0, mine1, theirs1] + extras,
        depth,
        [last],
    )
    head_grad = head_total(at, own_part, [back0, back1], extra_parts)
    return (head_grad, rows_grad, loss[:, 0])


def solution(mesh):
    placed = (
        P(("grp", "seq"), None),
        P(("grp", "seq"), None),
        P("seq", None),
        P("seq", None),
        P(("grp", "seq")),
        P(("grp", "seq")),
        P(("grp", "seq")),
    )
    return jax.shard_map(
        body,
        mesh=mesh,
        in_specs=placed,
        out_specs=(P(("grp", "seq"), None), P(("grp", "seq"), None), P(("grp", "seq"))),
        check_vma=False,
    )
```

time: 97.1 us -> 103 us (1.061)
  waiting for transfers between devices: 47.5 us -> 15.4 us
  Pallas kernels: 0 us -> 31.8 us
  local copies, waits for them, and re-layouts: 3.38 us -> 25.5 us
  matrix products: 21.8 us -> 0 us
  starting transfers between devices: 18.1 us -> 21.1 us
  other arithmetic: 5.06 us -> 7.22 us
    ppermute x16 -> x19, waiting for transfers between devices: 47.5 us -> 15.4 us  [permuted(): return lax.ppermute(value, BOTH, pairs)]
    pallas_call x0 -> x33, Pallas kernels: none -> 31.8 us  [the longest x5 18.9 us: meeting(): pl.pallas_call(kernel, out_shape=[jax.ShapeDtypeStruct((count, width), jn...]
    unnamed x26 -> x98, local copies, waits for them, and re-layouts: 0.47 us -> 24.3 us
    dot_general x13 -> x0, matrix products: 21.8 us -> none  [the longest x4 9.06 us: meeting(): lax.dot_general(teacher_rows, teacher_panel, (((1,), (1,)), ((), ())), pr...]
    concatenate x9 -> x0, other arithmetic: 4 us -> none  [the longest x4 2.17 us: body(): chunk = jnp.concatenate([mine_rows[lo:hi], mine_rows_t[lo:hi]], axis=1)]
    ppermute x16 -> x19, starting transfers between devices: 18.1 us -> 21.1 us  [permuted(): return lax.ppermute(value, BOTH, pairs)]
    slice x9 -> x0, local copies, waits for them, and re-layouts: 2.77 us -> none  [the longest x2 2.43 us: body(): chunk = jnp.concatenate([mine_rows[lo:hi], mine_rows_t[lo:hi]], axis=1)]
    select_n x1 -> x2, other arithmetic: 0.15 us -> 2.84 us  [body(): value = jnp.where(from_late, late[k], early[lo:hi])]
  transfers between devices with their start and end apart: 16 -> 19, of which waited for: 9 -> 7; matrix products, arithmetic and copies ran while one was open for 20% -> 8% of each run, Pallas kernels for 0% -> 27%
where the time goes in v4:
time: 103 us; the launch traced here: 102 us
  Pallas kernels  31.8 us (31%)
  local copies, waits for them, and re-layouts  25.5 us (25%)
  starting transfers between devices  21.1 us (20%)
  waiting for transfers between devices  15.4 us (15%)
  other arithmetic  7.22 us (7%)
  between operations  1.31 us (1%)
    unnamed x98, local copies, waits for them, and re-layouts  24.3 us
    ppermute x19, starting transfers between devices, permuted(): return lax.ppermute(value, BOTH, pairs)  21.1 us
    pallas_call x5, Pallas kernels, meeting(): pl.pallas_call(kernel, out_shape=[jax.ShapeDtypeStruct((count, width), jn...  18.9 us
    ppermute x19, waiting for transfers between devices, permuted(): return lax.ppermute(value, BOTH, pairs)  15.4 us
    pallas_call x1, Pallas kernels, rows_product(): pl.pallas_call(kernel, grid=(7,), out_shape=jax.ShapeDtypeStruct((count,...  5.32 us
    pallas_call x4, Pallas kernels, packed(): pl.pallas_call(kernel, out_shape=[jax.ShapeDtypeStruct((rows, depth + dep...  3.78 us
    pallas_call x1, Pallas kernels, head_total(): pl.pallas_call(kernel, grid=(4,), out_shape=jax.ShapeDtypeStruct((width,...  3.74 us
    select_n x2, other arithmetic, body(): value = jnp.where(from_late, late[k], early[lo:hi])  2.84 us
  transfers between devices with their start and end apart: 19, of which 7 were waited for; matrix products, arithmetic and copies ran while one was open for 8% of the time, Pallas kernels for 27%

profile of v4, /device:TPU:0, one launch (start us, length us, event | category | flops | bytes accessed | tf_op | source)
XLA Modules:
  0.0 102.4 jit_solution(1147873599168201682)
XLA Ops:
  0.6 1.2 %copy-done.3 = bf16[128,3584]{1,0:T(8,128)(2,1)S(1)} copy-done((bf16[128,3584]{1,0:T(8,128)(2,1)S(1)}, bf16[128,3584]{1,0:T(8,128)(2,1)}, u32[]{:S(2)}) %copy-start.3) | copy-done | bytes 917528
  1.8 1.3 %copy-done.5 = bf16[128,4608]{1,0:T(8,128)(2,1)S(1)} copy-done((bf16[128,4608]{1,0:T(8,128)(2,1)S(1)}, bf16[128,4608]{1,0:T(8,128)(2,1)}, u32[]{:S(2)}) %copy-start.5) | copy-done | bytes 1179672
  3.9 3.0 %collective-permute-start.1 = (bf16[16,8192]{1,0:T(8,128)(2,1)}, bf16[16,8192]{1,0:T(8,128)(2,1)S(1)}, u32[]{:S(2)}, u32[]{:S(2)}) collective-permute-start(bf16[16,8192]{1,0:T(8,128)(2,1)} %get-tuple-element.60), channel_id=1, source_target_pairs={{0,2},{1,3},{2,4},{3,5},{4,6},{5,7},{6,8},{7,9},{8,10},{9,11},{10,... | collective-permute-start | bytes 786440 | tf_op jit(solution)/shard_map/ppermute | solution.py:22
  6.9 1.5 %collective-permute-start = (bf16[16,8192]{1,0:T(8,128)(2,1)}, bf16[16,8192]{1,0:T(8,128)(2,1)S(1)}, u32[]{:S(2)}, u32[]{:S(2)}) collective-permute-start(bf16[16,8192]{1,0:T(8,128)(2,1)} %get-tuple-element.54.refs_1_), channel_id=1, source_target_pairs={{0,2},{1,3},{2,4},{3,5},{4,6},{5,7},{6,8},{7,9},{8,10},{9,11},{10,... | collective-permute-start | bytes 786440 | tf_op jit(solution)/shard_map/ppermute | solution.py:22
  8.5 1.7 %shard_map.95 = (bf16[16,8192]{1,0:T(8,128)(2,1)S(1)}, bf16[16,8192]{1,0:T(8,128)(2,1)S(1)}, bf16[128,8192]{1,0:T(8,128)(2,1)}) custom-call(s32[1]{0:T(128)} %bitcast.at_ref, bf16[128,3584]{1,0:T(8,128)(2,1)S(1)} %copy-done.4, bf16[128,4608]{1,0:T(8,128)(2,1)S(1)} %copy-done.6), custom_call_target="tpu_custom_call" | custom-call | tf_op jit(solution)/shard_map/pallas_call | solution.py:93
  10.9 1.9 %collective-permute-start.6 = (bf16[128,8192]{1,0:T(8,128)(2,1)}, bf16[128,8192]{1,0:T(8,128)(2,1)}, u32[]{:S(2)}, u32[]{:S(2)}) collective-permute-start(bf16[128,8192]{1,0:T(8,128)(2,1)} %get-tuple-element.69), channel_id=1, source_target_pairs={{0,1},{1,4},{2,3},{4,5},{5,8},{6,7},{8,9},{9,12},{10,11},{12,13},{... | collective-permute-start | bytes 6291464 | tf_op jit(solution)/shard_map/ppermute | solution.py:22
  15.3 6.7 %collective-permute-done.refs_0_ = bf16[16,8192]{1,0:T(8,128)(2,1)S(1)} collective-permute-done((bf16[16,8192]{1,0:T(8,128)(2,1)}, bf16[16,8192]{1,0:T(8,128)(2,1)S(1)}, u32[]{:S(2)}, u32[]{:S(2)}) %collective-permute-start) | collective-permute-done | bytes 262176 | tf_op jit(solution)/shard_map/ppermute | solution.py:22
  23.7 1.5 %collective-permute-start.2 = (bf16[16,8192]{1,0:T(8,128)(2,1)S(1)}, bf16[16,8192]{1,0:T(8,128)(2,1)S(1)}, u32[]{:S(2)}, u32[]{:S(2)}) collective-permute-start(bf16[16,8192]{1,0:T(8,128)(2,1)S(1)} %get-tuple-element.59), channel_id=1, source_target_pairs={{0,16},{1,17},{2,18},{3,19},{4,20},{5,21},{6,22},{7,23},{8,24},{9,... | collective-permute-start | bytes 786440 | tf_op jit(solution)/shard_map/ppermute | solution.py:22
  25.4 2.3 %copy-done = bf16[512,4608]{1,0:T(8,128)(2,1)S(1)} copy-done((bf16[512,4608]{1,0:T(8,128)(2,1)S(1)}, bf16[512,4608]{1,0:T(8,128)(2,1)}, u32[]{:S(2)}) %copy-start) | copy-done | bytes 4718616
  27.7 2.0 %copy-done.1 = bf16[512,3584]{1,0:T(8,128)(2,1)S(1)} copy-done((bf16[512,3584]{1,0:T(8,128)(2,1)S(1)}, bf16[512,3584]{1,0:T(8,128)(2,1)}, u32[]{:S(2)}) %copy-start.1) | copy-done | bytes 3670040
  29.8 3.5 %shard_map.98 = (bf16[512,128]{1,0:T(8,128)(2,1)S(1)}, f32[512,1]{1,0:T(8,128)S(1)}, f32[128,3584]{1,0:T(8,128)S(1)}) custom-call(bf16[512,3584]{1,0:T(8,128)(2,1)S(1)} %copy-done.1, bf16[512,4608]{1,0:T(8,128)(2,1)S(1)} %copy-done, f32[512,1]{1,0:T(8,128)S(1)} %copy.49.refs_2_, f32[512,1]{1,0:T(8,128)S(1)} %copy.50.refs_3_, s32[512,1]{1,0:T(8,128)S(1)} %copy.51.refs_4_, ...), custom_call_target="tpu_custom_call" | custom-call | tf_op jit(solution)/shard_map/pallas_call | solution.py:192
  33.3 1.2 %copy-done.23 = f32[128,3584]{1,0:T(8,128)} copy-done((f32[128,3584]{1,0:T(8,128)}, f32[128,3584]{1,0:T(8,128)S(1)}, u32[]{:S(2)}) %copy-start.23) | copy-done | bytes 1835032
  35.0 1.2 %collective-permute-start.7 = (bf16[16,8192]{1,0:T(8,128)(2,1)S(1)}, bf16[16,8192]{1,0:T(8,128)(2,1)S(1)}, u32[]{:S(2)}, u32[]{:S(2)}) collective-permute-start(bf16[16,8192]{1,0:T(8,128)(2,1)S(1)} %get-tuple-element.70), channel_id=1, source_target_pairs={{0,2},{1,3},{2,4},{3,5},{4,6},{5,7},{6,8},{7,9},{8,10},{9,11},{10,... | collective-permute-start | bytes 786440 | tf_op jit(solution)/shard_map/ppermute | solution.py:22
  36.2 1.5 %collective-permute-start.10 = (bf16[16,8192]{1,0:T(8,128)(2,1)S(1)}, bf16[16,8192]{1,0:T(8,128)(2,1)S(1)}, u32[]{:S(2)}, u32[]{:S(2)}) collective-permute-start(bf16[16,8192]{1,0:T(8,128)(2,1)S(1)} %get-tuple-element.79), channel_id=1, source_target_pairs={{0,16},{1,17},{2,18},{3,19},{4,20},{5,21},{6,22},{7,23},{8,24},{9,... | collective-permute-start | bytes 786440 | tf_op jit(solution)/shard_map/ppermute | solution.py:22
  39.0 1.9 %collective-permute-start.15 = (bf16[96,8192]{1,0:T(8,128)(2,1)}, bf16[96,8192]{1,0:T(8,128)(2,1)}, u32[]{:S(2)}, u32[]{:S(2)}) collective-permute-start(bf16[96,8192]{1,0:T(8,128)(2,1)} %shard_map.117), channel_id=1, source_target_pairs={{3,6},{7,10},{11,14},{15,2},{19,22},{23,26},{27,30},{31,18}} | collective-permute-start | bytes 4718600 | tf_op jit(solution)/shard_map/ppermute | solution.py:22
  40.9 2.9 %collective-permute-done.3.refs_1_ = bf16[16,8192]{1,0:T(8,128)(2,1)S(1)} collective-permute-done((bf16[16,8192]{1,0:T(8,128)(2,1)S(1)}, bf16[16,8192]{1,0:T(8,128)(2,1)S(1)}, u32[]{:S(2)}, u32[]{:S(2)}) %collective-permute-start.3) | collective-permute-done | bytes 262176 | tf_op jit(solution)/shard_map/ppermute | solution.py:22
  44.8 1.3 %collective-permute-start.11 = (bf16[16,8192]{1,0:T(8,128)(2,1)S(1)}, bf16[16,8192]{1,0:T(8,128)(2,1)S(1)}, u32[]{:S(2)}, u32[]{:S(2)}) collective-permute-start(bf16[16,8192]{1,0:T(8,128)(2,1)S(1)} %get-tuple-element.80), channel_id=1, source_target_pairs={{0,16},{1,17},{2,18},{3,19},{4,20},{5,21},{6,22},{7,23},{8,24},{9,... | collective-permute-start | bytes 786440 | tf_op jit(solution)/shard_map/ppermute | solution.py:22
  47.0 3.5 %shard_map.108 = (bf16[512,128]{1,0:T(8,128)(2,1)S(1)}, f32[512,1]{1,0:T(8,128)S(1)}, f32[64,3584]{1,0:T(8,128)S(1)}, bf16[64,3584]{1,0:T(8,128)(2,1)S(1)}) custom-call(bf16[512,3584]{1,0:T(8,128)(2,1)S(1)} %copy-done.1, bf16[512,4608]{1,0:T(8,128)(2,1)S(1)} %bitcast.13, f32[512,1]{1,0:T(8,128)S(1)} %copy.49.refs_2_, f32[512,1]{1,0:T(8,128)S(1)} %copy.50.refs_3_, ...), custom_call_target="tpu_custom_call" | custom-call | tf_op jit(solution)/shard_map/pallas_call | solution.py:192
  51.2 1.2 %collective-permute-done.8.refs_0_ = bf16[64,3584]{1,0:T(8,128)(2,1)S(1)} collective-permute-done((bf16[64,3584]{1,0:T(8,128)(2,1)S(1)}, bf16[64,3584]{1,0:T(8,128)(2,1)S(1)}, u32[]{:S(2)}, u32[]{:S(2)}) %collective-permute-start.8) | collective-permute-done | bytes 458784 | tf_op jit(solution)/shard_map/ppermute | solution.py:22
  53.3 4.3 %collective-permute-start.9 = (bf16[64,3584]{1,0:T(8,128)(2,1)}, bf16[64,3584]{1,0:T(8,128)(2,1)}, u32[]{:S(2)}, u32[]{:S(2)}) collective-permute-start(bf16[64,3584]{1,0:T(8,128)(2,1)} %add_convert_fusion.1.refs_3_), channel_id=1, source_target_pairs={{0,14},{1,15},{2,0},{3,1},{4,2},{5,3},{6,4},{7,5},{8,6},{9,7},{10,... | collective-permute-start | bytes 1376264 | tf_op jit(solution)/shard_map/ppermute | solution.py:22
  58.6 1.9 %collective-permute-done.12.refs_0_ = bf16[64,8192]{1,0:T(8,128)(2,1)S(1)} collective-permute-done((bf16[64,8192]{1,0:T(8,128)(2,1)S(1)}, bf16[64,8192]{1,0:T(8,128)(2,1)S(1)}, u32[]{:S(2)}, u32[]{:S(2)}) %collective-permute-start.12) | collective-permute-done | bytes 1048608 | tf_op jit(solution)/shard_map/ppermute | solution.py:22
  60.5 3.5 %shard_map.114 = (bf16[512,128]{1,0:T(8,128)(2,1)S(1)}, f32[512,1]{1,0:T(8,128)S(1)}, f32[64,3584]{1,0:T(8,128)S(1)}, bf16[64,3584]{1,0:T(8,128)(2,1)S(1)}) custom-call(bf16[512,3584]{1,0:T(8,128)(2,1)S(1)} %copy-done.1, bf16[512,4608]{1,0:T(8,128)(2,1)S(1)} %bitcast.13, f32[512,1]{1,0:T(8,128)S(1)} %copy.49.refs_2_, f32[512,1]{1,0:T(8,128)S(1)} %copy.50.refs_3_, ...), custom_call_target="tpu_custom_call" | custom-call | tf_op jit(solution)/shard_map/pallas_call | solution.py:192
  64.7 1.2 %collective-permute-done.13.refs_0_ = bf16[64,3584]{1,0:T(8,128)(2,1)S(1)} collective-permute-done((bf16[64,3584]{1,0:T(8,128)(2,1)S(1)}, bf16[64,3584]{1,0:T(8,128)(2,1)S(1)}, u32[]{:S(2)}, u32[]{:S(2)}) %collective-permute-start.13) | collective-permute-done | bytes 458784 | tf_op jit(solution)/shard_map/ppermute | solution.py:22
  67.0 1.7 %slice_select_fusion.refs_7_.refs_8_.refs_10_ = bf16[96,8192]{1,0:T(8,128)(2,1)S(1)} fusion(bf16[96,8192]{1,0:T(8,128)(2,1)} %get-tuple-element.92, bf16[128,8192]{1,0:T(8,128)(2,1)} %get-tuple-element.93, pred[]{:T(512)S(6)} %and.37), kind=kLoop, calls=%fused_computation | loop fusion | flops 786432 | bytes 4718593 | tf_op jit(solution)/shard_map/jit(_where)/select_n | solution.py:342
  69.5 4.3 %shard_map.120 = (bf16[512,96]{1,0:T(8,128)(2,1)S(1)}, f32[512,1]{1,0:T(8,128)S(1)}, bf16[96,3584]{1,0:T(8,128)(2,1)}) custom-call(bf16[512,3584]{1,0:T(8,128)(2,1)S(1)} %copy-done.2, bf16[512,4608]{1,0:T(8,128)(2,1)S(1)} %bitcast.13, f32[512,1]{1,0:T(8,128)S(1)} %copy.49.refs_2_, f32[512,1]{1,0:T(8,128)S(1)} %copy.50.refs_3_, s32[512,1]{1,0:T(8,128)S(1)} %copy.51.refs_4_, ...), custom_call_target="tpu_custom_call" | custom-call | tf_op jit(solution)/shard_map/pallas_call | solution.py:192
  76.5 4.1 %shard_map.124 = (bf16[512,32]{1,0:T(8,128)(2,1)S(1)}, f32[512,1]{1,0:T(8,128)S(1)}, bf16[32,3584]{1,0:T(8,128)(2,1)}) custom-call(bf16[512,3584]{1,0:T(8,128)(2,1)S(1)} %copy-done.2, bf16[512,4608]{1,0:T(8,128)(2,1)S(1)} %bitcast.13, f32[512,1]{1,0:T(8,128)S(1)} %copy-done.18, f32[512,1]{1,0:T(8,128)S(1)} %copy-done.16, s32[512,1]{1,0:T(8,128)S(1)} %copy-done.20, ...), custom_call_target="tpu_custom_call" | custom-call | tf_op jit(solution)/shard_map/pallas_call | solution.py:192
  82.4 1.7 %reduce = f32[512]{0:T(512)} reduce(f32[512,1]{1,0:T(8,128)} %copy-done.32, f32[]{:T(128)} %constant.72), dimensions={1}, to_apply=%get-tuple-element.104.reduce_sub_computation | reduce | bytes 4100 | tf_op jit(solution)/shard_map/pallas_call | solution.py:192
  84.0 1.2 %copy-done.10 = bf16[64,8192]{1,0:T(8,128)(2,1)S(1)} copy-done((bf16[64,8192]{1,0:T(8,128)(2,1)S(1)}, bf16[64,8192]{1,0:T(8,128)(2,1)}, u32[]{:S(2)}) %copy-start.10) | copy-done | bytes 1048600
  85.3 1.2 %copy-done.12 = bf16[64,8192]{1,0:T(8,128)(2,1)S(1)} copy-done((bf16[64,8192]{1,0:T(8,128)(2,1)S(1)}, bf16[64,8192]{1,0:T(8,128)(2,1)}, u32[]{:S(2)}) %copy-start.12) | copy-done | bytes 1048600
  86.5 1.2 %copy-done.14 = bf16[64,8192]{1,0:T(8,128)(2,1)S(1)} copy-done((bf16[64,8192]{1,0:T(8,128)(2,1)S(1)}, bf16[64,8192]{1,0:T(8,128)(2,1)}, u32[]{:S(2)}) %copy-start.14) | copy-done | bytes 1048600
  93.3 5.3 %shard_map.126 = bf16[512,3584]{1,0:T(8,128)(2,1)} custom-call(bf16[512,128]{1,0:T(8,128)(2,1)S(1)} %copy-done.26, bf16[512,128]{1,0:T(8,128)(2,1)S(1)} %copy-done.34, bf16[512,128]{1,0:T(8,128)(2,1)S(1)} %copy-done.36, bf16[512,96]{1,0:T(8,128)(2,1)S(1)} %copy-done.38, bf16[512,32]{1,0:T(8,128)(2,1)S(1)} %copy-done.40, bf16[128,3584]{1,0:T(8,128)(2,1)S(1)} %copy-done.4, ...), custom_call_target="tpu_custom_call" | custom-call | tf_op jit(solution)/shard_map/pallas_call | solution.py:226
  98.6 3.7 %shard_map.125 = bf16[128,3584]{1,0:T(8,128)(2,1)} custom-call(s32[1]{0:T(128)} %bitcast.at_ref, f32[128,3584]{1,0:T(8,128)S(1)} %copy-done.24, bf16[64,3584]{1,0:T(8,128)(2,1)} %collective-permute-done.9.back0, bf16[64,3584]{1,0:T(8,128)(2,1)} %collective-permute-done.14.back1, bf16[96,3584]{1,0:T(8,128)(2,1)} %collective-permute-done.16.extra0, ...), custom_call_target="tpu_custom_call" | custom-call | tf_op jit(solution)/shard_map/pallas_call | solution.py:131
  (163 shorter events, 24.2 us)
Async XLA Ops:
  3.1 5.4 %copy-start.4 = (bf16[128,3584]{1,0:T(8,128)(2,1)S(1)}, bf16[128,3584]{1,0:T(8,128)(2,1)}, u32[]{:S(2)}) copy-start(bf16[128,3584]{1,0:T(8,128)(2,1)} %refs_5_.1) | copy-start | bytes 2752516
  3.1 5.4 %copy-start.6 = (bf16[128,4608]{1,0:T(8,128)(2,1)S(1)}, bf16[128,4608]{1,0:T(8,128)(2,1)}, u32[]{:S(2)}) copy-start(bf16[128,4608]{1,0:T(8,128)(2,1)} %teacher_ref.7) | copy-start | bytes 3538948
  3.9 29.4 %collective-permute-start.1 = (bf16[16,8192]{1,0:T(8,128)(2,1)}, bf16[16,8192]{1,0:T(8,128)(2,1)S(1)}, u32[]{:S(2)}, u32[]{:S(2)}) collective-permute-start(bf16[16,8192]{1,0:T(8,128)(2,1)} %get-tuple-element.60), channel_id=1, source_target_pairs={{0,2},{1,3},{2,4},{3,5},{4,6},{5,7},{6,8},{7,9},{8,10},{9,11},{10,... | collective-permute-start | bytes 786440 | tf_op jit(solution)/shard_map/ppermute | solution.py:22
  6.9 15.2 %collective-permute-start = (bf16[16,8192]{1,0:T(8,128)(2,1)}, bf16[16,8192]{1,0:T(8,128)(2,1)S(1)}, u32[]{:S(2)}, u32[]{:S(2)}) collective-permute-start(bf16[16,8192]{1,0:T(8,128)(2,1)} %get-tuple-element.54.refs_1_), channel_id=1, source_target_pairs={{0,2},{1,3},{2,4},{3,5},{4,6},{5,7},{6,8},{7,9},{8,10},{9,11},{10,... | collective-permute-start | bytes 786440 | tf_op jit(solution)/shard_map/ppermute | solution.py:22
  10.9 35.7 %collective-permute-start.6 = (bf16[128,8192]{1,0:T(8,128)(2,1)}, bf16[128,8192]{1,0:T(8,128)(2,1)}, u32[]{:S(2)}, u32[]{:S(2)}) collective-permute-start(bf16[128,8192]{1,0:T(8,128)(2,1)} %get-tuple-element.69), channel_id=1, source_target_pairs={{0,1},{1,4},{2,3},{4,5},{5,8},{6,7},{8,9},{9,12},{10,11},{12,13},{... | collective-permute-start | bytes 6291464 | tf_op jit(solution)/shard_map/ppermute | solution.py:22
  13.4 11.9 %copy-start.41 = (s32[1,128]{1,0:T(1,128)S(1)}, s32[1,128]{1,0:T(1,128)}, u32[]{:S(2)}) copy-start(s32[1,128]{1,0:T(1,128)} %iota_add_fusion.3.refs_5_) | copy-start | bytes 1540
  14.3 54.4 %copy-start.15 = (f32[512,1]{1,0:T(8,128)}, f32[512,1]{1,0:T(8,128)S(1)}, u32[]{:S(2)}) copy-start(f32[512,1]{1,0:T(8,128)S(1)} %copy.50.refs_3_) | copy-start | bytes 6148
  14.4 54.3 %copy-start.17 = (f32[512,1]{1,0:T(8,128)}, f32[512,1]{1,0:T(8,128)S(1)}, u32[]{:S(2)}) copy-start(f32[512,1]{1,0:T(8,128)S(1)} %copy.49.refs_2_) | copy-start | bytes 6148
  15.3 53.4 %copy-start.19 = (s32[512,1]{1,0:T(8,128)}, s32[512,1]{1,0:T(8,128)S(1)}, u32[]{:S(2)}) copy-start(s32[512,1]{1,0:T(8,128)S(1)} %copy.51.refs_4_) | copy-start | bytes 6148
  23.7 15.2 %collective-permute-start.2 = (bf16[16,8192]{1,0:T(8,128)(2,1)S(1)}, bf16[16,8192]{1,0:T(8,128)(2,1)S(1)}, u32[]{:S(2)}, u32[]{:S(2)}) collective-permute-start(bf16[16,8192]{1,0:T(8,128)(2,1)S(1)} %get-tuple-element.59), channel_id=1, source_target_pairs={{0,16},{1,17},{2,18},{3,19},{4,20},{5,21},{6,22},{7,23},{8,24},{9,... | collective-permute-start | bytes 786440 | tf_op jit(solution)/shard_map/ppermute | solution.py:22
  25.3 11.0 %collective-permute-start.4 = (bf16[16,8192]{1,0:T(8,128)(2,1)}, bf16[16,8192]{1,0:T(8,128)(2,1)S(1)}, u32[]{:S(2)}, u32[]{:S(2)}) collective-permute-start(bf16[16,8192]{1,0:T(8,128)(2,1)} %copy-done.31), channel_id=1, source_target_pairs={{0,2},{1,3},{2,4},{3,5},{4,6},{5,7},{6,8},{7,9},{8,10},{9,11},{10,... | collective-permute-start | bytes 786440 | tf_op jit(solution)/shard_map/ppermute | solution.py:22
  29.8 3.5 %copy-start.28 = (bf16[16,8192]{1,0:T(8,128)(2,1)S(1)}, bf16[16,8192]{1,0:T(8,128)(2,1)}, u32[]{:S(2)}) copy-start(bf16[16,8192]{1,0:T(8,128)(2,1)} %copy-done.27) | copy-start | bytes 786436
  34.5 9.2 %collective-permute-start.3 = (bf16[16,8192]{1,0:T(8,128)(2,1)S(1)}, bf16[16,8192]{1,0:T(8,128)(2,1)S(1)}, u32[]{:S(2)}, u32[]{:S(2)}) collective-permute-start(bf16[16,8192]{1,0:T(8,128)(2,1)S(1)} %get-tuple-element.63), channel_id=1, source_target_pairs={{0,16},{1,17},{2,18},{3,19},{4,20},{5,21},{6,22},{7,23},{8,24},{9,... | collective-permute-start | bytes 786440 | tf_op jit(solution)/shard_map/ppermute | solution.py:22
  35.0 9.7 %collective-permute-start.7 = (bf16[16,8192]{1,0:T(8,128)(2,1)S(1)}, bf16[16,8192]{1,0:T(8,128)(2,1)S(1)}, u32[]{:S(2)}, u32[]{:S(2)}) collective-permute-start(bf16[16,8192]{1,0:T(8,128)(2,1)S(1)} %get-tuple-element.70), channel_id=1, source_target_pairs={{0,2},{1,3},{2,4},{3,5},{4,6},{5,7},{6,8},{7,9},{8,10},{9,11},{10,... | collective-permute-start | bytes 786440 | tf_op jit(solution)/shard_map/ppermute | solution.py:22
  36.2 21.3 %collective-permute-start.10 = (bf16[16,8192]{1,0:T(8,128)(2,1)S(1)}, bf16[16,8192]{1,0:T(8,128)(2,1)S(1)}, u32[]{:S(2)}, u32[]{:S(2)}) collective-permute-start(bf16[16,8192]{1,0:T(8,128)(2,1)S(1)} %get-tuple-element.79), channel_id=1, source_target_pairs={{0,16},{1,17},{2,18},{3,19},{4,20},{5,21},{6,22},{7,23},{8,24},{9,... | collective-permute-start | bytes 786440 | tf_op jit(solution)/shard_map/ppermute | solution.py:22
  39.0 28.0 %collective-permute-start.15 = (bf16[96,8192]{1,0:T(8,128)(2,1)}, bf16[96,8192]{1,0:T(8,128)(2,1)}, u32[]{:S(2)}, u32[]{:S(2)}) collective-permute-start(bf16[96,8192]{1,0:T(8,128)(2,1)} %shard_map.117), channel_id=1, source_target_pairs={{3,6},{7,10},{11,14},{15,2},{19,22},{23,26},{27,30},{31,18}} | collective-permute-start | bytes 4718600 | tf_op jit(solution)/shard_map/ppermute | solution.py:22
  43.8 2.7 %copy-start.13 = (bf16[64,8192]{1,0:T(8,128)(2,1)}, bf16[64,8192]{1,0:T(8,128)(2,1)S(1)}, u32[]{:S(2)}) copy-start(bf16[64,8192]{1,0:T(8,128)(2,1)S(1)} %constant_dynamic-update-slice_fusion.refs_1_.refs_7_.refs_9_.refs_6_) | copy-start | bytes 3145732
  43.8 2.7 %collective-permute-start.5 = (bf16[64,8192]{1,0:T(8,128)(2,1)S(1)}, bf16[64,8192]{1,0:T(8,128)(2,1)S(1)}, u32[]{:S(2)}, u32[]{:S(2)}) collective-permute-start(bf16[64,8192]{1,0:T(8,128)(2,1)S(1)} %constant_dynamic-update-slice_fusion.refs_1_.refs_7_.refs_9_.refs_6_), channel_id=1, source_target_pairs={{0,1},{1,0},{2,3},{3,2},{4,5},{5,4},{6,7},{7,6},{8,9},{9,8},{10,11... | collective-permute-start | bytes 3145736 | tf_op jit(solution)/shard_map/ppermute | solution.py:22
  44.8 12.8 %collective-permute-start.11 = (bf16[16,8192]{1,0:T(8,128)(2,1)S(1)}, bf16[16,8192]{1,0:T(8,128)(2,1)S(1)}, u32[]{:S(2)}, u32[]{:S(2)}) collective-permute-start(bf16[16,8192]{1,0:T(8,128)(2,1)S(1)} %get-tuple-element.80), channel_id=1, source_target_pairs={{0,16},{1,17},{2,18},{3,19},{4,20},{5,21},{6,22},{7,23},{8,24},{9,... | collective-permute-start | bytes 786440 | tf_op jit(solution)/shard_map/ppermute | solution.py:22
  46.6 4.0 %copy-start.7 = (bf16[64,8192]{1,0:T(8,128)(2,1)}, bf16[64,8192]{1,0:T(8,128)(2,1)S(1)}, u32[]{:S(2)}) copy-start(bf16[64,8192]{1,0:T(8,128)(2,1)S(1)} %get-tuple-element.73.refs_8_.refs_10_.refs_7_) | copy-start | bytes 3145732
  50.6 1.9 %collective-permute-start.8 = (bf16[64,3584]{1,0:T(8,128)(2,1)S(1)}, bf16[64,3584]{1,0:T(8,128)(2,1)S(1)}, u32[]{:S(2)}, u32[]{:S(2)}) collective-permute-start(bf16[64,3584]{1,0:T(8,128)(2,1)S(1)} %get-tuple-element.76.refs_1_), channel_id=1, source_target_pairs={{0,1},{1,0},{2,3},{3,2},{4,5},{5,4},{6,7},{7,6},{8,9},{9,8},{10,11... | collective-permute-start | bytes 1376264 | tf_op jit(solution)/shard_map/ppermute | solution.py:22
  53.3 45.3 %collective-permute-start.9 = (bf16[64,3584]{1,0:T(8,128)(2,1)}, bf16[64,3584]{1,0:T(8,128)(2,1)}, u32[]{:S(2)}, u32[]{:S(2)}) collective-permute-start(bf16[64,3584]{1,0:T(8,128)(2,1)} %add_convert_fusion.1.refs_3_), channel_id=1, source_target_pairs={{0,14},{1,15},{2,0},{3,1},{4,2},{5,3},{6,4},{7,5},{8,6},{9,7},{10,... | collective-permute-start | bytes 1376264 | tf_op jit(solution)/shard_map/ppermute | solution.py:22
  57.8 2.7 %collective-permute-start.12 = (bf16[64,8192]{1,0:T(8,128)(2,1)S(1)}, bf16[64,8192]{1,0:T(8,128)(2,1)S(1)}, u32[]{:S(2)}, u32[]{:S(2)}) collective-permute-start(bf16[64,8192]{1,0:T(8,128)(2,1)S(1)} %constant_dynamic-update-slice_fusion.4.refs_1_.refs_7_.refs_9_.refs_8_), channel_id=1, source_target_pairs={{0,1},{1,0},{2,3},{3,2},{4,5},{5,4},{6,7},{7,6},{8,9},{9,8},{10,11... | collective-permute-start | bytes 3145736 | tf_op jit(solution)/shard_map/ppermute | solution.py:22
  57.9 17.4 %collective-permute-start.17 = (bf16[32,8192]{1,0:T(8,128)(2,1)S(1)}, bf16[32,8192]{1,0:T(8,128)(2,1)S(1)}, u32[]{:S(2)}, u32[]{:S(2)}) collective-permute-start(bf16[32,8192]{1,0:T(8,128)(2,1)S(1)} %shard_map.121), channel_id=1, source_target_pairs={{3,6},{7,10},{11,14},{15,2},{19,22},{23,26},{27,30},{31,18}} | collective-permute-start | bytes 1572872 | tf_op jit(solution)/shard_map/ppermute | solution.py:22
  60.5 3.5 %copy-start.9 = (bf16[64,8192]{1,0:T(8,128)(2,1)}, bf16[64,8192]{1,0:T(8,128)(2,1)S(1)}, u32[]{:S(2)}) copy-start(bf16[64,8192]{1,0:T(8,128)(2,1)S(1)} %get-tuple-element.85.refs_8_.refs_10_.refs_9_) | copy-start | bytes 3145732
  64.0 1.9 %collective-permute-start.13 = (bf16[64,3584]{1,0:T(8,128)(2,1)S(1)}, bf16[64,3584]{1,0:T(8,128)(2,1)S(1)}, u32[]{:S(2)}, u32[]{:S(2)}) collective-permute-start(bf16[64,3584]{1,0:T(8,128)(2,1)S(1)} %get-tuple-element.88.refs_1_), channel_id=1, source_target_pairs={{0,1},{1,0},{2,3},{3,2},{4,5},{5,4},{6,7},{7,6},{8,9},{9,8},{10,11... | collective-permute-start | bytes 1376264 | tf_op jit(solution)/shard_map/ppermute | solution.py:22
  66.8 31.8 %collective-permute-start.14 = (bf16[64,3584]{1,0:T(8,128)(2,1)}, bf16[64,3584]{1,0:T(8,128)(2,1)}, u32[]{:S(2)}, u32[]{:S(2)}) collective-permute-start(bf16[64,3584]{1,0:T(8,128)(2,1)} %add_convert_fusion.refs_1_), channel_id=1, source_target_pairs={{0,14},{1,15},{2,0},{3,1},{4,2},{5,3},{6,4},{7,5},{8,6},{9,7},{10,... | collective-permute-start | bytes 1376264 | tf_op jit(solution)/shard_map/ppermute | solution.py:22
  74.5 24.1 %collective-permute-start.16 = (bf16[96,3584]{1,0:T(8,128)(2,1)}, bf16[96,3584]{1,0:T(8,128)(2,1)}, u32[]{:S(2)}, u32[]{:S(2)}) collective-permute-start(bf16[96,3584]{1,0:T(8,128)(2,1)} %get-tuple-element.95.refs_1_), channel_id=1, source_target_pairs={{0,13},{1,0},{2,15},{3,2},{4,1},{5,4},{6,3},{7,6},{8,5},{9,8},{10,... | collective-permute-start | bytes 2064392 | tf_op jit(solution)/shard_map/ppermute | solution.py:22
  76.4 4.2 %copy-start.21 = (bf16[32,8192]{1,0:T(8,128)(2,1)}, bf16[32,8192]{1,0:T(8,128)(2,1)S(1)}, u32[]{:S(2)}) copy-start(bf16[32,8192]{1,0:T(8,128)(2,1)S(1)} %slice_select_fusion.1.refs_7_.refs_8_.refs_11_) | copy-start | bytes 1572868
  76.5 7.6 %copy-start.8 = (bf16[64,8192]{1,0:T(8,128)(2,1)S(1)}, bf16[64,8192]{1,0:T(8,128)(2,1)}, u32[]{:S(2)}) copy-start(bf16[64,8192]{1,0:T(8,128)(2,1)} %copy-done.7) | copy-start | bytes 3145732
  81.9 16.7 %collective-permute-start.18 = (bf16[32,3584]{1,0:T(8,128)(2,1)}, bf16[32,3584]{1,0:T(8,128)(2,1)}, u32[]{:S(2)}, u32[]{:S(2)}) collective-permute-start(bf16[32,3584]{1,0:T(8,128)(2,1)} %get-tuple-element.99.refs_12_), channel_id=1, source_target_pairs={{0,13},{1,0},{2,15},{3,2},{4,1},{5,4},{6,3},{7,6},{8,5},{9,8},{10,... | collective-permute-start | bytes 688136 | tf_op jit(solution)/shard_map/ppermute | solution.py:22
  93.3 5.3 %copy-start.24 = (f32[128,3584]{1,0:T(8,128)S(1)}, f32[128,3584]{1,0:T(8,128)}, u32[]{:S(2)}) copy-start(f32[128,3584]{1,0:T(8,128)} %copy-done.23) | copy-start | bytes 5505028
  (33 other events, 43.8 us)

commit v5 on v4

--- a/solution.py
+++ b/solution.py
@@ -8,6 +8,8 @@
 hard_weight = 0.5
 CHUNKS = 4
 GATE_VMEM = 128 * 1024
+MEETING_VMEM = 12 * 1024 * 1024
+WIDE_VMEM = 56 * 1024 * 1024
 BOTH = ("grp", "seq")
 
 
@@ -100,7 +102,7 @@
         + [anywhere] * len(ready),
         out_specs=[anywhere] * len(places),
         scratch_shapes=[pltpu.SemaphoreType.DMA((2 * len(places),))],
-        compiler_params=pltpu.CompilerParams(vmem_limit_bytes=GATE_VMEM),
+        compiler_params=pltpu.CompilerParams(vmem_limit_bytes=WIDE_VMEM),
     )(at, student_head, teacher_head, *ready)
 
 
@@ -108,35 +110,39 @@
     width, depth = own_part.shape
     half = width // 2
     quarter = half // 2
-    block = depth // 4
-
-    def kernel(at_ref, own_ref, back0, back1, extra0, extra1, out_ref):
-        for side in range(2):
-            base = at_ref[0] if side == 0 else half - at_ref[0]
-            low = base == 0
-            for stage, back in enumerate((back0, back1)):
+    whole = pl.BlockSpec(memory_space=pltpu.VMEM)
+
+    def kernel(at_ref, own_ref, back0, back1, extra0, extra1, out_ref, sum_ref, sems):
+        low = at_ref[0] == 0
+        copies = []
+        for stage, back in enumerate((back0, back1)):
+            for side in range(2):
+                base = at_ref[0] if side == 0 else half - at_ref[0]
                 rows = pl.ds(pl.multiple_of(base + stage * quarter, quarter), quarter)
                 picked = pl.ds(stage * quarter, quarter)
-                upper = extra0[pl.ds(half, quarter), :] if stage == 0 else extra1[...]
-                extra = jnp.where(low, extra0[picked, :], upper)
-                out_ref[rows, :] = (
+                first = low if side == 0 else jnp.logical_not(low)
+                extra = jnp.where(first, extra0[picked, :], extra1[picked, :])
+                sum_ref[rows, :] = (
                     own_ref[rows, :]
                     + back[pl.ds(side * quarter, quarter), :].astype(jnp.float32)
                     + extra.astype(jnp.float32)
-                ).astype(out_ref.dtype)
-
-    def columns(rows):
-        return pl.BlockSpec((rows, block), lambda index: (0, index))
+                ).astype(sum_ref.dtype)
+                copies.append(
+                    pltpu.make_async_copy(
+                        sum_ref.at[rows, :], out_ref.at[rows, :], sems.at[2 * stage + side]
+                    )
+                )
+                copies[-1].start()
+        for copy in copies:
+            copy.wait()
 
     return pl.pallas_call(
         kernel,
-        grid=(4,),
         out_shape=jax.ShapeDtypeStruct((width, depth), jnp.bfloat16),
-        in_specs=[pl.BlockSpec(memory_space=pltpu.SMEM), columns(width)]
-        + [columns(half)] * 2
-        + [columns(extra.shape[0]) for extra in extras],
-        out_specs=columns(width),
-        compiler_params=pltpu.CompilerParams(vmem_limit_bytes=8 * 1024 * 1024),
+        in_specs=[pl.BlockSpec(memory_space=pltpu.SMEM)] + [whole] * 5,
+        out_specs=pl.BlockSpec(memory_space=pl.ANY),
+        scratch_shapes=[pltpu.VMEM((width, depth), jnp.bfloat16), pltpu.SemaphoreType.DMA((4,))],
+        compiler_params=pltpu.CompilerParams(vmem_limit_bytes=6 * 1024 * 1024),
     )(at, own_part, *backs, *extras)
 
 
@@ -148,28 +154,44 @@
     return pl.CostEstimate(flops=0, bytes_accessed=0, transcendentals=0)
 
 
-def meeting(rows_s, rows_t, panels, panels_t, norm, norm_t, targets, ids, loss, kinds, ready=()):
+def meeting(rows_s, rows_t, panels, panels_t, norm, norm_t, targets, ids, loss, kinds, ready=(), flag=None):
     count, depth = rows_s.shape
     depth_t = rows_t.shape[1]
+    start = 0
+    if flag is not None:
+        panels, start = panels[:2], panels[2]
+        panels_t = []
     pieces = len(panels)
-    width = sum(panel.shape[0] for panel in panels)
+    pieces_t = len(panels_t)
+    width = panels[0].shape[0] if flag is not None else sum(panel.shape[0] for panel in panels)
     block = count // 2
     part_rows = width // len(kinds)
     whole = pl.BlockSpec(memory_space=pltpu.VMEM)
     contract = (((1,), (1,)), ((), ()))
+    flags = [] if flag is None else [flag]
 
     def kernel(*refs):
         s_ref, t_ref, norm_ref, norm_t_ref, target_ref, ids_ref, loss_in = refs[:7]
         panel_refs = refs[7 : 7 + pieces]
-        panel_t_refs = refs[7 + pieces : 7 + 2 * pieces]
-        score_ref, loss_ref = refs[7 + 2 * pieces + len(ready) :][:2]
-        part_refs = refs[9 + 2 * pieces + len(ready) :]
-        panel = jnp.concatenate([ref[:, :depth] for ref in panel_refs], axis=0)
-        panel_t = jnp.concatenate([ref[:, ref.shape[1] - depth_t :] for ref in panel_t_refs], axis=0)
-
-        @pl.loop(0, 2)
-        def _(step):
-            rows = pl.ds(pl.multiple_of(step * block, block), block)
+        panel_t_refs = refs[7 + pieces : 7 + pieces + pieces_t]
+        flag_refs = refs[7 + pieces + pieces_t :][: len(flags)]
+        outs = refs[7 + pieces + pieces_t + len(flags) + len(ready) :]
+        score_ref, loss_ref = outs[:2]
+        part_refs = outs[2 : 2 + len(kinds)]
+        if flags:
+            chosen = jnp.where(
+                flag_refs[0][0] == 1, panel_refs[0][...], panel_refs[1][pl.ds(start, width), :]
+            )
+            panel, panel_t = chosen[:, :depth], chosen[:, depth:]
+            outs[-1][...] = panel
+        else:
+            panel = jnp.concatenate([ref[:, :depth] for ref in panel_refs], axis=0)
+            panel_t = jnp.concatenate(
+                [ref[:, ref.shape[1] - depth_t :] for ref in panel_t_refs], axis=0
+            )
+
+        for step in range(2):
+            rows = pl.ds(step * block, block)
             zs = lax.dot_general(s_ref[rows, :], panel, contract, preferred_element_type=jnp.float32)
             zt = lax.dot_general(t_ref[rows, :], panel_t, contract, preferred_element_type=jnp.float32)
             ls = zs - norm_ref[rows, :]
@@ -179,8 +201,13 @@
             onehot = (target_ref[rows, :] == ids_ref[...]).astype(jnp.float32)
             scores = ((1.0 + hard_weight) * ps - pt - hard_weight * onehot).astype(jnp.bfloat16)
             score_ref[rows, :] = scores
-            loss_ref[rows, :] = loss_in[rows, :] + jnp.sum(
-                pt * (lt - ls) - hard_weight * onehot * ls, axis=1, keepdims=True
+            terms = pt * (lt - ls) - hard_weight * onehot * ls
+            loss_ref[:, rows] = loss_in[:, rows] + lax.dot_general(
+                jnp.ones((8, width), jnp.float32),
+                terms,
+                contract,
+                precision=lax.Precision.HIGHEST,
+                preferred_element_type=jnp.float32,
             )
 
         part = lax.dot_general(
@@ -189,25 +216,28 @@
         for index, part_ref in enumerate(part_refs):
             part_ref[...] = part[index * part_rows : (index + 1) * part_rows].astype(part_ref.dtype)
 
+    out_shape = [
+        jax.ShapeDtypeStruct((count, width), jnp.bfloat16),
+        jax.ShapeDtypeStruct((8, count), jnp.float32),
+    ] + [jax.ShapeDtypeStruct((part_rows, depth), kind) for kind in kinds]
+    if flags:
+        out_shape.append(jax.ShapeDtypeStruct((width, depth), jnp.bfloat16))
     return pl.pallas_call(
         kernel,
-        out_shape=[
-            jax.ShapeDtypeStruct((count, width), jnp.bfloat16),
-            jax.ShapeDtypeStruct((count, 1), jnp.float32),
-        ]
-        + [jax.ShapeDtypeStruct((part_rows, depth), kind) for kind in kinds],
-        in_specs=[whole] * (7 + 2 * pieces) + [pl.BlockSpec(memory_space=pl.ANY)] * len(ready),
-        out_specs=[whole] * (2 + len(kinds)),
-        compiler_params=pltpu.CompilerParams(vmem_limit_bytes=16 * 1024 * 1024),
+        out_shape=out_shape,
+        in_specs=[whole] * (7 + pieces + pieces_t)
+        + [pl.BlockSpec(memory_space=pltpu.SMEM)] * len(flags)
+        + [pl.BlockSpec(memory_space=pl.ANY)] * len(ready),
+        out_specs=[whole] * len(out_shape),
+        compiler_params=pltpu.CompilerParams(vmem_limit_bytes=MEETING_VMEM),
         cost_estimate=free(),
-    )(rows_s, rows_t, norm, norm_t, targets, ids, loss, *panels, *panels_t, *ready)
+    )(rows_s, rows_t, norm, norm_t, targets, ids, loss, *panels, *panels_t, *flags, *ready)
 
 
 def rows_product(scores, panels, depth, ready):
     count = scores[0].shape[0]
     block = depth // 7
     inner = sum(panel.shape[0] for panel in panels)
-    whole = pl.BlockSpec(memory_space=pltpu.VMEM)
 
     def kernel(*refs):
         score_refs = refs[: len(scores)]
@@ -227,13 +257,13 @@
         kernel,
         grid=(7,),
         out_shape=jax.ShapeDtypeStruct((count, depth), jnp.bfloat16),
-        in_specs=[whole] * len(scores)
+        in_specs=[pl.BlockSpec((count, score.shape[1]), lambda index: (0, 0)) for score in scores]
         + [pl.BlockSpec((panel.shape[0], block), lambda index: (0, index)) for panel in panels]
         + [pl.BlockSpec(memory_space=pl.ANY)] * len(ready),
         out_specs=pl.BlockSpec((count, block), lambda index: (0, index)),
         scratch_shapes=[pltpu.VMEM((count, inner), jnp.bfloat16)],
-        compiler_params=pltpu.CompilerParams(vmem_limit_bytes=16 * 1024 * 1024),
-        cost_estimate=free(),
+        compiler_params=pltpu.CompilerParams(vmem_limit_bytes=WIDE_VMEM),
+        cost_estimate=pl.CostEstimate(flops=30_000_000_000, bytes_accessed=0, transcendentals=0),
     )(*scores, *panels, *ready)
 
 
@@ -244,7 +274,6 @@
     core = place % 2
     width, depth = student_head.shape
     half = width // 2
-    quarter = half // 2
     piece = half // CHUNKS
     norm = student_lse.astype(jnp.float32)[:, None]
     norm_t = teacher_lse.astype(jnp.float32)[:, None]
@@ -254,16 +283,16 @@
     near = (place - 2) % count
     far = (place - 1 - 2 * core) % count
     extra_id = jnp.where(core == 1, place - 1, place - 3) % count
-    from_late = jnp.logical_and(core == 0, place // 2 % 2 == 1)
+    from_late = jnp.reshape(jnp.logical_and(core == 0, place // 2 % 2 == 1), (1,)).astype(jnp.int32)
 
     def stage_ids(stage):
         rows = jnp.arange(half // 2, dtype=jnp.int32) + stage * (half // 2)
         inside = jnp.concatenate([plane * half + rows, (1 - plane) * half + rows])
         return jnp.concatenate([near * width + inside, far * width + inside])
 
-    def meet(panels, panels_t, ids, loss, kinds, ready):
+    def meet(panels, panels_t, ids, loss, kinds, ready, flag=None):
         return meeting(
-            student_rows, teacher_rows, panels, panels_t, norm, norm_t, wanted, ids[None, :], loss, kinds, ready
+            student_rows, teacher_rows, panels, panels_t, norm, norm_t, wanted, ids[None, :], loss, kinds, ready, flag
         )
 
     at = jnp.reshape(plane * half, (1,)).astype(jnp.int32)
@@ -280,25 +309,26 @@
     crossed = [permuted(chunks[0], next_chip), permuted(chunks[1], next_chip), None, None]
     early = permuted(send, extra_early)
     swapped = [None] * 4
-    order = pause(order, [chunks[0]])
-    crossed[0], chunks[2], order = gate([crossed[0], chunks[2], order], [])
-    swapped[0] = permuted(crossed[0], other_plane)
-    crossed[2] = permuted(chunks[2], next_chip)
     own_scores, loss, own_part = meet(
         [student_head],
         [teacher_head],
         place * width + ids_in,
-        jnp.zeros_like(norm),
+        jnp.zeros((8, student_rows.shape[0]), jnp.float32),
         [jnp.float32],
-        [order],
+        [chunks[2]],
     )
-    crossed[1], chunks[3], order = gate([crossed[1], chunks[3], order], [own_scores])
+    order = pause(order, [own_scores])
+    crossed[0], chunks[2], order = gate([crossed[0], chunks[2], order], [])
+    swapped[0] = permuted(crossed[0], other_plane)
+    crossed[2] = permuted(chunks[2], next_chip)
+    order = pause(order, [chunks[2]])
+    crossed[1], chunks[3], order = gate([crossed[1], chunks[3], order], [])
     swapped[1] = permuted(crossed[1], other_plane)
     crossed[3] = permuted(chunks[3], next_chip)
-    order = pause(order, [])
+    order = pause(order, [chunks[3]])
     crossed[2], order = gate([crossed[2], order], [])
     swapped[2] = permuted(crossed[2], other_plane)
-    send, = packed(at, student_head, teacher_head, [(False, 0, width - quarter)], [order])
+    send, = packed(at, student_head, teacher_head, [(False, 0, half)], [order])
     late = [permuted(send, extra_late), None]
     order = pause(order, [])
     swapped[0], swapped[1], order = gate([swapped[0], swapped[1], order], [])
@@ -321,7 +351,7 @@
     swapped[2], swapped[3], order = gate([swapped[2], swapped[3], order], [total])
     mine1 = jnp.concatenate([crossed[2], crossed[3], swapped[2], swapped[3]], axis=0)
     theirs1 = permuted(mine1, other_core)
-    send, = packed(at, student_head, teacher_head, [(False, width - quarter, quarter)], [order])
+    send, = packed(at, student_head, teacher_head, [(False, half, half)], [order])
     late[1] = permuted(send, extra_late)
     order = pause(order, [mine1])
     theirs1, order = gate([theirs1, order], [])
@@ -338,10 +368,10 @@
     for k in range(2):
         order = pause(order, [last])
         late[k], order = gate([late[k], order], [])
-        lo, hi = (0, width - quarter) if k == 0 else (width - quarter, width)
-        value = jnp.where(from_late, late[k], early[lo:hi])
-        ids = extra_id * width + ids_in[lo:hi]
-        scores, loss, last = meet([value], [value], ids, loss, [jnp.bfloat16], [order])
+        ids = extra_id * width + k * half + ids_in[:half]
+        scores, loss, last, value = meet(
+            [late[k], early, k * half], None, ids, loss, [jnp.bfloat16], [order], from_late
+        )
         extra_parts.append(permuted(last, extra_back))
         extra_scores.append(scores)
         extras.append(value)
@@ -353,7 +383,7 @@
         [last],
     )
     head_grad = head_total(at, own_part, [back0, back1], extra_parts)
-    return (head_grad, rows_grad, loss[:, 0])
+    return (head_grad, rows_grad, loss[0])
 
 
 def solution(mesh):

time: 103 us -> 258 us (2.50)
  Pallas kernels: 31.8 us -> 196 us
  other arithmetic: 7.22 us -> 1.28 us
  waiting for transfers between devices: 15.4 us -> 9.63 us
  starting transfers between devices: 21.1 us -> 24.3 us
    pallas_call x4, Pallas kernels: 3.78 us -> 163 us  [packed(): pl.pallas_call(kernel, out_shape=[jax.ShapeDtypeStruct((rows, depth + dep...]
    ppermute x19, waiting for transfers between devices: 15.4 us -> 9.63 us  [permuted(): return lax.ppermute(value, BOTH, pairs)]
    ppermute x19, starting transfers between devices: 21.1 us -> 24.3 us  [permuted(): return lax.ppermute(value, BOTH, pairs)]
    unnamed x98 -> x74, local copies, waits for them, and re-layouts: 24.3 us -> 21.3 us
    select_n x2 -> x0, other arithmetic: 2.84 us -> none  [body(): value = jnp.where(from_late, late[k], early[lo:hi])]
    pallas_call x1, Pallas kernels: 5.32 us -> 7.94 us  [rows_product(): pl.pallas_call(kernel, grid=(7,), out_shape=jax.ShapeDtypeStruct((count,...]
  transfers between devices with their start and end apart: 19 -> 19, of which waited for: 7 -> 6; matrix products, arithmetic and copies ran while one was open for 8% -> 3% of each run, Pallas kernels for 27% -> 69%
where the time goes in v5:
time: 258 us; the launch traced here: 256 us
  Pallas kernels  196 us (76%)
  starting transfers between devices  24.3 us (9%)
  local copies, waits for them, and re-layouts  23.1 us (9%)
  waiting for transfers between devices  9.63 us (4%)
    pallas_call x4, Pallas kernels, packed(): pl.pallas_call(kernel, out_shape=[jax.ShapeDtypeStruct((rows, depth + dep...  163 us
    ppermute x19, starting transfers between devices, permuted(): return lax.ppermute(value, BOTH, pairs)  24.3 us
    pallas_call x5, Pallas kernels, meeting(): pl.pallas_call(kernel, out_shape=out_shape, in_specs=[whole] * (7 + piece...  23 us
    unnamed x74, local copies, waits for them, and re-layouts  21.3 us
    ppermute x19, waiting for transfers between devices, permuted(): return lax.ppermute(value, BOTH, pairs)  9.63 us
    pallas_call x1, Pallas kernels, rows_product(): pl.pallas_call(kernel, grid=(7,), out_shape=jax.ShapeDtypeStruct((count,...  7.94 us
  transfers between devices with their start and end apart: 19, of which 6 were waited for; matrix products, arithmetic and copies ran while one was open for 3% of the time, Pallas kernels for 69%

profile of v5, /device:TPU:0, one launch (start us, length us, event | category | flops | bytes accessed | tf_op | source)
XLA Modules:
  0.0 256.0 jit_solution(1408665839717410022)
XLA Ops:
  0.7 17.0 %shard_map.96 = (bf16[16,8192]{1,0:T(8,128)(2,1)}, bf16[16,8192]{1,0:T(8,128)(2,1)}) custom-call(s32[1]{0:T(128)} %bitcast.at_ref, bf16[128,3584]{1,0:T(8,128)(2,1)} %refs_5_.1, bf16[128,4608]{1,0:T(8,128)(2,1)} %teacher_ref.7), custom_call_target="tpu_custom_call" | custom-call | tf_op jit(solution)/shard_map/pallas_call | solution.py:95
  17.7 3.0 %collective-permute-start = (bf16[16,8192]{1,0:T(8,128)(2,1)}, bf16[16,8192]{1,0:T(8,128)(2,1)S(1)}, u32[]{:S(2)}, u32[]{:S(2)}) collective-permute-start(bf16[16,8192]{1,0:T(8,128)(2,1)} %get-tuple-element.59), channel_id=1, source_target_pairs={{0,2},{1,3},{2,4},{3,5},{4,6},{5,7},{6,8},{7,9},{8,10},{9,11},{10,... | collective-permute-start | bytes 786440 | tf_op jit(solution)/shard_map/ppermute | solution.py:24
  20.7 1.5 collective-permute-start.1
  22.3 80.6 %shard_map.94 = (bf16[16,8192]{1,0:T(8,128)(2,1)}, bf16[16,8192]{1,0:T(8,128)(2,1)}, bf16[128,8192]{1,0:T(8,128)(2,1)}) custom-call(s32[1]{0:T(128)} %bitcast.at_ref, bf16[128,3584]{1,0:T(8,128)(2,1)} %refs_5_.1, bf16[128,4608]{1,0:T(8,128)(2,1)} %teacher_ref.7), custom_call_target="tpu_custom_call" | custom-call | tf_op jit(solution)/shard_map/pallas_call | solution.py:95
  102.8 1.9 collective-permute-start.6
  105.6 2.3 copy-done
  108.0 2.0 copy-done.1
  111.0 3.6 %shard_map.95 = (bf16[512,128]{1,0:T(8,128)(2,1)S(1)}, f32[8,512]{1,0:T(8,128)S(1)}, f32[128,3584]{1,0:T(8,128)S(1)}) custom-call(bf16[512,3584]{1,0:T(8,128)(2,1)S(1)} %copy-done.1, bf16[512,4608]{1,0:T(8,128)(2,1)S(1)} %copy-done, f32[512,1]{1,0:T(8,128)S(1)} %copy.50.refs_2_, f32[512,1]{1,0:T(8,128)S(1)} %copy.51.refs_3_, s32[512,1]{1,0:T(8,128)S(1)} %copy.52.refs_4_, ...), custom_call_target="tpu_custom_call" | custom-call | tf_op jit(solution)/shard_map/pallas_call | solution.py:225
  114.6 1.2 copy-done.9
  116.0 2.1 collective-permute-start.4
  118.1 1.5 collective-permute-start.2
  122.6 4.8 %collective-permute-done.4.refs_0_ = bf16[16,8192]{1,0:T(8,128)(2,1)} collective-permute-done((bf16[16,8192]{1,0:T(8,128)(2,1)S(1)}, bf16[16,8192]{1,0:T(8,128)(2,1)}, u32[]{:S(2)}, u32[]{:S(2)}) %collective-permute-start.4) | collective-permute-done | bytes 262176 | tf_op jit(solution)/shard_map/ppermute | solution.py:24
  127.9 1.5 collective-permute-start.10
  129.4 32.9 %shard_map.118 = bf16[64,8192]{1,0:T(8,128)(2,1)} custom-call(s32[1]{0:T(128)} %bitcast.at_ref, bf16[128,3584]{1,0:T(8,128)(2,1)} %refs_5_.1, bf16[128,4608]{1,0:T(8,128)(2,1)} %teacher_ref.7, f32[8,128]{1,0:T(8,128)} %copy-done.11), custom_call_target="tpu_custom_call" | custom-call | tf_op jit(solution)/shard_map/pallas_call | solution.py:95
  163.3 1.7 collective-permute-start.15
  166.5 1.1 collective-permute-start.5
  168.3 1.1 copy-done.18
  170.6 1.5 copy-done.2
  172.2 5.1 %shard_map.109 = (bf16[512,128]{1,0:T(8,128)(2,1)S(1)}, f32[8,512]{1,0:T(8,128)S(1)}, f32[64,3584]{1,0:T(8,128)S(1)}, bf16[64,3584]{1,0:T(8,128)(2,1)S(1)}) custom-call(bf16[512,3584]{1,0:T(8,128)(2,1)S(1)} %copy-done.2, bf16[512,4608]{1,0:T(8,128)(2,1)S(1)} %bitcast.15, f32[512,1]{1,0:T(8,128)S(1)} %copy.50.refs_2_, f32[512,1]{1,0:T(8,128)S(1)} %copy.51.refs_3_, ...), custom_call_target="tpu_custom_call" | custom-call | tf_op jit(solution)/shard_map/pallas_call | solution.py:225
  178.0 1.2 collective-permute-done.8.refs_0_
  180.1 3.6 %collective-permute-start.9 = (bf16[64,3584]{1,0:T(8,128)(2,1)}, bf16[64,3584]{1,0:T(8,128)(2,1)}, u32[]{:S(2)}, u32[]{:S(2)}) collective-permute-start(bf16[64,3584]{1,0:T(8,128)(2,1)} %add_convert_fusion.1.refs_3_), channel_id=1, source_target_pairs={{0,14},{1,15},{2,0},{3,1},{4,2},{5,3},{6,4},{7,5},{8,6},{9,7},{10,... | collective-permute-start | bytes 1376264 | tf_op jit(solution)/shard_map/ppermute | solution.py:24
  184.3 32.9 %shard_map.122 = bf16[64,8192]{1,0:T(8,128)(2,1)} custom-call(s32[1]{0:T(128)} %bitcast.at_ref, bf16[128,3584]{1,0:T(8,128)(2,1)} %refs_5_.1, bf16[128,4608]{1,0:T(8,128)(2,1)} %teacher_ref.7, f32[8,128]{1,0:T(8,128)} %copy-done.13), custom_call_target="tpu_custom_call" | custom-call | tf_op jit(solution)/shard_map/pallas_call | solution.py:95
  218.3 1.5 copy-done.28
  219.8 1.0 collective-permute-start.17
  220.9 3.6 %shard_map.115 = (bf16[512,128]{1,0:T(8,128)(2,1)S(1)}, f32[8,512]{1,0:T(8,128)S(1)}, f32[64,3584]{1,0:T(8,128)S(1)}, bf16[64,3584]{1,0:T(8,128)(2,1)S(1)}) custom-call(bf16[512,3584]{1,0:T(8,128)(2,1)S(1)} %copy-done.3, bf16[512,4608]{1,0:T(8,128)(2,1)S(1)} %bitcast.15, f32[512,1]{1,0:T(8,128)S(1)} %copy.50.refs_2_, f32[512,1]{1,0:T(8,128)S(1)} %copy.51.refs_3_, ...), custom_call_target="tpu_custom_call" | custom-call | tf_op jit(solution)/shard_map/pallas_call | solution.py:225
  225.2 1.2 collective-permute-done.13.refs_0_
  226.6 5.5 %shard_map.121 = (bf16[512,64]{1,0:T(8,128)(2,1)S(1)}, f32[8,512]{1,0:T(8,128)S(1)}, bf16[64,3584]{1,0:T(8,128)(2,1)S(1)}, bf16[64,3584]{1,0:T(8,128)(2,1)S(1)}) custom-call(bf16[512,3584]{1,0:T(8,128)(2,1)S(1)} %copy-done.3, bf16[512,4608]{1,0:T(8,128)(2,1)S(1)} %bitcast.15, f32[512,1]{1,0:T(8,128)S(1)} %copy.50.refs_2_, f32[512,1]{1,0:T(8,128)S(1)} %copy.51.refs_3_, ...), custom_call_target="tpu_custom_call" | custom-call | tf_op jit(solution)/shard_map/pallas_call | solution.py:225
  233.1 2.8 %collective-permute-start.14 = (bf16[64,3584]{1,0:T(8,128)(2,1)S(1)}, bf16[64,3584]{1,0:T(8,128)(2,1)S(1)}, u32[]{:S(2)}, u32[]{:S(2)}) collective-permute-start(bf16[64,3584]{1,0:T(8,128)(2,1)S(1)} %add_convert_fusion.refs_1_), channel_id=1, source_target_pairs={{0,14},{1,15},{2,0},{3,1},{4,2},{5,3},{6,4},{7,5},{8,6},{9,7},{10,... | collective-permute-start | bytes 1376264 | tf_op jit(solution)/shard_map/ppermute | solution.py:24
  235.8 5.2 %shard_map.125 = (bf16[512,64]{1,0:T(8,128)(2,1)S(1)}, f32[8,512]{1,0:T(8,128)S(1)}, bf16[64,3584]{1,0:T(8,128)(2,1)S(1)}, bf16[64,3584]{1,0:T(8,128)(2,1)S(1)}) custom-call(bf16[512,3584]{1,0:T(8,128)(2,1)S(1)} %copy-done.3, bf16[512,4608]{1,0:T(8,128)(2,1)S(1)} %bitcast.15, f32[512,1]{1,0:T(8,128)S(1)} %copy.50.refs_2_, f32[512,1]{1,0:T(8,128)S(1)} %copy.51.refs_3_, ...), custom_call_target="tpu_custom_call" | custom-call | tf_op jit(solution)/shard_map/pallas_call | solution.py:225
  243.2 7.9 %shard_map.127 = bf16[512,3584]{1,0:T(8,128)(2,1)} custom-call(bf16[512,128]{1,0:T(8,128)(2,1)} %copy-done.23, bf16[512,128]{1,0:T(8,128)(2,1)} %copy-done.24, bf16[512,128]{1,0:T(8,128)(2,1)} %copy-done.25, bf16[512,64]{1,0:T(8,128)(2,1)} %copy-done.26, bf16[512,64]{1,0:T(8,128)(2,1)} %copy-done.27, bf16[128,3584]{1,0:T(8,128)(2,1)} %refs_5_.1, ...), custom_call_target="tpu_custom_call" | custom-call | flops 30000001024 | tf_op jit(solution)/shard_map/pallas_call | solution.py:256
  251.7 2.1 collective-permute-done.18.extra1
  253.8 2.0 shard_map.126
  (136 shorter events, 17.5 us)
Async XLA Ops:
  0.6 104.2 %copy-start.30 = (bf16[512]{0:T(512)(128)(2,1)S(1)}, bf16[512]{0:T(512)(128)(2,1)}, u32[]{:S(2)}) copy-start(bf16[512]{0:T(512)(128)(2,1)} %param.11) | copy-start | bytes 3076
  0.6 104.2 %copy-start.31 = (bf16[512]{0:T(512)(128)(2,1)S(1)}, bf16[512]{0:T(512)(128)(2,1)}, u32[]{:S(2)}) copy-start(bf16[512]{0:T(512)(128)(2,1)} %param.12) | copy-start | bytes 3076
  0.7 104.6 %copy-start.29 = (s32[512]{0:T(512)S(1)}, s32[512]{0:T(512)}, u32[]{:S(2)}) copy-start(s32[512]{0:T(512)} %param.13) | copy-start | bytes 6148
  0.7 105.0 %copy-start.4 = (bf16[128,4608]{1,0:T(8,128)(2,1)S(1)}, bf16[128,4608]{1,0:T(8,128)(2,1)}, u32[]{:S(2)}) copy-start(bf16[128,4608]{1,0:T(8,128)(2,1)} %teacher_ref.7) | copy-start | bytes 3538948
  0.7 105.0 %copy-start.5 = (bf16[128,3584]{1,0:T(8,128)(2,1)S(1)}, bf16[128,3584]{1,0:T(8,128)(2,1)}, u32[]{:S(2)}) copy-start(bf16[128,3584]{1,0:T(8,128)(2,1)} %refs_5_.1) | copy-start | bytes 2752516
  17.7 98.2 %collective-permute-start = (bf16[16,8192]{1,0:T(8,128)(2,1)}, bf16[16,8192]{1,0:T(8,128)(2,1)S(1)}, u32[]{:S(2)}, u32[]{:S(2)}) collective-permute-start(bf16[16,8192]{1,0:T(8,128)(2,1)} %get-tuple-element.59), channel_id=1, source_target_pairs={{0,2},{1,3},{2,4},{3,5},{4,6},{5,7},{6,8},{7,9},{8,10},{9,11},{10,... | collective-permute-start | bytes 786440 | tf_op jit(solution)/shard_map/ppermute | solution.py:24
  20.7 99.6 %collective-permute-start.1 = (bf16[16,8192]{1,0:T(8,128)(2,1)}, bf16[16,8192]{1,0:T(8,128)(2,1)S(1)}, u32[]{:S(2)}, u32[]{:S(2)}) collective-permute-start(bf16[16,8192]{1,0:T(8,128)(2,1)} %get-tuple-element.62), channel_id=1, source_target_pairs={{0,2},{1,3},{2,4},{3,5},{4,6},{5,7},{6,8},{7,9},{8,10},{9,11},{10,... | collective-permute-start | bytes 786440 | tf_op jit(solution)/shard_map/ppermute | solution.py:24
  102.8 67.2 %collective-permute-start.6 = (bf16[128,8192]{1,0:T(8,128)(2,1)}, bf16[128,8192]{1,0:T(8,128)(2,1)}, u32[]{:S(2)}, u32[]{:S(2)}) collective-permute-start(bf16[128,8192]{1,0:T(8,128)(2,1)} %get-tuple-element.72), channel_id=1, source_target_pairs={{0,1},{1,4},{2,3},{4,5},{5,8},{6,7},{8,9},{9,12},{10,11},{12,13},{... | collective-permute-start | bytes 6291464 | tf_op jit(solution)/shard_map/ppermute | solution.py:24
  116.0 11.4 %collective-permute-start.4 = (bf16[16,8192]{1,0:T(8,128)(2,1)S(1)}, bf16[16,8192]{1,0:T(8,128)(2,1)}, u32[]{:S(2)}, u32[]{:S(2)}) collective-permute-start(bf16[16,8192]{1,0:T(8,128)(2,1)S(1)} %get-tuple-element.65.refs_1_), channel_id=1, source_target_pairs={{0,2},{1,3},{2,4},{3,5},{4,6},{5,7},{6,8},{7,9},{8,10},{9,11},{10,... | collective-permute-start | bytes 786440 | tf_op jit(solution)/shard_map/ppermute | solution.py:24
  118.1 46.9 %collective-permute-start.2 = (bf16[16,8192]{1,0:T(8,128)(2,1)S(1)}, bf16[16,8192]{1,0:T(8,128)(2,1)S(1)}, u32[]{:S(2)}, u32[]{:S(2)}) collective-permute-start(bf16[16,8192]{1,0:T(8,128)(2,1)S(1)} %get-tuple-element.61), channel_id=1, source_target_pairs={{0,16},{1,17},{2,18},{3,19},{4,20},{5,21},{6,22},{7,23},{8,24},{9,... | collective-permute-start | bytes 786440 | tf_op jit(solution)/shard_map/ppermute | solution.py:24
  120.4 47.2 %collective-permute-start.7 = (bf16[16,8192]{1,0:T(8,128)(2,1)S(1)}, bf16[16,8192]{1,0:T(8,128)(2,1)S(1)}, u32[]{:S(2)}, u32[]{:S(2)}) collective-permute-start(bf16[16,8192]{1,0:T(8,128)(2,1)S(1)} %get-tuple-element.68.refs_1_), channel_id=1, source_target_pairs={{0,2},{1,3},{2,4},{3,5},{4,6},{5,7},{6,8},{7,9},{8,10},{9,11},{10,... | collective-permute-start | bytes 786440 | tf_op jit(solution)/shard_map/ppermute | solution.py:24
  121.3 42.0 %collective-permute-start.3 = (bf16[16,8192]{1,0:T(8,128)(2,1)S(1)}, bf16[16,8192]{1,0:T(8,128)(2,1)S(1)}, u32[]{:S(2)}, u32[]{:S(2)}) collective-permute-start(bf16[16,8192]{1,0:T(8,128)(2,1)S(1)} %get-tuple-element.66), channel_id=1, source_target_pairs={{0,16},{1,17},{2,18},{3,19},{4,20},{5,21},{6,22},{7,23},{8,24},{9,... | collective-permute-start | bytes 786440 | tf_op jit(solution)/shard_map/ppermute | solution.py:24
  127.9 34.4 %copy-start.12 = (f32[8,128]{1,0:T(8,128)S(1)}, f32[8,128]{1,0:T(8,128)}, u32[]{:S(2)}) copy-start(f32[8,128]{1,0:T(8,128)} %copy-done.11) | copy-start | bytes 12292
  127.9 55.8 %collective-permute-start.10 = (bf16[16,8192]{1,0:T(8,128)(2,1)}, bf16[16,8192]{1,0:T(8,128)(2,1)}, u32[]{:S(2)}, u32[]{:S(2)}) collective-permute-start(bf16[16,8192]{1,0:T(8,128)(2,1)} %get-tuple-element.81), channel_id=1, source_target_pairs={{0,16},{1,17},{2,18},{3,19},{4,20},{5,21},{6,22},{7,23},{8,24},{9,... | collective-permute-start | bytes 786440 | tf_op jit(solution)/shard_map/ppermute | solution.py:24
  163.3 63.2 %collective-permute-start.15 = (bf16[64,8192]{1,0:T(8,128)(2,1)}, bf16[64,8192]{1,0:T(8,128)(2,1)}, u32[]{:S(2)}, u32[]{:S(2)}) collective-permute-start(bf16[64,8192]{1,0:T(8,128)(2,1)} %shard_map.118), channel_id=1, source_target_pairs={{3,6},{7,10},{11,14},{15,2},{19,22},{23,26},{27,30},{31,18}} | collective-permute-start | bytes 3145736 | tf_op jit(solution)/shard_map/ppermute | solution.py:24
  166.5 3.6 %collective-permute-start.5 = (bf16[64,8192]{1,0:T(8,128)(2,1)}, bf16[64,8192]{1,0:T(8,128)(2,1)S(1)}, u32[]{:S(2)}, u32[]{:S(2)}) collective-permute-start(bf16[64,8192]{1,0:T(8,128)(2,1)} %constant_dynamic-update-slice_fusion.refs_1_.refs_7_.refs_9_.refs_6_), channel_id=1, source_target_pairs={{0,1},{1,0},{2,3},{3,2},{4,5},{5,4},{6,7},{7,6},{8,9},{9,8},{10,11... | collective-permute-start | bytes 3145736 | tf_op jit(solution)/shard_map/ppermute | solution.py:24
  168.3 3.9 %copy-start.2 = (bf16[512,3584]{1,0:T(8,128)(2,1)S(1)}, bf16[512,3584]{1,0:T(8,128)(2,1)}, u32[]{:S(2)}) copy-start(bf16[512,3584]{1,0:T(8,128)(2,1)} %refs_0_.9) | copy-start | bytes 11010052
  169.3 14.3 %collective-permute-start.11 = (bf16[16,8192]{1,0:T(8,128)(2,1)S(1)}, bf16[16,8192]{1,0:T(8,128)(2,1)S(1)}, u32[]{:S(2)}, u32[]{:S(2)}) collective-permute-start(bf16[16,8192]{1,0:T(8,128)(2,1)S(1)} %copy-done.18), channel_id=1, source_target_pairs={{0,16},{1,17},{2,18},{3,19},{4,20},{5,21},{6,22},{7,23},{8,24},{9,... | collective-permute-start | bytes 786440 | tf_op jit(solution)/shard_map/ppermute | solution.py:24
  170.0 7.3 %copy-start.6 = (bf16[64,8192]{1,0:T(8,128)(2,1)}, bf16[64,8192]{1,0:T(8,128)(2,1)S(1)}, u32[]{:S(2)}) copy-start(bf16[64,8192]{1,0:T(8,128)(2,1)S(1)} %get-tuple-element.75.refs_8_.refs_10_.refs_7_) | copy-start | bytes 3145732
  177.3 1.9 collective-permute-start.8
  180.1 71.7 %collective-permute-start.9 = (bf16[64,3584]{1,0:T(8,128)(2,1)}, bf16[64,3584]{1,0:T(8,128)(2,1)}, u32[]{:S(2)}, u32[]{:S(2)}) collective-permute-start(bf16[64,3584]{1,0:T(8,128)(2,1)} %add_convert_fusion.1.refs_3_), channel_id=1, source_target_pairs={{0,14},{1,15},{2,0},{3,1},{4,2},{5,3},{6,4},{7,5},{8,6},{9,7},{10,... | collective-permute-start | bytes 1376264 | tf_op jit(solution)/shard_map/ppermute | solution.py:24
  184.3 34.0 %copy-start.14 = (f32[8,128]{1,0:T(8,128)S(1)}, f32[8,128]{1,0:T(8,128)}, u32[]{:S(2)}) copy-start(f32[8,128]{1,0:T(8,128)} %copy-done.13) | copy-start | bytes 12292
  218.2 2.8 %copy-start.8 = (bf16[64,8192]{1,0:T(8,128)(2,1)}, bf16[64,8192]{1,0:T(8,128)(2,1)S(1)}, u32[]{:S(2)}) copy-start(bf16[64,8192]{1,0:T(8,128)(2,1)S(1)} %constant_dynamic-update-slice_fusion.4.refs_1_.refs_7_.refs_9_.refs_8_) | copy-start | bytes 3145732
  218.2 2.7 %collective-permute-start.12 = (bf16[64,8192]{1,0:T(8,128)(2,1)S(1)}, bf16[64,8192]{1,0:T(8,128)(2,1)S(1)}, u32[]{:S(2)}, u32[]{:S(2)}) collective-permute-start(bf16[64,8192]{1,0:T(8,128)(2,1)S(1)} %constant_dynamic-update-slice_fusion.4.refs_1_.refs_7_.refs_9_.refs_8_), channel_id=1, source_target_pairs={{0,1},{1,0},{2,3},{3,2},{4,5},{5,4},{6,7},{7,6},{8,9},{9,8},{10,11... | collective-permute-start | bytes 3145736 | tf_op jit(solution)/shard_map/ppermute | solution.py:24
  218.3 2.6 %copy-start.3 = (bf16[512,3584]{1,0:T(8,128)(2,1)S(1)}, bf16[512,3584]{1,0:T(8,128)(2,1)}, u32[]{:S(2)}) copy-start(bf16[512,3584]{1,0:T(8,128)(2,1)} %refs_0_.9) | copy-start | bytes 11010052
  219.8 16.0 %collective-permute-start.17 = (bf16[64,8192]{1,0:T(8,128)(2,1)S(1)}, bf16[64,8192]{1,0:T(8,128)(2,1)S(1)}, u32[]{:S(2)}, u32[]{:S(2)}) collective-permute-start(bf16[64,8192]{1,0:T(8,128)(2,1)S(1)} %copy-done.28), channel_id=1, source_target_pairs={{3,6},{7,10},{11,14},{15,2},{19,22},{23,26},{27,30},{31,18}} | collective-permute-start | bytes 3145736 | tf_op jit(solution)/shard_map/ppermute | solution.py:24
  220.9 3.6 %copy-start.7 = (bf16[64,8192]{1,0:T(8,128)(2,1)}, bf16[64,8192]{1,0:T(8,128)(2,1)S(1)}, u32[]{:S(2)}) copy-start(bf16[64,8192]{1,0:T(8,128)(2,1)S(1)} %get-tuple-element.87.refs_8_.refs_10_.refs_9_) | copy-start | bytes 3145732
  224.6 1.9 collective-permute-start.13
  232.9 20.9 %collective-permute-start.16 = (bf16[64,3584]{1,0:T(8,128)(2,1)S(1)}, bf16[64,3584]{1,0:T(8,128)(2,1)S(1)}, u32[]{:S(2)}, u32[]{:S(2)}) collective-permute-start(bf16[64,3584]{1,0:T(8,128)(2,1)S(1)} %get-tuple-element.97.refs_1_), channel_id=1, source_target_pairs={{0,13},{1,0},{2,15},{3,2},{4,1},{5,4},{6,3},{7,6},{8,5},{9,8},{10,... | collective-permute-start | bytes 1376264 | tf_op jit(solution)/shard_map/ppermute | solution.py:24
  233.1 20.8 %collective-permute-start.14 = (bf16[64,3584]{1,0:T(8,128)(2,1)S(1)}, bf16[64,3584]{1,0:T(8,128)(2,1)S(1)}, u32[]{:S(2)}, u32[]{:S(2)}) collective-permute-start(bf16[64,3584]{1,0:T(8,128)(2,1)S(1)} %add_convert_fusion.refs_1_), channel_id=1, source_target_pairs={{0,14},{1,15},{2,0},{3,1},{4,2},{5,3},{6,4},{7,5},{8,6},{9,7},{10,... | collective-permute-start | bytes 1376264 | tf_op jit(solution)/shard_map/ppermute | solution.py:24
  242.4 11.4 %collective-permute-start.18 = (bf16[64,3584]{1,0:T(8,128)(2,1)S(1)}, bf16[64,3584]{1,0:T(8,128)(2,1)S(1)}, u32[]{:S(2)}, u32[]{:S(2)}) collective-permute-start(bf16[64,3584]{1,0:T(8,128)(2,1)S(1)} %get-tuple-element.101.refs_12_), channel_id=1, source_target_pairs={{0,13},{1,0},{2,15},{3,2},{4,1},{5,4},{6,3},{7,6},{8,5},{9,8},{10,... | collective-permute-start | bytes 1376264 | tf_op jit(solution)/shard_map/ppermute | solution.py:24
  243.2 10.6 %copy-start.10 = (f32[128,3584]{1,0:T(8,128)S(1)}, f32[128,3584]{1,0:T(8,128)}, u32[]{:S(2)}) copy-start(f32[128,3584]{1,0:T(8,128)} %copy-done.9) | copy-start | bytes 5505028
  (21 other events, 25.8 us)

commit v6 on v5

--- a/solution.py
+++ b/solution.py
@@ -102,7 +102,7 @@
         + [anywhere] * len(ready),
         out_specs=[anywhere] * len(places),
         scratch_shapes=[pltpu.SemaphoreType.DMA((2 * len(places),))],
-        compiler_params=pltpu.CompilerParams(vmem_limit_bytes=WIDE_VMEM),
+        compiler_params=pltpu.CompilerParams(vmem_limit_bytes=GATE_VMEM),
     )(at, student_head, teacher_head, *ready)
 
 
@@ -302,9 +302,11 @@
         at,
         student_head,
         teacher_head,
-        [(True, k * piece, piece) for k in range(2, 4)] + [(False, 0, width)],
+        [(True, k * piece, piece) for k in range(2, 4)]
+        + [(False, 0, width), (False, 0, half), (False, half, half)],
     )
-    send = chunks.pop()
+    send, send0, send1 = chunks[4:]
+    chunks = chunks[:4]
 
     crossed = [permuted(chunks[0], next_chip), permuted(chunks[1], next_chip), None, None]
     early = permuted(send, extra_early)
@@ -326,11 +328,10 @@
     swapped[1] = permuted(crossed[1], other_plane)
     crossed[3] = permuted(chunks[3], next_chip)
     order = pause(order, [chunks[3]])
-    crossed[2], order = gate([crossed[2], order], [])
+    crossed[2], send0, order = gate([crossed[2], send0, order], [])
     swapped[2] = permuted(crossed[2], other_plane)
-    send, = packed(at, student_head, teacher_head, [(False, 0, half)], [order])
-    late = [permuted(send, extra_late), None]
-    order = pause(order, [])
+    late = [permuted(send0, extra_late), None]
+    order = pause(order, [crossed[2], send0])
     swapped[0], swapped[1], order = gate([swapped[0], swapped[1], order], [])
     mine0 = jnp.concatenate([crossed[0], crossed[1], swapped[0], swapped[1]], axis=0)
     theirs0 = permuted(mine0, other_core)
@@ -351,8 +352,8 @@
     swapped[2], swapped[3], order = gate([swapped[2], swapped[3], order], [total])
     mine1 = jnp.concatenate([crossed[2], crossed[3], swapped[2], swapped[3]], axis=0)
     theirs1 = permuted(mine1, other_core)
-    send, = packed(at, student_head, teacher_head, [(False, half, half)], [order])
-    late[1] = permuted(send, extra_late)
+    send1, order = gate([send1, order], [])
+    late[1] = permuted(send1, extra_late)
     order = pause(order, [mine1])
     theirs1, order = gate([theirs1, order], [])
     pair = [mine1, theirs1]

time: 258 us -> 97.3 us (0.38)
  Pallas kernels: 196 us -> 34.4 us
  waiting for transfers between devices: 9.63 us -> 17.3 us
  local copies, waits for them, and re-layouts: 23.1 us -> 16.9 us
    pallas_call x4 -> x2, Pallas kernels: 163 us -> 2.91 us  [packed(): pl.pallas_call(kernel, out_shape=[jax.ShapeDtypeStruct((rows, depth + dep...]
    ppermute x19, waiting for transfers between devices: 9.63 us -> 17.3 us  [permuted(): return lax.ppermute(value, BOTH, pairs)]
    unnamed x74 -> x66, local copies, waits for them, and re-layouts: 21.3 us -> 15.9 us
  transfers between devices with their start and end apart: 19 -> 19, of which waited for: 6 -> 7; matrix products, arithmetic and copies ran while one was open for 3% -> 4% of each run, Pallas kernels for 69% -> 33%
where the time goes in v6:
time: 97.3 us; the launch traced here: 96.8 us
  Pallas kernels  34.4 us (35%)
  starting transfers between devices  25.3 us (26%)
  waiting for transfers between devices  17.3 us (18%)
  local copies, waits for them, and re-layouts  16.9 us (17%)
  between operations  1.45 us (1%)
  other arithmetic  1.28 us (1%)
    ppermute x19, starting transfers between devices, permuted(): return lax.ppermute(value, BOTH, pairs)  25.3 us
    pallas_call x5, Pallas kernels, meeting(): pl.pallas_call(kernel, out_shape=out_shape, in_specs=[whole] * (7 + piece...  21.5 us
    ppermute x19, waiting for transfers between devices, permuted(): return lax.ppermute(value, BOTH, pairs)  17.3 us
    unnamed x66, local copies, waits for them, and re-layouts  15.9 us
    pallas_call x1, Pallas kernels, rows_product(): pl.pallas_call(kernel, grid=(7,), out_shape=jax.ShapeDtypeStruct((count,...  7.94 us
    pallas_call x2, Pallas kernels, packed(): pl.pallas_call(kernel, out_shape=[jax.ShapeDtypeStruct((rows, depth + dep...  2.91 us
    pallas_call x1, Pallas kernels, head_total(): pl.pallas_call(kernel, out_shape=jax.ShapeDtypeStruct((width, depth), jnp...  2.05 us
  transfers between devices with their start and end apart: 19, of which 7 were waited for; matrix products, arithmetic and copies ran while one was open for 4% of the time, Pallas kernels for 33%

profile of v6, /device:TPU:0, one launch (start us, length us, event | category | flops | bytes accessed | tf_op | source)
XLA Modules:
  0.0 96.8 jit_solution(7759909663195273010)
XLA Ops:
  0.6 1.3 %copy-done.3 = bf16[128,4608]{1,0:T(8,128)(2,1)S(1)} copy-done((bf16[128,4608]{1,0:T(8,128)(2,1)S(1)}, bf16[128,4608]{1,0:T(8,128)(2,1)}, u32[]{:S(2)}) %copy-start.3) | copy-done | bytes 1179672
  1.9 1.2 %copy-done.7 = bf16[128,3584]{1,0:T(8,128)(2,1)S(1)} copy-done((bf16[128,3584]{1,0:T(8,128)(2,1)S(1)}, bf16[128,3584]{1,0:T(8,128)(2,1)}, u32[]{:S(2)}) %copy-start.7) | copy-done | bytes 917528
  3.9 3.0 %collective-permute-start = (bf16[16,8192]{1,0:T(8,128)(2,1)}, bf16[16,8192]{1,0:T(8,128)(2,1)}, u32[]{:S(2)}, u32[]{:S(2)}) collective-permute-start(bf16[16,8192]{1,0:T(8,128)(2,1)} %get-tuple-element.64), channel_id=1, source_target_pairs={{0,2},{1,3},{2,4},{3,5},{4,6},{5,7},{6,8},{7,9},{8,10},{9,11},{10,... | collective-permute-start | bytes 786440 | tf_op jit(solution)/shard_map/ppermute | solution.py:24
  6.9 1.5 %collective-permute-start.1 = (bf16[16,8192]{1,0:T(8,128)(2,1)}, bf16[16,8192]{1,0:T(8,128)(2,1)S(1)}, u32[]{:S(2)}, u32[]{:S(2)}) collective-permute-start(bf16[16,8192]{1,0:T(8,128)(2,1)} %get-tuple-element.67), channel_id=1, source_target_pairs={{0,2},{1,3},{2,4},{3,5},{4,6},{5,7},{6,8},{7,9},{8,10},{9,11},{10,... | collective-permute-start | bytes 786440 | tf_op jit(solution)/shard_map/ppermute | solution.py:24
  8.5 2.1 %shard_map.94 = (bf16[16,8192]{1,0:T(8,128)(2,1)S(1)}, bf16[16,8192]{1,0:T(8,128)(2,1)S(1)}, bf16[128,8192]{1,0:T(8,128)(2,1)}, bf16[64,8192]{1,0:T(8,128)(2,1)}, bf16[64,8192]{1,0:T(8,128)(2,1)S(1)}) custom-call(s32[1]{0:T(128)} %bitcast.at_ref, bf16[128,3584]{1,0:T(8,128)(2,1)S(1)} %copy-done.8, bf16[128,4608]{1,0:T(8,128)(2,1)S(1)} %copy-done.4), custom_call_target="tpu_custom_call" | custom-call | tf_op jit(solution)/shard_map/pallas_call | solution.py:95
  12.3 1.9 %collective-permute-start.6 = (bf16[128,8192]{1,0:T(8,128)(2,1)}, bf16[128,8192]{1,0:T(8,128)(2,1)}, u32[]{:S(2)}, u32[]{:S(2)}) collective-permute-start(bf16[128,8192]{1,0:T(8,128)(2,1)} %get-tuple-element.80), channel_id=1, source_target_pairs={{0,1},{1,4},{2,3},{4,5},{5,8},{6,7},{8,9},{9,12},{10,11},{12,13},{... | collective-permute-start | bytes 6291464 | tf_op jit(solution)/shard_map/ppermute | solution.py:24
  14.8 2.3 %copy-done = bf16[512,4608]{1,0:T(8,128)(2,1)S(1)} copy-done((bf16[512,4608]{1,0:T(8,128)(2,1)S(1)}, bf16[512,4608]{1,0:T(8,128)(2,1)}, u32[]{:S(2)}) %copy-start) | copy-done | bytes 4718616
  17.2 2.0 %copy-done.1 = bf16[512,3584]{1,0:T(8,128)(2,1)S(1)} copy-done((bf16[512,3584]{1,0:T(8,128)(2,1)S(1)}, bf16[512,3584]{1,0:T(8,128)(2,1)}, u32[]{:S(2)}) %copy-start.1) | copy-done | bytes 3670040
  19.2 3.6 %shard_map.95 = (bf16[512,128]{1,0:T(8,128)(2,1)S(1)}, f32[8,512]{1,0:T(8,128)S(1)}, f32[128,3584]{1,0:T(8,128)S(1)}) custom-call(bf16[512,3584]{1,0:T(8,128)(2,1)S(1)} %copy-done.1, bf16[512,4608]{1,0:T(8,128)(2,1)S(1)} %copy-done, f32[512,1]{1,0:T(8,128)S(1)} %copy.53.refs_2_, f32[512,1]{1,0:T(8,128)S(1)} %copy.54.refs_3_, s32[512,1]{1,0:T(8,128)S(1)} %copy.55.refs_4_, ...), custom_call_target="tpu_custom_call" | custom-call | tf_op jit(solution)/shard_map/pallas_call | solution.py:225
  22.8 1.2 %copy-done.11 = f32[128,3584]{1,0:T(8,128)} copy-done((f32[128,3584]{1,0:T(8,128)}, f32[128,3584]{1,0:T(8,128)S(1)}, u32[]{:S(2)}) %copy-start.11) | copy-done | bytes 1835032
  24.4 2.2 %collective-permute-start.4 = (bf16[16,8192]{1,0:T(8,128)(2,1)S(1)}, bf16[16,8192]{1,0:T(8,128)(2,1)S(1)}, u32[]{:S(2)}, u32[]{:S(2)}) collective-permute-start(bf16[16,8192]{1,0:T(8,128)(2,1)S(1)} %get-tuple-element.70.refs_1_), channel_id=1, source_target_pairs={{0,2},{1,3},{2,4},{3,5},{4,6},{5,7},{6,8},{7,9},{8,10},{9,11},{10,... | collective-permute-start | bytes 786440 | tf_op jit(solution)/shard_map/ppermute | solution.py:24
  26.6 1.5 %collective-permute-start.2 = (bf16[16,8192]{1,0:T(8,128)(2,1)}, bf16[16,8192]{1,0:T(8,128)(2,1)S(1)}, u32[]{:S(2)}, u32[]{:S(2)}) collective-permute-start(bf16[16,8192]{1,0:T(8,128)(2,1)} %get-tuple-element.66), channel_id=1, source_target_pairs={{0,16},{1,17},{2,18},{3,19},{4,20},{5,21},{6,22},{7,23},{8,24},{9,... | collective-permute-start | bytes 786440 | tf_op jit(solution)/shard_map/ppermute | solution.py:24
  28.1 1.0 %constant_dynamic-update-slice_fusion.3 = bf16[64,8192]{1,0:T(8,128)(2,1)S(1)} fusion(bf16[16,8192]{1,0:T(8,128)(2,1)} %get-tuple-element.66), kind=kLoop, calls=%fused_computation.5 | loop fusion | bytes 524288
  29.2 1.0 %collective-permute-start.7 = (bf16[16,8192]{1,0:T(8,128)(2,1)S(1)}, bf16[16,8192]{1,0:T(8,128)(2,1)S(1)}, u32[]{:S(2)}, u32[]{:S(2)}) collective-permute-start(bf16[16,8192]{1,0:T(8,128)(2,1)S(1)} %get-tuple-element.74.refs_1_), channel_id=1, source_target_pairs={{0,2},{1,3},{2,4},{3,5},{4,6},{5,7},{6,8},{7,9},{8,10},{9,11},{10,... | collective-permute-start | bytes 786440 | tf_op jit(solution)/shard_map/ppermute | solution.py:24
  30.7 5.0 %collective-permute-done.4.refs_0_ = bf16[16,8192]{1,0:T(8,128)(2,1)S(1)} collective-permute-done((bf16[16,8192]{1,0:T(8,128)(2,1)S(1)}, bf16[16,8192]{1,0:T(8,128)(2,1)S(1)}, u32[]{:S(2)}, u32[]{:S(2)}) %collective-permute-start.4) | collective-permute-done | bytes 262176 | tf_op jit(solution)/shard_map/ppermute | solution.py:24
  35.7 1.5 %collective-permute-start.10 = (bf16[16,8192]{1,0:T(8,128)(2,1)S(1)}, bf16[16,8192]{1,0:T(8,128)(2,1)S(1)}, u32[]{:S(2)}, u32[]{:S(2)}) collective-permute-start(bf16[16,8192]{1,0:T(8,128)(2,1)S(1)} %get-tuple-element.76.refs_1_), channel_id=1, source_target_pairs={{0,16},{1,17},{2,18},{3,19},{4,20},{5,21},{6,22},{7,23},{8,24},{9,... | collective-permute-start | bytes 786440 | tf_op jit(solution)/shard_map/ppermute | solution.py:24
  37.2 3.6 %collective-permute-done.3.refs_1_ = bf16[16,8192]{1,0:T(8,128)(2,1)S(1)} collective-permute-done((bf16[16,8192]{1,0:T(8,128)(2,1)S(1)}, bf16[16,8192]{1,0:T(8,128)(2,1)S(1)}, u32[]{:S(2)}, u32[]{:S(2)}) %collective-permute-start.3) | collective-permute-done | bytes 262176 | tf_op jit(solution)/shard_map/ppermute | solution.py:24
  40.8 1.6 %collective-permute-start.15 = (bf16[64,8192]{1,0:T(8,128)(2,1)}, bf16[64,8192]{1,0:T(8,128)(2,1)}, u32[]{:S(2)}, u32[]{:S(2)}) collective-permute-start(bf16[64,8192]{1,0:T(8,128)(2,1)} %get-tuple-element.77.refs_2_), channel_id=1, source_target_pairs={{3,6},{7,10},{11,14},{15,2},{19,22},{23,26},{27,30},{31,18}} | collective-permute-start | bytes 3145736 | tf_op jit(solution)/shard_map/ppermute | solution.py:24
  42.7 1.6 %collective-permute-start.11 = (bf16[16,8192]{1,0:T(8,128)(2,1)S(1)}, bf16[16,8192]{1,0:T(8,128)(2,1)S(1)}, u32[]{:S(2)}, u32[]{:S(2)}) collective-permute-start(bf16[16,8192]{1,0:T(8,128)(2,1)S(1)} %get-tuple-element.89), channel_id=1, source_target_pairs={{0,16},{1,17},{2,18},{3,19},{4,20},{5,21},{6,22},{7,23},{8,24},{9,... | collective-permute-start | bytes 786440 | tf_op jit(solution)/shard_map/ppermute | solution.py:24
  45.3 1.3 %copy-done.2 = bf16[512,3584]{1,0:T(8,128)(2,1)S(1)} copy-done((bf16[512,3584]{1,0:T(8,128)(2,1)S(1)}, bf16[512,3584]{1,0:T(8,128)(2,1)}, u32[]{:S(2)}) %copy-start.2) | copy-done | bytes 3670040
  46.6 3.6 %shard_map.109 = (bf16[512,128]{1,0:T(8,128)(2,1)S(1)}, f32[8,512]{1,0:T(8,128)S(1)}, f32[64,3584]{1,0:T(8,128)S(1)}, bf16[64,3584]{1,0:T(8,128)(2,1)S(1)}) custom-call(bf16[512,3584]{1,0:T(8,128)(2,1)S(1)} %copy-done.2, bf16[512,4608]{1,0:T(8,128)(2,1)S(1)} %bitcast.15, f32[512,1]{1,0:T(8,128)S(1)} %copy.53.refs_2_, f32[512,1]{1,0:T(8,128)S(1)} %copy.54.refs_3_, ...), custom_call_target="tpu_custom_call" | custom-call | tf_op jit(solution)/shard_map/pallas_call | solution.py:225
  50.9 1.2 %collective-permute-done.8.refs_0_ = bf16[64,3584]{1,0:T(8,128)(2,1)S(1)} collective-permute-done((bf16[64,3584]{1,0:T(8,128)(2,1)S(1)}, bf16[64,3584]{1,0:T(8,128)(2,1)S(1)}, u32[]{:S(2)}, u32[]{:S(2)}) %collective-permute-start.8) | collective-permute-done | bytes 458784 | tf_op jit(solution)/shard_map/ppermute | solution.py:24
  53.0 5.9 %collective-permute-start.9 = (bf16[64,3584]{1,0:T(8,128)(2,1)}, bf16[64,3584]{1,0:T(8,128)(2,1)}, u32[]{:S(2)}, u32[]{:S(2)}) collective-permute-start(bf16[64,3584]{1,0:T(8,128)(2,1)} %add_convert_fusion.1.refs_3_), channel_id=1, source_target_pairs={{0,14},{1,15},{2,0},{3,1},{4,2},{5,3},{6,4},{7,5},{8,6},{9,7},{10,... | collective-permute-start | bytes 1376264 | tf_op jit(solution)/shard_map/ppermute | solution.py:24
  59.9 1.7 %collective-permute-done.12.refs_0_ = bf16[64,8192]{1,0:T(8,128)(2,1)S(1)} collective-permute-done((bf16[64,8192]{1,0:T(8,128)(2,1)S(1)}, bf16[64,8192]{1,0:T(8,128)(2,1)S(1)}, u32[]{:S(2)}, u32[]{:S(2)}) %collective-permute-start.12) | collective-permute-done | bytes 1048608 | tf_op jit(solution)/shard_map/ppermute | solution.py:24
  61.6 3.6 %shard_map.116 = (bf16[512,128]{1,0:T(8,128)(2,1)S(1)}, f32[8,512]{1,0:T(8,128)S(1)}, f32[64,3584]{1,0:T(8,128)S(1)}, bf16[64,3584]{1,0:T(8,128)(2,1)S(1)}) custom-call(bf16[512,3584]{1,0:T(8,128)(2,1)S(1)} %copy-done.2, bf16[512,4608]{1,0:T(8,128)(2,1)S(1)} %bitcast.15, f32[512,1]{1,0:T(8,128)S(1)} %copy.53.refs_2_, f32[512,1]{1,0:T(8,128)S(1)} %copy.54.refs_3_, ...), custom_call_target="tpu_custom_call" | custom-call | tf_op jit(solution)/shard_map/pallas_call | solution.py:225
  65.9 1.2 %collective-permute-done.13.refs_0_ = bf16[64,3584]{1,0:T(8,128)(2,1)S(1)} collective-permute-done((bf16[64,3584]{1,0:T(8,128)(2,1)S(1)}, bf16[64,3584]{1,0:T(8,128)(2,1)S(1)}, u32[]{:S(2)}, u32[]{:S(2)}) %collective-permute-start.13) | collective-permute-done | bytes 458784 | tf_op jit(solution)/shard_map/ppermute | solution.py:24
  67.3 5.5 %shard_map.121 = (bf16[512,64]{1,0:T(8,128)(2,1)S(1)}, f32[8,512]{1,0:T(8,128)S(1)}, bf16[64,3584]{1,0:T(8,128)(2,1)S(1)}, bf16[64,3584]{1,0:T(8,128)(2,1)S(1)}) custom-call(bf16[512,3584]{1,0:T(8,128)(2,1)S(1)} %copy-done.2, bf16[512,4608]{1,0:T(8,128)(2,1)S(1)} %bitcast.15, f32[512,1]{1,0:T(8,128)S(1)} %copy.53.refs_2_, f32[512,1]{1,0:T(8,128)S(1)} %copy.54.refs_3_, ...), custom_call_target="tpu_custom_call" | custom-call | tf_op jit(solution)/shard_map/pallas_call | solution.py:225
  73.8 1.3 %collective-permute-start.14 = (bf16[64,3584]{1,0:T(8,128)(2,1)S(1)}, bf16[64,3584]{1,0:T(8,128)(2,1)S(1)}, u32[]{:S(2)}, u32[]{:S(2)}) collective-permute-start(bf16[64,3584]{1,0:T(8,128)(2,1)S(1)} %add_convert_fusion.refs_1_), channel_id=1, source_target_pairs={{0,14},{1,15},{2,0},{3,1},{4,2},{5,3},{6,4},{7,5},{8,6},{9,7},{10,... | collective-permute-start | bytes 1376264 | tf_op jit(solution)/shard_map/ppermute | solution.py:24
  75.1 5.2 %shard_map.124 = (bf16[512,64]{1,0:T(8,128)(2,1)S(1)}, f32[8,512]{1,0:T(8,128)S(1)}, bf16[64,3584]{1,0:T(8,128)(2,1)S(1)}, bf16[64,3584]{1,0:T(8,128)(2,1)S(1)}) custom-call(bf16[512,3584]{1,0:T(8,128)(2,1)S(1)} %copy-done.2, bf16[512,4608]{1,0:T(8,128)(2,1)S(1)} %bitcast.15, f32[512,1]{1,0:T(8,128)S(1)} %copy.53.refs_2_, f32[512,1]{1,0:T(8,128)S(1)} %copy.54.refs_3_, ...), custom_call_target="tpu_custom_call" | custom-call | tf_op jit(solution)/shard_map/pallas_call | solution.py:225
  82.5 7.9 %shard_map.126 = bf16[512,3584]{1,0:T(8,128)(2,1)} custom-call(bf16[512,128]{1,0:T(8,128)(2,1)} %copy-done.20, bf16[512,128]{1,0:T(8,128)(2,1)} %copy-done.21, bf16[512,128]{1,0:T(8,128)(2,1)} %copy-done.22, bf16[512,64]{1,0:T(8,128)(2,1)} %copy-done.23, bf16[512,64]{1,0:T(8,128)(2,1)} %copy-done.24, bf16[128,3584]{1,0:T(8,128)(2,1)} %refs_5_.1, ...), custom_call_target="tpu_custom_call" | custom-call | flops 30000001024 | tf_op jit(solution)/shard_map/pallas_call | solution.py:256
  91.0 3.5 %collective-permute-done.18.extra1 = bf16[64,3584]{1,0:T(8,128)(2,1)S(1)} collective-permute-done((bf16[64,3584]{1,0:T(8,128)(2,1)S(1)}, bf16[64,3584]{1,0:T(8,128)(2,1)S(1)}, u32[]{:S(2)}, u32[]{:S(2)}) %collective-permute-start.18) | collective-permute-done | bytes 458784 | tf_op jit(solution)/shard_map/ppermute | solution.py:24
  94.6 2.0 %shard_map.125 = bf16[128,3584]{1,0:T(8,128)(2,1)} custom-call(s32[1]{0:T(128)} %bitcast.at_ref, f32[128,3584]{1,0:T(8,128)S(1)} %copy-done.12, bf16[64,3584]{1,0:T(8,128)(2,1)} %collective-permute-done.9.back0, bf16[64,3584]{1,0:T(8,128)(2,1)S(1)} %collective-permute-done.14.back1, bf16[64,3584]{1,0:T(8,128)(2,1)S(1)} %collective-permute-done.16.extra0, ...), custom_call_target="tpu_custom_call" | custom-call | tf_op jit(solution)/shard_map/pallas_call | solution.py:139
  (127 shorter events, 12.1 us)
Async XLA Ops:
  3.1 5.4 %copy-start.4 = (bf16[128,4608]{1,0:T(8,128)(2,1)S(1)}, bf16[128,4608]{1,0:T(8,128)(2,1)}, u32[]{:S(2)}) copy-start(bf16[128,4608]{1,0:T(8,128)(2,1)} %teacher_ref.3) | copy-start | bytes 3538948
  3.1 5.4 %copy-start.8 = (bf16[128,3584]{1,0:T(8,128)(2,1)S(1)}, bf16[128,3584]{1,0:T(8,128)(2,1)}, u32[]{:S(2)}) copy-start(bf16[128,3584]{1,0:T(8,128)(2,1)} %refs_5_.1) | copy-start | bytes 2752516
  3.1 11.2 %copy-start.26 = (bf16[512]{0:T(512)(128)(2,1)S(1)}, bf16[512]{0:T(512)(128)(2,1)}, u32[]{:S(2)}) copy-start(bf16[512]{0:T(512)(128)(2,1)} %param.11) | copy-start | bytes 3076
  3.1 11.4 %copy-start.27 = (bf16[512]{0:T(512)(128)(2,1)S(1)}, bf16[512]{0:T(512)(128)(2,1)}, u32[]{:S(2)}) copy-start(bf16[512]{0:T(512)(128)(2,1)} %param.12) | copy-start | bytes 3076
  3.1 11.5 %copy-start.25 = (s32[512]{0:T(512)S(1)}, s32[512]{0:T(512)}, u32[]{:S(2)}) copy-start(s32[512]{0:T(512)} %param.13) | copy-start | bytes 6148
  3.9 20.5 %collective-permute-start = (bf16[16,8192]{1,0:T(8,128)(2,1)}, bf16[16,8192]{1,0:T(8,128)(2,1)}, u32[]{:S(2)}, u32[]{:S(2)}) collective-permute-start(bf16[16,8192]{1,0:T(8,128)(2,1)} %get-tuple-element.64), channel_id=1, source_target_pairs={{0,2},{1,3},{2,4},{3,5},{4,6},{5,7},{6,8},{7,9},{8,10},{9,11},{10,... | collective-permute-start | bytes 786440 | tf_op jit(solution)/shard_map/ppermute | solution.py:24
  6.9 22.2 %collective-permute-start.1 = (bf16[16,8192]{1,0:T(8,128)(2,1)}, bf16[16,8192]{1,0:T(8,128)(2,1)S(1)}, u32[]{:S(2)}, u32[]{:S(2)}) collective-permute-start(bf16[16,8192]{1,0:T(8,128)(2,1)} %get-tuple-element.67), channel_id=1, source_target_pairs={{0,2},{1,3},{2,4},{3,5},{4,6},{5,7},{6,8},{7,9},{8,10},{9,11},{10,... | collective-permute-start | bytes 786440 | tf_op jit(solution)/shard_map/ppermute | solution.py:24
  12.3 32.9 %collective-permute-start.6 = (bf16[128,8192]{1,0:T(8,128)(2,1)}, bf16[128,8192]{1,0:T(8,128)(2,1)}, u32[]{:S(2)}, u32[]{:S(2)}) collective-permute-start(bf16[128,8192]{1,0:T(8,128)(2,1)} %get-tuple-element.80), channel_id=1, source_target_pairs={{0,1},{1,4},{2,3},{4,5},{5,8},{6,7},{8,9},{9,12},{10,11},{12,13},{... | collective-permute-start | bytes 6291464 | tf_op jit(solution)/shard_map/ppermute | solution.py:24
  24.4 11.3 %collective-permute-start.4 = (bf16[16,8192]{1,0:T(8,128)(2,1)S(1)}, bf16[16,8192]{1,0:T(8,128)(2,1)S(1)}, u32[]{:S(2)}, u32[]{:S(2)}) collective-permute-start(bf16[16,8192]{1,0:T(8,128)(2,1)S(1)} %get-tuple-element.70.refs_1_), channel_id=1, source_target_pairs={{0,2},{1,3},{2,4},{3,5},{4,6},{5,7},{6,8},{7,9},{8,10},{9,11},{10,... | collective-permute-start | bytes 786440 | tf_op jit(solution)/shard_map/ppermute | solution.py:24
  26.6 15.8 %collective-permute-start.2 = (bf16[16,8192]{1,0:T(8,128)(2,1)}, bf16[16,8192]{1,0:T(8,128)(2,1)S(1)}, u32[]{:S(2)}, u32[]{:S(2)}) collective-permute-start(bf16[16,8192]{1,0:T(8,128)(2,1)} %get-tuple-element.66), channel_id=1, source_target_pairs={{0,16},{1,17},{2,18},{3,19},{4,20},{5,21},{6,22},{7,23},{8,24},{9,... | collective-permute-start | bytes 786440 | tf_op jit(solution)/shard_map/ppermute | solution.py:24
  29.2 13.4 %collective-permute-start.7 = (bf16[16,8192]{1,0:T(8,128)(2,1)S(1)}, bf16[16,8192]{1,0:T(8,128)(2,1)S(1)}, u32[]{:S(2)}, u32[]{:S(2)}) collective-permute-start(bf16[16,8192]{1,0:T(8,128)(2,1)S(1)} %get-tuple-element.74.refs_1_), channel_id=1, source_target_pairs={{0,2},{1,3},{2,4},{3,5},{4,6},{5,7},{6,8},{7,9},{8,10},{9,11},{10,... | collective-permute-start | bytes 786440 | tf_op jit(solution)/shard_map/ppermute | solution.py:24
  30.1 10.7 %collective-permute-start.3 = (bf16[16,8192]{1,0:T(8,128)(2,1)S(1)}, bf16[16,8192]{1,0:T(8,128)(2,1)S(1)}, u32[]{:S(2)}, u32[]{:S(2)}) collective-permute-start(bf16[16,8192]{1,0:T(8,128)(2,1)S(1)} %get-tuple-element.71), channel_id=1, source_target_pairs={{0,16},{1,17},{2,18},{3,19},{4,20},{5,21},{6,22},{7,23},{8,24},{9,... | collective-permute-start | bytes 786440 | tf_op jit(solution)/shard_map/ppermute | solution.py:24
  35.7 23.1 %collective-permute-start.10 = (bf16[16,8192]{1,0:T(8,128)(2,1)S(1)}, bf16[16,8192]{1,0:T(8,128)(2,1)S(1)}, u32[]{:S(2)}, u32[]{:S(2)}) collective-permute-start(bf16[16,8192]{1,0:T(8,128)(2,1)S(1)} %get-tuple-element.76.refs_1_), channel_id=1, source_target_pairs={{0,16},{1,17},{2,18},{3,19},{4,20},{5,21},{6,22},{7,23},{8,24},{9,... | collective-permute-start | bytes 786440 | tf_op jit(solution)/shard_map/ppermute | solution.py:24
  40.8 26.4 %collective-permute-start.15 = (bf16[64,8192]{1,0:T(8,128)(2,1)}, bf16[64,8192]{1,0:T(8,128)(2,1)}, u32[]{:S(2)}, u32[]{:S(2)}) collective-permute-start(bf16[64,8192]{1,0:T(8,128)(2,1)} %get-tuple-element.77.refs_2_), channel_id=1, source_target_pairs={{3,6},{7,10},{11,14},{15,2},{19,22},{23,26},{27,30},{31,18}} | collective-permute-start | bytes 3145736 | tf_op jit(solution)/shard_map/ppermute | solution.py:24
  42.5 2.7 %copy-start.10 = (bf16[64,8192]{1,0:T(8,128)(2,1)}, bf16[64,8192]{1,0:T(8,128)(2,1)S(1)}, u32[]{:S(2)}) copy-start(bf16[64,8192]{1,0:T(8,128)(2,1)S(1)} %constant_dynamic-update-slice_fusion.refs_1_.refs_7_.refs_9_.refs_6_) | copy-start | bytes 3145732
  42.5 2.7 %collective-permute-start.5 = (bf16[64,8192]{1,0:T(8,128)(2,1)S(1)}, bf16[64,8192]{1,0:T(8,128)(2,1)S(1)}, u32[]{:S(2)}, u32[]{:S(2)}) collective-permute-start(bf16[64,8192]{1,0:T(8,128)(2,1)S(1)} %constant_dynamic-update-slice_fusion.refs_1_.refs_7_.refs_9_.refs_6_), channel_id=1, source_target_pairs={{0,1},{1,0},{2,3},{3,2},{4,5},{5,4},{6,7},{7,6},{8,9},{9,8},{10,11... | collective-permute-start | bytes 3145736 | tf_op jit(solution)/shard_map/ppermute | solution.py:24
  42.6 2.6 %slice-start = ((s8[4718592]{0:T(1024)(128)(4,1)}), s8[4194304]{0:T(1024)(128)(4,1)S(1)}, s32[]{:S(2)}) async-start(s8[4718592]{0:T(1024)(128)(4,1)} %bitcast.14), calls=%async_computation | async-start | bytes 8388608
  42.6 3.9 %copy-start.2 = (bf16[512,3584]{1,0:T(8,128)(2,1)S(1)}, bf16[512,3584]{1,0:T(8,128)(2,1)}, u32[]{:S(2)}) copy-start(bf16[512,3584]{1,0:T(8,128)(2,1)} %refs_0_.9) | copy-start | bytes 11010052
  42.7 16.2 %collective-permute-start.11 = (bf16[16,8192]{1,0:T(8,128)(2,1)S(1)}, bf16[16,8192]{1,0:T(8,128)(2,1)S(1)}, u32[]{:S(2)}, u32[]{:S(2)}) collective-permute-start(bf16[16,8192]{1,0:T(8,128)(2,1)S(1)} %get-tuple-element.89), channel_id=1, source_target_pairs={{0,16},{1,17},{2,18},{3,19},{4,20},{5,21},{6,22},{7,23},{8,24},{9,... | collective-permute-start | bytes 786440 | tf_op jit(solution)/shard_map/ppermute | solution.py:24
  45.2 5.0 %copy-start.5 = (bf16[64,8192]{1,0:T(8,128)(2,1)}, bf16[64,8192]{1,0:T(8,128)(2,1)S(1)}, u32[]{:S(2)}) copy-start(bf16[64,8192]{1,0:T(8,128)(2,1)S(1)} %get-tuple-element.83.refs_8_.refs_10_.refs_7_) | copy-start | bytes 3145732
  50.2 1.9 %collective-permute-start.8 = (bf16[64,3584]{1,0:T(8,128)(2,1)S(1)}, bf16[64,3584]{1,0:T(8,128)(2,1)S(1)}, u32[]{:S(2)}, u32[]{:S(2)}) collective-permute-start(bf16[64,3584]{1,0:T(8,128)(2,1)S(1)} %get-tuple-element.86.refs_1_), channel_id=1, source_target_pairs={{0,1},{1,0},{2,3},{3,2},{4,5},{5,4},{6,7},{7,6},{8,9},{9,8},{10,11... | collective-permute-start | bytes 1376264 | tf_op jit(solution)/shard_map/ppermute | solution.py:24
  50.9 8.1 %copy-start.14 = (bf16[64,8192]{1,0:T(8,128)(2,1)S(1)}, bf16[64,8192]{1,0:T(8,128)(2,1)}, u32[]{:S(2)}) copy-start(bf16[64,8192]{1,0:T(8,128)(2,1)} %copy-done.13) | copy-start | bytes 3145732
  53.0 38.1 %collective-permute-start.9 = (bf16[64,3584]{1,0:T(8,128)(2,1)}, bf16[64,3584]{1,0:T(8,128)(2,1)}, u32[]{:S(2)}, u32[]{:S(2)}) collective-permute-start(bf16[64,3584]{1,0:T(8,128)(2,1)} %add_convert_fusion.1.refs_3_), channel_id=1, source_target_pairs={{0,14},{1,15},{2,0},{3,1},{4,2},{5,3},{6,4},{7,5},{8,6},{9,7},{10,... | collective-permute-start | bytes 1376264 | tf_op jit(solution)/shard_map/ppermute | solution.py:24
  58.9 2.7 %copy-start.9 = (bf16[64,8192]{1,0:T(8,128)(2,1)}, bf16[64,8192]{1,0:T(8,128)(2,1)S(1)}, u32[]{:S(2)}) copy-start(bf16[64,8192]{1,0:T(8,128)(2,1)S(1)} %constant_dynamic-update-slice_fusion.4.refs_1_.refs_7_.refs_9_.refs_8_) | copy-start | bytes 3145732
  58.9 2.7 %collective-permute-start.12 = (bf16[64,8192]{1,0:T(8,128)(2,1)S(1)}, bf16[64,8192]{1,0:T(8,128)(2,1)S(1)}, u32[]{:S(2)}, u32[]{:S(2)}) collective-permute-start(bf16[64,8192]{1,0:T(8,128)(2,1)S(1)} %constant_dynamic-update-slice_fusion.4.refs_1_.refs_7_.refs_9_.refs_8_), channel_id=1, source_target_pairs={{0,1},{1,0},{2,3},{3,2},{4,5},{5,4},{6,7},{7,6},{8,9},{9,8},{10,11... | collective-permute-start | bytes 3145736 | tf_op jit(solution)/shard_map/ppermute | solution.py:24
  59.0 16.1 %collective-permute-start.17 = (bf16[64,8192]{1,0:T(8,128)(2,1)S(1)}, bf16[64,8192]{1,0:T(8,128)(2,1)S(1)}, u32[]{:S(2)}, u32[]{:S(2)}) collective-permute-start(bf16[64,8192]{1,0:T(8,128)(2,1)S(1)} %get-tuple-element.108), channel_id=1, source_target_pairs={{3,6},{7,10},{11,14},{15,2},{19,22},{23,26},{27,30},{31,18}} | collective-permute-start | bytes 3145736 | tf_op jit(solution)/shard_map/ppermute | solution.py:24
  61.6 3.6 %copy-start.6 = (bf16[64,8192]{1,0:T(8,128)(2,1)}, bf16[64,8192]{1,0:T(8,128)(2,1)S(1)}, u32[]{:S(2)}) copy-start(bf16[64,8192]{1,0:T(8,128)(2,1)S(1)} %get-tuple-element.96.refs_8_.refs_10_.refs_9_) | copy-start | bytes 3145732
  65.3 1.9 %collective-permute-start.13 = (bf16[64,3584]{1,0:T(8,128)(2,1)S(1)}, bf16[64,3584]{1,0:T(8,128)(2,1)S(1)}, u32[]{:S(2)}, u32[]{:S(2)}) collective-permute-start(bf16[64,3584]{1,0:T(8,128)(2,1)S(1)} %get-tuple-element.99.refs_1_), channel_id=1, source_target_pairs={{0,1},{1,0},{2,3},{3,2},{4,5},{5,4},{6,7},{7,6},{8,9},{9,8},{10,11... | collective-permute-start | bytes 1376264 | tf_op jit(solution)/shard_map/ppermute | solution.py:24
  73.6 20.9 %collective-permute-start.16 = (bf16[64,3584]{1,0:T(8,128)(2,1)S(1)}, bf16[64,3584]{1,0:T(8,128)(2,1)S(1)}, u32[]{:S(2)}, u32[]{:S(2)}) collective-permute-start(bf16[64,3584]{1,0:T(8,128)(2,1)S(1)} %get-tuple-element.106.refs_1_), channel_id=1, source_target_pairs={{0,13},{1,0},{2,15},{3,2},{4,1},{5,4},{6,3},{7,6},{8,5},{9,8},{10,... | collective-permute-start | bytes 1376264 | tf_op jit(solution)/shard_map/ppermute | solution.py:24
  73.8 20.8 %collective-permute-start.14 = (bf16[64,3584]{1,0:T(8,128)(2,1)S(1)}, bf16[64,3584]{1,0:T(8,128)(2,1)S(1)}, u32[]{:S(2)}, u32[]{:S(2)}) collective-permute-start(bf16[64,3584]{1,0:T(8,128)(2,1)S(1)} %add_convert_fusion.refs_1_), channel_id=1, source_target_pairs={{0,14},{1,15},{2,0},{3,1},{4,2},{5,3},{6,4},{7,5},{8,6},{9,7},{10,... | collective-permute-start | bytes 1376264 | tf_op jit(solution)/shard_map/ppermute | solution.py:24
  81.7 12.9 %collective-permute-start.18 = (bf16[64,3584]{1,0:T(8,128)(2,1)S(1)}, bf16[64,3584]{1,0:T(8,128)(2,1)S(1)}, u32[]{:S(2)}, u32[]{:S(2)}) collective-permute-start(bf16[64,3584]{1,0:T(8,128)(2,1)S(1)} %get-tuple-element.111.refs_12_), channel_id=1, source_target_pairs={{0,13},{1,0},{2,15},{3,2},{4,1},{5,4},{6,3},{7,6},{8,5},{9,8},{10,... | collective-permute-start | bytes 1376264 | tf_op jit(solution)/shard_map/ppermute | solution.py:24
  82.5 12.1 %copy-start.12 = (f32[128,3584]{1,0:T(8,128)S(1)}, f32[128,3584]{1,0:T(8,128)}, u32[]{:S(2)}) copy-start(f32[128,3584]{1,0:T(8,128)} %copy-done.11) | copy-start | bytes 5505028
  (17 other events, 21.4 us)

commit v7 on v6

--- a/solution.py
+++ b/solution.py
@@ -179,11 +179,17 @@
         score_ref, loss_ref = outs[:2]
         part_refs = outs[2 : 2 + len(kinds)]
         if flags:
-            chosen = jnp.where(
-                flag_refs[0][0] == 1, panel_refs[0][...], panel_refs[1][pl.ds(start, width), :]
-            )
+            chosen = outs[-1]
+
+            @pl.when(flag_refs[0][0] == 1)
+            def _():
+                chosen[...] = panel_refs[0][...]
+
+            @pl.when(flag_refs[0][0] != 1)
+            def _():
+                chosen[...] = panel_refs[1][pl.ds(start, width), :]
+
             panel, panel_t = chosen[:, :depth], chosen[:, depth:]
-            outs[-1][...] = panel
         else:
             panel = jnp.concatenate([ref[:, :depth] for ref in panel_refs], axis=0)
             panel_t = jnp.concatenate(
@@ -221,7 +227,7 @@
         jax.ShapeDtypeStruct((8, count), jnp.float32),
     ] + [jax.ShapeDtypeStruct((part_rows, depth), kind) for kind in kinds]
     if flags:
-        out_shape.append(jax.ShapeDtypeStruct((width, depth), jnp.bfloat16))
+        out_shape.append(jax.ShapeDtypeStruct((width, depth + depth_t), jnp.bfloat16))
     return pl.pallas_call(
         kernel,
         out_shape=out_shape,
@@ -236,7 +242,7 @@
 
 def rows_product(scores, panels, depth, ready):
     count = scores[0].shape[0]
-    block = depth // 7
+    block = depth // 4
     inner = sum(panel.shape[0] for panel in panels)
 
     def kernel(*refs):
@@ -255,7 +261,7 @@
 
     return pl.pallas_call(
         kernel,
-        grid=(7,),
+        grid=(4,),
         out_shape=jax.ShapeDtypeStruct((count, depth), jnp.bfloat16),
         in_specs=[pl.BlockSpec((count, score.shape[1]), lambda index: (0, 0)) for score in scores]
         + [pl.BlockSpec((panel.shape[0], block), lambda index: (0, index)) for panel in panels]
@@ -311,15 +317,7 @@
     crossed = [permuted(chunks[0], next_chip), permuted(chunks[1], next_chip), None, None]
     early = permuted(send, extra_early)
     swapped = [None] * 4
-    own_scores, loss, own_part = meet(
-        [student_head],
-        [teacher_head],
-        place * width + ids_in,
-        jnp.zeros((8, student_rows.shape[0]), jnp.float32),
-        [jnp.float32],
-        [chunks[2]],
-    )
-    order = pause(order, [own_scores])
+    order = pause(order, [chunks[0]])
     crossed[0], chunks[2], order = gate([crossed[0], chunks[2], order], [])
     swapped[0] = permuted(crossed[0], other_plane)
     crossed[2] = permuted(chunks[2], next_chip)
@@ -331,7 +329,15 @@
     crossed[2], send0, order = gate([crossed[2], send0, order], [])
     swapped[2] = permuted(crossed[2], other_plane)
     late = [permuted(send0, extra_late), None]
-    order = pause(order, [crossed[2], send0])
+    own_scores, loss, own_part = meet(
+        [student_head],
+        [teacher_head],
+        place * width + ids_in,
+        jnp.zeros((8, student_rows.shape[0]), jnp.float32),
+        [jnp.float32],
+        [order],
+    )
+    order = pause(order, [crossed[2], send0, own_scores])
     swapped[0], swapped[1], order = gate([swapped[0], swapped[1], order], [])
     mine0 = jnp.concatenate([crossed[0], crossed[1], swapped[0], swapped[1]], axis=0)
     theirs0 = permuted(mine0, other_core)

time: 97.3 us -> 90.6 us (0.931)
  starting transfers between devices: 25.3 us -> 20.9 us
  local copies, waits for them, and re-layouts: 16.9 us -> 13.7 us
  waiting for transfers between devices: 17.3 us -> 19.7 us
  Pallas kernels: 34.4 us -> 33.2 us
    ppermute x19, starting transfers between devices: 25.3 us -> 20.9 us  [permuted(): return lax.ppermute(value, BOTH, pairs)]
    unnamed x66, local copies, waits for them, and re-layouts: 15.9 us -> 12.6 us
    ppermute x19, waiting for transfers between devices: 17.3 us -> 19.7 us  [permuted(): return lax.ppermute(value, BOTH, pairs)]
    pallas_call x1, Pallas kernels: 7.94 us -> 6.31 us  [rows_product(): pl.pallas_call(kernel, grid=(4,), out_shape=jax.ShapeDtypeStruct((count,...]
  transfers between devices with their start and end apart: 19 -> 19, of which waited for: 7 -> 6; matrix products, arithmetic and copies ran while one was open for 4% -> 3% of each run, Pallas kernels for 33% -> 34%
where the time goes in v7:
time: 90.6 us; the launch traced here: 90.1 us
  Pallas kernels  33.2 us (37%)
  starting transfers between devices  20.9 us (23%)
  waiting for transfers between devices  19.7 us (22%)
  local copies, waits for them, and re-layouts  13.7 us (15%)
  between operations  1.35 us (1%)
  other arithmetic  1.29 us (1%)
    pallas_call x5, Pallas kernels, meeting(): pl.pallas_call(kernel, out_shape=out_shape, in_specs=[whole] * (7 + piece...  21.8 us
    ppermute x19, starting transfers between devices, permuted(): return lax.ppermute(value, BOTH, pairs)  20.9 us
    ppermute x19, waiting for transfers between devices, permuted(): return lax.ppermute(value, BOTH, pairs)  19.7 us
    unnamed x66, local copies, waits for them, and re-layouts  12.6 us
    pallas_call x1, Pallas kernels, rows_product(): pl.pallas_call(kernel, grid=(4,), out_shape=jax.ShapeDtypeStruct((count,...  6.31 us
    pallas_call x2, Pallas kernels, packed(): pl.pallas_call(kernel, out_shape=[jax.ShapeDtypeStruct((rows, depth + dep...  2.93 us
    pallas_call x1, Pallas kernels, head_total(): pl.pallas_call(kernel, out_shape=jax.ShapeDtypeStruct((width, depth), jnp...  2.06 us
  transfers between devices with their start and end apart: 19, of which 6 were waited for; matrix products, arithmetic and copies ran while one was open for 3% of the time, Pallas kernels for 34%

profile of v7, /device:TPU:0, one launch (start us, length us, event | category | flops | bytes accessed | tf_op | source)
XLA Modules:
  0.0 90.1 jit_solution(1528946507768504294)
XLA Ops:
  0.6 1.3 %copy-done.1 = bf16[128,4608]{1,0:T(8,128)(2,1)S(1)} copy-done((bf16[128,4608]{1,0:T(8,128)(2,1)S(1)}, bf16[128,4608]{1,0:T(8,128)(2,1)}, u32[]{:S(2)}) %copy-start.1) | copy-done | bytes 1179672
  1.9 1.2 %copy-done.5 = bf16[128,3584]{1,0:T(8,128)(2,1)S(1)} copy-done((bf16[128,3584]{1,0:T(8,128)(2,1)S(1)}, bf16[128,3584]{1,0:T(8,128)(2,1)}, u32[]{:S(2)}) %copy-start.5) | copy-done | bytes 917528
  3.9 3.0 %collective-permute-start.2 = (bf16[16,8192]{1,0:T(8,128)(2,1)}, bf16[16,8192]{1,0:T(8,128)(2,1)S(1)}, u32[]{:S(2)}, u32[]{:S(2)}) collective-permute-start(bf16[16,8192]{1,0:T(8,128)(2,1)} %get-tuple-element.65), channel_id=1, source_target_pairs={{0,2},{1,3},{2,4},{3,5},{4,6},{5,7},{6,8},{7,9},{8,10},{9,11},{10,... | collective-permute-start | bytes 786440 | tf_op jit(solution)/shard_map/ppermute | solution.py:24
  6.9 1.5 %collective-permute-start = (bf16[16,8192]{1,0:T(8,128)(2,1)}, bf16[16,8192]{1,0:T(8,128)(2,1)S(1)}, u32[]{:S(2)}, u32[]{:S(2)}) collective-permute-start(bf16[16,8192]{1,0:T(8,128)(2,1)} %get-tuple-element.61.refs_1_), channel_id=1, source_target_pairs={{0,2},{1,3},{2,4},{3,5},{4,6},{5,7},{6,8},{7,9},{8,10},{9,11},{10,... | collective-permute-start | bytes 786440 | tf_op jit(solution)/shard_map/ppermute | solution.py:24
  8.5 2.1 %shard_map.95 = (bf16[16,8192]{1,0:T(8,128)(2,1)S(1)}, bf16[16,8192]{1,0:T(8,128)(2,1)S(1)}, bf16[128,8192]{1,0:T(8,128)(2,1)}, bf16[64,8192]{1,0:T(8,128)(2,1)}, bf16[64,8192]{1,0:T(8,128)(2,1)S(1)}) custom-call(s32[1]{0:T(128)} %bitcast.at_ref, bf16[128,3584]{1,0:T(8,128)(2,1)S(1)} %copy-done.6, bf16[128,4608]{1,0:T(8,128)(2,1)S(1)} %copy-done.2), custom_call_target="tpu_custom_call" | custom-call | tf_op jit(solution)/shard_map/pallas_call | solution.py:95
  10.6 1.0 %copy-done.9 = bf16[64,8192]{1,0:T(8,128)(2,1)} copy-done((bf16[64,8192]{1,0:T(8,128)(2,1)}, bf16[64,8192]{1,0:T(8,128)(2,1)S(1)}, u32[]{:S(2)}) %copy-start.9) | copy-done | bytes 1048600
  13.0 1.9 %collective-permute-start.6 = (bf16[128,8192]{1,0:T(8,128)(2,1)}, bf16[128,8192]{1,0:T(8,128)(2,1)}, u32[]{:S(2)}, u32[]{:S(2)}) collective-permute-start(bf16[128,8192]{1,0:T(8,128)(2,1)} %get-tuple-element.80), channel_id=1, source_target_pairs={{0,1},{1,4},{2,3},{4,5},{5,8},{6,7},{8,9},{9,12},{10,11},{12,13},{... | collective-permute-start | bytes 6291464 | tf_op jit(solution)/shard_map/ppermute | solution.py:24
  16.2 5.8 %collective-permute-done.refs_0_ = bf16[16,8192]{1,0:T(8,128)(2,1)S(1)} collective-permute-done((bf16[16,8192]{1,0:T(8,128)(2,1)}, bf16[16,8192]{1,0:T(8,128)(2,1)S(1)}, u32[]{:S(2)}, u32[]{:S(2)}) %collective-permute-start) | collective-permute-done | bytes 262176 | tf_op jit(solution)/shard_map/ppermute | solution.py:24
  22.1 0.9 %copy-done.14 = bf16[16,8192]{1,0:T(8,128)(2,1)S(1)} copy-done((bf16[16,8192]{1,0:T(8,128)(2,1)S(1)}, bf16[16,8192]{1,0:T(8,128)(2,1)}, u32[]{:S(2)}) %copy-start.14) | copy-done | bytes 262168
  23.7 1.0 %copy-done.16 = bf16[16,8192]{1,0:T(8,128)(2,1)S(1)} copy-done((bf16[16,8192]{1,0:T(8,128)(2,1)S(1)}, bf16[16,8192]{1,0:T(8,128)(2,1)}, u32[]{:S(2)}) %copy-start.16) | copy-done | bytes 262168
  24.7 1.5 %collective-permute-start.3 = (bf16[16,8192]{1,0:T(8,128)(2,1)S(1)}, bf16[16,8192]{1,0:T(8,128)(2,1)S(1)}, u32[]{:S(2)}, u32[]{:S(2)}) collective-permute-start(bf16[16,8192]{1,0:T(8,128)(2,1)S(1)} %get-tuple-element.73), channel_id=1, source_target_pairs={{0,16},{1,17},{2,18},{3,19},{4,20},{5,21},{6,22},{7,23},{8,24},{9,... | collective-permute-start | bytes 786440 | tf_op jit(solution)/shard_map/ppermute | solution.py:24
  26.3 1.2 %collective-permute-start.7 = (bf16[16,8192]{1,0:T(8,128)(2,1)S(1)}, bf16[16,8192]{1,0:T(8,128)(2,1)S(1)}, u32[]{:S(2)}, u32[]{:S(2)}) collective-permute-start(bf16[16,8192]{1,0:T(8,128)(2,1)S(1)} %get-tuple-element.69.refs_1_), channel_id=1, source_target_pairs={{0,2},{1,3},{2,4},{3,5},{4,6},{5,7},{6,8},{7,9},{8,10},{9,11},{10,... | collective-permute-start | bytes 786440 | tf_op jit(solution)/shard_map/ppermute | solution.py:24
  28.4 7.5 %collective-permute-done.1.refs_0_ = bf16[16,8192]{1,0:T(8,128)(2,1)S(1)} collective-permute-done((bf16[16,8192]{1,0:T(8,128)(2,1)}, bf16[16,8192]{1,0:T(8,128)(2,1)S(1)}, u32[]{:S(2)}, u32[]{:S(2)}) %collective-permute-start.1) | collective-permute-done | bytes 262176 | tf_op jit(solution)/shard_map/ppermute | solution.py:24
  35.9 1.5 %collective-permute-start.10 = (bf16[16,8192]{1,0:T(8,128)(2,1)S(1)}, bf16[16,8192]{1,0:T(8,128)(2,1)S(1)}, u32[]{:S(2)}, u32[]{:S(2)}) collective-permute-start(bf16[16,8192]{1,0:T(8,128)(2,1)S(1)} %get-tuple-element.75.refs_1_), channel_id=1, source_target_pairs={{0,16},{1,17},{2,18},{3,19},{4,20},{5,21},{6,22},{7,23},{8,24},{9,... | collective-permute-start | bytes 786440 | tf_op jit(solution)/shard_map/ppermute | solution.py:24
  37.4 3.6 %shard_map.102 = (bf16[512,128]{1,0:T(8,128)(2,1)S(1)}, f32[8,512]{1,0:T(8,128)S(1)}, f32[128,3584]{1,0:T(8,128)S(1)}) custom-call(bf16[512,3584]{1,0:T(8,128)(2,1)S(1)} %copy-done, bf16[512,4608]{1,0:T(8,128)(2,1)S(1)} %bitcast.15, f32[512,1]{1,0:T(8,128)S(1)} %copy.53.refs_2_, f32[512,1]{1,0:T(8,128)S(1)} %copy.54.refs_3_, s32[512,1]{1,0:T(8,128)S(1)} %copy.55.refs_4_, ...), custom_call_target="tpu_custom_call" | custom-call | tf_op jit(solution)/shard_map/pallas_call | solution.py:231
  41.7 1.7 %collective-permute-start.15 = (bf16[64,8192]{1,0:T(8,128)(2,1)}, bf16[64,8192]{1,0:T(8,128)(2,1)}, u32[]{:S(2)}, u32[]{:S(2)}) collective-permute-start(bf16[64,8192]{1,0:T(8,128)(2,1)} %get-tuple-element.76.refs_2_), channel_id=1, source_target_pairs={{3,6},{7,10},{11,14},{15,2},{19,22},{23,26},{27,30},{31,18}} | collective-permute-start | bytes 3145736 | tf_op jit(solution)/shard_map/ppermute | solution.py:24
  44.2 2.0 %collective-permute-done.5.refs_0_ = bf16[64,8192]{1,0:T(8,128)(2,1)S(1)} collective-permute-done((bf16[64,8192]{1,0:T(8,128)(2,1)S(1)}, bf16[64,8192]{1,0:T(8,128)(2,1)S(1)}, u32[]{:S(2)}, u32[]{:S(2)}) %collective-permute-start.5) | collective-permute-done | bytes 1048608 | tf_op jit(solution)/shard_map/ppermute | solution.py:24
  46.2 3.6 %shard_map.109 = (bf16[512,128]{1,0:T(8,128)(2,1)S(1)}, f32[8,512]{1,0:T(8,128)S(1)}, f32[64,3584]{1,0:T(8,128)S(1)}, bf16[64,3584]{1,0:T(8,128)(2,1)S(1)}) custom-call(bf16[512,3584]{1,0:T(8,128)(2,1)S(1)} %copy-done, bf16[512,4608]{1,0:T(8,128)(2,1)S(1)} %bitcast.15, f32[512,1]{1,0:T(8,128)S(1)} %copy.53.refs_2_, f32[512,1]{1,0:T(8,128)S(1)} %copy.54.refs_3_, ...), custom_call_target="tpu_custom_call" | custom-call | tf_op jit(solution)/shard_map/pallas_call | solution.py:231
  50.5 1.2 %collective-permute-done.8.refs_0_ = bf16[64,3584]{1,0:T(8,128)(2,1)S(1)} collective-permute-done((bf16[64,3584]{1,0:T(8,128)(2,1)S(1)}, bf16[64,3584]{1,0:T(8,128)(2,1)S(1)}, u32[]{:S(2)}, u32[]{:S(2)}) %collective-permute-start.8) | collective-permute-done | bytes 458784 | tf_op jit(solution)/shard_map/ppermute | solution.py:24
  51.8 0.8 add_convert_fusion.1.refs_3_
  52.6 3.3 %collective-permute-start.9 = (bf16[64,3584]{1,0:T(8,128)(2,1)}, bf16[64,3584]{1,0:T(8,128)(2,1)}, u32[]{:S(2)}, u32[]{:S(2)}) collective-permute-start(bf16[64,3584]{1,0:T(8,128)(2,1)} %add_convert_fusion.1.refs_3_), channel_id=1, source_target_pairs={{0,14},{1,15},{2,0},{3,1},{4,2},{5,3},{6,4},{7,5},{8,6},{9,7},{10,... | collective-permute-start | bytes 1376264 | tf_op jit(solution)/shard_map/ppermute | solution.py:24
  56.8 1.9 %collective-permute-done.12.refs_0_ = bf16[64,8192]{1,0:T(8,128)(2,1)S(1)} collective-permute-done((bf16[64,8192]{1,0:T(8,128)(2,1)S(1)}, bf16[64,8192]{1,0:T(8,128)(2,1)S(1)}, u32[]{:S(2)}, u32[]{:S(2)}) %collective-permute-start.12) | collective-permute-done | bytes 1048608 | tf_op jit(solution)/shard_map/ppermute | solution.py:24
  58.6 3.6 %shard_map.116 = (bf16[512,128]{1,0:T(8,128)(2,1)S(1)}, f32[8,512]{1,0:T(8,128)S(1)}, f32[64,3584]{1,0:T(8,128)S(1)}, bf16[64,3584]{1,0:T(8,128)(2,1)S(1)}) custom-call(bf16[512,3584]{1,0:T(8,128)(2,1)S(1)} %copy-done, bf16[512,4608]{1,0:T(8,128)(2,1)S(1)} %bitcast.15, f32[512,1]{1,0:T(8,128)S(1)} %copy.53.refs_2_, f32[512,1]{1,0:T(8,128)S(1)} %copy.54.refs_3_, ...), custom_call_target="tpu_custom_call" | custom-call | tf_op jit(solution)/shard_map/pallas_call | solution.py:231
  62.9 1.2 %collective-permute-done.13.refs_0_ = bf16[64,3584]{1,0:T(8,128)(2,1)S(1)} collective-permute-done((bf16[64,3584]{1,0:T(8,128)(2,1)S(1)}, bf16[64,3584]{1,0:T(8,128)(2,1)S(1)}, u32[]{:S(2)}, u32[]{:S(2)}) %collective-permute-start.13) | collective-permute-done | bytes 458784 | tf_op jit(solution)/shard_map/ppermute | solution.py:24
  64.3 1.2 %collective-permute-start.14 = (bf16[64,3584]{1,0:T(8,128)(2,1)S(1)}, bf16[64,3584]{1,0:T(8,128)(2,1)S(1)}, u32[]{:S(2)}, u32[]{:S(2)}) collective-permute-start(bf16[64,3584]{1,0:T(8,128)(2,1)S(1)} %add_convert_fusion.refs_1_), channel_id=1, source_target_pairs={{0,14},{1,15},{2,0},{3,1},{4,2},{5,3},{6,4},{7,5},{8,6},{9,7},{10,... | collective-permute-start | bytes 1376264 | tf_op jit(solution)/shard_map/ppermute | solution.py:24
  65.5 5.7 %shard_map.121 = (bf16[512,64]{1,0:T(8,128)(2,1)S(1)}, f32[8,512]{1,0:T(8,128)S(1)}, bf16[64,3584]{1,0:T(8,128)(2,1)S(1)}, bf16[64,8192]{1,0:T(8,128)(2,1)S(1)}) custom-call(bf16[512,3584]{1,0:T(8,128)(2,1)S(1)} %copy-done, bf16[512,4608]{1,0:T(8,128)(2,1)S(1)} %bitcast.15, f32[512,1]{1,0:T(8,128)S(1)} %copy.53.refs_2_, f32[512,1]{1,0:T(8,128)S(1)} %copy.54.refs_3_, ...), custom_call_target="tpu_custom_call" | custom-call | tf_op jit(solution)/shard_map/pallas_call | solution.py:231
  71.3 1.0 %copy-done.17 = bf16[64,8192]{1,0:T(8,128)(2,1)} copy-done((bf16[64,8192]{1,0:T(8,128)(2,1)}, bf16[64,8192]{1,0:T(8,128)(2,1)S(1)}, u32[]{:S(2)}) %copy-start.17) | copy-done | bytes 1048600
  72.4 0.9 %collective-permute-start.16 = (bf16[64,3584]{1,0:T(8,128)(2,1)S(1)}, bf16[64,3584]{1,0:T(8,128)(2,1)S(1)}, u32[]{:S(2)}, u32[]{:S(2)}) collective-permute-start(bf16[64,3584]{1,0:T(8,128)(2,1)S(1)} %get-tuple-element.106.refs_1_), channel_id=1, source_target_pairs={{0,13},{1,0},{2,15},{3,2},{4,1},{5,4},{6,3},{7,6},{8,5},{9,8},{10,... | collective-permute-start | bytes 1376264 | tf_op jit(solution)/shard_map/ppermute | solution.py:24
  73.3 5.3 %shard_map.124 = (bf16[512,64]{1,0:T(8,128)(2,1)S(1)}, f32[8,512]{1,0:T(8,128)S(1)}, bf16[64,3584]{1,0:T(8,128)(2,1)S(1)}, bf16[64,8192]{1,0:T(8,128)(2,1)S(1)}) custom-call(bf16[512,3584]{1,0:T(8,128)(2,1)S(1)} %copy-done, bf16[512,4608]{1,0:T(8,128)(2,1)S(1)} %bitcast.15, f32[512,1]{1,0:T(8,128)S(1)} %copy.53.refs_2_, f32[512,1]{1,0:T(8,128)S(1)} %copy.54.refs_3_, ...), custom_call_target="tpu_custom_call" | custom-call | tf_op jit(solution)/shard_map/pallas_call | solution.py:231
  78.6 1.0 %copy-done.18 = bf16[64,8192]{1,0:T(8,128)(2,1)} copy-done((bf16[64,8192]{1,0:T(8,128)(2,1)}, bf16[64,8192]{1,0:T(8,128)(2,1)S(1)}, u32[]{:S(2)}) %copy-start.18) | copy-done | bytes 1048600
  81.0 6.3 %shard_map.126 = bf16[512,3584]{1,0:T(8,128)(2,1)} custom-call(bf16[512,128]{1,0:T(8,128)(2,1)} %copy-done.20, bf16[512,128]{1,0:T(8,128)(2,1)} %copy-done.21, bf16[512,128]{1,0:T(8,128)(2,1)} %copy-done.22, bf16[512,64]{1,0:T(8,128)(2,1)} %copy-done.23, bf16[512,64]{1,0:T(8,128)(2,1)} %copy-done.24, bf16[128,3584]{1,0:T(8,128)(2,1)} %refs_5_.1, ...), custom_call_target="tpu_custom_call" | custom-call | flops 30000001024 | tf_op jit(solution)/shard_map/pallas_call | solution.py:262
  87.9 2.1 %shard_map.125 = bf16[128,3584]{1,0:T(8,128)(2,1)} custom-call(s32[1]{0:T(128)} %bitcast.at_ref, f32[128,3584]{1,0:T(8,128)S(1)} %get-tuple-element.71.own_ref, bf16[64,3584]{1,0:T(8,128)(2,1)} %collective-permute-done.9.back0, bf16[64,3584]{1,0:T(8,128)(2,1)S(1)} %collective-permute-done.14.back1, bf16[64,3584]{1,0:T(8,128)(2,1)S(1)} %collective-permute-done.16.extra0, ...), custom_call_target="tpu_custom_call" | custom-call | tf_op jit(solution)/shard_map/pallas_call | solution.py:139
  (127 shorter events, 10.8 us)
Async XLA Ops:
  0.6 1.3 %copy-start.1 = (bf16[128,4608]{1,0:T(8,128)(2,1)S(1)}, bf16[128,4608]{1,0:T(8,128)(2,1)}, u32[]{:S(2)}) copy-start(bf16[128,4608]{1,0:T(8,128)(2,1)} %refs_8_.1) | copy-start | bytes 3538948
  1.9 1.2 %copy-start.5 = (bf16[128,3584]{1,0:T(8,128)(2,1)S(1)}, bf16[128,3584]{1,0:T(8,128)(2,1)}, u32[]{:S(2)}) copy-start(bf16[128,3584]{1,0:T(8,128)(2,1)} %refs_5_.1) | copy-start | bytes 2752516
  3.1 5.4 %copy-start.2 = (bf16[128,4608]{1,0:T(8,128)(2,1)S(1)}, bf16[128,4608]{1,0:T(8,128)(2,1)}, u32[]{:S(2)}) copy-start(bf16[128,4608]{1,0:T(8,128)(2,1)} %refs_8_.1) | copy-start | bytes 3538948
  3.1 5.4 %copy-start.6 = (bf16[128,3584]{1,0:T(8,128)(2,1)S(1)}, bf16[128,3584]{1,0:T(8,128)(2,1)}, u32[]{:S(2)}) copy-start(bf16[128,3584]{1,0:T(8,128)(2,1)} %refs_5_.1) | copy-start | bytes 2752516
  3.9 22.4 %collective-permute-start.2 = (bf16[16,8192]{1,0:T(8,128)(2,1)}, bf16[16,8192]{1,0:T(8,128)(2,1)S(1)}, u32[]{:S(2)}, u32[]{:S(2)}) collective-permute-start(bf16[16,8192]{1,0:T(8,128)(2,1)} %get-tuple-element.65), channel_id=1, source_target_pairs={{0,2},{1,3},{2,4},{3,5},{4,6},{5,7},{6,8},{7,9},{8,10},{9,11},{10,... | collective-permute-start | bytes 786440 | tf_op jit(solution)/shard_map/ppermute | solution.py:24
  6.9 15.2 %collective-permute-start = (bf16[16,8192]{1,0:T(8,128)(2,1)}, bf16[16,8192]{1,0:T(8,128)(2,1)S(1)}, u32[]{:S(2)}, u32[]{:S(2)}) collective-permute-start(bf16[16,8192]{1,0:T(8,128)(2,1)} %get-tuple-element.61.refs_1_), channel_id=1, source_target_pairs={{0,2},{1,3},{2,4},{3,5},{4,6},{5,7},{6,8},{7,9},{8,10},{9,11},{10,... | collective-permute-start | bytes 786440 | tf_op jit(solution)/shard_map/ppermute | solution.py:24
  13.0 33.2 %collective-permute-start.6 = (bf16[128,8192]{1,0:T(8,128)(2,1)}, bf16[128,8192]{1,0:T(8,128)(2,1)}, u32[]{:S(2)}, u32[]{:S(2)}) collective-permute-start(bf16[128,8192]{1,0:T(8,128)(2,1)} %get-tuple-element.80), channel_id=1, source_target_pairs={{0,1},{1,4},{2,3},{4,5},{5,8},{6,7},{8,9},{9,12},{10,11},{12,13},{... | collective-permute-start | bytes 6291464 | tf_op jit(solution)/shard_map/ppermute | solution.py:24
  23.7 12.1 %collective-permute-start.1 = (bf16[16,8192]{1,0:T(8,128)(2,1)}, bf16[16,8192]{1,0:T(8,128)(2,1)S(1)}, u32[]{:S(2)}, u32[]{:S(2)}) collective-permute-start(bf16[16,8192]{1,0:T(8,128)(2,1)} %copy-done.15), channel_id=1, source_target_pairs={{0,2},{1,3},{2,4},{3,5},{4,6},{5,7},{6,8},{7,9},{8,10},{9,11},{10,... | collective-permute-start | bytes 786440 | tf_op jit(solution)/shard_map/ppermute | solution.py:24
  24.7 1.6 %copy-start.12 = (bf16[16,8192]{1,0:T(8,128)(2,1)S(1)}, bf16[16,8192]{1,0:T(8,128)(2,1)}, u32[]{:S(2)}) copy-start(bf16[16,8192]{1,0:T(8,128)(2,1)} %copy-done.11) | copy-start | bytes 786436
  24.7 18.7 %collective-permute-start.3 = (bf16[16,8192]{1,0:T(8,128)(2,1)S(1)}, bf16[16,8192]{1,0:T(8,128)(2,1)S(1)}, u32[]{:S(2)}, u32[]{:S(2)}) collective-permute-start(bf16[16,8192]{1,0:T(8,128)(2,1)S(1)} %get-tuple-element.73), channel_id=1, source_target_pairs={{0,16},{1,17},{2,18},{3,19},{4,20},{5,21},{6,22},{7,23},{8,24},{9,... | collective-permute-start | bytes 786440 | tf_op jit(solution)/shard_map/ppermute | solution.py:24
  26.3 17.3 %collective-permute-start.7 = (bf16[16,8192]{1,0:T(8,128)(2,1)S(1)}, bf16[16,8192]{1,0:T(8,128)(2,1)S(1)}, u32[]{:S(2)}, u32[]{:S(2)}) collective-permute-start(bf16[16,8192]{1,0:T(8,128)(2,1)S(1)} %get-tuple-element.69.refs_1_), channel_id=1, source_target_pairs={{0,2},{1,3},{2,4},{3,5},{4,6},{5,7},{6,8},{7,9},{8,10},{9,11},{10,... | collective-permute-start | bytes 786440 | tf_op jit(solution)/shard_map/ppermute | solution.py:24
  27.5 9.9 %slice-start = ((s8[4718592]{0:T(1024)(128)(4,1)}), s8[4194304]{0:T(1024)(128)(4,1)S(1)}, s32[]{:S(2)}) async-start(s8[4718592]{0:T(1024)(128)(4,1)} %bitcast.14), calls=%async_computation | async-start | bytes 8388608
  27.5 9.9 %slice-start.1 = ((s8[4718592]{0:T(1024)(128)(4,1)}), s8[524288]{0:T(1024)(128)(4,1)S(1)}, s32[]{:S(2)}) async-start(s8[4718592]{0:T(1024)(128)(4,1)} %bitcast.14), calls=%async_computation.1 | async-start | bytes 1048576
  27.5 9.9 %copy-start = (bf16[512,3584]{1,0:T(8,128)(2,1)S(1)}, bf16[512,3584]{1,0:T(8,128)(2,1)}, u32[]{:S(2)}) copy-start(bf16[512,3584]{1,0:T(8,128)(2,1)} %refs_0_.9) | copy-start | bytes 11010052
  27.5 14.2 %collective-permute-start.4 = (bf16[16,8192]{1,0:T(8,128)(2,1)S(1)}, bf16[16,8192]{1,0:T(8,128)(2,1)S(1)}, u32[]{:S(2)}, u32[]{:S(2)}) collective-permute-start(bf16[16,8192]{1,0:T(8,128)(2,1)S(1)} %get-tuple-element.74), channel_id=1, source_target_pairs={{0,16},{1,17},{2,18},{3,19},{4,20},{5,21},{6,22},{7,23},{8,24},{9,... | collective-permute-start | bytes 786440 | tf_op jit(solution)/shard_map/ppermute | solution.py:24
  35.9 20.0 %collective-permute-start.10 = (bf16[16,8192]{1,0:T(8,128)(2,1)S(1)}, bf16[16,8192]{1,0:T(8,128)(2,1)S(1)}, u32[]{:S(2)}, u32[]{:S(2)}) collective-permute-start(bf16[16,8192]{1,0:T(8,128)(2,1)S(1)} %get-tuple-element.75.refs_1_), channel_id=1, source_target_pairs={{0,16},{1,17},{2,18},{3,19},{4,20},{5,21},{6,22},{7,23},{8,24},{9,... | collective-permute-start | bytes 786440 | tf_op jit(solution)/shard_map/ppermute | solution.py:24
  41.7 23.8 %collective-permute-start.15 = (bf16[64,8192]{1,0:T(8,128)(2,1)}, bf16[64,8192]{1,0:T(8,128)(2,1)}, u32[]{:S(2)}, u32[]{:S(2)}) collective-permute-start(bf16[64,8192]{1,0:T(8,128)(2,1)} %get-tuple-element.76.refs_2_), channel_id=1, source_target_pairs={{3,6},{7,10},{11,14},{15,2},{19,22},{23,26},{27,30},{31,18}} | collective-permute-start | bytes 3145736 | tf_op jit(solution)/shard_map/ppermute | solution.py:24
  43.5 2.7 %copy-start.8 = (bf16[64,8192]{1,0:T(8,128)(2,1)}, bf16[64,8192]{1,0:T(8,128)(2,1)S(1)}, u32[]{:S(2)}) copy-start(bf16[64,8192]{1,0:T(8,128)(2,1)S(1)} %constant_dynamic-update-slice_fusion.refs_1_.refs_7_.refs_9_.refs_6_) | copy-start | bytes 3145732
  43.5 2.7 %collective-permute-start.5 = (bf16[64,8192]{1,0:T(8,128)(2,1)S(1)}, bf16[64,8192]{1,0:T(8,128)(2,1)S(1)}, u32[]{:S(2)}, u32[]{:S(2)}) collective-permute-start(bf16[64,8192]{1,0:T(8,128)(2,1)S(1)} %constant_dynamic-update-slice_fusion.refs_1_.refs_7_.refs_9_.refs_6_), channel_id=1, source_target_pairs={{0,1},{1,0},{2,3},{3,2},{4,5},{5,4},{6,7},{7,6},{8,9},{9,8},{10,11... | collective-permute-start | bytes 3145736 | tf_op jit(solution)/shard_map/ppermute | solution.py:24
  43.6 12.3 %collective-permute-start.11 = (bf16[16,8192]{1,0:T(8,128)(2,1)S(1)}, bf16[16,8192]{1,0:T(8,128)(2,1)S(1)}, u32[]{:S(2)}, u32[]{:S(2)}) collective-permute-start(bf16[16,8192]{1,0:T(8,128)(2,1)S(1)} %get-tuple-element.89), channel_id=1, source_target_pairs={{0,16},{1,17},{2,18},{3,19},{4,20},{5,21},{6,22},{7,23},{8,24},{9,... | collective-permute-start | bytes 786440 | tf_op jit(solution)/shard_map/ppermute | solution.py:24
  46.2 3.6 %copy-start.3 = (bf16[64,8192]{1,0:T(8,128)(2,1)}, bf16[64,8192]{1,0:T(8,128)(2,1)S(1)}, u32[]{:S(2)}) copy-start(bf16[64,8192]{1,0:T(8,128)(2,1)S(1)} %get-tuple-element.83.refs_8_.refs_10_.refs_7_) | copy-start | bytes 3145732
  49.9 1.9 %collective-permute-start.8 = (bf16[64,3584]{1,0:T(8,128)(2,1)S(1)}, bf16[64,3584]{1,0:T(8,128)(2,1)S(1)}, u32[]{:S(2)}, u32[]{:S(2)}) collective-permute-start(bf16[64,3584]{1,0:T(8,128)(2,1)S(1)} %get-tuple-element.86.refs_1_), channel_id=1, source_target_pairs={{0,1},{1,0},{2,3},{3,2},{4,5},{5,4},{6,7},{7,6},{8,9},{9,8},{10,11... | collective-permute-start | bytes 1376264 | tf_op jit(solution)/shard_map/ppermute | solution.py:24
  50.5 5.5 %copy-start.10 = (bf16[64,8192]{1,0:T(8,128)(2,1)S(1)}, bf16[64,8192]{1,0:T(8,128)(2,1)}, u32[]{:S(2)}) copy-start(bf16[64,8192]{1,0:T(8,128)(2,1)} %copy-done.9) | copy-start | bytes 3145732
  52.6 35.3 %collective-permute-start.9 = (bf16[64,3584]{1,0:T(8,128)(2,1)}, bf16[64,3584]{1,0:T(8,128)(2,1)}, u32[]{:S(2)}, u32[]{:S(2)}) collective-permute-start(bf16[64,3584]{1,0:T(8,128)(2,1)} %add_convert_fusion.1.refs_3_), channel_id=1, source_target_pairs={{0,14},{1,15},{2,0},{3,1},{4,2},{5,3},{6,4},{7,5},{8,6},{9,7},{10,... | collective-permute-start | bytes 1376264 | tf_op jit(solution)/shard_map/ppermute | solution.py:24
  55.9 2.7 %copy-start.7 = (bf16[64,8192]{1,0:T(8,128)(2,1)}, bf16[64,8192]{1,0:T(8,128)(2,1)S(1)}, u32[]{:S(2)}) copy-start(bf16[64,8192]{1,0:T(8,128)(2,1)S(1)} %constant_dynamic-update-slice_fusion.4.refs_1_.refs_7_.refs_9_.refs_8_) | copy-start | bytes 3145732
  55.9 2.7 %collective-permute-start.12 = (bf16[64,8192]{1,0:T(8,128)(2,1)S(1)}, bf16[64,8192]{1,0:T(8,128)(2,1)S(1)}, u32[]{:S(2)}, u32[]{:S(2)}) collective-permute-start(bf16[64,8192]{1,0:T(8,128)(2,1)S(1)} %constant_dynamic-update-slice_fusion.4.refs_1_.refs_7_.refs_9_.refs_8_), channel_id=1, source_target_pairs={{0,1},{1,0},{2,3},{3,2},{4,5},{5,4},{6,7},{7,6},{8,9},{9,8},{10,11... | collective-permute-start | bytes 3145736 | tf_op jit(solution)/shard_map/ppermute | solution.py:24
  56.1 17.3 %collective-permute-start.17 = (bf16[64,8192]{1,0:T(8,128)(2,1)S(1)}, bf16[64,8192]{1,0:T(8,128)(2,1)S(1)}, u32[]{:S(2)}, u32[]{:S(2)}) collective-permute-start(bf16[64,8192]{1,0:T(8,128)(2,1)S(1)} %get-tuple-element.108), channel_id=1, source_target_pairs={{3,6},{7,10},{11,14},{15,2},{19,22},{23,26},{27,30},{31,18}} | collective-permute-start | bytes 3145736 | tf_op jit(solution)/shard_map/ppermute | solution.py:24
  58.6 3.6 %copy-start.4 = (bf16[64,8192]{1,0:T(8,128)(2,1)}, bf16[64,8192]{1,0:T(8,128)(2,1)S(1)}, u32[]{:S(2)}) copy-start(bf16[64,8192]{1,0:T(8,128)(2,1)S(1)} %get-tuple-element.96.refs_8_.refs_10_.refs_9_) | copy-start | bytes 3145732
  62.3 1.9 %collective-permute-start.13 = (bf16[64,3584]{1,0:T(8,128)(2,1)S(1)}, bf16[64,3584]{1,0:T(8,128)(2,1)S(1)}, u32[]{:S(2)}, u32[]{:S(2)}) collective-permute-start(bf16[64,3584]{1,0:T(8,128)(2,1)S(1)} %get-tuple-element.99.refs_1_), channel_id=1, source_target_pairs={{0,1},{1,0},{2,3},{3,2},{4,5},{5,4},{6,7},{7,6},{8,9},{9,8},{10,11... | collective-permute-start | bytes 1376264 | tf_op jit(solution)/shard_map/ppermute | solution.py:24
  64.3 23.6 %collective-permute-start.14 = (bf16[64,3584]{1,0:T(8,128)(2,1)S(1)}, bf16[64,3584]{1,0:T(8,128)(2,1)S(1)}, u32[]{:S(2)}, u32[]{:S(2)}) collective-permute-start(bf16[64,3584]{1,0:T(8,128)(2,1)S(1)} %add_convert_fusion.refs_1_), channel_id=1, source_target_pairs={{0,14},{1,15},{2,0},{3,1},{4,2},{5,3},{6,4},{7,5},{8,6},{9,7},{10,... | collective-permute-start | bytes 1376264 | tf_op jit(solution)/shard_map/ppermute | solution.py:24
  72.4 15.5 %collective-permute-start.16 = (bf16[64,3584]{1,0:T(8,128)(2,1)S(1)}, bf16[64,3584]{1,0:T(8,128)(2,1)S(1)}, u32[]{:S(2)}, u32[]{:S(2)}) collective-permute-start(bf16[64,3584]{1,0:T(8,128)(2,1)S(1)} %get-tuple-element.106.refs_1_), channel_id=1, source_target_pairs={{0,13},{1,0},{2,15},{3,2},{4,1},{5,4},{6,3},{7,6},{8,5},{9,8},{10,... | collective-permute-start | bytes 1376264 | tf_op jit(solution)/shard_map/ppermute | solution.py:24
  80.2 7.7 %collective-permute-start.18 = (bf16[64,3584]{1,0:T(8,128)(2,1)S(1)}, bf16[64,3584]{1,0:T(8,128)(2,1)S(1)}, u32[]{:S(2)}, u32[]{:S(2)}) collective-permute-start(bf16[64,3584]{1,0:T(8,128)(2,1)S(1)} %get-tuple-element.111.refs_12_), channel_id=1, source_target_pairs={{0,13},{1,0},{2,15},{3,2},{4,1},{5,4},{6,3},{7,6},{8,5},{9,8},{10,... | collective-permute-start | bytes 1376264 | tf_op jit(solution)/shard_map/ppermute | solution.py:24
  (17 other events, 13.9 us)

commit v8 on v7

--- a/solution.py
+++ b/solution.py
@@ -106,26 +106,22 @@
     )(at, student_head, teacher_head, *ready)
 
 
-def head_total(at, own_part, backs, extras):
+def head_total(at, own_part, backs, extra):
     width, depth = own_part.shape
     half = width // 2
     quarter = half // 2
     whole = pl.BlockSpec(memory_space=pltpu.VMEM)
 
-    def kernel(at_ref, own_ref, back0, back1, extra0, extra1, out_ref, sum_ref, sems):
-        low = at_ref[0] == 0
+    def kernel(at_ref, own_ref, back0, back1, extra_ref, out_ref, sum_ref, sems):
         copies = []
         for stage, back in enumerate((back0, back1)):
             for side in range(2):
                 base = at_ref[0] if side == 0 else half - at_ref[0]
                 rows = pl.ds(pl.multiple_of(base + stage * quarter, quarter), quarter)
-                picked = pl.ds(stage * quarter, quarter)
-                first = low if side == 0 else jnp.logical_not(low)
-                extra = jnp.where(first, extra0[picked, :], extra1[picked, :])
                 sum_ref[rows, :] = (
                     own_ref[rows, :]
                     + back[pl.ds(side * quarter, quarter), :].astype(jnp.float32)
-                    + extra.astype(jnp.float32)
+                    + extra_ref[rows, :].astype(jnp.float32)
                 ).astype(sum_ref.dtype)
                 copies.append(
                     pltpu.make_async_copy(
@@ -139,11 +135,11 @@
     return pl.pallas_call(
         kernel,
         out_shape=jax.ShapeDtypeStruct((width, depth), jnp.bfloat16),
-        in_specs=[pl.BlockSpec(memory_space=pltpu.SMEM)] + [whole] * 5,
+        in_specs=[pl.BlockSpec(memory_space=pltpu.SMEM)] + [whole] * 4,
         out_specs=pl.BlockSpec(memory_space=pl.ANY),
         scratch_shapes=[pltpu.VMEM((width, depth), jnp.bfloat16), pltpu.SemaphoreType.DMA((4,))],
         compiler_params=pltpu.CompilerParams(vmem_limit_bytes=6 * 1024 * 1024),
-    )(at, own_part, *backs, *extras)
+    )(at, own_part, *backs, extra)
 
 
 def pause(order, ready):
@@ -309,9 +305,9 @@
         student_head,
         teacher_head,
         [(True, k * piece, piece) for k in range(2, 4)]
-        + [(False, 0, width), (False, 0, half), (False, half, half)],
-    )
-    send, send0, send1 = chunks[4:]
+        + [(False, 0, width)] * 2,
+    )
+    send, send0 = chunks[4:]
     chunks = chunks[:4]
 
     crossed = [permuted(chunks[0], next_chip), permuted(chunks[1], next_chip), None, None]
@@ -328,7 +324,7 @@
     order = pause(order, [chunks[3]])
     crossed[2], send0, order = gate([crossed[2], send0, order], [])
     swapped[2] = permuted(crossed[2], other_plane)
-    late = [permuted(send0, extra_late), None]
+    late = permuted(send0, extra_late)
     own_scores, loss, own_part = meet(
         [student_head],
         [teacher_head],
@@ -358,8 +354,6 @@
     swapped[2], swapped[3], order = gate([swapped[2], swapped[3], order], [total])
     mine1 = jnp.concatenate([crossed[2], crossed[3], swapped[2], swapped[3]], axis=0)
     theirs1 = permuted(mine1, other_core)
-    send1, order = gate([send1, order], [])
-    late[1] = permuted(send1, extra_late)
     order = pause(order, [mine1])
     theirs1, order = gate([theirs1, order], [])
     pair = [mine1, theirs1]
@@ -370,26 +364,20 @@
     total = (keep + got.astype(jnp.float32)).astype(jnp.bfloat16)
     back1 = permuted(total, previous_chip)
 
-    extra_parts, extra_scores, extras = [], [], []
-    last = total
-    for k in range(2):
-        order = pause(order, [last])
-        late[k], order = gate([late[k], order], [])
-        ids = extra_id * width + k * half + ids_in[:half]
-        scores, loss, last, value = meet(
-            [late[k], early, k * half], None, ids, loss, [jnp.bfloat16], [order], from_late
-        )
-        extra_parts.append(permuted(last, extra_back))
-        extra_scores.append(scores)
-        extras.append(value)
+    order = pause(order, [total])
+    late, order = gate([late, order], [])
+    extra_scores, loss, extra_part, extra = meet(
+        [late, early, 0], None, extra_id * width + ids_in, loss, [jnp.bfloat16], [order], from_late
+    )
+    extra_part = permuted(extra_part, extra_back)
 
     rows_grad = rows_product(
-        [own_scores, scores0, scores1] + extra_scores,
-        [student_head, mine0, theirs0, mine1, theirs1] + extras,
+        [own_scores, scores0, scores1, extra_scores],
+        [student_head, mine0, theirs0, mine1, theirs1, extra],
         depth,
-        [last],
-    )
-    head_grad = head_total(at, own_part, [back0, back1], extra_parts)
+        [extra_scores],
+    )
+    head_grad = head_total(at, own_part, [back0, back1], extra_part)
     return (head_grad, rows_grad, loss[0])
 
 

time: 90.6 us -> 88.7 us (0.979)
  the two profiles are of different devices: /device:TPU:0 before, /device:TPU:23 now
where the time goes in v8:
time: 88.7 us; the launch traced here: 88.3 us
  Pallas kernels  27.6 us (31%)
  waiting for transfers between devices  24.3 us (27%)
  starting transfers between devices  20.6 us (23%)
  local copies, waits for them, and re-layouts  13.9 us (16%)
  between operations  1.32 us (1%)
    ppermute x17, waiting for transfers between devices, permuted(): return lax.ppermute(value, BOTH, pairs)  24.3 us
    ppermute x17, starting transfers between devices, permuted(): return lax.ppermute(value, BOTH, pairs)  20.6 us
    pallas_call x4, Pallas kernels, meeting(): pl.pallas_call(kernel, out_shape=out_shape, in_specs=[whole] * (7 + piece...  17 us
    unnamed x60, local copies, waits for them, and re-layouts  12.9 us
    pallas_call x1, Pallas kernels, rows_product(): pl.pallas_call(kernel, grid=(4,), out_shape=jax.ShapeDtypeStruct((count,...  6.34 us
    pallas_call x2, Pallas kernels, packed(): pl.pallas_call(kernel, out_shape=[jax.ShapeDtypeStruct((rows, depth + dep...  3.26 us
  transfers between devices with their start and end apart: 17, of which 9 were waited for; matrix products, arithmetic and copies ran while one was open for 2% of the time, Pallas kernels for 29%

profile of v8, /device:TPU:23, one launch (start us, length us, event | category | flops | bytes accessed | tf_op | source)
XLA Modules:
  0.0 88.3 jit_solution(7039262493907505584)
XLA Ops:
  0.6 1.3 %copy-done.1 = bf16[128,4608]{1,0:T(8,128)(2,1)S(1)} copy-done((bf16[128,4608]{1,0:T(8,128)(2,1)S(1)}, bf16[128,4608]{1,0:T(8,128)(2,1)}, u32[]{:S(2)}) %copy-start.1) | copy-done | bytes 1179672
  1.9 1.2 %copy-done.5 = bf16[128,3584]{1,0:T(8,128)(2,1)S(1)} copy-done((bf16[128,3584]{1,0:T(8,128)(2,1)S(1)}, bf16[128,3584]{1,0:T(8,128)(2,1)}, u32[]{:S(2)}) %copy-start.5) | copy-done | bytes 917528
  3.1 0.8 shard_map.94
  3.9 1.3 %collective-permute-start.2 = (bf16[16,8192]{1,0:T(8,128)(2,1)}, bf16[16,8192]{1,0:T(8,128)(2,1)S(1)}, u32[]{:S(2)}, u32[]{:S(2)}) collective-permute-start(bf16[16,8192]{1,0:T(8,128)(2,1)} %get-tuple-element.56), channel_id=1, source_target_pairs={{0,2},{1,3},{2,4},{3,5},{4,6},{5,7},{6,8},{7,9},{8,10},{9,11},{10,... | collective-permute-start | bytes 786440 | tf_op jit(solution)/shard_map/ppermute | solution.py:24
  5.2 1.2 %collective-permute-start = (bf16[16,8192]{1,0:T(8,128)(2,1)}, bf16[16,8192]{1,0:T(8,128)(2,1)S(1)}, u32[]{:S(2)}, u32[]{:S(2)}) collective-permute-start(bf16[16,8192]{1,0:T(8,128)(2,1)} %get-tuple-element.52.refs_1_), channel_id=1, source_target_pairs={{0,2},{1,3},{2,4},{3,5},{4,6},{5,7},{6,8},{7,9},{8,10},{9,11},{10,... | collective-permute-start | bytes 786440 | tf_op jit(solution)/shard_map/ppermute | solution.py:24
  6.5 2.4 %shard_map.95 = (bf16[16,8192]{1,0:T(8,128)(2,1)S(1)}, bf16[16,8192]{1,0:T(8,128)(2,1)S(1)}, bf16[128,8192]{1,0:T(8,128)(2,1)}, bf16[128,8192]{1,0:T(8,128)(2,1)}) custom-call(s32[1]{0:T(128)} %bitcast.at_ref, bf16[128,3584]{1,0:T(8,128)(2,1)S(1)} %copy-done.6, bf16[128,4608]{1,0:T(8,128)(2,1)S(1)} %copy-done.2), custom_call_target="tpu_custom_call" | custom-call | tf_op jit(solution)/shard_map/pallas_call | solution.py:95
  10.3 1.3 %collective-permute-start.6 = (bf16[128,8192]{1,0:T(8,128)(2,1)}, bf16[128,8192]{1,0:T(8,128)(2,1)}, u32[]{:S(2)}, u32[]{:S(2)}) collective-permute-start(bf16[128,8192]{1,0:T(8,128)(2,1)} %get-tuple-element.71), channel_id=1, source_target_pairs={{0,1},{1,4},{2,3},{4,5},{5,8},{6,7},{8,9},{9,12},{10,11},{12,13},{... | collective-permute-start | bytes 6291464 | tf_op jit(solution)/shard_map/ppermute | solution.py:24
  13.1 3.9 %collective-permute-done.refs_0_ = bf16[16,8192]{1,0:T(8,128)(2,1)S(1)} collective-permute-done((bf16[16,8192]{1,0:T(8,128)(2,1)}, bf16[16,8192]{1,0:T(8,128)(2,1)S(1)}, u32[]{:S(2)}, u32[]{:S(2)}) %collective-permute-start) | collective-permute-done | bytes 262176 | tf_op jit(solution)/shard_map/ppermute | solution.py:24
  17.0 0.9 %copy-done.14 = bf16[16,8192]{1,0:T(8,128)(2,1)S(1)} copy-done((bf16[16,8192]{1,0:T(8,128)(2,1)S(1)}, bf16[16,8192]{1,0:T(8,128)(2,1)}, u32[]{:S(2)}) %copy-start.14) | copy-done | bytes 262168
  17.9 0.7 copy-done.15
  18.6 2.2 %collective-permute-start.1 = (bf16[16,8192]{1,0:T(8,128)(2,1)}, bf16[16,8192]{1,0:T(8,128)(2,1)S(1)}, u32[]{:S(2)}, u32[]{:S(2)}) collective-permute-start(bf16[16,8192]{1,0:T(8,128)(2,1)} %copy-done.15), channel_id=1, source_target_pairs={{0,2},{1,3},{2,4},{3,5},{4,6},{5,7},{6,8},{7,9},{8,10},{9,11},{10,... | collective-permute-start | bytes 786440 | tf_op jit(solution)/shard_map/ppermute | solution.py:24
  20.8 1.0 %copy-done.16 = bf16[16,8192]{1,0:T(8,128)(2,1)S(1)} copy-done((bf16[16,8192]{1,0:T(8,128)(2,1)S(1)}, bf16[16,8192]{1,0:T(8,128)(2,1)}, u32[]{:S(2)}) %copy-start.16) | copy-done | bytes 262168
  23.7 1.5 %collective-permute-done.1.refs_0_ = bf16[16,8192]{1,0:T(8,128)(2,1)S(1)} collective-permute-done((bf16[16,8192]{1,0:T(8,128)(2,1)}, bf16[16,8192]{1,0:T(8,128)(2,1)S(1)}, u32[]{:S(2)}, u32[]{:S(2)}) %collective-permute-start.1) | collective-permute-done | bytes 262176 | tf_op jit(solution)/shard_map/ppermute | solution.py:24
  25.4 1.1 %copy-done = bf16[512,3584]{1,0:T(8,128)(2,1)S(1)} copy-done((bf16[512,3584]{1,0:T(8,128)(2,1)S(1)}, bf16[512,3584]{1,0:T(8,128)(2,1)}, u32[]{:S(2)}) %copy-start) | copy-done | bytes 3670040
  26.5 3.6 %shard_map.102 = (bf16[512,128]{1,0:T(8,128)(2,1)S(1)}, f32[8,512]{1,0:T(8,128)S(1)}, f32[128,3584]{1,0:T(8,128)S(1)}) custom-call(bf16[512,3584]{1,0:T(8,128)(2,1)S(1)} %copy-done, bf16[512,4608]{1,0:T(8,128)(2,1)S(1)} %bitcast.11, f32[512,1]{1,0:T(8,128)S(1)} %copy.48.refs_2_, f32[512,1]{1,0:T(8,128)S(1)} %copy.49.refs_3_, s32[512,1]{1,0:T(8,128)S(1)} %copy.50.refs_4_, ...), custom_call_target="tpu_custom_call" | custom-call | tf_op jit(solution)/shard_map/pallas_call | solution.py:227
  30.2 1.3 %copy-done.9 = f32[128,3584]{1,0:T(8,128)} copy-done((f32[128,3584]{1,0:T(8,128)}, f32[128,3584]{1,0:T(8,128)S(1)}, u32[]{:S(2)}) %copy-start.9) | copy-done | bytes 1835032
  31.5 1.9 %collective-permute-done.4.refs_1_ = bf16[16,8192]{1,0:T(8,128)(2,1)S(1)} collective-permute-done((bf16[16,8192]{1,0:T(8,128)(2,1)S(1)}, bf16[16,8192]{1,0:T(8,128)(2,1)S(1)}, u32[]{:S(2)}, u32[]{:S(2)}) %collective-permute-start.4) | collective-permute-done | bytes 262176 | tf_op jit(solution)/shard_map/ppermute | solution.py:24
  33.4 10.1 %collective-permute-start.15 = (bf16[128,8192]{1,0:T(8,128)(2,1)}, bf16[128,8192]{1,0:T(8,128)(2,1)}, u32[]{:S(2)}, u32[]{:S(2)}) collective-permute-start(bf16[128,8192]{1,0:T(8,128)(2,1)} %get-tuple-element.67.refs_2_), channel_id=1, source_target_pairs={{3,6},{7,10},{11,14},{15,2},{19,22},{23,26},{27,30},{31,18}} | collective-permute-start | bytes 6291464 | tf_op jit(solution)/shard_map/ppermute | solution.py:24
  43.9 2.3 %collective-permute-done.5.refs_0_ = bf16[64,8192]{1,0:T(8,128)(2,1)S(1)} collective-permute-done((bf16[64,8192]{1,0:T(8,128)(2,1)S(1)}, bf16[64,8192]{1,0:T(8,128)(2,1)S(1)}, u32[]{:S(2)}, u32[]{:S(2)}) %collective-permute-start.5) | collective-permute-done | bytes 1048608 | tf_op jit(solution)/shard_map/ppermute | solution.py:24
  46.2 3.6 %shard_map.109 = (bf16[512,128]{1,0:T(8,128)(2,1)S(1)}, f32[8,512]{1,0:T(8,128)S(1)}, f32[64,3584]{1,0:T(8,128)S(1)}, bf16[64,3584]{1,0:T(8,128)(2,1)S(1)}) custom-call(bf16[512,3584]{1,0:T(8,128)(2,1)S(1)} %copy-done, bf16[512,4608]{1,0:T(8,128)(2,1)S(1)} %bitcast.11, f32[512,1]{1,0:T(8,128)S(1)} %copy.48.refs_2_, f32[512,1]{1,0:T(8,128)S(1)} %copy.49.refs_3_, ...), custom_call_target="tpu_custom_call" | custom-call | tf_op jit(solution)/shard_map/pallas_call | solution.py:227
  50.5 1.2 %collective-permute-done.8.refs_0_ = bf16[64,3584]{1,0:T(8,128)(2,1)S(1)} collective-permute-done((bf16[64,3584]{1,0:T(8,128)(2,1)S(1)}, bf16[64,3584]{1,0:T(8,128)(2,1)S(1)}, u32[]{:S(2)}, u32[]{:S(2)}) %collective-permute-start.8) | collective-permute-done | bytes 458784 | tf_op jit(solution)/shard_map/ppermute | solution.py:24
  52.5 2.3 %collective-permute-done.12.refs_0_ = bf16[64,8192]{1,0:T(8,128)(2,1)S(1)} collective-permute-done((bf16[64,8192]{1,0:T(8,128)(2,1)S(1)}, bf16[64,8192]{1,0:T(8,128)(2,1)S(1)}, u32[]{:S(2)}, u32[]{:S(2)}) %collective-permute-start.12) | collective-permute-done | bytes 1048608 | tf_op jit(solution)/shard_map/ppermute | solution.py:24
  54.8 3.6 %shard_map.115 = (bf16[512,128]{1,0:T(8,128)(2,1)S(1)}, f32[8,512]{1,0:T(8,128)S(1)}, f32[64,3584]{1,0:T(8,128)S(1)}, bf16[64,3584]{1,0:T(8,128)(2,1)S(1)}) custom-call(bf16[512,3584]{1,0:T(8,128)(2,1)S(1)} %copy-done, bf16[512,4608]{1,0:T(8,128)(2,1)S(1)} %bitcast.11, f32[512,1]{1,0:T(8,128)S(1)} %copy.48.refs_2_, f32[512,1]{1,0:T(8,128)S(1)} %copy.49.refs_3_, ...), custom_call_target="tpu_custom_call" | custom-call | tf_op jit(solution)/shard_map/pallas_call | solution.py:227
  59.1 1.2 %collective-permute-done.13.refs_0_ = bf16[64,3584]{1,0:T(8,128)(2,1)S(1)} collective-permute-done((bf16[64,3584]{1,0:T(8,128)(2,1)S(1)}, bf16[64,3584]{1,0:T(8,128)(2,1)S(1)}, u32[]{:S(2)}, u32[]{:S(2)}) %collective-permute-start.13) | collective-permute-done | bytes 458784 | tf_op jit(solution)/shard_map/ppermute | solution.py:24
  60.4 0.8 collective-permute-start.14
  61.2 4.1 %collective-permute-done.15.refs_0_ = bf16[128,8192]{1,0:T(8,128)(2,1)} collective-permute-done((bf16[128,8192]{1,0:T(8,128)(2,1)}, bf16[128,8192]{1,0:T(8,128)(2,1)}, u32[]{:S(2)}, u32[]{:S(2)}) %collective-permute-start.15) | collective-permute-done | bytes 2097184 | tf_op jit(solution)/shard_map/ppermute | solution.py:24
  65.4 6.1 %shard_map.120 = (bf16[512,128]{1,0:T(8,128)(2,1)S(1)}, f32[8,512]{1,0:T(8,128)S(1)}, bf16[128,3584]{1,0:T(8,128)(2,1)S(1)}, bf16[128,8192]{1,0:T(8,128)(2,1)S(1)}) custom-call(bf16[512,3584]{1,0:T(8,128)(2,1)S(1)} %copy-done, bf16[512,4608]{1,0:T(8,128)(2,1)S(1)} %bitcast.11, f32[512,1]{1,0:T(8,128)S(1)} %copy.48.refs_2_, f32[512,1]{1,0:T(8,128)S(1)} %copy.49.refs_3_, ...), custom_call_target="tpu_custom_call" | custom-call | tf_op jit(solution)/shard_map/pallas_call | solution.py:227
  71.5 1.3 %copy-done.17 = bf16[128,8192]{1,0:T(8,128)(2,1)} copy-done((bf16[128,8192]{1,0:T(8,128)(2,1)}, bf16[128,8192]{1,0:T(8,128)(2,1)S(1)}, u32[]{:S(2)}) %copy-start.17) | copy-done | bytes 2097176
  73.5 0.8 collective-permute-start.16
  74.3 6.3 %shard_map.122 = bf16[512,3584]{1,0:T(8,128)(2,1)} custom-call(bf16[512,128]{1,0:T(8,128)(2,1)} %copy-done.18, bf16[512,128]{1,0:T(8,128)(2,1)} %copy-done.19, bf16[512,128]{1,0:T(8,128)(2,1)} %copy-done.20, bf16[512,128]{1,0:T(8,128)(2,1)} %copy-done.21, bf16[128,3584]{1,0:T(8,128)(2,1)} %refs_4_.1, bf16[64,8192]{1,0:T(8,128)(2,1)} %copy-done.8, ...), custom_call_target="tpu_custom_call" | custom-call | flops 30000001024 | tf_op jit(solution)/shard_map/pallas_call | solution.py:258
  81.2 5.9 %collective-permute-done.16.extra_ref = bf16[128,3584]{1,0:T(8,128)(2,1)S(1)} collective-permute-done((bf16[128,3584]{1,0:T(8,128)(2,1)S(1)}, bf16[128,3584]{1,0:T(8,128)(2,1)S(1)}, u32[]{:S(2)}, u32[]{:S(2)}) %collective-permute-start.16) | collective-permute-done | bytes 917536 | tf_op jit(solution)/shard_map/ppermute | solution.py:24
  87.1 1.0 %shard_map.121 = bf16[128,3584]{1,0:T(8,128)(2,1)} custom-call(s32[1]{0:T(128)} %bitcast.at_ref, f32[128,3584]{1,0:T(8,128)S(1)} %copy-done.10, bf16[64,3584]{1,0:T(8,128)(2,1)S(1)} %collective-permute-done.9.back0, bf16[64,3584]{1,0:T(8,128)(2,1)S(1)} %collective-permute-done.14.back1, bf16[128,3584]{1,0:T(8,128)(2,1)S(1)} %collective-permute-done.16.extra_ref), custom_call_target="tpu_custom_call" | custom-call | tf_op jit(solution)/shard_map/pallas_call | solution.py:135
  (112 shorter events, 8.7 us)
Async XLA Ops:
  0.6 1.3 %copy-start.1 = (bf16[128,4608]{1,0:T(8,128)(2,1)S(1)}, bf16[128,4608]{1,0:T(8,128)(2,1)}, u32[]{:S(2)}) copy-start(bf16[128,4608]{1,0:T(8,128)(2,1)} %refs_8_.1) | copy-start | bytes 3538948
  1.9 1.2 %copy-start.5 = (bf16[128,3584]{1,0:T(8,128)(2,1)S(1)}, bf16[128,3584]{1,0:T(8,128)(2,1)}, u32[]{:S(2)}) copy-start(bf16[128,3584]{1,0:T(8,128)(2,1)} %refs_4_.1) | copy-start | bytes 2752516
  3.1 3.4 %copy-start.2 = (bf16[128,4608]{1,0:T(8,128)(2,1)S(1)}, bf16[128,4608]{1,0:T(8,128)(2,1)}, u32[]{:S(2)}) copy-start(bf16[128,4608]{1,0:T(8,128)(2,1)} %refs_8_.1) | copy-start | bytes 3538948
  3.1 3.4 %copy-start.6 = (bf16[128,3584]{1,0:T(8,128)(2,1)S(1)}, bf16[128,3584]{1,0:T(8,128)(2,1)}, u32[]{:S(2)}) copy-start(bf16[128,3584]{1,0:T(8,128)(2,1)} %refs_4_.1) | copy-start | bytes 2752516
  3.9 18.1 %collective-permute-start.2 = (bf16[16,8192]{1,0:T(8,128)(2,1)}, bf16[16,8192]{1,0:T(8,128)(2,1)S(1)}, u32[]{:S(2)}, u32[]{:S(2)}) collective-permute-start(bf16[16,8192]{1,0:T(8,128)(2,1)} %get-tuple-element.56), channel_id=1, source_target_pairs={{0,2},{1,3},{2,4},{3,5},{4,6},{5,7},{6,8},{7,9},{8,10},{9,11},{10,... | collective-permute-start | bytes 786440 | tf_op jit(solution)/shard_map/ppermute | solution.py:24
  5.2 11.7 %collective-permute-start = (bf16[16,8192]{1,0:T(8,128)(2,1)}, bf16[16,8192]{1,0:T(8,128)(2,1)S(1)}, u32[]{:S(2)}, u32[]{:S(2)}) collective-permute-start(bf16[16,8192]{1,0:T(8,128)(2,1)} %get-tuple-element.52.refs_1_), channel_id=1, source_target_pairs={{0,2},{1,3},{2,4},{3,5},{4,6},{5,7},{6,8},{7,9},{8,10},{9,11},{10,... | collective-permute-start | bytes 786440 | tf_op jit(solution)/shard_map/ppermute | solution.py:24
  10.3 35.9 %collective-permute-start.6 = (bf16[128,8192]{1,0:T(8,128)(2,1)}, bf16[128,8192]{1,0:T(8,128)(2,1)}, u32[]{:S(2)}, u32[]{:S(2)}) collective-permute-start(bf16[128,8192]{1,0:T(8,128)(2,1)} %get-tuple-element.71), channel_id=1, source_target_pairs={{0,1},{1,4},{2,3},{4,5},{5,8},{6,7},{8,9},{9,12},{10,11},{12,13},{... | collective-permute-start | bytes 6291464 | tf_op jit(solution)/shard_map/ppermute | solution.py:24
  18.6 6.5 %collective-permute-start.1 = (bf16[16,8192]{1,0:T(8,128)(2,1)}, bf16[16,8192]{1,0:T(8,128)(2,1)S(1)}, u32[]{:S(2)}, u32[]{:S(2)}) collective-permute-start(bf16[16,8192]{1,0:T(8,128)(2,1)} %copy-done.15), channel_id=1, source_target_pairs={{0,2},{1,3},{2,4},{3,5},{4,6},{5,7},{6,8},{7,9},{8,10},{9,11},{10,... | collective-permute-start | bytes 786440 | tf_op jit(solution)/shard_map/ppermute | solution.py:24
  21.8 21.6 %collective-permute-start.3 = (bf16[16,8192]{1,0:T(8,128)(2,1)S(1)}, bf16[16,8192]{1,0:T(8,128)(2,1)S(1)}, u32[]{:S(2)}, u32[]{:S(2)}) collective-permute-start(bf16[16,8192]{1,0:T(8,128)(2,1)S(1)} %get-tuple-element.64), channel_id=1, source_target_pairs={{0,16},{1,17},{2,18},{3,19},{4,20},{5,21},{6,22},{7,23},{8,24},{9,... | collective-permute-start | bytes 786440 | tf_op jit(solution)/shard_map/ppermute | solution.py:24
  22.7 20.9 %collective-permute-start.7 = (bf16[16,8192]{1,0:T(8,128)(2,1)S(1)}, bf16[16,8192]{1,0:T(8,128)(2,1)S(1)}, u32[]{:S(2)}, u32[]{:S(2)}) collective-permute-start(bf16[16,8192]{1,0:T(8,128)(2,1)S(1)} %get-tuple-element.60.refs_1_), channel_id=1, source_target_pairs={{0,2},{1,3},{2,4},{3,5},{4,6},{5,7},{6,8},{7,9},{8,10},{9,11},{10,... | collective-permute-start | bytes 786440 | tf_op jit(solution)/shard_map/ppermute | solution.py:24
  23.0 2.4 %slice-start = ((s8[4718592]{0:T(1024)(128)(4,1)}), s8[4194304]{0:T(1024)(128)(4,1)S(1)}, s32[]{:S(2)}) async-start(s8[4718592]{0:T(1024)(128)(4,1)} %bitcast.10), calls=%async_computation | async-start | bytes 8388608
  23.0 2.4 %slice-start.1 = ((s8[4718592]{0:T(1024)(128)(4,1)}), s8[524288]{0:T(1024)(128)(4,1)S(1)}, s32[]{:S(2)}) async-start(s8[4718592]{0:T(1024)(128)(4,1)} %bitcast.10), calls=%async_computation.1 | async-start | bytes 1048576
  23.0 3.5 %copy-start = (bf16[512,3584]{1,0:T(8,128)(2,1)S(1)}, bf16[512,3584]{1,0:T(8,128)(2,1)}, u32[]{:S(2)}) copy-start(bf16[512,3584]{1,0:T(8,128)(2,1)} %refs_0_.7) | copy-start | bytes 11010052
  23.1 10.3 %collective-permute-start.4 = (bf16[16,8192]{1,0:T(8,128)(2,1)S(1)}, bf16[16,8192]{1,0:T(8,128)(2,1)S(1)}, u32[]{:S(2)}, u32[]{:S(2)}) collective-permute-start(bf16[16,8192]{1,0:T(8,128)(2,1)S(1)} %get-tuple-element.65), channel_id=1, source_target_pairs={{0,16},{1,17},{2,18},{3,19},{4,20},{5,21},{6,22},{7,23},{8,24},{9,... | collective-permute-start | bytes 786440 | tf_op jit(solution)/shard_map/ppermute | solution.py:24
  25.2 26.8 %collective-permute-start.10 = (bf16[16,8192]{1,0:T(8,128)(2,1)S(1)}, bf16[16,8192]{1,0:T(8,128)(2,1)S(1)}, u32[]{:S(2)}, u32[]{:S(2)}) collective-permute-start(bf16[16,8192]{1,0:T(8,128)(2,1)S(1)} %get-tuple-element.66.refs_1_), channel_id=1, source_target_pairs={{0,16},{1,17},{2,18},{3,19},{4,20},{5,21},{6,22},{7,23},{8,24},{9,... | collective-permute-start | bytes 786440 | tf_op jit(solution)/shard_map/ppermute | solution.py:24
  30.1 1.3 %copy-start.9 = (f32[128,3584]{1,0:T(8,128)}, f32[128,3584]{1,0:T(8,128)S(1)}, u32[]{:S(2)}) copy-start(f32[128,3584]{1,0:T(8,128)S(1)} %get-tuple-element.62.own_ref) | copy-start | bytes 5505028
  30.1 1.3 %copy-start.18 = (bf16[512,128]{1,0:T(8,128)(2,1)}, bf16[512,128]{1,0:T(8,128)(2,1)S(1)}, u32[]{:S(2)}) copy-start(bf16[512,128]{1,0:T(8,128)(2,1)S(1)} %get-tuple-element.68.refs_3_.refs_0_) | copy-start | bytes 393220
  33.4 32.0 %collective-permute-start.15 = (bf16[128,8192]{1,0:T(8,128)(2,1)}, bf16[128,8192]{1,0:T(8,128)(2,1)}, u32[]{:S(2)}, u32[]{:S(2)}) collective-permute-start(bf16[128,8192]{1,0:T(8,128)(2,1)} %get-tuple-element.67.refs_2_), channel_id=1, source_target_pairs={{3,6},{7,10},{11,14},{15,2},{19,22},{23,26},{27,30},{31,18}} | collective-permute-start | bytes 6291464 | tf_op jit(solution)/shard_map/ppermute | solution.py:24
  43.5 2.7 %copy-start.8 = (bf16[64,8192]{1,0:T(8,128)(2,1)}, bf16[64,8192]{1,0:T(8,128)(2,1)S(1)}, u32[]{:S(2)}) copy-start(bf16[64,8192]{1,0:T(8,128)(2,1)S(1)} %constant_dynamic-update-slice_fusion.refs_1_.refs_7_.refs_9_.refs_5_) | copy-start | bytes 3145732
  43.5 2.7 %collective-permute-start.5 = (bf16[64,8192]{1,0:T(8,128)(2,1)S(1)}, bf16[64,8192]{1,0:T(8,128)(2,1)S(1)}, u32[]{:S(2)}, u32[]{:S(2)}) collective-permute-start(bf16[64,8192]{1,0:T(8,128)(2,1)S(1)} %constant_dynamic-update-slice_fusion.refs_1_.refs_7_.refs_9_.refs_5_), channel_id=1, source_target_pairs={{0,1},{1,0},{2,3},{3,2},{4,5},{5,4},{6,7},{7,6},{8,9},{9,8},{10,11... | collective-permute-start | bytes 3145736 | tf_op jit(solution)/shard_map/ppermute | solution.py:24
  43.6 8.3 %collective-permute-start.11 = (bf16[16,8192]{1,0:T(8,128)(2,1)S(1)}, bf16[16,8192]{1,0:T(8,128)(2,1)S(1)}, u32[]{:S(2)}, u32[]{:S(2)}) collective-permute-start(bf16[16,8192]{1,0:T(8,128)(2,1)S(1)} %get-tuple-element.80), channel_id=1, source_target_pairs={{0,16},{1,17},{2,18},{3,19},{4,20},{5,21},{6,22},{7,23},{8,24},{9,... | collective-permute-start | bytes 786440 | tf_op jit(solution)/shard_map/ppermute | solution.py:24
  46.2 3.6 %copy-start.3 = (bf16[64,8192]{1,0:T(8,128)(2,1)}, bf16[64,8192]{1,0:T(8,128)(2,1)S(1)}, u32[]{:S(2)}) copy-start(bf16[64,8192]{1,0:T(8,128)(2,1)S(1)} %get-tuple-element.74.refs_8_.refs_10_.refs_6_) | copy-start | bytes 3145732
  49.9 1.9 %collective-permute-start.8 = (bf16[64,3584]{1,0:T(8,128)(2,1)S(1)}, bf16[64,3584]{1,0:T(8,128)(2,1)S(1)}, u32[]{:S(2)}, u32[]{:S(2)}) collective-permute-start(bf16[64,3584]{1,0:T(8,128)(2,1)S(1)} %get-tuple-element.77.refs_1_), channel_id=1, source_target_pairs={{0,1},{1,0},{2,3},{3,2},{4,5},{5,4},{6,7},{7,6},{8,9},{9,8},{10,11... | collective-permute-start | bytes 1376264 | tf_op jit(solution)/shard_map/ppermute | solution.py:24
  51.9 29.3 %collective-permute-start.9 = (bf16[64,3584]{1,0:T(8,128)(2,1)S(1)}, bf16[64,3584]{1,0:T(8,128)(2,1)S(1)}, u32[]{:S(2)}, u32[]{:S(2)}) collective-permute-start(bf16[64,3584]{1,0:T(8,128)(2,1)S(1)} %add_convert_fusion.1.refs_3_), channel_id=1, source_target_pairs={{0,14},{1,15},{2,0},{3,1},{4,2},{5,3},{6,4},{7,5},{8,6},{9,7},{10,... | collective-permute-start | bytes 1376264 | tf_op jit(solution)/shard_map/ppermute | solution.py:24
  52.0 2.8 %copy-start.7 = (bf16[64,8192]{1,0:T(8,128)(2,1)}, bf16[64,8192]{1,0:T(8,128)(2,1)S(1)}, u32[]{:S(2)}) copy-start(bf16[64,8192]{1,0:T(8,128)(2,1)S(1)} %constant_dynamic-update-slice_fusion.4.refs_1_.refs_7_.refs_9_) | copy-start | bytes 3145732
  52.0 2.8 %collective-permute-start.12 = (bf16[64,8192]{1,0:T(8,128)(2,1)S(1)}, bf16[64,8192]{1,0:T(8,128)(2,1)S(1)}, u32[]{:S(2)}, u32[]{:S(2)}) collective-permute-start(bf16[64,8192]{1,0:T(8,128)(2,1)S(1)} %constant_dynamic-update-slice_fusion.4.refs_1_.refs_7_.refs_9_), channel_id=1, source_target_pairs={{0,1},{1,0},{2,3},{3,2},{4,5},{5,4},{6,7},{7,6},{8,9},{9,8},{10,11... | collective-permute-start | bytes 3145736 | tf_op jit(solution)/shard_map/ppermute | solution.py:24
  54.8 3.6 %copy-start.4 = (bf16[64,8192]{1,0:T(8,128)(2,1)}, bf16[64,8192]{1,0:T(8,128)(2,1)S(1)}, u32[]{:S(2)}) copy-start(bf16[64,8192]{1,0:T(8,128)(2,1)S(1)} %get-tuple-element.85.refs_8_.refs_10_) | copy-start | bytes 3145732
  58.5 1.9 %collective-permute-start.13 = (bf16[64,3584]{1,0:T(8,128)(2,1)S(1)}, bf16[64,3584]{1,0:T(8,128)(2,1)S(1)}, u32[]{:S(2)}, u32[]{:S(2)}) collective-permute-start(bf16[64,3584]{1,0:T(8,128)(2,1)S(1)} %get-tuple-element.88.refs_1_), channel_id=1, source_target_pairs={{0,1},{1,0},{2,3},{3,2},{4,5},{5,4},{6,7},{7,6},{8,9},{9,8},{10,11... | collective-permute-start | bytes 1376264 | tf_op jit(solution)/shard_map/ppermute | solution.py:24
  60.4 20.8 %collective-permute-start.14 = (bf16[64,3584]{1,0:T(8,128)(2,1)S(1)}, bf16[64,3584]{1,0:T(8,128)(2,1)S(1)}, u32[]{:S(2)}, u32[]{:S(2)}) collective-permute-start(bf16[64,3584]{1,0:T(8,128)(2,1)S(1)} %add_convert_fusion.refs_1_), channel_id=1, source_target_pairs={{0,14},{1,15},{2,0},{3,1},{4,2},{5,3},{6,4},{7,5},{8,6},{9,7},{10,... | collective-permute-start | bytes 1376264 | tf_op jit(solution)/shard_map/ppermute | solution.py:24
  71.5 1.3 %copy-start.17 = (bf16[128,8192]{1,0:T(8,128)(2,1)}, bf16[128,8192]{1,0:T(8,128)(2,1)S(1)}, u32[]{:S(2)}) copy-start(bf16[128,8192]{1,0:T(8,128)(2,1)S(1)} %get-tuple-element.99.refs_9_) | copy-start | bytes 6291460
  73.5 13.6 %collective-permute-start.16 = (bf16[128,3584]{1,0:T(8,128)(2,1)S(1)}, bf16[128,3584]{1,0:T(8,128)(2,1)S(1)}, u32[]{:S(2)}, u32[]{:S(2)}) collective-permute-start(bf16[128,3584]{1,0:T(8,128)(2,1)S(1)} %get-tuple-element.95), channel_id=1, source_target_pairs={{0,13},{1,0},{2,15},{3,2},{4,1},{5,4},{6,3},{7,6},{8,5},{9,8},{10,... | collective-permute-start | bytes 2752520 | tf_op jit(solution)/shard_map/ppermute | solution.py:24
  74.3 12.8 %copy-start.10 = (f32[128,3584]{1,0:T(8,128)S(1)}, f32[128,3584]{1,0:T(8,128)}, u32[]{:S(2)}) copy-start(f32[128,3584]{1,0:T(8,128)} %copy-done.9) | copy-start | bytes 5505028
  (12 other events, 9.3 us)

commit v9 on v8

--- a/solution.py
+++ b/solution.py
@@ -300,6 +300,8 @@
     at = jnp.reshape(plane * half, (1,)).astype(jnp.int32)
     chunks = packed(at, student_head, teacher_head, [(True, k * piece, piece) for k in range(2)])
     chunks = list(chunks)
+    chunks[0], = gate([chunks[0]], [])
+    chunks[1], = gate([chunks[1]], [chunks[0]])
     chunks += packed(
         at,
         student_head,
@@ -310,18 +312,16 @@
     send, send0 = chunks[4:]
     chunks = chunks[:4]
 
-    crossed = [permuted(chunks[0], next_chip), permuted(chunks[1], next_chip), None, None]
+    crossed = [permuted(chunk, next_chip) for chunk in chunks]
     early = permuted(send, extra_early)
     swapped = [None] * 4
     order = pause(order, [chunks[0]])
-    crossed[0], chunks[2], order = gate([crossed[0], chunks[2], order], [])
+    crossed[0], order = gate([crossed[0], order], [])
     swapped[0] = permuted(crossed[0], other_plane)
-    crossed[2] = permuted(chunks[2], next_chip)
-    order = pause(order, [chunks[2]])
-    crossed[1], chunks[3], order = gate([crossed[1], chunks[3], order], [])
+    order = pause(order, [crossed[0]])
+    crossed[1], order = gate([crossed[1], order], [])
     swapped[1] = permuted(crossed[1], other_plane)
-    crossed[3] = permuted(chunks[3], next_chip)
-    order = pause(order, [chunks[3]])
+    order = pause(order, [crossed[1]])
     crossed[2], send0, order = gate([crossed[2], send0, order], [])
     swapped[2] = permuted(crossed[2], other_plane)
     late = permuted(send0, extra_late)

time: 88.7 us -> 82.8 us (0.933)
  the two profiles are of different devices: /device:TPU:23 before, /device:TPU:27 now
where the time goes in v9:
time: 82.8 us; the launch traced here: 82.4 us
  Pallas kernels  27.6 us (33%)
  starting transfers between devices  21.8 us (26%)
  waiting for transfers between devices  20.1 us (24%)
  local copies, waits for them, and re-layouts  11.1 us (13%)
  between operations  1.33 us (2%)
    ppermute x17, starting transfers between devices, permuted(): return lax.ppermute(value, BOTH, pairs)  21.8 us
    ppermute x17, waiting for transfers between devices, permuted(): return lax.ppermute(value, BOTH, pairs)  20.1 us
    pallas_call x4, Pallas kernels, meeting(): pl.pallas_call(kernel, out_shape=out_shape, in_specs=[whole] * (7 + piece...  17 us
    unnamed x48, local copies, waits for them, and re-layouts  10.1 us
    pallas_call x1, Pallas kernels, rows_product(): pl.pallas_call(kernel, grid=(4,), out_shape=jax.ShapeDtypeStruct((count,...  6.34 us
    pallas_call x2, Pallas kernels, packed(): pl.pallas_call(kernel, out_shape=[jax.ShapeDtypeStruct((rows, depth + dep...  3.17 us
  transfers between devices with their start and end apart: 17, of which 8 were waited for; matrix products, arithmetic and copies ran while one was open for 6% of the time, Pallas kernels for 31%

profile of v9, /device:TPU:27, one launch (start us, length us, event | category | flops | bytes accessed | tf_op | source)
XLA Modules:
  0.0 82.4 jit_solution(4993834260506738674)
XLA Ops:
  0.6 1.3 %copy-done.1 = bf16[128,4608]{1,0:T(8,128)(2,1)S(1)} copy-done((bf16[128,4608]{1,0:T(8,128)(2,1)S(1)}, bf16[128,4608]{1,0:T(8,128)(2,1)}, u32[]{:S(2)}) %copy-start.1) | copy-done | bytes 1179672
  1.9 1.2 %copy-done.5 = bf16[128,3584]{1,0:T(8,128)(2,1)S(1)} copy-done((bf16[128,3584]{1,0:T(8,128)(2,1)S(1)}, bf16[128,3584]{1,0:T(8,128)(2,1)}, u32[]{:S(2)}) %copy-start.5) | copy-done | bytes 917528
  4.1 1.1 %collective-permute-start.1 = (bf16[16,8192]{1,0:T(8,128)(2,1)}, bf16[16,8192]{1,0:T(8,128)(2,1)}, u32[]{:S(2)}, u32[]{:S(2)}) collective-permute-start(bf16[16,8192]{1,0:T(8,128)(2,1)} %shard_map.97), channel_id=1, source_target_pairs={{0,2},{1,3},{2,4},{3,5},{4,6},{5,7},{6,8},{7,9},{8,10},{9,11},{10,... | collective-permute-start | bytes 786440 | tf_op jit(solution)/shard_map/ppermute | solution.py:24
  5.2 2.3 %shard_map.94 = (bf16[16,8192]{1,0:T(8,128)(2,1)}, bf16[16,8192]{1,0:T(8,128)(2,1)}, bf16[128,8192]{1,0:T(8,128)(2,1)}, bf16[128,8192]{1,0:T(8,128)(2,1)}) custom-call(s32[1]{0:T(128)} %bitcast.at_ref, bf16[128,3584]{1,0:T(8,128)(2,1)S(1)} %copy-done.6, bf16[128,4608]{1,0:T(8,128)(2,1)S(1)} %copy-done.2), custom_call_target="tpu_custom_call" | custom-call | tf_op jit(solution)/shard_map/pallas_call | solution.py:95
  7.5 1.3 %collective-permute-start = (bf16[16,8192]{1,0:T(8,128)(2,1)}, bf16[16,8192]{1,0:T(8,128)(2,1)S(1)}, u32[]{:S(2)}, u32[]{:S(2)}) collective-permute-start(bf16[16,8192]{1,0:T(8,128)(2,1)} %get-tuple-element.50), channel_id=1, source_target_pairs={{0,2},{1,3},{2,4},{3,5},{4,6},{5,7},{6,8},{7,9},{8,10},{9,11},{10,... | collective-permute-start | bytes 786440 | tf_op jit(solution)/shard_map/ppermute | solution.py:24
  8.8 1.2 %collective-permute-start.7 = (bf16[16,8192]{1,0:T(8,128)(2,1)}, bf16[16,8192]{1,0:T(8,128)(2,1)}, u32[]{:S(2)}, u32[]{:S(2)}) collective-permute-start(bf16[16,8192]{1,0:T(8,128)(2,1)} %get-tuple-element.67), channel_id=1, source_target_pairs={{0,2},{1,3},{2,4},{3,5},{4,6},{5,7},{6,8},{7,9},{8,10},{9,11},{10,... | collective-permute-start | bytes 786440 | tf_op jit(solution)/shard_map/ppermute | solution.py:24
  10.0 1.3 %collective-permute-start.6 = (bf16[128,8192]{1,0:T(8,128)(2,1)}, bf16[128,8192]{1,0:T(8,128)(2,1)}, u32[]{:S(2)}, u32[]{:S(2)}) collective-permute-start(bf16[128,8192]{1,0:T(8,128)(2,1)} %get-tuple-element.66), channel_id=1, source_target_pairs={{0,1},{1,4},{2,3},{4,5},{5,8},{6,7},{8,9},{9,12},{10,11},{12,13},{... | collective-permute-start | bytes 6291464 | tf_op jit(solution)/shard_map/ppermute | solution.py:24
  12.8 1.3 %collective-permute-start.3 = (bf16[16,8192]{1,0:T(8,128)(2,1)}, bf16[16,8192]{1,0:T(8,128)(2,1)S(1)}, u32[]{:S(2)}, u32[]{:S(2)}) collective-permute-start(bf16[16,8192]{1,0:T(8,128)(2,1)} %get-tuple-element.55.refs_1_), channel_id=1, source_target_pairs={{0,16},{1,17},{2,18},{3,19},{4,20},{5,21},{6,22},{7,23},{8,24},{9,... | collective-permute-start | bytes 786440 | tf_op jit(solution)/shard_map/ppermute | solution.py:24
  14.0 2.9 %collective-permute-done.1.refs_0_ = bf16[16,8192]{1,0:T(8,128)(2,1)} collective-permute-done((bf16[16,8192]{1,0:T(8,128)(2,1)}, bf16[16,8192]{1,0:T(8,128)(2,1)}, u32[]{:S(2)}, u32[]{:S(2)}) %collective-permute-start.1) | collective-permute-done | bytes 262176 | tf_op jit(solution)/shard_map/ppermute | solution.py:24
  17.0 1.2 %collective-permute-start.4 = (bf16[16,8192]{1,0:T(8,128)(2,1)}, bf16[16,8192]{1,0:T(8,128)(2,1)S(1)}, u32[]{:S(2)}, u32[]{:S(2)}) collective-permute-start(bf16[16,8192]{1,0:T(8,128)(2,1)} %get-tuple-element.57.refs_1_), channel_id=1, source_target_pairs={{0,16},{1,17},{2,18},{3,19},{4,20},{5,21},{6,22},{7,23},{8,24},{9,... | collective-permute-start | bytes 786440 | tf_op jit(solution)/shard_map/ppermute | solution.py:24
  18.2 1.1 %constant_dynamic-update-slice_fusion.3 = bf16[64,8192]{1,0:T(8,128)(2,1)S(1)} fusion(bf16[16,8192]{1,0:T(8,128)(2,1)} %get-tuple-element.55.refs_1_), kind=kLoop, calls=%fused_computation.5 | loop fusion | bytes 524288
  19.3 3.1 %collective-permute-done.refs_0_ = bf16[16,8192]{1,0:T(8,128)(2,1)S(1)} collective-permute-done((bf16[16,8192]{1,0:T(8,128)(2,1)}, bf16[16,8192]{1,0:T(8,128)(2,1)S(1)}, u32[]{:S(2)}, u32[]{:S(2)}) %collective-permute-start) | collective-permute-done | bytes 262176 | tf_op jit(solution)/shard_map/ppermute | solution.py:24
  22.5 1.2 %collective-permute-start.10 = (bf16[16,8192]{1,0:T(8,128)(2,1)S(1)}, bf16[16,8192]{1,0:T(8,128)(2,1)S(1)}, u32[]{:S(2)}, u32[]{:S(2)}) collective-permute-start(bf16[16,8192]{1,0:T(8,128)(2,1)S(1)} %get-tuple-element.61.refs_1_), channel_id=1, source_target_pairs={{0,16},{1,17},{2,18},{3,19},{4,20},{5,21},{6,22},{7,23},{8,24},{9,... | collective-permute-start | bytes 786440 | tf_op jit(solution)/shard_map/ppermute | solution.py:24
  23.8 3.6 %shard_map.104 = (bf16[512,128]{1,0:T(8,128)(2,1)S(1)}, f32[8,512]{1,0:T(8,128)S(1)}, f32[128,3584]{1,0:T(8,128)S(1)}) custom-call(bf16[512,3584]{1,0:T(8,128)(2,1)S(1)} %copy-done, bf16[512,4608]{1,0:T(8,128)(2,1)S(1)} %bitcast.11, f32[512,1]{1,0:T(8,128)S(1)} %copy.48.refs_2_, f32[512,1]{1,0:T(8,128)S(1)} %copy.49.refs_3_, s32[512,1]{1,0:T(8,128)S(1)} %copy.50.refs_4_, ...), custom_call_target="tpu_custom_call" | custom-call | tf_op jit(solution)/shard_map/pallas_call | solution.py:227
  27.4 1.3 %copy-done.9 = f32[128,3584]{1,0:T(8,128)} copy-done((f32[128,3584]{1,0:T(8,128)}, f32[128,3584]{1,0:T(8,128)S(1)}, u32[]{:S(2)}) %copy-start.9) | copy-done | bytes 1835032
  28.7 1.0 %constant_dynamic-update-slice_fusion.2 = bf16[64,8192]{1,0:T(8,128)(2,1)S(1)} fusion(bf16[64,8192]{1,0:T(8,128)(2,1)S(1)} %constant_dynamic-update-slice_fusion.3, bf16[16,8192]{1,0:T(8,128)(2,1)} %get-tuple-element.57.refs_1_), kind=kLoop, calls=%fused_computation.4 | loop fusion | bytes 524288
  29.7 6.1 %collective-permute-start.15 = (bf16[128,8192]{1,0:T(8,128)(2,1)}, bf16[128,8192]{1,0:T(8,128)(2,1)}, u32[]{:S(2)}, u32[]{:S(2)}) collective-permute-start(bf16[128,8192]{1,0:T(8,128)(2,1)} %get-tuple-element.62.refs_2_), channel_id=1, source_target_pairs={{3,6},{7,10},{11,14},{15,2},{19,22},{23,26},{27,30},{31,18}} | collective-permute-start | bytes 6291464 | tf_op jit(solution)/shard_map/ppermute | solution.py:24
  36.3 1.0 %constant_dynamic-update-slice_fusion.6 = bf16[64,8192]{1,0:T(8,128)(2,1)S(1)} fusion(bf16[64,8192]{1,0:T(8,128)(2,1)S(1)} %constant_dynamic-update-slice_fusion.7, bf16[16,8192]{1,0:T(8,128)(2,1)} %get-tuple-element.76), kind=kLoop, calls=%fused_computation.8 | loop fusion | bytes 524288
  37.3 1.3 %collective-permute-done.5.refs_0_ = bf16[64,8192]{1,0:T(8,128)(2,1)S(1)} collective-permute-done((bf16[64,8192]{1,0:T(8,128)(2,1)S(1)}, bf16[64,8192]{1,0:T(8,128)(2,1)S(1)}, u32[]{:S(2)}, u32[]{:S(2)}) %collective-permute-start.5) | collective-permute-done | bytes 1048608 | tf_op jit(solution)/shard_map/ppermute | solution.py:24
  38.6 3.6 %shard_map.111 = (bf16[512,128]{1,0:T(8,128)(2,1)S(1)}, f32[8,512]{1,0:T(8,128)S(1)}, f32[64,3584]{1,0:T(8,128)S(1)}, bf16[64,3584]{1,0:T(8,128)(2,1)S(1)}) custom-call(bf16[512,3584]{1,0:T(8,128)(2,1)S(1)} %copy-done, bf16[512,4608]{1,0:T(8,128)(2,1)S(1)} %bitcast.11, f32[512,1]{1,0:T(8,128)S(1)} %copy.48.refs_2_, f32[512,1]{1,0:T(8,128)S(1)} %copy.49.refs_3_, ...), custom_call_target="tpu_custom_call" | custom-call | tf_op jit(solution)/shard_map/pallas_call | solution.py:227
  42.9 1.2 %collective-permute-done.8.refs_0_ = bf16[64,3584]{1,0:T(8,128)(2,1)S(1)} collective-permute-done((bf16[64,3584]{1,0:T(8,128)(2,1)S(1)}, bf16[64,3584]{1,0:T(8,128)(2,1)S(1)}, u32[]{:S(2)}, u32[]{:S(2)}) %collective-permute-start.8) | collective-permute-done | bytes 458784 | tf_op jit(solution)/shard_map/ppermute | solution.py:24
  45.8 2.3 %collective-permute-done.12.refs_0_ = bf16[64,8192]{1,0:T(8,128)(2,1)S(1)} collective-permute-done((bf16[64,8192]{1,0:T(8,128)(2,1)S(1)}, bf16[64,8192]{1,0:T(8,128)(2,1)S(1)}, u32[]{:S(2)}, u32[]{:S(2)}) %collective-permute-start.12) | collective-permute-done | bytes 1048608 | tf_op jit(solution)/shard_map/ppermute | solution.py:24
  48.1 3.6 %shard_map.117 = (bf16[512,128]{1,0:T(8,128)(2,1)S(1)}, f32[8,512]{1,0:T(8,128)S(1)}, f32[64,3584]{1,0:T(8,128)S(1)}, bf16[64,3584]{1,0:T(8,128)(2,1)S(1)}) custom-call(bf16[512,3584]{1,0:T(8,128)(2,1)S(1)} %copy-done, bf16[512,4608]{1,0:T(8,128)(2,1)S(1)} %bitcast.11, f32[512,1]{1,0:T(8,128)S(1)} %copy.48.refs_2_, f32[512,1]{1,0:T(8,128)S(1)} %copy.49.refs_3_, ...), custom_call_target="tpu_custom_call" | custom-call | tf_op jit(solution)/shard_map/pallas_call | solution.py:227
  52.4 1.2 %collective-permute-done.13.refs_0_ = bf16[64,3584]{1,0:T(8,128)(2,1)S(1)} collective-permute-done((bf16[64,3584]{1,0:T(8,128)(2,1)S(1)}, bf16[64,3584]{1,0:T(8,128)(2,1)S(1)}, u32[]{:S(2)}, u32[]{:S(2)}) %collective-permute-start.13) | collective-permute-done | bytes 458784 | tf_op jit(solution)/shard_map/ppermute | solution.py:24
  53.7 1.8 %collective-permute-start.14 = (bf16[64,3584]{1,0:T(8,128)(2,1)S(1)}, bf16[64,3584]{1,0:T(8,128)(2,1)S(1)}, u32[]{:S(2)}, u32[]{:S(2)}) collective-permute-start(bf16[64,3584]{1,0:T(8,128)(2,1)S(1)} %add_convert_fusion.refs_1_), channel_id=1, source_target_pairs={{0,14},{1,15},{2,0},{3,1},{4,2},{5,3},{6,4},{7,5},{8,6},{9,7},{10,... | collective-permute-start | bytes 1376264 | tf_op jit(solution)/shard_map/ppermute | solution.py:24
  55.5 2.2 %collective-permute-done.15.refs_0_ = bf16[128,8192]{1,0:T(8,128)(2,1)} collective-permute-done((bf16[128,8192]{1,0:T(8,128)(2,1)}, bf16[128,8192]{1,0:T(8,128)(2,1)}, u32[]{:S(2)}, u32[]{:S(2)}) %collective-permute-start.15) | collective-permute-done | bytes 2097184 | tf_op jit(solution)/shard_map/ppermute | solution.py:24
  57.7 6.2 %shard_map.122 = (bf16[512,128]{1,0:T(8,128)(2,1)S(1)}, f32[8,512]{1,0:T(8,128)S(1)}, bf16[128,3584]{1,0:T(8,128)(2,1)S(1)}, bf16[128,8192]{1,0:T(8,128)(2,1)S(1)}) custom-call(bf16[512,3584]{1,0:T(8,128)(2,1)S(1)} %copy-done, bf16[512,4608]{1,0:T(8,128)(2,1)S(1)} %bitcast.11, f32[512,1]{1,0:T(8,128)S(1)} %copy.48.refs_2_, f32[512,1]{1,0:T(8,128)S(1)} %copy.49.refs_3_, ...), custom_call_target="tpu_custom_call" | custom-call | tf_op jit(solution)/shard_map/pallas_call | solution.py:227
  63.9 1.3 %copy-done.11 = bf16[128,8192]{1,0:T(8,128)(2,1)} copy-done((bf16[128,8192]{1,0:T(8,128)(2,1)}, bf16[128,8192]{1,0:T(8,128)(2,1)S(1)}, u32[]{:S(2)}) %copy-start.11) | copy-done | bytes 2097176
  65.9 2.7 %collective-permute-start.16 = (bf16[128,3584]{1,0:T(8,128)(2,1)S(1)}, bf16[128,3584]{1,0:T(8,128)(2,1)S(1)}, u32[]{:S(2)}, u32[]{:S(2)}) collective-permute-start(bf16[128,3584]{1,0:T(8,128)(2,1)S(1)} %get-tuple-element.91), channel_id=1, source_target_pairs={{0,13},{1,0},{2,15},{3,2},{4,1},{5,4},{6,3},{7,6},{8,5},{9,8},{10,... | collective-permute-start | bytes 2752520 | tf_op jit(solution)/shard_map/ppermute | solution.py:24
  68.5 6.3 %shard_map.124 = bf16[512,3584]{1,0:T(8,128)(2,1)} custom-call(bf16[512,128]{1,0:T(8,128)(2,1)} %copy-done.12, bf16[512,128]{1,0:T(8,128)(2,1)} %copy-done.13, bf16[512,128]{1,0:T(8,128)(2,1)} %copy-done.14, bf16[512,128]{1,0:T(8,128)(2,1)} %copy-done.15, bf16[128,3584]{1,0:T(8,128)(2,1)} %refs_4_.1, bf16[64,8192]{1,0:T(8,128)(2,1)} %copy-done.8, ...), custom_call_target="tpu_custom_call" | custom-call | flops 30000001024 | tf_op jit(solution)/shard_map/pallas_call | solution.py:258
  75.5 5.8 %collective-permute-done.16.extra_ref = bf16[128,3584]{1,0:T(8,128)(2,1)S(1)} collective-permute-done((bf16[128,3584]{1,0:T(8,128)(2,1)S(1)}, bf16[128,3584]{1,0:T(8,128)(2,1)S(1)}, u32[]{:S(2)}, u32[]{:S(2)}) %collective-permute-start.16) | collective-permute-done | bytes 917536 | tf_op jit(solution)/shard_map/ppermute | solution.py:24
  81.2 1.0 %shard_map.123 = bf16[128,3584]{1,0:T(8,128)(2,1)} custom-call(s32[1]{0:T(128)} %bitcast.at_ref, f32[128,3584]{1,0:T(8,128)S(1)} %copy-done.10, bf16[64,3584]{1,0:T(8,128)(2,1)S(1)} %collective-permute-done.9.back0, bf16[64,3584]{1,0:T(8,128)(2,1)S(1)} %collective-permute-done.14.back1, bf16[128,3584]{1,0:T(8,128)(2,1)S(1)} %collective-permute-done.16.extra_ref), custom_call_target="tpu_custom_call" | custom-call | tf_op jit(solution)/shard_map/pallas_call | solution.py:135
  (102 shorter events, 7.0 us)
Async XLA Ops:
  0.6 1.3 %copy-start.1 = (bf16[128,4608]{1,0:T(8,128)(2,1)S(1)}, bf16[128,4608]{1,0:T(8,128)(2,1)}, u32[]{:S(2)}) copy-start(bf16[128,4608]{1,0:T(8,128)(2,1)} %refs_8_.1) | copy-start | bytes 3538948
  1.9 1.2 %copy-start.5 = (bf16[128,3584]{1,0:T(8,128)(2,1)S(1)}, bf16[128,3584]{1,0:T(8,128)(2,1)}, u32[]{:S(2)}) copy-start(bf16[128,3584]{1,0:T(8,128)(2,1)} %refs_4_.1) | copy-start | bytes 2752516
  3.1 2.1 %copy-start.2 = (bf16[128,4608]{1,0:T(8,128)(2,1)S(1)}, bf16[128,4608]{1,0:T(8,128)(2,1)}, u32[]{:S(2)}) copy-start(bf16[128,4608]{1,0:T(8,128)(2,1)} %refs_8_.1) | copy-start | bytes 3538948
  3.1 2.1 %copy-start.6 = (bf16[128,3584]{1,0:T(8,128)(2,1)S(1)}, bf16[128,3584]{1,0:T(8,128)(2,1)}, u32[]{:S(2)}) copy-start(bf16[128,3584]{1,0:T(8,128)(2,1)} %refs_4_.1) | copy-start | bytes 2752516
  4.0 8.8 %collective-permute-start.2 = (bf16[16,8192]{1,0:T(8,128)(2,1)S(1)}, bf16[16,8192]{1,0:T(8,128)(2,1)}, u32[]{:S(2)}, u32[]{:S(2)}) collective-permute-start(bf16[16,8192]{1,0:T(8,128)(2,1)S(1)} %shard_map.96.refs_1_), channel_id=1, source_target_pairs={{0,2},{1,3},{2,4},{3,5},{4,6},{5,7},{6,8},{7,9},{8,10},{9,11},{10,... | collective-permute-start | bytes 786440 | tf_op jit(solution)/shard_map/ppermute | solution.py:24
  4.1 12.9 %collective-permute-start.1 = (bf16[16,8192]{1,0:T(8,128)(2,1)}, bf16[16,8192]{1,0:T(8,128)(2,1)}, u32[]{:S(2)}, u32[]{:S(2)}) collective-permute-start(bf16[16,8192]{1,0:T(8,128)(2,1)} %shard_map.97), channel_id=1, source_target_pairs={{0,2},{1,3},{2,4},{3,5},{4,6},{5,7},{6,8},{7,9},{8,10},{9,11},{10,... | collective-permute-start | bytes 786440 | tf_op jit(solution)/shard_map/ppermute | solution.py:24
  7.5 15.0 %collective-permute-start = (bf16[16,8192]{1,0:T(8,128)(2,1)}, bf16[16,8192]{1,0:T(8,128)(2,1)S(1)}, u32[]{:S(2)}, u32[]{:S(2)}) collective-permute-start(bf16[16,8192]{1,0:T(8,128)(2,1)} %get-tuple-element.50), channel_id=1, source_target_pairs={{0,2},{1,3},{2,4},{3,5},{4,6},{5,7},{6,8},{7,9},{8,10},{9,11},{10,... | collective-permute-start | bytes 786440 | tf_op jit(solution)/shard_map/ppermute | solution.py:24
  8.8 27.2 %collective-permute-start.7 = (bf16[16,8192]{1,0:T(8,128)(2,1)}, bf16[16,8192]{1,0:T(8,128)(2,1)}, u32[]{:S(2)}, u32[]{:S(2)}) collective-permute-start(bf16[16,8192]{1,0:T(8,128)(2,1)} %get-tuple-element.67), channel_id=1, source_target_pairs={{0,2},{1,3},{2,4},{3,5},{4,6},{5,7},{6,8},{7,9},{8,10},{9,11},{10,... | collective-permute-start | bytes 786440 | tf_op jit(solution)/shard_map/ppermute | solution.py:24
  10.0 28.6 %collective-permute-start.6 = (bf16[128,8192]{1,0:T(8,128)(2,1)}, bf16[128,8192]{1,0:T(8,128)(2,1)}, u32[]{:S(2)}, u32[]{:S(2)}) collective-permute-start(bf16[128,8192]{1,0:T(8,128)(2,1)} %get-tuple-element.66), channel_id=1, source_target_pairs={{0,1},{1,4},{2,3},{4,5},{5,8},{6,7},{8,9},{9,12},{10,11},{12,13},{... | collective-permute-start | bytes 6291464 | tf_op jit(solution)/shard_map/ppermute | solution.py:24
  12.8 23.0 %collective-permute-start.3 = (bf16[16,8192]{1,0:T(8,128)(2,1)}, bf16[16,8192]{1,0:T(8,128)(2,1)S(1)}, u32[]{:S(2)}, u32[]{:S(2)}) collective-permute-start(bf16[16,8192]{1,0:T(8,128)(2,1)} %get-tuple-element.55.refs_1_), channel_id=1, source_target_pairs={{0,16},{1,17},{2,18},{3,19},{4,20},{5,21},{6,22},{7,23},{8,24},{9,... | collective-permute-start | bytes 786440 | tf_op jit(solution)/shard_map/ppermute | solution.py:24
  17.0 12.8 %collective-permute-start.4 = (bf16[16,8192]{1,0:T(8,128)(2,1)}, bf16[16,8192]{1,0:T(8,128)(2,1)S(1)}, u32[]{:S(2)}, u32[]{:S(2)}) collective-permute-start(bf16[16,8192]{1,0:T(8,128)(2,1)} %get-tuple-element.57.refs_1_), channel_id=1, source_target_pairs={{0,16},{1,17},{2,18},{3,19},{4,20},{5,21},{6,22},{7,23},{8,24},{9,... | collective-permute-start | bytes 786440 | tf_op jit(solution)/shard_map/ppermute | solution.py:24
  18.2 5.5 %slice-start = ((s8[4718592]{0:T(1024)(128)(4,1)}), s8[4194304]{0:T(1024)(128)(4,1)S(1)}, s32[]{:S(2)}) async-start(s8[4718592]{0:T(1024)(128)(4,1)} %bitcast.10), calls=%async_computation | async-start | bytes 8388608
  18.2 5.6 %slice-start.1 = ((s8[4718592]{0:T(1024)(128)(4,1)}), s8[524288]{0:T(1024)(128)(4,1)S(1)}, s32[]{:S(2)}) async-start(s8[4718592]{0:T(1024)(128)(4,1)} %bitcast.10), calls=%async_computation.1 | async-start | bytes 1048576
  18.2 5.6 %copy-start = (bf16[512,3584]{1,0:T(8,128)(2,1)S(1)}, bf16[512,3584]{1,0:T(8,128)(2,1)}, u32[]{:S(2)}) copy-start(bf16[512,3584]{1,0:T(8,128)(2,1)} %refs_0_.7) | copy-start | bytes 11010052
  22.5 22.6 %collective-permute-start.10 = (bf16[16,8192]{1,0:T(8,128)(2,1)S(1)}, bf16[16,8192]{1,0:T(8,128)(2,1)S(1)}, u32[]{:S(2)}, u32[]{:S(2)}) collective-permute-start(bf16[16,8192]{1,0:T(8,128)(2,1)S(1)} %get-tuple-element.61.refs_1_), channel_id=1, source_target_pairs={{0,16},{1,17},{2,18},{3,19},{4,20},{5,21},{6,22},{7,23},{8,24},{9,... | collective-permute-start | bytes 786440 | tf_op jit(solution)/shard_map/ppermute | solution.py:24
  27.4 1.3 %copy-start.9 = (f32[128,3584]{1,0:T(8,128)}, f32[128,3584]{1,0:T(8,128)S(1)}, u32[]{:S(2)}) copy-start(f32[128,3584]{1,0:T(8,128)S(1)} %get-tuple-element.59.own_ref) | copy-start | bytes 5505028
  27.4 1.3 %copy-start.12 = (bf16[512,128]{1,0:T(8,128)(2,1)}, bf16[512,128]{1,0:T(8,128)(2,1)S(1)}, u32[]{:S(2)}) copy-start(bf16[512,128]{1,0:T(8,128)(2,1)S(1)} %get-tuple-element.63.refs_3_.refs_0_) | copy-start | bytes 393220
  29.7 28.0 %collective-permute-start.15 = (bf16[128,8192]{1,0:T(8,128)(2,1)}, bf16[128,8192]{1,0:T(8,128)(2,1)}, u32[]{:S(2)}, u32[]{:S(2)}) collective-permute-start(bf16[128,8192]{1,0:T(8,128)(2,1)} %get-tuple-element.62.refs_2_), channel_id=1, source_target_pairs={{3,6},{7,10},{11,14},{15,2},{19,22},{23,26},{27,30},{31,18}} | collective-permute-start | bytes 6291464 | tf_op jit(solution)/shard_map/ppermute | solution.py:24
  35.9 2.7 %copy-start.8 = (bf16[64,8192]{1,0:T(8,128)(2,1)}, bf16[64,8192]{1,0:T(8,128)(2,1)S(1)}, u32[]{:S(2)}) copy-start(bf16[64,8192]{1,0:T(8,128)(2,1)S(1)} %constant_dynamic-update-slice_fusion.refs_1_.refs_7_.refs_9_.refs_5_) | copy-start | bytes 3145732
  35.9 2.7 %collective-permute-start.5 = (bf16[64,8192]{1,0:T(8,128)(2,1)S(1)}, bf16[64,8192]{1,0:T(8,128)(2,1)S(1)}, u32[]{:S(2)}, u32[]{:S(2)}) collective-permute-start(bf16[64,8192]{1,0:T(8,128)(2,1)S(1)} %constant_dynamic-update-slice_fusion.refs_1_.refs_7_.refs_9_.refs_5_), channel_id=1, source_target_pairs={{0,1},{1,0},{2,3},{3,2},{4,5},{5,4},{6,7},{7,6},{8,9},{9,8},{10,11... | collective-permute-start | bytes 3145736 | tf_op jit(solution)/shard_map/ppermute | solution.py:24
  36.0 9.0 %collective-permute-start.11 = (bf16[16,8192]{1,0:T(8,128)(2,1)}, bf16[16,8192]{1,0:T(8,128)(2,1)S(1)}, u32[]{:S(2)}, u32[]{:S(2)}) collective-permute-start(bf16[16,8192]{1,0:T(8,128)(2,1)} %get-tuple-element.76), channel_id=1, source_target_pairs={{0,16},{1,17},{2,18},{3,19},{4,20},{5,21},{6,22},{7,23},{8,24},{9,... | collective-permute-start | bytes 786440 | tf_op jit(solution)/shard_map/ppermute | solution.py:24
  38.6 3.6 %copy-start.3 = (bf16[64,8192]{1,0:T(8,128)(2,1)}, bf16[64,8192]{1,0:T(8,128)(2,1)S(1)}, u32[]{:S(2)}) copy-start(bf16[64,8192]{1,0:T(8,128)(2,1)S(1)} %get-tuple-element.70.refs_8_.refs_10_.refs_6_) | copy-start | bytes 3145732
  42.3 1.9 %collective-permute-start.8 = (bf16[64,3584]{1,0:T(8,128)(2,1)S(1)}, bf16[64,3584]{1,0:T(8,128)(2,1)S(1)}, u32[]{:S(2)}, u32[]{:S(2)}) collective-permute-start(bf16[64,3584]{1,0:T(8,128)(2,1)S(1)} %get-tuple-element.73.refs_1_), channel_id=1, source_target_pairs={{0,1},{1,0},{2,3},{3,2},{4,5},{5,4},{6,7},{7,6},{8,9},{9,8},{10,11... | collective-permute-start | bytes 1376264 | tf_op jit(solution)/shard_map/ppermute | solution.py:24
  44.2 31.2 %collective-permute-start.9 = (bf16[64,3584]{1,0:T(8,128)(2,1)S(1)}, bf16[64,3584]{1,0:T(8,128)(2,1)S(1)}, u32[]{:S(2)}, u32[]{:S(2)}) collective-permute-start(bf16[64,3584]{1,0:T(8,128)(2,1)S(1)} %add_convert_fusion.1.refs_3_), channel_id=1, source_target_pairs={{0,14},{1,15},{2,0},{3,1},{4,2},{5,3},{6,4},{7,5},{8,6},{9,7},{10,... | collective-permute-start | bytes 1376264 | tf_op jit(solution)/shard_map/ppermute | solution.py:24
  45.1 3.0 %copy-start.7 = (bf16[64,8192]{1,0:T(8,128)(2,1)}, bf16[64,8192]{1,0:T(8,128)(2,1)S(1)}, u32[]{:S(2)}) copy-start(bf16[64,8192]{1,0:T(8,128)(2,1)S(1)} %constant_dynamic-update-slice_fusion.4.refs_1_.refs_7_.refs_9_) | copy-start | bytes 3145732
  45.1 3.0 %collective-permute-start.12 = (bf16[64,8192]{1,0:T(8,128)(2,1)S(1)}, bf16[64,8192]{1,0:T(8,128)(2,1)S(1)}, u32[]{:S(2)}, u32[]{:S(2)}) collective-permute-start(bf16[64,8192]{1,0:T(8,128)(2,1)S(1)} %constant_dynamic-update-slice_fusion.4.refs_1_.refs_7_.refs_9_), channel_id=1, source_target_pairs={{0,1},{1,0},{2,3},{3,2},{4,5},{5,4},{6,7},{7,6},{8,9},{9,8},{10,11... | collective-permute-start | bytes 3145736 | tf_op jit(solution)/shard_map/ppermute | solution.py:24
  48.1 3.6 %copy-start.4 = (bf16[64,8192]{1,0:T(8,128)(2,1)}, bf16[64,8192]{1,0:T(8,128)(2,1)S(1)}, u32[]{:S(2)}) copy-start(bf16[64,8192]{1,0:T(8,128)(2,1)S(1)} %get-tuple-element.81.refs_8_.refs_10_) | copy-start | bytes 3145732
  51.8 1.9 %collective-permute-start.13 = (bf16[64,3584]{1,0:T(8,128)(2,1)S(1)}, bf16[64,3584]{1,0:T(8,128)(2,1)S(1)}, u32[]{:S(2)}, u32[]{:S(2)}) collective-permute-start(bf16[64,3584]{1,0:T(8,128)(2,1)S(1)} %get-tuple-element.84.refs_1_), channel_id=1, source_target_pairs={{0,1},{1,0},{2,3},{3,2},{4,5},{5,4},{6,7},{7,6},{8,9},{9,8},{10,11... | collective-permute-start | bytes 1376264 | tf_op jit(solution)/shard_map/ppermute | solution.py:24
  53.7 21.7 %collective-permute-start.14 = (bf16[64,3584]{1,0:T(8,128)(2,1)S(1)}, bf16[64,3584]{1,0:T(8,128)(2,1)S(1)}, u32[]{:S(2)}, u32[]{:S(2)}) collective-permute-start(bf16[64,3584]{1,0:T(8,128)(2,1)S(1)} %add_convert_fusion.refs_1_), channel_id=1, source_target_pairs={{0,14},{1,15},{2,0},{3,1},{4,2},{5,3},{6,4},{7,5},{8,6},{9,7},{10,... | collective-permute-start | bytes 1376264 | tf_op jit(solution)/shard_map/ppermute | solution.py:24
  63.9 1.4 %copy-start.11 = (bf16[128,8192]{1,0:T(8,128)(2,1)}, bf16[128,8192]{1,0:T(8,128)(2,1)S(1)}, u32[]{:S(2)}) copy-start(bf16[128,8192]{1,0:T(8,128)(2,1)S(1)} %get-tuple-element.95.refs_9_) | copy-start | bytes 6291460
  65.9 15.4 %collective-permute-start.16 = (bf16[128,3584]{1,0:T(8,128)(2,1)S(1)}, bf16[128,3584]{1,0:T(8,128)(2,1)S(1)}, u32[]{:S(2)}, u32[]{:S(2)}) collective-permute-start(bf16[128,3584]{1,0:T(8,128)(2,1)S(1)} %get-tuple-element.91), channel_id=1, source_target_pairs={{0,13},{1,0},{2,15},{3,2},{4,1},{5,4},{6,3},{7,6},{8,5},{9,8},{10,... | collective-permute-start | bytes 2752520 | tf_op jit(solution)/shard_map/ppermute | solution.py:24
  68.5 12.7 %copy-start.10 = (f32[128,3584]{1,0:T(8,128)S(1)}, f32[128,3584]{1,0:T(8,128)}, u32[]{:S(2)}) copy-start(f32[128,3584]{1,0:T(8,128)} %copy-done.9) | copy-start | bytes 5505028
  (6 other events, 4.3 us)

commit v10 on v9

--- a/solution.py
+++ b/solution.py
@@ -325,6 +325,14 @@
     crossed[2], send0, order = gate([crossed[2], send0, order], [])
     swapped[2] = permuted(crossed[2], other_plane)
     late = permuted(send0, extra_late)
+    order = pause(order, [crossed[2], send0])
+    swapped[0], swapped[1], order = gate([swapped[0], swapped[1], order], [])
+    mine0 = jnp.concatenate([crossed[0], crossed[1], swapped[0], swapped[1]], axis=0)
+    theirs0 = permuted(mine0, other_core)
+    order = pause(order, [mine0])
+    crossed[3], order = gate([crossed[3], order], [])
+    swapped[3] = permuted(crossed[3], other_plane)
+
     own_scores, loss, own_part = meet(
         [student_head],
         [teacher_head],
@@ -333,15 +341,7 @@
         [jnp.float32],
         [order],
     )
-    order = pause(order, [crossed[2], send0, own_scores])
-    swapped[0], swapped[1], order = gate([swapped[0], swapped[1], order], [])
-    mine0 = jnp.concatenate([crossed[0], crossed[1], swapped[0], swapped[1]], axis=0)
-    theirs0 = permuted(mine0, other_core)
-    order = pause(order, [mine0])
-    crossed[3], order = gate([crossed[3], order], [])
-    swapped[3] = permuted(crossed[3], other_plane)
-
-    order = pause(order, [])
+    order = pause(order, [own_scores])
     theirs0, early, order = gate([theirs0, early, order], [])
     pair = [mine0, theirs0]
     scores0, loss, keep, give = meet(pair, pair, stage_ids(0), loss, [jnp.float32, jnp.bfloat16], [order])
@@ -369,13 +369,15 @@
     extra_scores, loss, extra_part, extra = meet(
         [late, early, 0], None, extra_id * width + ids_in, loss, [jnp.bfloat16], [order], from_late
     )
+    extra_part, order = gate([extra_part, order], [])
+    order = pause(order, [extra_part])
     extra_part = permuted(extra_part, extra_back)
 
     rows_grad = rows_product(
         [own_scores, scores0, scores1, extra_scores],
         [student_head, mine0, theirs0, mine1, theirs1, extra],
         depth,
-        [extra_scores],
+        [order],
     )
     head_grad = head_total(at, own_part, [back0, back1], extra_part)
     return (head_grad, rows_grad, loss[0])

time: 82.8 us -> 88.7 us (1.071)
  the two profiles are of different devices: /device:TPU:27 before, /device:TPU:0 now
where the time goes in v10:
time: 88.7 us; the launch traced here: 88.3 us
  Pallas kernels  28 us (32%)
  waiting for transfers between devices  24.4 us (28%)
  starting transfers between devices  22.2 us (25%)
  local copies, waits for them, and re-layouts  11 us (12%)
  between operations  1.37 us (2%)
  other arithmetic  1.29 us (1%)
    ppermute x17, waiting for transfers between devices, permuted(): return lax.ppermute(value, BOTH, pairs)  24.4 us
    ppermute x17, starting transfers between devices, permuted(): return lax.ppermute(value, BOTH, pairs)  22.2 us
    pallas_call x4, Pallas kernels, meeting(): pl.pallas_call(kernel, out_shape=out_shape, in_specs=[whole] * (7 + piece...  17 us
    unnamed x50, local copies, waits for them, and re-layouts  9.97 us
    pallas_call x1, Pallas kernels, rows_product(): pl.pallas_call(kernel, grid=(4,), out_shape=jax.ShapeDtypeStruct((count,...  6.22 us
    pallas_call x2, Pallas kernels, packed(): pl.pallas_call(kernel, out_shape=[jax.ShapeDtypeStruct((rows, depth + dep...  2.73 us
    pallas_call x1, Pallas kernels, head_total(): pl.pallas_call(kernel, out_shape=jax.ShapeDtypeStruct((width, depth), jnp...  2.04 us
  transfers between devices with their start and end apart: 17, of which 6 were waited for; matrix products, arithmetic and copies ran while one was open for 4% of the time, Pallas kernels for 29%

profile of v10, /device:TPU:0, one launch (start us, length us, event | category | flops | bytes accessed | tf_op | source)
XLA Modules:
  0.0 88.3 jit_solution(2457403314262438311)
XLA Ops:
  0.6 1.3 %copy-done.1 = bf16[128,4608]{1,0:T(8,128)(2,1)S(1)} copy-done((bf16[128,4608]{1,0:T(8,128)(2,1)S(1)}, bf16[128,4608]{1,0:T(8,128)(2,1)}, u32[]{:S(2)}) %copy-start.1) | copy-done | bytes 1179672
  1.9 1.2 %copy-done.6 = bf16[128,3584]{1,0:T(8,128)(2,1)S(1)} copy-done((bf16[128,3584]{1,0:T(8,128)(2,1)S(1)}, bf16[128,3584]{1,0:T(8,128)(2,1)}, u32[]{:S(2)}) %copy-start.6) | copy-done | bytes 917528
  3.5 3.0 %collective-permute-start.1 = (bf16[16,8192]{1,0:T(8,128)(2,1)S(1)}, bf16[16,8192]{1,0:T(8,128)(2,1)S(1)}, u32[]{:S(2)}, u32[]{:S(2)}) collective-permute-start(bf16[16,8192]{1,0:T(8,128)(2,1)S(1)} %shard_map.96.refs_1_), channel_id=1, source_target_pairs={{0,2},{1,3},{2,4},{3,5},{4,6},{5,7},{6,8},{7,9},{8,10},{9,11},{10,... | collective-permute-start | bytes 786440 | tf_op jit(solution)/shard_map/ppermute | solution.py:24
  6.5 1.5 %collective-permute-start.3 = (bf16[16,8192]{1,0:T(8,128)(2,1)S(1)}, bf16[16,8192]{1,0:T(8,128)(2,1)S(1)}, u32[]{:S(2)}, u32[]{:S(2)}) collective-permute-start(bf16[16,8192]{1,0:T(8,128)(2,1)S(1)} %shard_map.99), channel_id=1, source_target_pairs={{0,2},{1,3},{2,4},{3,5},{4,6},{5,7},{6,8},{7,9},{8,10},{9,11},{10,... | collective-permute-start | bytes 786440 | tf_op jit(solution)/shard_map/ppermute | solution.py:24
  8.0 2.4 %shard_map.94 = (bf16[16,8192]{1,0:T(8,128)(2,1)S(1)}, bf16[16,8192]{1,0:T(8,128)(2,1)}, bf16[128,8192]{1,0:T(8,128)(2,1)}, bf16[128,8192]{1,0:T(8,128)(2,1)}) custom-call(s32[1]{0:T(128)} %bitcast.at_ref, bf16[128,3584]{1,0:T(8,128)(2,1)S(1)} %copy-done.7, bf16[128,4608]{1,0:T(8,128)(2,1)S(1)} %copy-done.2), custom_call_target="tpu_custom_call" | custom-call | tf_op jit(solution)/shard_map/pallas_call | solution.py:95
  10.4 1.5 %collective-permute-start = (bf16[16,8192]{1,0:T(8,128)(2,1)}, bf16[16,8192]{1,0:T(8,128)(2,1)}, u32[]{:S(2)}, u32[]{:S(2)}) collective-permute-start(bf16[16,8192]{1,0:T(8,128)(2,1)} %get-tuple-element.52), channel_id=1, source_target_pairs={{0,2},{1,3},{2,4},{3,5},{4,6},{5,7},{6,8},{7,9},{8,10},{9,11},{10,... | collective-permute-start | bytes 786440 | tf_op jit(solution)/shard_map/ppermute | solution.py:24
  11.9 1.5 %collective-permute-start.5 = (bf16[16,8192]{1,0:T(8,128)(2,1)S(1)}, bf16[16,8192]{1,0:T(8,128)(2,1)S(1)}, u32[]{:S(2)}, u32[]{:S(2)}) collective-permute-start(bf16[16,8192]{1,0:T(8,128)(2,1)S(1)} %get-tuple-element.58), channel_id=1, source_target_pairs={{0,2},{1,3},{2,4},{3,5},{4,6},{5,7},{6,8},{7,9},{8,10},{9,11},{10,... | collective-permute-start | bytes 786440 | tf_op jit(solution)/shard_map/ppermute | solution.py:24
  13.5 1.9 %collective-permute-start.7 = (bf16[128,8192]{1,0:T(8,128)(2,1)}, bf16[128,8192]{1,0:T(8,128)(2,1)}, u32[]{:S(2)}, u32[]{:S(2)}) collective-permute-start(bf16[128,8192]{1,0:T(8,128)(2,1)} %get-tuple-element.70), channel_id=1, source_target_pairs={{0,1},{1,4},{2,3},{4,5},{5,8},{6,7},{8,9},{9,12},{10,11},{12,13},{... | collective-permute-start | bytes 6291464 | tf_op jit(solution)/shard_map/ppermute | solution.py:24
  16.9 1.5 %collective-permute-start.2 = (bf16[16,8192]{1,0:T(8,128)(2,1)S(1)}, bf16[16,8192]{1,0:T(8,128)(2,1)S(1)}, u32[]{:S(2)}, u32[]{:S(2)}) collective-permute-start(bf16[16,8192]{1,0:T(8,128)(2,1)S(1)} %get-tuple-element.54.refs_1_), channel_id=1, source_target_pairs={{0,16},{1,17},{2,18},{3,19},{4,20},{5,21},{6,22},{7,23},{8,24},{9,... | collective-permute-start | bytes 786440 | tf_op jit(solution)/shard_map/ppermute | solution.py:24
  18.4 3.8 %collective-permute-done.3.refs_0_ = bf16[16,8192]{1,0:T(8,128)(2,1)S(1)} collective-permute-done((bf16[16,8192]{1,0:T(8,128)(2,1)S(1)}, bf16[16,8192]{1,0:T(8,128)(2,1)S(1)}, u32[]{:S(2)}, u32[]{:S(2)}) %collective-permute-start.3) | collective-permute-done | bytes 262176 | tf_op jit(solution)/shard_map/ppermute | solution.py:24
  22.3 1.7 %collective-permute-start.4 = (bf16[16,8192]{1,0:T(8,128)(2,1)S(1)}, bf16[16,8192]{1,0:T(8,128)(2,1)S(1)}, u32[]{:S(2)}, u32[]{:S(2)}) collective-permute-start(bf16[16,8192]{1,0:T(8,128)(2,1)S(1)} %get-tuple-element.57.refs_1_), channel_id=1, source_target_pairs={{0,16},{1,17},{2,18},{3,19},{4,20},{5,21},{6,22},{7,23},{8,24},{9,... | collective-permute-start | bytes 786440 | tf_op jit(solution)/shard_map/ppermute | solution.py:24
  24.0 8.6 %collective-permute-done.5.refs_0_ = bf16[16,8192]{1,0:T(8,128)(2,1)S(1)} collective-permute-done((bf16[16,8192]{1,0:T(8,128)(2,1)S(1)}, bf16[16,8192]{1,0:T(8,128)(2,1)S(1)}, u32[]{:S(2)}, u32[]{:S(2)}) %collective-permute-start.5) | collective-permute-done | bytes 262176 | tf_op jit(solution)/shard_map/ppermute | solution.py:24
  32.7 1.5 %collective-permute-start.10 = (bf16[16,8192]{1,0:T(8,128)(2,1)S(1)}, bf16[16,8192]{1,0:T(8,128)(2,1)S(1)}, u32[]{:S(2)}, u32[]{:S(2)}) collective-permute-start(bf16[16,8192]{1,0:T(8,128)(2,1)S(1)} %get-tuple-element.62.refs_1_), channel_id=1, source_target_pairs={{0,16},{1,17},{2,18},{3,19},{4,20},{5,21},{6,22},{7,23},{8,24},{9,... | collective-permute-start | bytes 786440 | tf_op jit(solution)/shard_map/ppermute | solution.py:24
  34.3 2.0 %collective-permute-start.15 = (bf16[128,8192]{1,0:T(8,128)(2,1)}, bf16[128,8192]{1,0:T(8,128)(2,1)}, u32[]{:S(2)}, u32[]{:S(2)}) collective-permute-start(bf16[128,8192]{1,0:T(8,128)(2,1)} %get-tuple-element.63.refs_2_), channel_id=1, source_target_pairs={{3,6},{7,10},{11,14},{15,2},{19,22},{23,26},{27,30},{31,18}} | collective-permute-start | bytes 6291464 | tf_op jit(solution)/shard_map/ppermute | solution.py:24
  37.1 1.8 %slice-done = s8[4194304]{0:T(1024)(128)(4,1)S(1)} async-done(((s8[4718592]{0:T(1024)(128)(4,1)}), s8[4194304]{0:T(1024)(128)(4,1)S(1)}, s32[]{:S(2)}) %slice-start) | async-done | bytes 4194328
  39.0 1.2 %copy-done = bf16[512,3584]{1,0:T(8,128)(2,1)S(1)} copy-done((bf16[512,3584]{1,0:T(8,128)(2,1)S(1)}, bf16[512,3584]{1,0:T(8,128)(2,1)}, u32[]{:S(2)}) %copy-start) | copy-done | bytes 3670040
  40.7 3.6 %shard_map.108 = (bf16[512,128]{1,0:T(8,128)(2,1)S(1)}, f32[8,512]{1,0:T(8,128)S(1)}, f32[128,3584]{1,0:T(8,128)S(1)}) custom-call(bf16[512,3584]{1,0:T(8,128)(2,1)S(1)} %copy-done, bf16[512,4608]{1,0:T(8,128)(2,1)S(1)} %bitcast.11, f32[512,1]{1,0:T(8,128)S(1)} %copy.51.refs_2_, f32[512,1]{1,0:T(8,128)S(1)} %copy.52.refs_3_, s32[512,1]{1,0:T(8,128)S(1)} %copy.53.refs_4_, ...), custom_call_target="tpu_custom_call" | custom-call | tf_op jit(solution)/shard_map/pallas_call | solution.py:227
  44.4 0.6 copy-done.13
  45.0 1.0 %constant_dynamic-update-slice_fusion.6 = bf16[64,8192]{1,0:T(8,128)(2,1)S(1)} fusion(bf16[64,8192]{1,0:T(8,128)(2,1)S(1)} %constant_dynamic-update-slice_fusion.7, bf16[16,8192]{1,0:T(8,128)(2,1)} %get-tuple-element.78), kind=kLoop, calls=%fused_computation.8 | loop fusion | bytes 524288
  46.0 3.6 %shard_map.111 = (bf16[512,128]{1,0:T(8,128)(2,1)S(1)}, f32[8,512]{1,0:T(8,128)S(1)}, f32[64,3584]{1,0:T(8,128)S(1)}, bf16[64,3584]{1,0:T(8,128)(2,1)S(1)}) custom-call(bf16[512,3584]{1,0:T(8,128)(2,1)S(1)} %copy-done, bf16[512,4608]{1,0:T(8,128)(2,1)S(1)} %bitcast.11, f32[512,1]{1,0:T(8,128)S(1)} %copy.51.refs_2_, f32[512,1]{1,0:T(8,128)S(1)} %copy.52.refs_3_, ...), custom_call_target="tpu_custom_call" | custom-call | tf_op jit(solution)/shard_map/pallas_call | solution.py:227
  49.7 0.6 copy-done.14
  50.5 1.6 %collective-permute-done.8.refs_0_ = bf16[64,3584]{1,0:T(8,128)(2,1)S(1)} collective-permute-done((bf16[64,3584]{1,0:T(8,128)(2,1)S(1)}, bf16[64,3584]{1,0:T(8,128)(2,1)S(1)}, u32[]{:S(2)}, u32[]{:S(2)}) %collective-permute-start.8) | collective-permute-done | bytes 458784 | tf_op jit(solution)/shard_map/ppermute | solution.py:24
  52.1 0.9 add_convert_fusion.1.refs_3_
  53.0 3.0 %collective-permute-start.9 = (bf16[64,3584]{1,0:T(8,128)(2,1)}, bf16[64,3584]{1,0:T(8,128)(2,1)}, u32[]{:S(2)}, u32[]{:S(2)}) collective-permute-start(bf16[64,3584]{1,0:T(8,128)(2,1)} %add_convert_fusion.1.refs_3_), channel_id=1, source_target_pairs={{0,14},{1,15},{2,0},{3,1},{4,2},{5,3},{6,4},{7,5},{8,6},{9,7},{10,... | collective-permute-start | bytes 1376264 | tf_op jit(solution)/shard_map/ppermute | solution.py:24
  56.1 2.6 %collective-permute-done.12.refs_0_ = bf16[64,8192]{1,0:T(8,128)(2,1)S(1)} collective-permute-done((bf16[64,8192]{1,0:T(8,128)(2,1)S(1)}, bf16[64,8192]{1,0:T(8,128)(2,1)S(1)}, u32[]{:S(2)}, u32[]{:S(2)}) %collective-permute-start.12) | collective-permute-done | bytes 1048608 | tf_op jit(solution)/shard_map/ppermute | solution.py:24
  58.8 3.6 %shard_map.117 = (bf16[512,128]{1,0:T(8,128)(2,1)S(1)}, f32[8,512]{1,0:T(8,128)S(1)}, f32[64,3584]{1,0:T(8,128)S(1)}, bf16[64,3584]{1,0:T(8,128)(2,1)S(1)}) custom-call(bf16[512,3584]{1,0:T(8,128)(2,1)S(1)} %copy-done, bf16[512,4608]{1,0:T(8,128)(2,1)S(1)} %bitcast.11, f32[512,1]{1,0:T(8,128)S(1)} %copy.51.refs_2_, f32[512,1]{1,0:T(8,128)S(1)} %copy.52.refs_3_, ...), custom_call_target="tpu_custom_call" | custom-call | tf_op jit(solution)/shard_map/pallas_call | solution.py:227
  63.1 1.2 %collective-permute-done.13.refs_0_ = bf16[64,3584]{1,0:T(8,128)(2,1)S(1)} collective-permute-done((bf16[64,3584]{1,0:T(8,128)(2,1)S(1)}, bf16[64,3584]{1,0:T(8,128)(2,1)S(1)}, u32[]{:S(2)}, u32[]{:S(2)}) %collective-permute-start.13) | collective-permute-done | bytes 458784 | tf_op jit(solution)/shard_map/ppermute | solution.py:24
  64.6 6.2 %shard_map.122 = (bf16[512,128]{1,0:T(8,128)(2,1)S(1)}, f32[8,512]{1,0:T(8,128)S(1)}, bf16[128,3584]{1,0:T(8,128)(2,1)S(1)}, bf16[128,8192]{1,0:T(8,128)(2,1)S(1)}) custom-call(bf16[512,3584]{1,0:T(8,128)(2,1)S(1)} %copy-done, bf16[512,4608]{1,0:T(8,128)(2,1)S(1)} %bitcast.11, f32[512,1]{1,0:T(8,128)S(1)} %copy.51.refs_2_, f32[512,1]{1,0:T(8,128)S(1)} %copy.52.refs_3_, ...), custom_call_target="tpu_custom_call" | custom-call | tf_op jit(solution)/shard_map/pallas_call | solution.py:227
  70.8 1.5 %collective-permute-start.16 = (bf16[128,3584]{1,0:T(8,128)(2,1)S(1)}, bf16[128,3584]{1,0:T(8,128)(2,1)S(1)}, u32[]{:S(2)}, u32[]{:S(2)}) collective-permute-start(bf16[128,3584]{1,0:T(8,128)(2,1)S(1)} %get-tuple-element.94.refs_1_), channel_id=1, source_target_pairs={{0,13},{1,0},{2,15},{3,2},{4,1},{5,4},{6,3},{7,6},{8,5},{9,8},{10,... | collective-permute-start | bytes 2752520 | tf_op jit(solution)/shard_map/ppermute | solution.py:24
  72.9 6.2 %shard_map.126 = bf16[512,3584]{1,0:T(8,128)(2,1)} custom-call(bf16[512,128]{1,0:T(8,128)(2,1)} %copy-done.13, bf16[512,128]{1,0:T(8,128)(2,1)} %copy-done.14, bf16[512,128]{1,0:T(8,128)(2,1)} %copy-done.15, bf16[512,128]{1,0:T(8,128)(2,1)} %copy-done.16, bf16[128,3584]{1,0:T(8,128)(2,1)} %refs_4_.1, bf16[64,8192]{1,0:T(8,128)(2,1)} %copy-done.10, ...), custom_call_target="tpu_custom_call" | custom-call | flops 30000001024 | tf_op jit(solution)/shard_map/pallas_call | solution.py:258
  79.7 6.4 %collective-permute-done.16.extra_ref = bf16[128,3584]{1,0:T(8,128)(2,1)S(1)} collective-permute-done((bf16[128,3584]{1,0:T(8,128)(2,1)S(1)}, bf16[128,3584]{1,0:T(8,128)(2,1)S(1)}, u32[]{:S(2)}, u32[]{:S(2)}) %collective-permute-start.16) | collective-permute-done | bytes 917536 | tf_op jit(solution)/shard_map/ppermute | solution.py:24
  86.1 2.0 %shard_map.124 = bf16[128,3584]{1,0:T(8,128)(2,1)} custom-call(s32[1]{0:T(128)} %bitcast.at_ref, f32[128,3584]{1,0:T(8,128)S(1)} %get-tuple-element.68.own_ref, bf16[64,3584]{1,0:T(8,128)(2,1)} %collective-permute-done.9.back0, bf16[64,3584]{1,0:T(8,128)(2,1)S(1)} %collective-permute-done.14.back1, bf16[128,3584]{1,0:T(8,128)(2,1)S(1)} %collective-permute-done.16.extra_ref), custom_call_target="tpu_custom_call" | custom-call | tf_op jit(solution)/shard_map/pallas_call | solution.py:135
  (106 shorter events, 5.6 us)
Async XLA Ops:
  0.6 1.3 %copy-start.1 = (bf16[128,4608]{1,0:T(8,128)(2,1)S(1)}, bf16[128,4608]{1,0:T(8,128)(2,1)}, u32[]{:S(2)}) copy-start(bf16[128,4608]{1,0:T(8,128)(2,1)} %refs_8_.1) | copy-start | bytes 3538948
  1.9 1.2 %copy-start.6 = (bf16[128,3584]{1,0:T(8,128)(2,1)S(1)}, bf16[128,3584]{1,0:T(8,128)(2,1)}, u32[]{:S(2)}) copy-start(bf16[128,3584]{1,0:T(8,128)(2,1)} %refs_4_.1) | copy-start | bytes 2752516
  3.1 4.9 %copy-start.2 = (bf16[128,4608]{1,0:T(8,128)(2,1)S(1)}, bf16[128,4608]{1,0:T(8,128)(2,1)}, u32[]{:S(2)}) copy-start(bf16[128,4608]{1,0:T(8,128)(2,1)} %refs_8_.1) | copy-start | bytes 3538948
  3.1 4.9 %copy-start.7 = (bf16[128,3584]{1,0:T(8,128)(2,1)S(1)}, bf16[128,3584]{1,0:T(8,128)(2,1)}, u32[]{:S(2)}) copy-start(bf16[128,3584]{1,0:T(8,128)(2,1)} %refs_4_.1) | copy-start | bytes 2752516
  3.5 13.4 %collective-permute-start.1 = (bf16[16,8192]{1,0:T(8,128)(2,1)S(1)}, bf16[16,8192]{1,0:T(8,128)(2,1)S(1)}, u32[]{:S(2)}, u32[]{:S(2)}) collective-permute-start(bf16[16,8192]{1,0:T(8,128)(2,1)S(1)} %shard_map.96.refs_1_), channel_id=1, source_target_pairs={{0,2},{1,3},{2,4},{3,5},{4,6},{5,7},{6,8},{7,9},{8,10},{9,11},{10,... | collective-permute-start | bytes 786440 | tf_op jit(solution)/shard_map/ppermute | solution.py:24
  6.5 15.8 %collective-permute-start.3 = (bf16[16,8192]{1,0:T(8,128)(2,1)S(1)}, bf16[16,8192]{1,0:T(8,128)(2,1)S(1)}, u32[]{:S(2)}, u32[]{:S(2)}) collective-permute-start(bf16[16,8192]{1,0:T(8,128)(2,1)S(1)} %shard_map.99), channel_id=1, source_target_pairs={{0,2},{1,3},{2,4},{3,5},{4,6},{5,7},{6,8},{7,9},{8,10},{9,11},{10,... | collective-permute-start | bytes 786440 | tf_op jit(solution)/shard_map/ppermute | solution.py:24
  10.4 26.1 %collective-permute-start = (bf16[16,8192]{1,0:T(8,128)(2,1)}, bf16[16,8192]{1,0:T(8,128)(2,1)}, u32[]{:S(2)}, u32[]{:S(2)}) collective-permute-start(bf16[16,8192]{1,0:T(8,128)(2,1)} %get-tuple-element.52), channel_id=1, source_target_pairs={{0,2},{1,3},{2,4},{3,5},{4,6},{5,7},{6,8},{7,9},{8,10},{9,11},{10,... | collective-permute-start | bytes 786440 | tf_op jit(solution)/shard_map/ppermute | solution.py:24
  11.9 20.7 %collective-permute-start.5 = (bf16[16,8192]{1,0:T(8,128)(2,1)S(1)}, bf16[16,8192]{1,0:T(8,128)(2,1)S(1)}, u32[]{:S(2)}, u32[]{:S(2)}) collective-permute-start(bf16[16,8192]{1,0:T(8,128)(2,1)S(1)} %get-tuple-element.58), channel_id=1, source_target_pairs={{0,2},{1,3},{2,4},{3,5},{4,6},{5,7},{6,8},{7,9},{8,10},{9,11},{10,... | collective-permute-start | bytes 786440 | tf_op jit(solution)/shard_map/ppermute | solution.py:24
  13.5 32.5 %collective-permute-start.7 = (bf16[128,8192]{1,0:T(8,128)(2,1)}, bf16[128,8192]{1,0:T(8,128)(2,1)}, u32[]{:S(2)}, u32[]{:S(2)}) collective-permute-start(bf16[128,8192]{1,0:T(8,128)(2,1)} %get-tuple-element.70), channel_id=1, source_target_pairs={{0,1},{1,4},{2,3},{4,5},{5,8},{6,7},{8,9},{9,12},{10,11},{12,13},{... | collective-permute-start | bytes 6291464 | tf_op jit(solution)/shard_map/ppermute | solution.py:24
  16.9 19.4 %collective-permute-start.2 = (bf16[16,8192]{1,0:T(8,128)(2,1)S(1)}, bf16[16,8192]{1,0:T(8,128)(2,1)S(1)}, u32[]{:S(2)}, u32[]{:S(2)}) collective-permute-start(bf16[16,8192]{1,0:T(8,128)(2,1)S(1)} %get-tuple-element.54.refs_1_), channel_id=1, source_target_pairs={{0,16},{1,17},{2,18},{3,19},{4,20},{5,21},{6,22},{7,23},{8,24},{9,... | collective-permute-start | bytes 786440 | tf_op jit(solution)/shard_map/ppermute | solution.py:24
  22.3 12.0 %collective-permute-start.4 = (bf16[16,8192]{1,0:T(8,128)(2,1)S(1)}, bf16[16,8192]{1,0:T(8,128)(2,1)S(1)}, u32[]{:S(2)}, u32[]{:S(2)}) collective-permute-start(bf16[16,8192]{1,0:T(8,128)(2,1)S(1)} %get-tuple-element.57.refs_1_), channel_id=1, source_target_pairs={{0,16},{1,17},{2,18},{3,19},{4,20},{5,21},{6,22},{7,23},{8,24},{9,... | collective-permute-start | bytes 786440 | tf_op jit(solution)/shard_map/ppermute | solution.py:24
  32.7 23.3 %collective-permute-start.10 = (bf16[16,8192]{1,0:T(8,128)(2,1)S(1)}, bf16[16,8192]{1,0:T(8,128)(2,1)S(1)}, u32[]{:S(2)}, u32[]{:S(2)}) collective-permute-start(bf16[16,8192]{1,0:T(8,128)(2,1)S(1)} %get-tuple-element.62.refs_1_), channel_id=1, source_target_pairs={{0,16},{1,17},{2,18},{3,19},{4,20},{5,21},{6,22},{7,23},{8,24},{9,... | collective-permute-start | bytes 786440 | tf_op jit(solution)/shard_map/ppermute | solution.py:24
  34.3 30.4 %collective-permute-start.15 = (bf16[128,8192]{1,0:T(8,128)(2,1)}, bf16[128,8192]{1,0:T(8,128)(2,1)}, u32[]{:S(2)}, u32[]{:S(2)}) collective-permute-start(bf16[128,8192]{1,0:T(8,128)(2,1)} %get-tuple-element.63.refs_2_), channel_id=1, source_target_pairs={{3,6},{7,10},{11,14},{15,2},{19,22},{23,26},{27,30},{31,18}} | collective-permute-start | bytes 6291464 | tf_op jit(solution)/shard_map/ppermute | solution.py:24
  36.3 9.7 %copy-start.10 = (bf16[64,8192]{1,0:T(8,128)(2,1)}, bf16[64,8192]{1,0:T(8,128)(2,1)S(1)}, u32[]{:S(2)}) copy-start(bf16[64,8192]{1,0:T(8,128)(2,1)S(1)} %constant_dynamic-update-slice_fusion.refs_1_.refs_7_.refs_9_.refs_5_) | copy-start | bytes 3145732
  36.3 9.6 %collective-permute-start.6 = (bf16[64,8192]{1,0:T(8,128)(2,1)S(1)}, bf16[64,8192]{1,0:T(8,128)(2,1)S(1)}, u32[]{:S(2)}, u32[]{:S(2)}) collective-permute-start(bf16[64,8192]{1,0:T(8,128)(2,1)S(1)} %constant_dynamic-update-slice_fusion.refs_1_.refs_7_.refs_9_.refs_5_), channel_id=1, source_target_pairs={{0,1},{1,0},{2,3},{3,2},{4,5},{5,4},{6,7},{7,6},{8,9},{9,8},{10,11... | collective-permute-start | bytes 3145736 | tf_op jit(solution)/shard_map/ppermute | solution.py:24
  36.4 2.5 %slice-start = ((s8[4718592]{0:T(1024)(128)(4,1)}), s8[4194304]{0:T(1024)(128)(4,1)S(1)}, s32[]{:S(2)}) async-start(s8[4718592]{0:T(1024)(128)(4,1)} %bitcast.10), calls=%async_computation | async-start | bytes 8388608
  36.4 2.6 %slice-start.1 = ((s8[4718592]{0:T(1024)(128)(4,1)}), s8[524288]{0:T(1024)(128)(4,1)S(1)}, s32[]{:S(2)}) async-start(s8[4718592]{0:T(1024)(128)(4,1)} %bitcast.10), calls=%async_computation.1 | async-start | bytes 1048576
  36.4 3.7 %copy-start = (bf16[512,3584]{1,0:T(8,128)(2,1)S(1)}, bf16[512,3584]{1,0:T(8,128)(2,1)}, u32[]{:S(2)}) copy-start(bf16[512,3584]{1,0:T(8,128)(2,1)} %refs_0_.7) | copy-start | bytes 11010052
  36.5 4.0 %copy-start.3 = (bf16[128,4608]{1,0:T(8,128)(2,1)S(1)}, bf16[128,4608]{1,0:T(8,128)(2,1)}, u32[]{:S(2)}) copy-start(bf16[128,4608]{1,0:T(8,128)(2,1)} %refs_8_.1) | copy-start | bytes 3538948
  36.5 4.2 %copy-start.8 = (bf16[128,3584]{1,0:T(8,128)(2,1)S(1)}, bf16[128,3584]{1,0:T(8,128)(2,1)}, u32[]{:S(2)}) copy-start(bf16[128,3584]{1,0:T(8,128)(2,1)} %refs_4_.1) | copy-start | bytes 2752516
  36.5 19.5 %collective-permute-start.11 = (bf16[16,8192]{1,0:T(8,128)(2,1)}, bf16[16,8192]{1,0:T(8,128)(2,1)S(1)}, u32[]{:S(2)}, u32[]{:S(2)}) collective-permute-start(bf16[16,8192]{1,0:T(8,128)(2,1)} %get-tuple-element.78), channel_id=1, source_target_pairs={{0,16},{1,17},{2,18},{3,19},{4,20},{5,21},{6,22},{7,23},{8,24},{9,... | collective-permute-start | bytes 786440 | tf_op jit(solution)/shard_map/ppermute | solution.py:24
  46.0 3.6 %copy-start.4 = (bf16[64,8192]{1,0:T(8,128)(2,1)}, bf16[64,8192]{1,0:T(8,128)(2,1)S(1)}, u32[]{:S(2)}) copy-start(bf16[64,8192]{1,0:T(8,128)(2,1)S(1)} %get-tuple-element.72.refs_8_.refs_10_.refs_6_) | copy-start | bytes 3145732
  50.3 1.8 %collective-permute-start.8 = (bf16[64,3584]{1,0:T(8,128)(2,1)S(1)}, bf16[64,3584]{1,0:T(8,128)(2,1)S(1)}, u32[]{:S(2)}, u32[]{:S(2)}) collective-permute-start(bf16[64,3584]{1,0:T(8,128)(2,1)S(1)} %get-tuple-element.75.refs_1_), channel_id=1, source_target_pairs={{0,1},{1,0},{2,3},{3,2},{4,5},{5,4},{6,7},{7,6},{8,9},{9,8},{10,11... | collective-permute-start | bytes 1376264 | tf_op jit(solution)/shard_map/ppermute | solution.py:24
  53.0 26.7 %collective-permute-start.9 = (bf16[64,3584]{1,0:T(8,128)(2,1)}, bf16[64,3584]{1,0:T(8,128)(2,1)}, u32[]{:S(2)}, u32[]{:S(2)}) collective-permute-start(bf16[64,3584]{1,0:T(8,128)(2,1)} %add_convert_fusion.1.refs_3_), channel_id=1, source_target_pairs={{0,14},{1,15},{2,0},{3,1},{4,2},{5,3},{6,4},{7,5},{8,6},{9,7},{10,... | collective-permute-start | bytes 1376264 | tf_op jit(solution)/shard_map/ppermute | solution.py:24
  56.0 2.7 %copy-start.9 = (bf16[64,8192]{1,0:T(8,128)(2,1)}, bf16[64,8192]{1,0:T(8,128)(2,1)S(1)}, u32[]{:S(2)}) copy-start(bf16[64,8192]{1,0:T(8,128)(2,1)S(1)} %constant_dynamic-update-slice_fusion.4.refs_1_.refs_7_.refs_9_) | copy-start | bytes 3145732
  56.0 2.7 %collective-permute-start.12 = (bf16[64,8192]{1,0:T(8,128)(2,1)S(1)}, bf16[64,8192]{1,0:T(8,128)(2,1)S(1)}, u32[]{:S(2)}, u32[]{:S(2)}) collective-permute-start(bf16[64,8192]{1,0:T(8,128)(2,1)S(1)} %constant_dynamic-update-slice_fusion.4.refs_1_.refs_7_.refs_9_), channel_id=1, source_target_pairs={{0,1},{1,0},{2,3},{3,2},{4,5},{5,4},{6,7},{7,6},{8,9},{9,8},{10,11... | collective-permute-start | bytes 3145736 | tf_op jit(solution)/shard_map/ppermute | solution.py:24
  58.8 3.6 %copy-start.5 = (bf16[64,8192]{1,0:T(8,128)(2,1)}, bf16[64,8192]{1,0:T(8,128)(2,1)S(1)}, u32[]{:S(2)}) copy-start(bf16[64,8192]{1,0:T(8,128)(2,1)S(1)} %get-tuple-element.83.refs_8_.refs_10_) | copy-start | bytes 3145732
  62.4 1.9 %collective-permute-start.13 = (bf16[64,3584]{1,0:T(8,128)(2,1)S(1)}, bf16[64,3584]{1,0:T(8,128)(2,1)S(1)}, u32[]{:S(2)}, u32[]{:S(2)}) collective-permute-start(bf16[64,3584]{1,0:T(8,128)(2,1)S(1)} %get-tuple-element.86.refs_1_), channel_id=1, source_target_pairs={{0,1},{1,0},{2,3},{3,2},{4,5},{5,4},{6,7},{7,6},{8,9},{9,8},{10,11... | collective-permute-start | bytes 1376264 | tf_op jit(solution)/shard_map/ppermute | solution.py:24
  64.4 15.3 %collective-permute-start.14 = (bf16[64,3584]{1,0:T(8,128)(2,1)S(1)}, bf16[64,3584]{1,0:T(8,128)(2,1)S(1)}, u32[]{:S(2)}, u32[]{:S(2)}) collective-permute-start(bf16[64,3584]{1,0:T(8,128)(2,1)S(1)} %add_convert_fusion.refs_1_), channel_id=1, source_target_pairs={{0,14},{1,15},{2,0},{3,1},{4,2},{5,3},{6,4},{7,5},{8,6},{9,7},{10,... | collective-permute-start | bytes 1376264 | tf_op jit(solution)/shard_map/ppermute | solution.py:24
  70.8 1.5 %copy-start.12 = (bf16[128,8192]{1,0:T(8,128)(2,1)}, bf16[128,8192]{1,0:T(8,128)(2,1)S(1)}, u32[]{:S(2)}) copy-start(bf16[128,8192]{1,0:T(8,128)(2,1)S(1)} %get-tuple-element.98.refs_9_) | copy-start | bytes 6291460
  70.8 1.5 %copy-start.16 = (bf16[512,128]{1,0:T(8,128)(2,1)}, bf16[512,128]{1,0:T(8,128)(2,1)S(1)}, u32[]{:S(2)}) copy-start(bf16[512,128]{1,0:T(8,128)(2,1)S(1)} %get-tuple-element.97.refs_3_) | copy-start | bytes 393220
  70.8 15.3 %collective-permute-start.16 = (bf16[128,3584]{1,0:T(8,128)(2,1)S(1)}, bf16[128,3584]{1,0:T(8,128)(2,1)S(1)}, u32[]{:S(2)}, u32[]{:S(2)}) collective-permute-start(bf16[128,3584]{1,0:T(8,128)(2,1)S(1)} %get-tuple-element.94.refs_1_), channel_id=1, source_target_pairs={{0,13},{1,0},{2,15},{3,2},{4,1},{5,4},{6,3},{7,6},{8,5},{9,8},{10,... | collective-permute-start | bytes 2752520 | tf_op jit(solution)/shard_map/ppermute | solution.py:24
  (7 other events, 4.9 us)

commit v11 on v10

--- a/solution.py
+++ b/solution.py
@@ -311,6 +311,8 @@
     )
     send, send0 = chunks[4:]
     chunks = chunks[:4]
+    chunks[2], = gate([chunks[2]], [])
+    chunks[3], = gate([chunks[3]], [chunks[2]])
 
     crossed = [permuted(chunk, next_chip) for chunk in chunks]
     early = permuted(send, extra_early)

time: 88.7 us -> 88.9 us (level)
  starting transfers between devices: 22.2 us -> 25.4 us
  waiting for transfers between devices: 24.4 us -> 21.5 us
    ppermute x17, starting transfers between devices: 22.2 us -> 25.4 us  [permuted(): return lax.ppermute(value, BOTH, pairs)]
    ppermute x17, waiting for transfers between devices: 24.4 us -> 21.5 us  [permuted(): return lax.ppermute(value, BOTH, pairs)]
  transfers between devices with their start and end apart: 17 -> 17, of which waited for: 6 -> 7; matrix products, arithmetic and copies ran while one was open for 4% -> 4% of each run, Pallas kernels for 29% -> 29%
where the time goes in v11:
time: 88.9 us; the launch traced here: 88.5 us
  Pallas kernels  28 us (31%)
  starting transfers between devices  25.4 us (29%)
  waiting for transfers between devices  21.5 us (24%)
  local copies, waits for them, and re-layouts  10.9 us (12%)
  between operations  1.35 us (2%)
  other arithmetic  1.29 us (1%)
    ppermute x17, starting transfers between devices, permuted(): return lax.ppermute(value, BOTH, pairs)  25.4 us
    ppermute x17, waiting for transfers between devices, permuted(): return lax.ppermute(value, BOTH, pairs)  21.5 us
    pallas_call x4, Pallas kernels, meeting(): pl.pallas_call(kernel, out_shape=out_shape, in_specs=[whole] * (7 + piece...  17 us
    unnamed x50, local copies, waits for them, and re-layouts  9.82 us
    pallas_call x1, Pallas kernels, rows_product(): pl.pallas_call(kernel, grid=(4,), out_shape=jax.ShapeDtypeStruct((count,...  6.22 us
    pallas_call x2, Pallas kernels, packed(): pl.pallas_call(kernel, out_shape=[jax.ShapeDtypeStruct((rows, depth + dep...  2.73 us
    pallas_call x1, Pallas kernels, head_total(): pl.pallas_call(kernel, out_shape=jax.ShapeDtypeStruct((width, depth), jnp...  2.04 us
  transfers between devices with their start and end apart: 17, of which 7 were waited for; matrix products, arithmetic and copies ran while one was open for 4% of the time, Pallas kernels for 29%

profile of v11, /device:TPU:0, one launch (start us, length us, event | category | flops | bytes accessed | tf_op | source)
XLA Modules:
  0.0 88.5 jit_solution(15834215731791610595)
XLA Ops:
  0.6 1.3 %copy-done.1 = bf16[128,4608]{1,0:T(8,128)(2,1)S(1)} copy-done((bf16[128,4608]{1,0:T(8,128)(2,1)S(1)}, bf16[128,4608]{1,0:T(8,128)(2,1)}, u32[]{:S(2)}) %copy-start.1) | copy-done | bytes 1179672
  1.9 1.2 %copy-done.6 = bf16[128,3584]{1,0:T(8,128)(2,1)S(1)} copy-done((bf16[128,3584]{1,0:T(8,128)(2,1)S(1)}, bf16[128,3584]{1,0:T(8,128)(2,1)}, u32[]{:S(2)}) %copy-start.6) | copy-done | bytes 917528
  3.5 3.0 %collective-permute-start.1 = (bf16[16,8192]{1,0:T(8,128)(2,1)S(1)}, bf16[16,8192]{1,0:T(8,128)(2,1)S(1)}, u32[]{:S(2)}, u32[]{:S(2)}) collective-permute-start(bf16[16,8192]{1,0:T(8,128)(2,1)S(1)} %shard_map.98.refs_1_), channel_id=1, source_target_pairs={{0,2},{1,3},{2,4},{3,5},{4,6},{5,7},{6,8},{7,9},{8,10},{9,11},{10,... | collective-permute-start | bytes 786440 | tf_op jit(solution)/shard_map/ppermute | solution.py:24
  6.5 1.5 %collective-permute-start.3 = (bf16[16,8192]{1,0:T(8,128)(2,1)S(1)}, bf16[16,8192]{1,0:T(8,128)(2,1)S(1)}, u32[]{:S(2)}, u32[]{:S(2)}) collective-permute-start(bf16[16,8192]{1,0:T(8,128)(2,1)S(1)} %shard_map.101), channel_id=1, source_target_pairs={{0,2},{1,3},{2,4},{3,5},{4,6},{5,7},{6,8},{7,9},{8,10},{9,11},{10,... | collective-permute-start | bytes 786440 | tf_op jit(solution)/shard_map/ppermute | solution.py:24
  8.0 2.4 %shard_map.94 = (bf16[16,8192]{1,0:T(8,128)(2,1)S(1)}, bf16[16,8192]{1,0:T(8,128)(2,1)}, bf16[128,8192]{1,0:T(8,128)(2,1)}, bf16[128,8192]{1,0:T(8,128)(2,1)}) custom-call(s32[1]{0:T(128)} %bitcast.at_ref, bf16[128,3584]{1,0:T(8,128)(2,1)S(1)} %copy-done.7, bf16[128,4608]{1,0:T(8,128)(2,1)S(1)} %copy-done.2), custom_call_target="tpu_custom_call" | custom-call | tf_op jit(solution)/shard_map/pallas_call | solution.py:95
  10.4 1.5 %collective-permute-start.5 = (bf16[16,8192]{1,0:T(8,128)(2,1)S(1)}, bf16[16,8192]{1,0:T(8,128)(2,1)S(1)}, u32[]{:S(2)}, u32[]{:S(2)}) collective-permute-start(bf16[16,8192]{1,0:T(8,128)(2,1)S(1)} %shard_map.95.refs_1_), channel_id=1, source_target_pairs={{0,2},{1,3},{2,4},{3,5},{4,6},{5,7},{6,8},{7,9},{8,10},{9,11},{10,... | collective-permute-start | bytes 786440 | tf_op jit(solution)/shard_map/ppermute | solution.py:24
  12.0 1.5 %collective-permute-start = (bf16[16,8192]{1,0:T(8,128)(2,1)}, bf16[16,8192]{1,0:T(8,128)(2,1)}, u32[]{:S(2)}, u32[]{:S(2)}) collective-permute-start(bf16[16,8192]{1,0:T(8,128)(2,1)} %shard_map.96), channel_id=1, source_target_pairs={{0,2},{1,3},{2,4},{3,5},{4,6},{5,7},{6,8},{7,9},{8,10},{9,11},{10,... | collective-permute-start | bytes 786440 | tf_op jit(solution)/shard_map/ppermute | solution.py:24
  13.5 1.9 %collective-permute-start.7 = (bf16[128,8192]{1,0:T(8,128)(2,1)}, bf16[128,8192]{1,0:T(8,128)(2,1)}, u32[]{:S(2)}, u32[]{:S(2)}) collective-permute-start(bf16[128,8192]{1,0:T(8,128)(2,1)} %get-tuple-element.70), channel_id=1, source_target_pairs={{0,1},{1,4},{2,3},{4,5},{5,8},{6,7},{8,9},{9,12},{10,11},{12,13},{... | collective-permute-start | bytes 6291464 | tf_op jit(solution)/shard_map/ppermute | solution.py:24
  16.9 1.5 %collective-permute-start.2 = (bf16[16,8192]{1,0:T(8,128)(2,1)S(1)}, bf16[16,8192]{1,0:T(8,128)(2,1)S(1)}, u32[]{:S(2)}, u32[]{:S(2)}) collective-permute-start(bf16[16,8192]{1,0:T(8,128)(2,1)S(1)} %get-tuple-element.55.refs_1_), channel_id=1, source_target_pairs={{0,16},{1,17},{2,18},{3,19},{4,20},{5,21},{6,22},{7,23},{8,24},{9,... | collective-permute-start | bytes 786440 | tf_op jit(solution)/shard_map/ppermute | solution.py:24
  18.5 3.8 %collective-permute-done.3.refs_0_ = bf16[16,8192]{1,0:T(8,128)(2,1)S(1)} collective-permute-done((bf16[16,8192]{1,0:T(8,128)(2,1)S(1)}, bf16[16,8192]{1,0:T(8,128)(2,1)S(1)}, u32[]{:S(2)}, u32[]{:S(2)}) %collective-permute-start.3) | collective-permute-done | bytes 262176 | tf_op jit(solution)/shard_map/ppermute | solution.py:24
  22.3 1.7 %collective-permute-start.4 = (bf16[16,8192]{1,0:T(8,128)(2,1)S(1)}, bf16[16,8192]{1,0:T(8,128)(2,1)S(1)}, u32[]{:S(2)}, u32[]{:S(2)}) collective-permute-start(bf16[16,8192]{1,0:T(8,128)(2,1)S(1)} %get-tuple-element.58.refs_1_), channel_id=1, source_target_pairs={{0,16},{1,17},{2,18},{3,19},{4,20},{5,21},{6,22},{7,23},{8,24},{9,... | collective-permute-start | bytes 786440 | tf_op jit(solution)/shard_map/ppermute | solution.py:24
  24.0 3.9 %collective-permute-done.5.refs_0_ = bf16[16,8192]{1,0:T(8,128)(2,1)S(1)} collective-permute-done((bf16[16,8192]{1,0:T(8,128)(2,1)S(1)}, bf16[16,8192]{1,0:T(8,128)(2,1)S(1)}, u32[]{:S(2)}, u32[]{:S(2)}) %collective-permute-start.5) | collective-permute-done | bytes 262176 | tf_op jit(solution)/shard_map/ppermute | solution.py:24
  27.9 1.7 %collective-permute-start.10 = (bf16[16,8192]{1,0:T(8,128)(2,1)S(1)}, bf16[16,8192]{1,0:T(8,128)(2,1)S(1)}, u32[]{:S(2)}, u32[]{:S(2)}) collective-permute-start(bf16[16,8192]{1,0:T(8,128)(2,1)S(1)} %get-tuple-element.62.refs_1_), channel_id=1, source_target_pairs={{0,16},{1,17},{2,18},{3,19},{4,20},{5,21},{6,22},{7,23},{8,24},{9,... | collective-permute-start | bytes 786440 | tf_op jit(solution)/shard_map/ppermute | solution.py:24
  29.7 1.8 %collective-permute-done.4.refs_1_ = bf16[16,8192]{1,0:T(8,128)(2,1)S(1)} collective-permute-done((bf16[16,8192]{1,0:T(8,128)(2,1)S(1)}, bf16[16,8192]{1,0:T(8,128)(2,1)S(1)}, u32[]{:S(2)}, u32[]{:S(2)}) %collective-permute-start.4) | collective-permute-done | bytes 262176 | tf_op jit(solution)/shard_map/ppermute | solution.py:24
  31.5 2.0 %collective-permute-start.15 = (bf16[128,8192]{1,0:T(8,128)(2,1)}, bf16[128,8192]{1,0:T(8,128)(2,1)}, u32[]{:S(2)}, u32[]{:S(2)}) collective-permute-start(bf16[128,8192]{1,0:T(8,128)(2,1)} %get-tuple-element.63.refs_2_), channel_id=1, source_target_pairs={{3,6},{7,10},{11,14},{15,2},{19,22},{23,26},{27,30},{31,18}} | collective-permute-start | bytes 6291464 | tf_op jit(solution)/shard_map/ppermute | solution.py:24
  34.4 1.4 %collective-permute-start.11 = (bf16[16,8192]{1,0:T(8,128)(2,1)}, bf16[16,8192]{1,0:T(8,128)(2,1)S(1)}, u32[]{:S(2)}, u32[]{:S(2)}) collective-permute-start(bf16[16,8192]{1,0:T(8,128)(2,1)} %get-tuple-element.78), channel_id=1, source_target_pairs={{0,16},{1,17},{2,18},{3,19},{4,20},{5,21},{6,22},{7,23},{8,24},{9,... | collective-permute-start | bytes 786440 | tf_op jit(solution)/shard_map/ppermute | solution.py:24
  35.7 0.8 slice-done
  36.6 1.2 %copy-done = bf16[512,3584]{1,0:T(8,128)(2,1)S(1)} copy-done((bf16[512,3584]{1,0:T(8,128)(2,1)S(1)}, bf16[512,3584]{1,0:T(8,128)(2,1)}, u32[]{:S(2)}) %copy-start) | copy-done | bytes 3670040
  38.3 3.6 %shard_map.110 = (bf16[512,128]{1,0:T(8,128)(2,1)S(1)}, f32[8,512]{1,0:T(8,128)S(1)}, f32[128,3584]{1,0:T(8,128)S(1)}) custom-call(bf16[512,3584]{1,0:T(8,128)(2,1)S(1)} %copy-done, bf16[512,4608]{1,0:T(8,128)(2,1)S(1)} %bitcast.11, f32[512,1]{1,0:T(8,128)S(1)} %copy.53.refs_2_, f32[512,1]{1,0:T(8,128)S(1)} %copy.54.refs_3_, s32[512,1]{1,0:T(8,128)S(1)} %copy.55.refs_4_, ...), custom_call_target="tpu_custom_call" | custom-call | tf_op jit(solution)/shard_map/pallas_call | solution.py:227
  42.6 1.0 %constant_dynamic-update-slice_fusion.6 = bf16[64,8192]{1,0:T(8,128)(2,1)S(1)} fusion(bf16[64,8192]{1,0:T(8,128)(2,1)S(1)} %constant_dynamic-update-slice_fusion.7, bf16[16,8192]{1,0:T(8,128)(2,1)} %get-tuple-element.78), kind=kLoop, calls=%fused_computation.8 | loop fusion | bytes 524288
  43.6 3.6 %shard_map.113 = (bf16[512,128]{1,0:T(8,128)(2,1)S(1)}, f32[8,512]{1,0:T(8,128)S(1)}, f32[64,3584]{1,0:T(8,128)S(1)}, bf16[64,3584]{1,0:T(8,128)(2,1)S(1)}) custom-call(bf16[512,3584]{1,0:T(8,128)(2,1)S(1)} %copy-done, bf16[512,4608]{1,0:T(8,128)(2,1)S(1)} %bitcast.11, f32[512,1]{1,0:T(8,128)S(1)} %copy.53.refs_2_, f32[512,1]{1,0:T(8,128)S(1)} %copy.54.refs_3_, ...), custom_call_target="tpu_custom_call" | custom-call | tf_op jit(solution)/shard_map/pallas_call | solution.py:227
  48.2 1.5 %collective-permute-done.8.refs_0_ = bf16[64,3584]{1,0:T(8,128)(2,1)S(1)} collective-permute-done((bf16[64,3584]{1,0:T(8,128)(2,1)S(1)}, bf16[64,3584]{1,0:T(8,128)(2,1)S(1)}, u32[]{:S(2)}, u32[]{:S(2)}) %collective-permute-start.8) | collective-permute-done | bytes 458784 | tf_op jit(solution)/shard_map/ppermute | solution.py:24
  49.7 0.9 add_convert_fusion.1.refs_3_
  50.6 5.6 %collective-permute-start.9 = (bf16[64,3584]{1,0:T(8,128)(2,1)}, bf16[64,3584]{1,0:T(8,128)(2,1)}, u32[]{:S(2)}, u32[]{:S(2)}) collective-permute-start(bf16[64,3584]{1,0:T(8,128)(2,1)} %add_convert_fusion.1.refs_3_), channel_id=1, source_target_pairs={{0,14},{1,15},{2,0},{3,1},{4,2},{5,3},{6,4},{7,5},{8,6},{9,7},{10,... | collective-permute-start | bytes 1376264 | tf_op jit(solution)/shard_map/ppermute | solution.py:24
  56.3 2.6 %collective-permute-done.12.refs_0_ = bf16[64,8192]{1,0:T(8,128)(2,1)S(1)} collective-permute-done((bf16[64,8192]{1,0:T(8,128)(2,1)S(1)}, bf16[64,8192]{1,0:T(8,128)(2,1)S(1)}, u32[]{:S(2)}, u32[]{:S(2)}) %collective-permute-start.12) | collective-permute-done | bytes 1048608 | tf_op jit(solution)/shard_map/ppermute | solution.py:24
  59.0 3.6 %shard_map.119 = (bf16[512,128]{1,0:T(8,128)(2,1)S(1)}, f32[8,512]{1,0:T(8,128)S(1)}, f32[64,3584]{1,0:T(8,128)S(1)}, bf16[64,3584]{1,0:T(8,128)(2,1)S(1)}) custom-call(bf16[512,3584]{1,0:T(8,128)(2,1)S(1)} %copy-done, bf16[512,4608]{1,0:T(8,128)(2,1)S(1)} %bitcast.11, f32[512,1]{1,0:T(8,128)S(1)} %copy.53.refs_2_, f32[512,1]{1,0:T(8,128)S(1)} %copy.54.refs_3_, ...), custom_call_target="tpu_custom_call" | custom-call | tf_op jit(solution)/shard_map/pallas_call | solution.py:227
  63.3 1.2 %collective-permute-done.13.refs_0_ = bf16[64,3584]{1,0:T(8,128)(2,1)S(1)} collective-permute-done((bf16[64,3584]{1,0:T(8,128)(2,1)S(1)}, bf16[64,3584]{1,0:T(8,128)(2,1)S(1)}, u32[]{:S(2)}, u32[]{:S(2)}) %collective-permute-start.13) | collective-permute-done | bytes 458784 | tf_op jit(solution)/shard_map/ppermute | solution.py:24
  64.7 6.2 %shard_map.124 = (bf16[512,128]{1,0:T(8,128)(2,1)S(1)}, f32[8,512]{1,0:T(8,128)S(1)}, bf16[128,3584]{1,0:T(8,128)(2,1)S(1)}, bf16[128,8192]{1,0:T(8,128)(2,1)S(1)}) custom-call(bf16[512,3584]{1,0:T(8,128)(2,1)S(1)} %copy-done, bf16[512,4608]{1,0:T(8,128)(2,1)S(1)} %bitcast.11, f32[512,1]{1,0:T(8,128)S(1)} %copy.53.refs_2_, f32[512,1]{1,0:T(8,128)S(1)} %copy.54.refs_3_, ...), custom_call_target="tpu_custom_call" | custom-call | tf_op jit(solution)/shard_map/pallas_call | solution.py:227
  71.3 0.9 %copy-done.12 = bf16[128,8192]{1,0:T(8,128)(2,1)} copy-done((bf16[128,8192]{1,0:T(8,128)(2,1)}, bf16[128,8192]{1,0:T(8,128)(2,1)S(1)}, u32[]{:S(2)}) %copy-start.12) | copy-done | bytes 2097176
  72.8 6.2 %shard_map.128 = bf16[512,3584]{1,0:T(8,128)(2,1)} custom-call(bf16[512,128]{1,0:T(8,128)(2,1)} %copy-done.13, bf16[512,128]{1,0:T(8,128)(2,1)} %copy-done.14, bf16[512,128]{1,0:T(8,128)(2,1)} %copy-done.15, bf16[512,128]{1,0:T(8,128)(2,1)} %copy-done.16, bf16[128,3584]{1,0:T(8,128)(2,1)} %refs_4_.1, bf16[64,8192]{1,0:T(8,128)(2,1)} %copy-done.10, ...), custom_call_target="tpu_custom_call" | custom-call | flops 30000001024 | tf_op jit(solution)/shard_map/pallas_call | solution.py:258
  79.6 6.7 %collective-permute-done.16.extra_ref = bf16[128,3584]{1,0:T(8,128)(2,1)S(1)} collective-permute-done((bf16[128,3584]{1,0:T(8,128)(2,1)S(1)}, bf16[128,3584]{1,0:T(8,128)(2,1)S(1)}, u32[]{:S(2)}, u32[]{:S(2)}) %collective-permute-start.16) | collective-permute-done | bytes 917536 | tf_op jit(solution)/shard_map/ppermute | solution.py:24
  86.3 2.0 %shard_map.126 = bf16[128,3584]{1,0:T(8,128)(2,1)} custom-call(s32[1]{0:T(128)} %bitcast.at_ref, f32[128,3584]{1,0:T(8,128)S(1)} %get-tuple-element.68.own_ref, bf16[64,3584]{1,0:T(8,128)(2,1)} %collective-permute-done.9.back0, bf16[64,3584]{1,0:T(8,128)(2,1)S(1)} %collective-permute-done.14.back1, bf16[128,3584]{1,0:T(8,128)(2,1)S(1)} %collective-permute-done.16.extra_ref), custom_call_target="tpu_custom_call" | custom-call | tf_op jit(solution)/shard_map/pallas_call | solution.py:135
  (108 shorter events, 7.3 us)
Async XLA Ops:
  0.6 1.3 %copy-start.1 = (bf16[128,4608]{1,0:T(8,128)(2,1)S(1)}, bf16[128,4608]{1,0:T(8,128)(2,1)}, u32[]{:S(2)}) copy-start(bf16[128,4608]{1,0:T(8,128)(2,1)} %refs_8_.1) | copy-start | bytes 3538948
  1.9 1.2 %copy-start.6 = (bf16[128,3584]{1,0:T(8,128)(2,1)S(1)}, bf16[128,3584]{1,0:T(8,128)(2,1)}, u32[]{:S(2)}) copy-start(bf16[128,3584]{1,0:T(8,128)(2,1)} %refs_4_.1) | copy-start | bytes 2752516
  3.1 4.9 %copy-start.2 = (bf16[128,4608]{1,0:T(8,128)(2,1)S(1)}, bf16[128,4608]{1,0:T(8,128)(2,1)}, u32[]{:S(2)}) copy-start(bf16[128,4608]{1,0:T(8,128)(2,1)} %refs_8_.1) | copy-start | bytes 3538948
  3.1 4.9 %copy-start.7 = (bf16[128,3584]{1,0:T(8,128)(2,1)S(1)}, bf16[128,3584]{1,0:T(8,128)(2,1)}, u32[]{:S(2)}) copy-start(bf16[128,3584]{1,0:T(8,128)(2,1)} %refs_4_.1) | copy-start | bytes 2752516
  3.5 13.4 %collective-permute-start.1 = (bf16[16,8192]{1,0:T(8,128)(2,1)S(1)}, bf16[16,8192]{1,0:T(8,128)(2,1)S(1)}, u32[]{:S(2)}, u32[]{:S(2)}) collective-permute-start(bf16[16,8192]{1,0:T(8,128)(2,1)S(1)} %shard_map.98.refs_1_), channel_id=1, source_target_pairs={{0,2},{1,3},{2,4},{3,5},{4,6},{5,7},{6,8},{7,9},{8,10},{9,11},{10,... | collective-permute-start | bytes 786440 | tf_op jit(solution)/shard_map/ppermute | solution.py:24
  6.5 15.8 %collective-permute-start.3 = (bf16[16,8192]{1,0:T(8,128)(2,1)S(1)}, bf16[16,8192]{1,0:T(8,128)(2,1)S(1)}, u32[]{:S(2)}, u32[]{:S(2)}) collective-permute-start(bf16[16,8192]{1,0:T(8,128)(2,1)S(1)} %shard_map.101), channel_id=1, source_target_pairs={{0,2},{1,3},{2,4},{3,5},{4,6},{5,7},{6,8},{7,9},{8,10},{9,11},{10,... | collective-permute-start | bytes 786440 | tf_op jit(solution)/shard_map/ppermute | solution.py:24
  10.4 17.5 %collective-permute-start.5 = (bf16[16,8192]{1,0:T(8,128)(2,1)S(1)}, bf16[16,8192]{1,0:T(8,128)(2,1)S(1)}, u32[]{:S(2)}, u32[]{:S(2)}) collective-permute-start(bf16[16,8192]{1,0:T(8,128)(2,1)S(1)} %shard_map.95.refs_1_), channel_id=1, source_target_pairs={{0,2},{1,3},{2,4},{3,5},{4,6},{5,7},{6,8},{7,9},{8,10},{9,11},{10,... | collective-permute-start | bytes 786440 | tf_op jit(solution)/shard_map/ppermute | solution.py:24
  12.0 22.4 %collective-permute-start = (bf16[16,8192]{1,0:T(8,128)(2,1)}, bf16[16,8192]{1,0:T(8,128)(2,1)}, u32[]{:S(2)}, u32[]{:S(2)}) collective-permute-start(bf16[16,8192]{1,0:T(8,128)(2,1)} %shard_map.96), channel_id=1, source_target_pairs={{0,2},{1,3},{2,4},{3,5},{4,6},{5,7},{6,8},{7,9},{8,10},{9,11},{10,... | collective-permute-start | bytes 786440 | tf_op jit(solution)/shard_map/ppermute | solution.py:24
  13.5 30.1 %collective-permute-start.7 = (bf16[128,8192]{1,0:T(8,128)(2,1)}, bf16[128,8192]{1,0:T(8,128)(2,1)}, u32[]{:S(2)}, u32[]{:S(2)}) collective-permute-start(bf16[128,8192]{1,0:T(8,128)(2,1)} %get-tuple-element.70), channel_id=1, source_target_pairs={{0,1},{1,4},{2,3},{4,5},{5,8},{6,7},{8,9},{9,12},{10,11},{12,13},{... | collective-permute-start | bytes 6291464 | tf_op jit(solution)/shard_map/ppermute | solution.py:24
  16.9 16.6 %collective-permute-start.2 = (bf16[16,8192]{1,0:T(8,128)(2,1)S(1)}, bf16[16,8192]{1,0:T(8,128)(2,1)S(1)}, u32[]{:S(2)}, u32[]{:S(2)}) collective-permute-start(bf16[16,8192]{1,0:T(8,128)(2,1)S(1)} %get-tuple-element.55.refs_1_), channel_id=1, source_target_pairs={{0,16},{1,17},{2,18},{3,19},{4,20},{5,21},{6,22},{7,23},{8,24},{9,... | collective-permute-start | bytes 786440 | tf_op jit(solution)/shard_map/ppermute | solution.py:24
  22.3 9.2 %collective-permute-start.4 = (bf16[16,8192]{1,0:T(8,128)(2,1)S(1)}, bf16[16,8192]{1,0:T(8,128)(2,1)S(1)}, u32[]{:S(2)}, u32[]{:S(2)}) collective-permute-start(bf16[16,8192]{1,0:T(8,128)(2,1)S(1)} %get-tuple-element.58.refs_1_), channel_id=1, source_target_pairs={{0,16},{1,17},{2,18},{3,19},{4,20},{5,21},{6,22},{7,23},{8,24},{9,... | collective-permute-start | bytes 786440 | tf_op jit(solution)/shard_map/ppermute | solution.py:24
  27.9 28.3 %collective-permute-start.10 = (bf16[16,8192]{1,0:T(8,128)(2,1)S(1)}, bf16[16,8192]{1,0:T(8,128)(2,1)S(1)}, u32[]{:S(2)}, u32[]{:S(2)}) collective-permute-start(bf16[16,8192]{1,0:T(8,128)(2,1)S(1)} %get-tuple-element.62.refs_1_), channel_id=1, source_target_pairs={{0,16},{1,17},{2,18},{3,19},{4,20},{5,21},{6,22},{7,23},{8,24},{9,... | collective-permute-start | bytes 786440 | tf_op jit(solution)/shard_map/ppermute | solution.py:24
  31.5 33.2 %collective-permute-start.15 = (bf16[128,8192]{1,0:T(8,128)(2,1)}, bf16[128,8192]{1,0:T(8,128)(2,1)}, u32[]{:S(2)}, u32[]{:S(2)}) collective-permute-start(bf16[128,8192]{1,0:T(8,128)(2,1)} %get-tuple-element.63.refs_2_), channel_id=1, source_target_pairs={{3,6},{7,10},{11,14},{15,2},{19,22},{23,26},{27,30},{31,18}} | collective-permute-start | bytes 6291464 | tf_op jit(solution)/shard_map/ppermute | solution.py:24
  33.6 10.0 %copy-start.10 = (bf16[64,8192]{1,0:T(8,128)(2,1)}, bf16[64,8192]{1,0:T(8,128)(2,1)S(1)}, u32[]{:S(2)}) copy-start(bf16[64,8192]{1,0:T(8,128)(2,1)S(1)} %constant_dynamic-update-slice_fusion.refs_1_.refs_7_.refs_9_.refs_5_) | copy-start | bytes 3145732
  33.6 10.0 %collective-permute-start.6 = (bf16[64,8192]{1,0:T(8,128)(2,1)S(1)}, bf16[64,8192]{1,0:T(8,128)(2,1)S(1)}, u32[]{:S(2)}, u32[]{:S(2)}) collective-permute-start(bf16[64,8192]{1,0:T(8,128)(2,1)S(1)} %constant_dynamic-update-slice_fusion.refs_1_.refs_7_.refs_9_.refs_5_), channel_id=1, source_target_pairs={{0,1},{1,0},{2,3},{3,2},{4,5},{5,4},{6,7},{7,6},{8,9},{9,8},{10,11... | collective-permute-start | bytes 3145736 | tf_op jit(solution)/shard_map/ppermute | solution.py:24
  34.3 2.2 %slice-start = ((s8[4718592]{0:T(1024)(128)(4,1)}), s8[4194304]{0:T(1024)(128)(4,1)S(1)}, s32[]{:S(2)}) async-start(s8[4718592]{0:T(1024)(128)(4,1)} %bitcast.10), calls=%async_computation | async-start | bytes 8388608
  34.3 2.3 %slice-start.1 = ((s8[4718592]{0:T(1024)(128)(4,1)}), s8[524288]{0:T(1024)(128)(4,1)S(1)}, s32[]{:S(2)}) async-start(s8[4718592]{0:T(1024)(128)(4,1)} %bitcast.10), calls=%async_computation.1 | async-start | bytes 1048576
  34.3 3.5 %copy-start = (bf16[512,3584]{1,0:T(8,128)(2,1)S(1)}, bf16[512,3584]{1,0:T(8,128)(2,1)}, u32[]{:S(2)}) copy-start(bf16[512,3584]{1,0:T(8,128)(2,1)} %refs_0_.7) | copy-start | bytes 11010052
  34.3 3.7 %copy-start.3 = (bf16[128,4608]{1,0:T(8,128)(2,1)S(1)}, bf16[128,4608]{1,0:T(8,128)(2,1)}, u32[]{:S(2)}) copy-start(bf16[128,4608]{1,0:T(8,128)(2,1)} %refs_8_.1) | copy-start | bytes 3538948
  34.3 4.0 %copy-start.8 = (bf16[128,3584]{1,0:T(8,128)(2,1)S(1)}, bf16[128,3584]{1,0:T(8,128)(2,1)}, u32[]{:S(2)}) copy-start(bf16[128,3584]{1,0:T(8,128)(2,1)} %refs_4_.1) | copy-start | bytes 2752516
  34.4 21.8 %collective-permute-start.11 = (bf16[16,8192]{1,0:T(8,128)(2,1)}, bf16[16,8192]{1,0:T(8,128)(2,1)S(1)}, u32[]{:S(2)}, u32[]{:S(2)}) collective-permute-start(bf16[16,8192]{1,0:T(8,128)(2,1)} %get-tuple-element.78), channel_id=1, source_target_pairs={{0,16},{1,17},{2,18},{3,19},{4,20},{5,21},{6,22},{7,23},{8,24},{9,... | collective-permute-start | bytes 786440 | tf_op jit(solution)/shard_map/ppermute | solution.py:24
  43.6 3.6 %copy-start.4 = (bf16[64,8192]{1,0:T(8,128)(2,1)}, bf16[64,8192]{1,0:T(8,128)(2,1)S(1)}, u32[]{:S(2)}) copy-start(bf16[64,8192]{1,0:T(8,128)(2,1)S(1)} %get-tuple-element.72.refs_8_.refs_10_.refs_6_) | copy-start | bytes 3145732
  47.9 1.8 %collective-permute-start.8 = (bf16[64,3584]{1,0:T(8,128)(2,1)S(1)}, bf16[64,3584]{1,0:T(8,128)(2,1)S(1)}, u32[]{:S(2)}, u32[]{:S(2)}) collective-permute-start(bf16[64,3584]{1,0:T(8,128)(2,1)S(1)} %get-tuple-element.75.refs_1_), channel_id=1, source_target_pairs={{0,1},{1,0},{2,3},{3,2},{4,5},{5,4},{6,7},{7,6},{8,9},{9,8},{10,11... | collective-permute-start | bytes 1376264 | tf_op jit(solution)/shard_map/ppermute | solution.py:24
  50.6 29.0 %collective-permute-start.9 = (bf16[64,3584]{1,0:T(8,128)(2,1)}, bf16[64,3584]{1,0:T(8,128)(2,1)}, u32[]{:S(2)}, u32[]{:S(2)}) collective-permute-start(bf16[64,3584]{1,0:T(8,128)(2,1)} %add_convert_fusion.1.refs_3_), channel_id=1, source_target_pairs={{0,14},{1,15},{2,0},{3,1},{4,2},{5,3},{6,4},{7,5},{8,6},{9,7},{10,... | collective-permute-start | bytes 1376264 | tf_op jit(solution)/shard_map/ppermute | solution.py:24
  56.2 2.7 %copy-start.9 = (bf16[64,8192]{1,0:T(8,128)(2,1)}, bf16[64,8192]{1,0:T(8,128)(2,1)S(1)}, u32[]{:S(2)}) copy-start(bf16[64,8192]{1,0:T(8,128)(2,1)S(1)} %constant_dynamic-update-slice_fusion.4.refs_1_.refs_7_.refs_9_) | copy-start | bytes 3145732
  56.2 2.7 %collective-permute-start.12 = (bf16[64,8192]{1,0:T(8,128)(2,1)S(1)}, bf16[64,8192]{1,0:T(8,128)(2,1)S(1)}, u32[]{:S(2)}, u32[]{:S(2)}) collective-permute-start(bf16[64,8192]{1,0:T(8,128)(2,1)S(1)} %constant_dynamic-update-slice_fusion.4.refs_1_.refs_7_.refs_9_), channel_id=1, source_target_pairs={{0,1},{1,0},{2,3},{3,2},{4,5},{5,4},{6,7},{7,6},{8,9},{9,8},{10,11... | collective-permute-start | bytes 3145736 | tf_op jit(solution)/shard_map/ppermute | solution.py:24
  58.9 3.6 %copy-start.5 = (bf16[64,8192]{1,0:T(8,128)(2,1)}, bf16[64,8192]{1,0:T(8,128)(2,1)S(1)}, u32[]{:S(2)}) copy-start(bf16[64,8192]{1,0:T(8,128)(2,1)S(1)} %get-tuple-element.83.refs_8_.refs_10_) | copy-start | bytes 3145732
  62.6 1.9 %collective-permute-start.13 = (bf16[64,3584]{1,0:T(8,128)(2,1)S(1)}, bf16[64,3584]{1,0:T(8,128)(2,1)S(1)}, u32[]{:S(2)}, u32[]{:S(2)}) collective-permute-start(bf16[64,3584]{1,0:T(8,128)(2,1)S(1)} %get-tuple-element.86.refs_1_), channel_id=1, source_target_pairs={{0,1},{1,0},{2,3},{3,2},{4,5},{5,4},{6,7},{7,6},{8,9},{9,8},{10,11... | collective-permute-start | bytes 1376264 | tf_op jit(solution)/shard_map/ppermute | solution.py:24
  64.6 15.0 %collective-permute-start.14 = (bf16[64,3584]{1,0:T(8,128)(2,1)S(1)}, bf16[64,3584]{1,0:T(8,128)(2,1)S(1)}, u32[]{:S(2)}, u32[]{:S(2)}) collective-permute-start(bf16[64,3584]{1,0:T(8,128)(2,1)S(1)} %add_convert_fusion.refs_1_), channel_id=1, source_target_pairs={{0,14},{1,15},{2,0},{3,1},{4,2},{5,3},{6,4},{7,5},{8,6},{9,7},{10,... | collective-permute-start | bytes 1376264 | tf_op jit(solution)/shard_map/ppermute | solution.py:24
  70.8 1.4 %copy-start.12 = (bf16[128,8192]{1,0:T(8,128)(2,1)}, bf16[128,8192]{1,0:T(8,128)(2,1)S(1)}, u32[]{:S(2)}) copy-start(bf16[128,8192]{1,0:T(8,128)(2,1)S(1)} %get-tuple-element.98.refs_9_) | copy-start | bytes 6291460
  70.9 1.4 %copy-start.16 = (bf16[512,128]{1,0:T(8,128)(2,1)}, bf16[512,128]{1,0:T(8,128)(2,1)S(1)}, u32[]{:S(2)}) copy-start(bf16[512,128]{1,0:T(8,128)(2,1)S(1)} %get-tuple-element.97.refs_3_) | copy-start | bytes 393220
  70.9 15.4 %collective-permute-start.16 = (bf16[128,3584]{1,0:T(8,128)(2,1)S(1)}, bf16[128,3584]{1,0:T(8,128)(2,1)S(1)}, u32[]{:S(2)}, u32[]{:S(2)}) collective-permute-start(bf16[128,3584]{1,0:T(8,128)(2,1)S(1)} %get-tuple-element.94.refs_1_), channel_id=1, source_target_pairs={{0,13},{1,0},{2,15},{3,2},{4,1},{5,4},{6,3},{7,6},{8,5},{9,8},{10,... | collective-permute-start | bytes 2752520 | tf_op jit(solution)/shard_map/ppermute | solution.py:24
  (7 other events, 4.9 us)

commit v12 on v9

--- a/solution.py
+++ b/solution.py
@@ -369,13 +369,15 @@
     extra_scores, loss, extra_part, extra = meet(
         [late, early, 0], None, extra_id * width + ids_in, loss, [jnp.bfloat16], [order], from_late
     )
+    extra_part, order = gate([extra_part, order], [])
+    order = pause(order, [extra_part])
     extra_part = permuted(extra_part, extra_back)
 
     rows_grad = rows_product(
         [own_scores, scores0, scores1, extra_scores],
         [student_head, mine0, theirs0, mine1, theirs1, extra],
         depth,
-        [extra_scores],
+        [order],
     )
     head_grad = head_total(at, own_part, [back0, back1], extra_part)
     return (head_grad, rows_grad, loss[0])

time: 82.8 us -> 84.1 us (1.016)
  the two profiles are of different devices: /device:TPU:27 before, /device:TPU:1 now
where the time goes in v12:
time: 84.1 us; the launch traced here: 83.7 us
  Pallas kernels  28.5 us (34%)
  starting transfers between devices  25.4 us (30%)
  waiting for transfers between devices  18 us (21%)
  local copies, waits for them, and re-layouts  9.23 us (11%)
  between operations  1.3 us (2%)
  other arithmetic  1.29 us (2%)
    ppermute x17, starting transfers between devices, permuted(): return lax.ppermute(value, BOTH, pairs)  25.4 us
    ppermute x17, waiting for transfers between devices, permuted(): return lax.ppermute(value, BOTH, pairs)  18 us
    pallas_call x4, Pallas kernels, meeting(): pl.pallas_call(kernel, out_shape=out_shape, in_specs=[whole] * (7 + piece...  17 us
    unnamed x46, local copies, waits for them, and re-layouts  8.16 us
    pallas_call x1, Pallas kernels, rows_product(): pl.pallas_call(kernel, grid=(4,), out_shape=jax.ShapeDtypeStruct((count,...  6.22 us
    pallas_call x2, Pallas kernels, packed(): pl.pallas_call(kernel, out_shape=[jax.ShapeDtypeStruct((rows, depth + dep...  3.16 us
    pallas_call x1, Pallas kernels, head_total(): pl.pallas_call(kernel, out_shape=jax.ShapeDtypeStruct((width, depth), jnp...  2.04 us
  transfers between devices with their start and end apart: 17, of which 8 were waited for; matrix products, arithmetic and copies ran while one was open for 7% of the time, Pallas kernels for 30%

profile of v12, /device:TPU:1, one launch (start us, length us, event | category | flops | bytes accessed | tf_op | source)
XLA Modules:
  0.0 83.7 jit_solution(10514527031147067663)
XLA Ops:
  0.6 1.3 %copy-done.1 = bf16[128,4608]{1,0:T(8,128)(2,1)S(1)} copy-done((bf16[128,4608]{1,0:T(8,128)(2,1)S(1)}, bf16[128,4608]{1,0:T(8,128)(2,1)}, u32[]{:S(2)}) %copy-start.1) | copy-done | bytes 1179672
  1.9 1.2 %copy-done.5 = bf16[128,3584]{1,0:T(8,128)(2,1)S(1)} copy-done((bf16[128,3584]{1,0:T(8,128)(2,1)S(1)}, bf16[128,3584]{1,0:T(8,128)(2,1)}, u32[]{:S(2)}) %copy-start.5) | copy-done | bytes 917528
  3.1 0.9 %shard_map.95 = (bf16[16,8192]{1,0:T(8,128)(2,1)S(1)}, bf16[16,8192]{1,0:T(8,128)(2,1)}) custom-call(s32[1]{0:T(128)} %bitcast.at_ref, bf16[128,3584]{1,0:T(8,128)(2,1)S(1)} %copy-done.5, bf16[128,4608]{1,0:T(8,128)(2,1)S(1)} %copy-done.1), custom_call_target="tpu_custom_call" | custom-call | tf_op jit(solution)/shard_map/pallas_call | solution.py:95
  4.0 2.1 %collective-permute-start.2 = (bf16[16,8192]{1,0:T(8,128)(2,1)S(1)}, bf16[16,8192]{1,0:T(8,128)(2,1)}, u32[]{:S(2)}, u32[]{:S(2)}) collective-permute-start(bf16[16,8192]{1,0:T(8,128)(2,1)S(1)} %shard_map.96.refs_1_), channel_id=1, source_target_pairs={{0,2},{1,3},{2,4},{3,5},{4,6},{5,7},{6,8},{7,9},{8,10},{9,11},{10,... | collective-permute-start | bytes 786440 | tf_op jit(solution)/shard_map/ppermute | solution.py:24
  6.1 1.3 %collective-permute-start.1 = (bf16[16,8192]{1,0:T(8,128)(2,1)}, bf16[16,8192]{1,0:T(8,128)(2,1)}, u32[]{:S(2)}, u32[]{:S(2)}) collective-permute-start(bf16[16,8192]{1,0:T(8,128)(2,1)} %shard_map.97), channel_id=1, source_target_pairs={{0,2},{1,3},{2,4},{3,5},{4,6},{5,7},{6,8},{7,9},{8,10},{9,11},{10,... | collective-permute-start | bytes 786440 | tf_op jit(solution)/shard_map/ppermute | solution.py:24
  7.4 2.3 %shard_map.94 = (bf16[16,8192]{1,0:T(8,128)(2,1)}, bf16[16,8192]{1,0:T(8,128)(2,1)}, bf16[128,8192]{1,0:T(8,128)(2,1)}, bf16[128,8192]{1,0:T(8,128)(2,1)}) custom-call(s32[1]{0:T(128)} %bitcast.at_ref, bf16[128,3584]{1,0:T(8,128)(2,1)S(1)} %copy-done.6, bf16[128,4608]{1,0:T(8,128)(2,1)S(1)} %copy-done.2), custom_call_target="tpu_custom_call" | custom-call | tf_op jit(solution)/shard_map/pallas_call | solution.py:95
  9.7 1.3 %collective-permute-start = (bf16[16,8192]{1,0:T(8,128)(2,1)}, bf16[16,8192]{1,0:T(8,128)(2,1)S(1)}, u32[]{:S(2)}, u32[]{:S(2)}) collective-permute-start(bf16[16,8192]{1,0:T(8,128)(2,1)} %get-tuple-element.52), channel_id=1, source_target_pairs={{0,2},{1,3},{2,4},{3,5},{4,6},{5,7},{6,8},{7,9},{8,10},{9,11},{10,... | collective-permute-start | bytes 786440 | tf_op jit(solution)/shard_map/ppermute | solution.py:24
  10.9 1.3 %collective-permute-start.7 = (bf16[16,8192]{1,0:T(8,128)(2,1)}, bf16[16,8192]{1,0:T(8,128)(2,1)}, u32[]{:S(2)}, u32[]{:S(2)}) collective-permute-start(bf16[16,8192]{1,0:T(8,128)(2,1)} %get-tuple-element.69), channel_id=1, source_target_pairs={{0,2},{1,3},{2,4},{3,5},{4,6},{5,7},{6,8},{7,9},{8,10},{9,11},{10,... | collective-permute-start | bytes 786440 | tf_op jit(solution)/shard_map/ppermute | solution.py:24
  12.2 4.9 %collective-permute-start.6 = (bf16[128,8192]{1,0:T(8,128)(2,1)}, bf16[128,8192]{1,0:T(8,128)(2,1)}, u32[]{:S(2)}, u32[]{:S(2)}) collective-permute-start(bf16[128,8192]{1,0:T(8,128)(2,1)} %get-tuple-element.68), channel_id=1, source_target_pairs={{0,1},{1,4},{2,3},{4,5},{5,8},{6,7},{8,9},{9,12},{10,11},{12,13},{... | collective-permute-start | bytes 6291464 | tf_op jit(solution)/shard_map/ppermute | solution.py:24
  18.6 1.3 %collective-permute-start.3 = (bf16[16,8192]{1,0:T(8,128)(2,1)}, bf16[16,8192]{1,0:T(8,128)(2,1)S(1)}, u32[]{:S(2)}, u32[]{:S(2)}) collective-permute-start(bf16[16,8192]{1,0:T(8,128)(2,1)} %get-tuple-element.57.refs_1_), channel_id=1, source_target_pairs={{0,16},{1,17},{2,18},{3,19},{4,20},{5,21},{6,22},{7,23},{8,24},{9,... | collective-permute-start | bytes 786440 | tf_op jit(solution)/shard_map/ppermute | solution.py:24
  19.8 1.1 %collective-permute-done.1.refs_0_ = bf16[16,8192]{1,0:T(8,128)(2,1)} collective-permute-done((bf16[16,8192]{1,0:T(8,128)(2,1)}, bf16[16,8192]{1,0:T(8,128)(2,1)}, u32[]{:S(2)}, u32[]{:S(2)}) %collective-permute-start.1) | collective-permute-done | bytes 262176 | tf_op jit(solution)/shard_map/ppermute | solution.py:24
  20.9 1.0 %collective-permute-start.4 = (bf16[16,8192]{1,0:T(8,128)(2,1)}, bf16[16,8192]{1,0:T(8,128)(2,1)S(1)}, u32[]{:S(2)}, u32[]{:S(2)}) collective-permute-start(bf16[16,8192]{1,0:T(8,128)(2,1)} %get-tuple-element.59.refs_1_), channel_id=1, source_target_pairs={{0,16},{1,17},{2,18},{3,19},{4,20},{5,21},{6,22},{7,23},{8,24},{9,... | collective-permute-start | bytes 786440 | tf_op jit(solution)/shard_map/ppermute | solution.py:24
  21.9 1.1 %constant_dynamic-update-slice_fusion.3 = bf16[64,8192]{1,0:T(8,128)(2,1)S(1)} fusion(bf16[16,8192]{1,0:T(8,128)(2,1)} %get-tuple-element.57.refs_1_), kind=kLoop, calls=%fused_computation.5 | loop fusion | bytes 524288
  23.0 3.4 %collective-permute-done.refs_0_ = bf16[16,8192]{1,0:T(8,128)(2,1)S(1)} collective-permute-done((bf16[16,8192]{1,0:T(8,128)(2,1)}, bf16[16,8192]{1,0:T(8,128)(2,1)S(1)}, u32[]{:S(2)}, u32[]{:S(2)}) %collective-permute-start) | collective-permute-done | bytes 262176 | tf_op jit(solution)/shard_map/ppermute | solution.py:24
  26.4 1.0 %collective-permute-start.10 = (bf16[16,8192]{1,0:T(8,128)(2,1)S(1)}, bf16[16,8192]{1,0:T(8,128)(2,1)S(1)}, u32[]{:S(2)}, u32[]{:S(2)}) collective-permute-start(bf16[16,8192]{1,0:T(8,128)(2,1)S(1)} %get-tuple-element.63.refs_1_), channel_id=1, source_target_pairs={{0,16},{1,17},{2,18},{3,19},{4,20},{5,21},{6,22},{7,23},{8,24},{9,... | collective-permute-start | bytes 786440 | tf_op jit(solution)/shard_map/ppermute | solution.py:24
  27.5 3.6 %shard_map.104 = (bf16[512,128]{1,0:T(8,128)(2,1)S(1)}, f32[8,512]{1,0:T(8,128)S(1)}, f32[128,3584]{1,0:T(8,128)S(1)}) custom-call(bf16[512,3584]{1,0:T(8,128)(2,1)S(1)} %copy-done, bf16[512,4608]{1,0:T(8,128)(2,1)S(1)} %bitcast.11, f32[512,1]{1,0:T(8,128)S(1)} %copy.51.refs_2_, f32[512,1]{1,0:T(8,128)S(1)} %copy.52.refs_3_, s32[512,1]{1,0:T(8,128)S(1)} %copy.53.refs_4_, ...), custom_call_target="tpu_custom_call" | custom-call | tf_op jit(solution)/shard_map/pallas_call | solution.py:227
  31.8 1.0 %constant_dynamic-update-slice_fusion.2 = bf16[64,8192]{1,0:T(8,128)(2,1)S(1)} fusion(bf16[64,8192]{1,0:T(8,128)(2,1)S(1)} %constant_dynamic-update-slice_fusion.3, bf16[16,8192]{1,0:T(8,128)(2,1)} %get-tuple-element.59.refs_1_), kind=kLoop, calls=%fused_computation.4 | loop fusion | bytes 524288
  32.8 2.0 %collective-permute-start.15 = (bf16[128,8192]{1,0:T(8,128)(2,1)}, bf16[128,8192]{1,0:T(8,128)(2,1)}, u32[]{:S(2)}, u32[]{:S(2)}) collective-permute-start(bf16[128,8192]{1,0:T(8,128)(2,1)} %get-tuple-element.64.refs_2_), channel_id=1, source_target_pairs={{3,6},{7,10},{11,14},{15,2},{19,22},{23,26},{27,30},{31,18}} | collective-permute-start | bytes 6291464 | tf_op jit(solution)/shard_map/ppermute | solution.py:24
  34.9 2.8 %collective-permute-start.5 = (bf16[64,8192]{1,0:T(8,128)(2,1)S(1)}, bf16[64,8192]{1,0:T(8,128)(2,1)S(1)}, u32[]{:S(2)}, u32[]{:S(2)}) collective-permute-start(bf16[64,8192]{1,0:T(8,128)(2,1)S(1)} %constant_dynamic-update-slice_fusion.refs_1_.refs_7_.refs_9_.refs_5_), channel_id=1, source_target_pairs={{0,1},{1,0},{2,3},{3,2},{4,5},{5,4},{6,7},{7,6},{8,9},{9,8},{10,11... | collective-permute-start | bytes 3145736 | tf_op jit(solution)/shard_map/ppermute | solution.py:24
  37.8 1.0 %constant_dynamic-update-slice_fusion.6 = bf16[64,8192]{1,0:T(8,128)(2,1)S(1)} fusion(bf16[64,8192]{1,0:T(8,128)(2,1)S(1)} %constant_dynamic-update-slice_fusion.7, bf16[16,8192]{1,0:T(8,128)(2,1)} %get-tuple-element.78), kind=kLoop, calls=%fused_computation.8 | loop fusion | bytes 524288
  38.8 1.2 %collective-permute-done.5.refs_0_ = bf16[64,8192]{1,0:T(8,128)(2,1)S(1)} collective-permute-done((bf16[64,8192]{1,0:T(8,128)(2,1)S(1)}, bf16[64,8192]{1,0:T(8,128)(2,1)S(1)}, u32[]{:S(2)}, u32[]{:S(2)}) %collective-permute-start.5) | collective-permute-done | bytes 1048608 | tf_op jit(solution)/shard_map/ppermute | solution.py:24
  40.3 3.6 %shard_map.111 = (bf16[512,128]{1,0:T(8,128)(2,1)S(1)}, f32[8,512]{1,0:T(8,128)S(1)}, f32[64,3584]{1,0:T(8,128)S(1)}, bf16[64,3584]{1,0:T(8,128)(2,1)S(1)}) custom-call(bf16[512,3584]{1,0:T(8,128)(2,1)S(1)} %copy-done, bf16[512,4608]{1,0:T(8,128)(2,1)S(1)} %bitcast.11, f32[512,1]{1,0:T(8,128)S(1)} %copy.51.refs_2_, f32[512,1]{1,0:T(8,128)S(1)} %copy.52.refs_3_, ...), custom_call_target="tpu_custom_call" | custom-call | tf_op jit(solution)/shard_map/pallas_call | solution.py:227
  44.0 3.2 %collective-permute-start.8 = (bf16[64,3584]{1,0:T(8,128)(2,1)S(1)}, bf16[64,3584]{1,0:T(8,128)(2,1)S(1)}, u32[]{:S(2)}, u32[]{:S(2)}) collective-permute-start(bf16[64,3584]{1,0:T(8,128)(2,1)S(1)} %get-tuple-element.75.refs_1_), channel_id=1, source_target_pairs={{0,1},{1,0},{2,3},{3,2},{4,5},{5,4},{6,7},{7,6},{8,9},{9,8},{10,11... | collective-permute-start | bytes 1376264 | tf_op jit(solution)/shard_map/ppermute | solution.py:24
  47.1 1.4 %collective-permute-done.8.refs_0_ = bf16[64,3584]{1,0:T(8,128)(2,1)S(1)} collective-permute-done((bf16[64,3584]{1,0:T(8,128)(2,1)S(1)}, bf16[64,3584]{1,0:T(8,128)(2,1)S(1)}, u32[]{:S(2)}, u32[]{:S(2)}) %collective-permute-start.8) | collective-permute-done | bytes 458784 | tf_op jit(solution)/shard_map/ppermute | solution.py:24
  50.0 2.3 %collective-permute-done.12.refs_0_ = bf16[64,8192]{1,0:T(8,128)(2,1)S(1)} collective-permute-done((bf16[64,8192]{1,0:T(8,128)(2,1)S(1)}, bf16[64,8192]{1,0:T(8,128)(2,1)S(1)}, u32[]{:S(2)}, u32[]{:S(2)}) %collective-permute-start.12) | collective-permute-done | bytes 1048608 | tf_op jit(solution)/shard_map/ppermute | solution.py:24
  52.3 3.6 %shard_map.117 = (bf16[512,128]{1,0:T(8,128)(2,1)S(1)}, f32[8,512]{1,0:T(8,128)S(1)}, f32[64,3584]{1,0:T(8,128)S(1)}, bf16[64,3584]{1,0:T(8,128)(2,1)S(1)}) custom-call(bf16[512,3584]{1,0:T(8,128)(2,1)S(1)} %copy-done, bf16[512,4608]{1,0:T(8,128)(2,1)S(1)} %bitcast.11, f32[512,1]{1,0:T(8,128)S(1)} %copy.51.refs_2_, f32[512,1]{1,0:T(8,128)S(1)} %copy.52.refs_3_, ...), custom_call_target="tpu_custom_call" | custom-call | tf_op jit(solution)/shard_map/pallas_call | solution.py:227
  56.6 1.2 %collective-permute-done.13.refs_0_ = bf16[64,3584]{1,0:T(8,128)(2,1)S(1)} collective-permute-done((bf16[64,3584]{1,0:T(8,128)(2,1)S(1)}, bf16[64,3584]{1,0:T(8,128)(2,1)S(1)}, u32[]{:S(2)}, u32[]{:S(2)}) %collective-permute-start.13) | collective-permute-done | bytes 458784 | tf_op jit(solution)/shard_map/ppermute | solution.py:24
  57.9 1.7 %collective-permute-start.14 = (bf16[64,3584]{1,0:T(8,128)(2,1)S(1)}, bf16[64,3584]{1,0:T(8,128)(2,1)S(1)}, u32[]{:S(2)}, u32[]{:S(2)}) collective-permute-start(bf16[64,3584]{1,0:T(8,128)(2,1)S(1)} %add_convert_fusion.refs_1_), channel_id=1, source_target_pairs={{0,14},{1,15},{2,0},{3,1},{4,2},{5,3},{6,4},{7,5},{8,6},{9,7},{10,... | collective-permute-start | bytes 1376264 | tf_op jit(solution)/shard_map/ppermute | solution.py:24
  59.6 6.2 %shard_map.122 = (bf16[512,128]{1,0:T(8,128)(2,1)S(1)}, f32[8,512]{1,0:T(8,128)S(1)}, bf16[128,3584]{1,0:T(8,128)(2,1)S(1)}, bf16[128,8192]{1,0:T(8,128)(2,1)S(1)}) custom-call(bf16[512,3584]{1,0:T(8,128)(2,1)S(1)} %copy-done, bf16[512,4608]{1,0:T(8,128)(2,1)S(1)} %bitcast.11, f32[512,1]{1,0:T(8,128)S(1)} %copy.51.refs_2_, f32[512,1]{1,0:T(8,128)S(1)} %copy.52.refs_3_, ...), custom_call_target="tpu_custom_call" | custom-call | tf_op jit(solution)/shard_map/pallas_call | solution.py:227
  67.7 6.2 %shard_map.126 = bf16[512,3584]{1,0:T(8,128)(2,1)} custom-call(bf16[512,128]{1,0:T(8,128)(2,1)} %copy-done.11, bf16[512,128]{1,0:T(8,128)(2,1)} %copy-done.12, bf16[512,128]{1,0:T(8,128)(2,1)} %copy-done.13, bf16[512,128]{1,0:T(8,128)(2,1)} %copy-done.14, bf16[128,3584]{1,0:T(8,128)(2,1)} %refs_4_.1, bf16[64,8192]{1,0:T(8,128)(2,1)} %copy-done.8, ...), custom_call_target="tpu_custom_call" | custom-call | flops 30000001024 | tf_op jit(solution)/shard_map/pallas_call | solution.py:258
  74.5 7.0 %collective-permute-done.16.extra_ref = bf16[128,3584]{1,0:T(8,128)(2,1)S(1)} collective-permute-done((bf16[128,3584]{1,0:T(8,128)(2,1)S(1)}, bf16[128,3584]{1,0:T(8,128)(2,1)S(1)}, u32[]{:S(2)}, u32[]{:S(2)}) %collective-permute-start.16) | collective-permute-done | bytes 917536 | tf_op jit(solution)/shard_map/ppermute | solution.py:24
  81.5 2.0 %shard_map.124 = bf16[128,3584]{1,0:T(8,128)(2,1)} custom-call(s32[1]{0:T(128)} %bitcast.at_ref, f32[128,3584]{1,0:T(8,128)S(1)} %get-tuple-element.61.own_ref, bf16[64,3584]{1,0:T(8,128)(2,1)} %collective-permute-done.9.back0, bf16[64,3584]{1,0:T(8,128)(2,1)S(1)} %collective-permute-done.14.back1, bf16[128,3584]{1,0:T(8,128)(2,1)S(1)} %collective-permute-done.16.extra_ref), custom_call_target="tpu_custom_call" | custom-call | tf_op jit(solution)/shard_map/pallas_call | solution.py:135
  (102 shorter events, 7.0 us)
Async XLA Ops:
  0.6 1.3 %copy-start.1 = (bf16[128,4608]{1,0:T(8,128)(2,1)S(1)}, bf16[128,4608]{1,0:T(8,128)(2,1)}, u32[]{:S(2)}) copy-start(bf16[128,4608]{1,0:T(8,128)(2,1)} %refs_8_.1) | copy-start | bytes 3538948
  1.9 1.2 %copy-start.5 = (bf16[128,3584]{1,0:T(8,128)(2,1)S(1)}, bf16[128,3584]{1,0:T(8,128)(2,1)}, u32[]{:S(2)}) copy-start(bf16[128,3584]{1,0:T(8,128)(2,1)} %refs_4_.1) | copy-start | bytes 2752516
  3.1 4.3 %copy-start.2 = (bf16[128,4608]{1,0:T(8,128)(2,1)S(1)}, bf16[128,4608]{1,0:T(8,128)(2,1)}, u32[]{:S(2)}) copy-start(bf16[128,4608]{1,0:T(8,128)(2,1)} %refs_8_.1) | copy-start | bytes 3538948
  3.1 4.3 %copy-start.6 = (bf16[128,3584]{1,0:T(8,128)(2,1)S(1)}, bf16[128,3584]{1,0:T(8,128)(2,1)}, u32[]{:S(2)}) copy-start(bf16[128,3584]{1,0:T(8,128)(2,1)} %refs_4_.1) | copy-start | bytes 2752516
  4.0 14.6 %collective-permute-start.2 = (bf16[16,8192]{1,0:T(8,128)(2,1)S(1)}, bf16[16,8192]{1,0:T(8,128)(2,1)}, u32[]{:S(2)}, u32[]{:S(2)}) collective-permute-start(bf16[16,8192]{1,0:T(8,128)(2,1)S(1)} %shard_map.96.refs_1_), channel_id=1, source_target_pairs={{0,2},{1,3},{2,4},{3,5},{4,6},{5,7},{6,8},{7,9},{8,10},{9,11},{10,... | collective-permute-start | bytes 786440 | tf_op jit(solution)/shard_map/ppermute | solution.py:24
  6.1 14.8 %collective-permute-start.1 = (bf16[16,8192]{1,0:T(8,128)(2,1)}, bf16[16,8192]{1,0:T(8,128)(2,1)}, u32[]{:S(2)}, u32[]{:S(2)}) collective-permute-start(bf16[16,8192]{1,0:T(8,128)(2,1)} %shard_map.97), channel_id=1, source_target_pairs={{0,2},{1,3},{2,4},{3,5},{4,6},{5,7},{6,8},{7,9},{8,10},{9,11},{10,... | collective-permute-start | bytes 786440 | tf_op jit(solution)/shard_map/ppermute | solution.py:24
  9.7 16.8 %collective-permute-start = (bf16[16,8192]{1,0:T(8,128)(2,1)}, bf16[16,8192]{1,0:T(8,128)(2,1)S(1)}, u32[]{:S(2)}, u32[]{:S(2)}) collective-permute-start(bf16[16,8192]{1,0:T(8,128)(2,1)} %get-tuple-element.52), channel_id=1, source_target_pairs={{0,2},{1,3},{2,4},{3,5},{4,6},{5,7},{6,8},{7,9},{8,10},{9,11},{10,... | collective-permute-start | bytes 786440 | tf_op jit(solution)/shard_map/ppermute | solution.py:24
  10.9 26.8 %collective-permute-start.7 = (bf16[16,8192]{1,0:T(8,128)(2,1)}, bf16[16,8192]{1,0:T(8,128)(2,1)}, u32[]{:S(2)}, u32[]{:S(2)}) collective-permute-start(bf16[16,8192]{1,0:T(8,128)(2,1)} %get-tuple-element.69), channel_id=1, source_target_pairs={{0,2},{1,3},{2,4},{3,5},{4,6},{5,7},{6,8},{7,9},{8,10},{9,11},{10,... | collective-permute-start | bytes 786440 | tf_op jit(solution)/shard_map/ppermute | solution.py:24
  12.2 28.2 %collective-permute-start.6 = (bf16[128,8192]{1,0:T(8,128)(2,1)}, bf16[128,8192]{1,0:T(8,128)(2,1)}, u32[]{:S(2)}, u32[]{:S(2)}) collective-permute-start(bf16[128,8192]{1,0:T(8,128)(2,1)} %get-tuple-element.68), channel_id=1, source_target_pairs={{0,1},{1,4},{2,3},{4,5},{5,8},{6,7},{8,9},{9,12},{10,11},{12,13},{... | collective-permute-start | bytes 6291464 | tf_op jit(solution)/shard_map/ppermute | solution.py:24
  17.2 1.0 %copy-start.15 = (s32[512]{0:T(512)S(1)}, s32[512]{0:T(512)}, u32[]{:S(2)}) copy-start(s32[512]{0:T(512)} %param.13) | copy-start | bytes 6148
  18.6 16.3 %collective-permute-start.3 = (bf16[16,8192]{1,0:T(8,128)(2,1)}, bf16[16,8192]{1,0:T(8,128)(2,1)S(1)}, u32[]{:S(2)}, u32[]{:S(2)}) collective-permute-start(bf16[16,8192]{1,0:T(8,128)(2,1)} %get-tuple-element.57.refs_1_), channel_id=1, source_target_pairs={{0,16},{1,17},{2,18},{3,19},{4,20},{5,21},{6,22},{7,23},{8,24},{9,... | collective-permute-start | bytes 786440 | tf_op jit(solution)/shard_map/ppermute | solution.py:24
  20.9 11.9 %collective-permute-start.4 = (bf16[16,8192]{1,0:T(8,128)(2,1)}, bf16[16,8192]{1,0:T(8,128)(2,1)S(1)}, u32[]{:S(2)}, u32[]{:S(2)}) collective-permute-start(bf16[16,8192]{1,0:T(8,128)(2,1)} %get-tuple-element.59.refs_1_), channel_id=1, source_target_pairs={{0,16},{1,17},{2,18},{3,19},{4,20},{5,21},{6,22},{7,23},{8,24},{9,... | collective-permute-start | bytes 786440 | tf_op jit(solution)/shard_map/ppermute | solution.py:24
  21.9 5.5 %slice-start = ((s8[4718592]{0:T(1024)(128)(4,1)}), s8[4194304]{0:T(1024)(128)(4,1)S(1)}, s32[]{:S(2)}) async-start(s8[4718592]{0:T(1024)(128)(4,1)} %bitcast.10), calls=%async_computation | async-start | bytes 8388608
  21.9 5.6 %slice-start.1 = ((s8[4718592]{0:T(1024)(128)(4,1)}), s8[524288]{0:T(1024)(128)(4,1)S(1)}, s32[]{:S(2)}) async-start(s8[4718592]{0:T(1024)(128)(4,1)} %bitcast.10), calls=%async_computation.1 | async-start | bytes 1048576
  21.9 5.6 %copy-start = (bf16[512,3584]{1,0:T(8,128)(2,1)S(1)}, bf16[512,3584]{1,0:T(8,128)(2,1)}, u32[]{:S(2)}) copy-start(bf16[512,3584]{1,0:T(8,128)(2,1)} %refs_0_.7) | copy-start | bytes 11010052
  26.4 23.0 %collective-permute-start.10 = (bf16[16,8192]{1,0:T(8,128)(2,1)S(1)}, bf16[16,8192]{1,0:T(8,128)(2,1)S(1)}, u32[]{:S(2)}, u32[]{:S(2)}) collective-permute-start(bf16[16,8192]{1,0:T(8,128)(2,1)S(1)} %get-tuple-element.63.refs_1_), channel_id=1, source_target_pairs={{0,16},{1,17},{2,18},{3,19},{4,20},{5,21},{6,22},{7,23},{8,24},{9,... | collective-permute-start | bytes 786440 | tf_op jit(solution)/shard_map/ppermute | solution.py:24
  32.8 26.8 %collective-permute-start.15 = (bf16[128,8192]{1,0:T(8,128)(2,1)}, bf16[128,8192]{1,0:T(8,128)(2,1)}, u32[]{:S(2)}, u32[]{:S(2)}) collective-permute-start(bf16[128,8192]{1,0:T(8,128)(2,1)} %get-tuple-element.64.refs_2_), channel_id=1, source_target_pairs={{3,6},{7,10},{11,14},{15,2},{19,22},{23,26},{27,30},{31,18}} | collective-permute-start | bytes 6291464 | tf_op jit(solution)/shard_map/ppermute | solution.py:24
  34.9 5.5 %copy-start.8 = (bf16[64,8192]{1,0:T(8,128)(2,1)}, bf16[64,8192]{1,0:T(8,128)(2,1)S(1)}, u32[]{:S(2)}) copy-start(bf16[64,8192]{1,0:T(8,128)(2,1)S(1)} %constant_dynamic-update-slice_fusion.refs_1_.refs_7_.refs_9_.refs_5_) | copy-start | bytes 3145732
  34.9 5.1 %collective-permute-start.5 = (bf16[64,8192]{1,0:T(8,128)(2,1)S(1)}, bf16[64,8192]{1,0:T(8,128)(2,1)S(1)}, u32[]{:S(2)}, u32[]{:S(2)}) collective-permute-start(bf16[64,8192]{1,0:T(8,128)(2,1)S(1)} %constant_dynamic-update-slice_fusion.refs_1_.refs_7_.refs_9_.refs_5_), channel_id=1, source_target_pairs={{0,1},{1,0},{2,3},{3,2},{4,5},{5,4},{6,7},{7,6},{8,9},{9,8},{10,11... | collective-permute-start | bytes 3145736 | tf_op jit(solution)/shard_map/ppermute | solution.py:24
  37.7 11.7 %collective-permute-start.11 = (bf16[16,8192]{1,0:T(8,128)(2,1)}, bf16[16,8192]{1,0:T(8,128)(2,1)S(1)}, u32[]{:S(2)}, u32[]{:S(2)}) collective-permute-start(bf16[16,8192]{1,0:T(8,128)(2,1)} %get-tuple-element.78), channel_id=1, source_target_pairs={{0,16},{1,17},{2,18},{3,19},{4,20},{5,21},{6,22},{7,23},{8,24},{9,... | collective-permute-start | bytes 786440 | tf_op jit(solution)/shard_map/ppermute | solution.py:24
  40.3 3.6 %copy-start.3 = (bf16[64,8192]{1,0:T(8,128)(2,1)}, bf16[64,8192]{1,0:T(8,128)(2,1)S(1)}, u32[]{:S(2)}) copy-start(bf16[64,8192]{1,0:T(8,128)(2,1)S(1)} %get-tuple-element.72.refs_8_.refs_10_.refs_6_) | copy-start | bytes 3145732
  44.0 3.2 %copy-start.12 = (bf16[512,128]{1,0:T(8,128)(2,1)}, bf16[512,128]{1,0:T(8,128)(2,1)S(1)}, u32[]{:S(2)}) copy-start(bf16[512,128]{1,0:T(8,128)(2,1)S(1)} %get-tuple-element.95.refs_1_) | copy-start | bytes 393220
  44.0 4.6 %collective-permute-start.8 = (bf16[64,3584]{1,0:T(8,128)(2,1)S(1)}, bf16[64,3584]{1,0:T(8,128)(2,1)S(1)}, u32[]{:S(2)}, u32[]{:S(2)}) collective-permute-start(bf16[64,3584]{1,0:T(8,128)(2,1)S(1)} %get-tuple-element.75.refs_1_), channel_id=1, source_target_pairs={{0,1},{1,0},{2,3},{3,2},{4,5},{5,4},{6,7},{7,6},{8,9},{9,8},{10,11... | collective-permute-start | bytes 1376264 | tf_op jit(solution)/shard_map/ppermute | solution.py:24
  49.4 25.0 %collective-permute-start.9 = (bf16[64,3584]{1,0:T(8,128)(2,1)}, bf16[64,3584]{1,0:T(8,128)(2,1)}, u32[]{:S(2)}, u32[]{:S(2)}) collective-permute-start(bf16[64,3584]{1,0:T(8,128)(2,1)} %add_convert_fusion.1.refs_3_), channel_id=1, source_target_pairs={{0,14},{1,15},{2,0},{3,1},{4,2},{5,3},{6,4},{7,5},{8,6},{9,7},{10,... | collective-permute-start | bytes 1376264 | tf_op jit(solution)/shard_map/ppermute | solution.py:24
  49.5 2.7 %copy-start.7 = (bf16[64,8192]{1,0:T(8,128)(2,1)}, bf16[64,8192]{1,0:T(8,128)(2,1)S(1)}, u32[]{:S(2)}) copy-start(bf16[64,8192]{1,0:T(8,128)(2,1)S(1)} %constant_dynamic-update-slice_fusion.4.refs_1_.refs_7_.refs_9_) | copy-start | bytes 3145732
  49.5 2.7 %collective-permute-start.12 = (bf16[64,8192]{1,0:T(8,128)(2,1)S(1)}, bf16[64,8192]{1,0:T(8,128)(2,1)S(1)}, u32[]{:S(2)}, u32[]{:S(2)}) collective-permute-start(bf16[64,8192]{1,0:T(8,128)(2,1)S(1)} %constant_dynamic-update-slice_fusion.4.refs_1_.refs_7_.refs_9_), channel_id=1, source_target_pairs={{0,1},{1,0},{2,3},{3,2},{4,5},{5,4},{6,7},{7,6},{8,9},{9,8},{10,11... | collective-permute-start | bytes 3145736 | tf_op jit(solution)/shard_map/ppermute | solution.py:24
  52.3 3.6 %copy-start.4 = (bf16[64,8192]{1,0:T(8,128)(2,1)}, bf16[64,8192]{1,0:T(8,128)(2,1)S(1)}, u32[]{:S(2)}) copy-start(bf16[64,8192]{1,0:T(8,128)(2,1)S(1)} %get-tuple-element.83.refs_8_.refs_10_) | copy-start | bytes 3145732
  55.9 1.9 %collective-permute-start.13 = (bf16[64,3584]{1,0:T(8,128)(2,1)S(1)}, bf16[64,3584]{1,0:T(8,128)(2,1)S(1)}, u32[]{:S(2)}, u32[]{:S(2)}) collective-permute-start(bf16[64,3584]{1,0:T(8,128)(2,1)S(1)} %get-tuple-element.86.refs_1_), channel_id=1, source_target_pairs={{0,1},{1,0},{2,3},{3,2},{4,5},{5,4},{6,7},{7,6},{8,9},{9,8},{10,11... | collective-permute-start | bytes 1376264 | tf_op jit(solution)/shard_map/ppermute | solution.py:24
  57.9 16.6 %collective-permute-start.14 = (bf16[64,3584]{1,0:T(8,128)(2,1)S(1)}, bf16[64,3584]{1,0:T(8,128)(2,1)S(1)}, u32[]{:S(2)}, u32[]{:S(2)}) collective-permute-start(bf16[64,3584]{1,0:T(8,128)(2,1)S(1)} %add_convert_fusion.refs_1_), channel_id=1, source_target_pairs={{0,14},{1,15},{2,0},{3,1},{4,2},{5,3},{6,4},{7,5},{8,6},{9,7},{10,... | collective-permute-start | bytes 1376264 | tf_op jit(solution)/shard_map/ppermute | solution.py:24
  65.7 1.4 %copy-start.10 = (bf16[128,8192]{1,0:T(8,128)(2,1)}, bf16[128,8192]{1,0:T(8,128)(2,1)S(1)}, u32[]{:S(2)}) copy-start(bf16[128,8192]{1,0:T(8,128)(2,1)S(1)} %get-tuple-element.98.refs_9_) | copy-start | bytes 6291460
  65.7 1.4 %copy-start.14 = (bf16[512,128]{1,0:T(8,128)(2,1)}, bf16[512,128]{1,0:T(8,128)(2,1)S(1)}, u32[]{:S(2)}) copy-start(bf16[512,128]{1,0:T(8,128)(2,1)S(1)} %get-tuple-element.97.refs_3_) | copy-start | bytes 393220
  65.8 15.7 %collective-permute-start.16 = (bf16[128,3584]{1,0:T(8,128)(2,1)S(1)}, bf16[128,3584]{1,0:T(8,128)(2,1)S(1)}, u32[]{:S(2)}, u32[]{:S(2)}) collective-permute-start(bf16[128,3584]{1,0:T(8,128)(2,1)S(1)} %get-tuple-element.94.refs_1_), channel_id=1, source_target_pairs={{0,13},{1,0},{2,15},{3,2},{4,1},{5,4},{6,3},{7,6},{8,5},{9,8},{10,... | collective-permute-start | bytes 2752520 | tf_op jit(solution)/shard_map/ppermute | solution.py:24
  (5 other events, 3.2 us)
